TPU v7x, 128 devices: a whole 4x4x4 slice. The times are simulated.
128 devices in a mesh: ctx: 16 (over z, x), tp: 8 (over y, core).
Axes of the slice: x: 4, y: 4, z: 4, core: 2. Of those that a mesh axis runs over, the one named last changes fastest.
Arguments:
- activations: bfloat16 [8192, 6144], P(('ctx', 'tp')), may hold values from -6 to 6
- w_qkv: bfloat16 [3, 6144, 4096], P(None, None, 'tp'), may hold values from -0.078125 to 0.078125
- log_decay: float32 [8192, 32], P('ctx', 'tp'), may hold values from -0.6 to 0, as said below
- gain: float32 [4096], P('tp'), may hold values from 0.1 to 1.9
- w_out: bfloat16 [4096, 6144], P('tp', 'ctx'), may hold values from -0.09375 to 0.09375
Outputs:
- layer_out: bfloat16 [8192, 6144], P(('ctx', 'tp'))
Inputs may be any that keep to these rules, and one draw needn't show every extreme that they name: `log_decay`: every entry is negative.
All inputs are finite; a program needn't handle non-finite values.
Results may differ from a plain program's by a relative error of at most 0.022.
Values may be sent and summed in bfloat16 or wider, within the bound.
No kernel may reach another device: no remote copies, remote signals or barrier semaphores. Data moves between devices by JAX's collectives and lax.ppermute only.
A program may use at most 128 MiB of HBM per device.

v0:
```python
import jax
import jax.numpy as jnp
from jax import lax
from jax.sharding import PartitionSpec as P

norm_eps = 1e-06


def carried_in(x, axis, join, neutral):
    place = lax.axis_index(axis)
    gathered = jax.tree.map(
        lambda a, kind: lax.all_gather(a.astype(kind), axis), x, (jnp.bfloat16, jnp.bfloat16)
    )
    state = jax.tree.map(lambda a, e: jnp.zeros_like(a) + jnp.asarray(e, a.dtype), x, neutral)

    def one(hop, state):
        return join(
            state,
            jax.tree.map(
                lambda a, own: lax.dynamic_index_in_dim(a, hop, 0, False).astype(own.dtype),
                gathered,
                x,
            ),
        )

    return lax.fori_loop(0, place, one, state)


def body(activations, w_qkv, log_decay, gain, w_out):
    head_count = log_decay.shape[1]
    head_size = w_qkv.shape[2] // head_count
    projected = jnp.einsum(
        "rd,cdh->rch",
        lax.all_gather(activations, "tp", axis=0, tiled=True),
        w_qkv,
        preferred_element_type=jnp.float32,
    )
    row_count = projected.shape[0]
    query = (
        jax.nn.silu(projected[:, 0]).astype(jnp.bfloat16).reshape(row_count, head_count, head_size)
    )
    keys = (
        jax.nn.silu(projected[:, 1]).astype(jnp.bfloat16).reshape(row_count, head_count, head_size)
    )
    values = projected[:, 2].astype(jnp.bfloat16).reshape(row_count, head_count, head_size)
    cumul = jnp.cumsum(log_decay, axis=0)
    final = cumul[-1]
    lower = jnp.arange(row_count)[:, None] >= jnp.arange(row_count)[None, :]
    scores = jnp.einsum("rhd,shd->hrs", query, keys, preferred_element_type=jnp.float32)
    lagged = cumul.T[:, :, None] - cumul.T[:, None, :]
    weight = jnp.where(lower[None], jnp.exp(jnp.minimum(lagged, 0.0)), 0.0)
    probs = (scores * weight).astype(jnp.bfloat16)
    inner = jnp.einsum("hrs,shd->rhd", probs, values, preferred_element_type=jnp.float32)
    scaled_k = keys.astype(jnp.float32) * jnp.exp(final[None, :] - cumul)[:, :, None]
    local_state = jnp.einsum(
        "shd,she->hde", scaled_k, values.astype(jnp.float32), precision=lax.Precision.HIGHEST
    )

    def combine(earlier, later):
        return (earlier[0] + later[0], jnp.exp(later[0])[:, None, None] * earlier[1] + later[1])

    identity = (jnp.zeros_like(final), jnp.zeros_like(local_state))
    _, carried = carried_in((final, local_state), "ctx", combine, identity)
    scaled_q = query.astype(jnp.float32) * jnp.exp(cumul)[:, :, None]
    outer = jnp.einsum("rhd,hde->rhe", scaled_q, carried, precision=lax.Precision.HIGHEST)
    mixed = inner + outer
    scale = lax.rsqrt(jnp.mean(mixed * mixed, axis=-1, keepdims=True) + norm_eps)
    normed = (mixed * scale * gain.reshape(head_count, head_size)).astype(jnp.bfloat16)
    normed = normed.reshape(row_count, head_count * head_size)
    spread = jnp.dot(
        lax.all_gather(normed, "ctx", axis=0, tiled=True), w_out, preferred_element_type=jnp.float32
    ).astype(jnp.bfloat16)
    partial_sum = lax.all_to_all(spread, "ctx", split_axis=0, concat_axis=1, tiled=True)
    widened = lax.optimization_barrier(partial_sum).astype(jnp.float32)
    total = lax.psum_scatter(widened.astype(jnp.bfloat16), "tp", scatter_dimension=0, tiled=True)
    return total


def solution(mesh):
    in_specs = (
        P(("ctx", "tp"), None),
        P(None, None, "tp"),
        P("ctx", "tp"),
        P("tp"),
        P("tp", "ctx"),
    )
    out_specs = P(("ctx", "tp"), None)
    return jax.shard_map(body, mesh=mesh, in_specs=in_specs, out_specs=out_specs, check_vma=False)
```

profile of v0, /device:TPU:1, one launch (start us, length us, event | category | flops | bytes accessed | tf_op | source)
XLA Modules:
  0.0 363.4 jit_solution(10763019707861270314)
XLA Ops:
  6.5 0.0 copy-start
  6.5 0.0 all-gather.6.cloned.1.call-start
  6.5 0.7 all-gather.6.cloned.1.call-update
  7.3 0.0 all-gather.10.cloned.1.call-start
  7.3 0.7 reshape.77
  8.0 1.2 reduce-window.6
  9.2 0.2 slice_reduce_fusion
  9.4 0.2 reduce-window.9
  9.6 0.1 add_bitcast_fusion
  9.6 0.2 slice_reduce_fusion.1
  9.8 0.7 bitcast_exponential_fusion
  10.5 43.1 %all-gather.6.cloned.1.call-done = bf16[512,6144]{1,0:T(8,128)(2,1)} async-done(((bf16[64,6144]{1,0:T(8,128)(2,1)}), bf16[512,6144]{1,0:T(8,128)(2,1)}) %all-gather.6.cloned.1.call-update) | async-done | bytes 6291472 | tf_op jit(solution)/shard_map/all_gather | solution.py:34
  53.7 15.0 %fusion = f32[512,3,512]{0,2,1:T(8,128)S(1)} fusion(bf16[3,6144,512]{2,1,0:T(8,128)(2,1)} %param.8, bf16[512,6144]{1,0:T(8,128)(2,1)} %all-gather.6.cloned.1.call-done), kind=kOutput, calls=%fused_computation.3 | convolution fusion | flops 9663676416 | bytes 28311552 | tf_op jit(solution)/shard_map/rd,cdh->rch/dot_general | solution.py:32
  68.7 0.0 copy-start.1
  68.7 1.7 copy-done.1
  70.3 0.9 slice.36
  71.2 1.7 fusion.13
  72.9 0.3 copy.63
  73.3 3.1 convolution_convert_fusion.1
  76.3 0.0 all-gather.10.cloned.1.call-update
  76.3 0.0 all-gather.8.cloned.1.call-start
  76.4 0.2 fusion.10
  76.6 17.0 %all-gather.1 = bf16[16,1,4]{2,1,0:T(2,128)(2,1)S(1)} all-gather(bf16[1,1,4]{2,1,0:T(2,128)(2,1)S(1)} %bitcast.66), channel_id=1, replica_groups=mesh['ctx'=16,'tp'=8] {'ctx'}, dimensions={0}, use_global_device_ids=true | all-gather | bytes 136 | tf_op jit(solution)/shard_map/all_gather | solution.py:12
  93.5 0.1 copy.64
  93.6 0.7 copy.67
  94.3 0.8 iota_compare_fusion
  95.1 0.3 copy.61
  95.5 4.4 %fusion.2 = f32[4,128,512]{2,1,0:T(8,128)} fusion(bf16[512,4,128]{0,2,1:T(8,128)(2,1)} %bitcast.57, f32[4,512]{1,0:T(4,128)S(1)} %bitcast.61, pred[512,512]{1,0:T(8,128)(4,1)} %iota_compare_fusion, f32[512,4,128]{2,0,1:T(8,128)S(1)} %copy.61, f32[512,4,128]{2,0,1:T(8,128)S(1)} %copy.63), kind=kOutput, calls=%fused_computation.6 | convolution fusion | flops 544735232 | bytes 3940352 | tf_op jit(solution)/shard_map/hrs,shd->rhd/dot_general | solution.py:53
  99.8 0.0 copy-start.2
  99.8 20.5 %all-gather.10.cloned.1.call-done = bf16[64,128,128]{2,1,0:T(8,128)(2,1)} async-done(((bf16[4,128,128]{2,1,0:T(8,128)(2,1)}), bf16[64,128,128]{2,1,0:T(8,128)(2,1)}) %all-gather.10.cloned.1.call-update) | async-done | bytes 2097168 | tf_op jit(solution)/shard_map/all_gather | solution.py:12
  120.4 2.7 multiply_reduce_fusion
  123.1 0.0 copy-done.2
  123.1 0.9 multiply_convert_fusion.1
  124.0 0.0 all-gather.8.cloned.1.call-update
  124.1 0.2 reduce-scatter.2.cloned.1.call-start
  124.3 102.9 %all-gather.8.cloned.1.call-done = bf16[8192,512]{0,1:T(8,128)(2,1)} async-done(((bf16[512,512]{0,1:T(8,128)(2,1)}), bf16[8192,512]{0,1:T(8,128)(2,1)}) %all-gather.8.cloned.1.call-update) | async-done | bytes 8388624 | tf_op jit(solution)/shard_map/all_gather | solution.py:71
  227.2 0.0 copy-done
  227.2 8.0 %convolution_convert_fusion = bf16[8192,384]{1,0:T(8,128)(2,1)S(1)} fusion(bf16[8192,512]{0,1:T(8,128)(2,1)} %all-gather.8.cloned.1.call-done, bf16[512,384]{1,0:T(8,128)(2,1)S(1)} %copy-done), kind=kOutput, calls=%fused_computation.2 | convolution fusion | flops 3224371200 | bytes 15073280 | tf_op jit(solution)/shard_map/dot_general | solution.py:70
  235.2 76.6 %all_to_all.19 = bf16[16,512,384]{2,1,0:T(8,128)(2,1)S(1)} all-to-all(bf16[16,512,384]{2,1,0:T(8,128)(2,1)S(1)} %bitcast.52), channel_id=1, replica_groups=mesh['ctx'=16,'tp'=8] {'ctx'}, dimensions={0} | all-to-all | bytes 12582912 | tf_op jit(solution)/shard_map/all_to_all | solution.py:73
  311.8 3.8 %copy.74 = bf16[16,64,8,384]{3,2,0,1:T(8,128)(2,1)} copy(bf16[16,64,8,384]{3,2,1,0:T(8,128)(2,1)S(1)} %bitcast.51) | data formatting | bytes 12582912 | tf_op jit(solution)/shard_map/all_to_all | solution.py:73
  315.6 0.0 reduce-scatter.2.cloned.1.call-update
  315.6 41.2 %reduce-scatter.2.cloned.1.call-done = bf16[64,6144]{1,0:T(8,128)(2,1)} async-done(((bf16[512,6144]{1,0:T(8,128)(2,1)}), bf16[64,6144]{1,0:T(8,128)(2,1)}) %reduce-scatter.2.cloned.1.call-update) | async-done | bytes 786448 | tf_op jit(solution)/shard_map/reduce_scatter | solution.py:75
  (4 shorter events, 0.0 us)
Async XLA Ops:
  6.5 220.7 %copy-start = (bf16[512,384]{1,0:T(8,128)(2,1)S(1)}, bf16[512,384]{1,0:T(8,128)(2,1)}, u32[]{:S(2)}) copy-start(bf16[512,384]{1,0:T(8,128)(2,1)} %param.11) | copy-start | bytes 1179652
  6.5 47.1 %all-gather.6.cloned.1.call-start = ((), (), s32[]{:S(2)}) async-start(), calls=%async_computation.2 | async-start | bytes 7077888 | tf_op jit(solution)/shard_map/all_gather | solution.py:34
  7.3 113.1 %all-gather.10.cloned.1.call-start = ((), (), s32[]{:S(2)}) async-start(), calls=%async_computation.5 | async-start | bytes 2228224 | tf_op jit(solution)/shard_map/all_gather | solution.py:12
  68.7 1.7 copy-start.1
  76.3 150.9 %all-gather.8.cloned.1.call-start = ((), (), s32[]{:S(2)}) async-start(), calls=%async_computation.3 | async-start | bytes 8912896 | tf_op jit(solution)/shard_map/all_gather | solution.py:71
  99.8 23.3 %copy-start.2 = (f32[512]{0:T(512)S(1)}, f32[512]{0:T(512)}, u32[]{:S(2)}) copy-start(f32[512]{0:T(512)} %param.10) | copy-start | bytes 6148
  124.1 232.8 %reduce-scatter.2.cloned.1.call-start = ((), (), s32[]{:S(2)}) async-start(), calls=%async_computation.4 | async-start | bytes 7077888 | tf_op jit(solution)/shard_map/reduce_scatter | solution.py:75
Sparse Core Ops, SparseCore 0:
  9.0 44.5 all-gather.5
  76.5 43.8 all-gather.9
  124.2 102.9 all-gather.7
  315.7 41.0 reduce-scatter.1
where the time goes:
time: 364 us; the launch traced here: 363 us
  waiting for transfers between devices  209 us (57%)
  blocking collectives  93.6 us (26%)
  matrix products  33.1 us (9%)
  between operations  13.2 us (4%)
  local copies, waits for them, and re-layouts  10.8 us (3%)
  other arithmetic  3.9 us (1%)
    all_gather x1, waiting for transfers between devices, body(): lax.all_gather(normed, 'ctx', axis=0, tiled=True)  103 us
    all_to_all x1, blocking collectives, body(): lax.all_to_all(spread, 'ctx', split_axis=0, concat_axis=1, tiled=True)  76.6 us
    all_gather x1, waiting for transfers between devices, body(): lax.all_gather(activations, 'tp', axis=0, tiled=True)  43.1 us
    reduce_scatter x1, waiting for transfers between devices, body(): lax.psum_scatter(widened.astype(jnp.bfloat16), 'tp', scatter_dimension=0,...  41.2 us
    all_gather x1, waiting for transfers between devices, carried_in(): lax.all_gather(a.astype(kind), axis)  20.5 us
    all_gather x1, blocking collectives, carried_in(): lax.all_gather(a.astype(kind), axis)  17 us
    dot_general x1, matrix products, body(): jnp.einsum('rd,cdh->rch', lax.all_gather(activations, 'tp', axis=0, tiled...  15 us
    dot_general x1, matrix products, body(): jnp.dot(lax.all_gather(normed, 'ctx', axis=0, tiled=True), w_out, preferr...  7.95 us
  transfers between devices with their start and end apart: 4, of which 4 were waited for; matrix products, arithmetic and copies ran while one was open for 3% of the time, Pallas kernels for 0%

commit v1 on v0

v1 whole, which is shorter than its diff:
```python
import jax
import jax.numpy as jnp
from jax import lax
from jax.sharding import PartitionSpec as P

norm_eps = 1e-06


def body(activations, w_qkv, log_decay, gain, w_out):
    heads = log_decay.shape[1]
    size = w_qkv.shape[2] // heads
    place = lax.axis_index("ctx")
    n_ctx = lax.axis_size("ctx")
    x = lax.all_gather(activations, "tp", axis=0, tiled=True)
    w_all = lax.all_gather(w_out, "ctx", axis=0)
    rows = x.shape[0]
    cumul = jnp.cumsum(log_decay.T, axis=1)
    final = cumul[:, -1]
    finals = lax.all_gather(final, "ctx")

    def split(a):
        return a.reshape(rows, heads, size)

    keys = split(jax.nn.silu(jnp.dot(x, w_qkv[1], preferred_element_type=jnp.float32)).astype(jnp.bfloat16))
    values = split(jnp.dot(x, w_qkv[2], preferred_element_type=jnp.float32).astype(jnp.bfloat16))
    scaled_k = (keys.astype(jnp.float32) * jnp.exp(final[:, None] - cumul).T[:, :, None]).astype(jnp.bfloat16)
    local_state = jnp.einsum("shd,she->hde", scaled_k, values, preferred_element_type=jnp.float32)
    states = lax.all_gather(local_state.astype(jnp.bfloat16), "ctx")
    block = jnp.arange(n_ctx)
    between = (block[None, :] > block[:, None]) & (block[None, :] < place)
    span = jnp.sum(jnp.where(between[:, :, None], finals[None], 0.0), axis=1)
    reach = jnp.where((block < place)[:, None], jnp.exp(span), 0.0)
    query = split(jax.nn.silu(jnp.dot(x, w_qkv[0], preferred_element_type=jnp.float32)).astype(jnp.bfloat16))
    scores = jnp.einsum("rhd,shd->hrs", query, keys, preferred_element_type=jnp.float32)
    lower = jnp.arange(rows)[:, None] >= jnp.arange(rows)[None, :]
    lagged = cumul[:, :, None] - cumul[:, None, :]
    weight = jnp.where(lower[None], jnp.exp(jnp.minimum(lagged, 0.0)), 0.0)
    probs = (scores * weight).astype(jnp.bfloat16)
    inner = jnp.einsum("hrs,shd->hrd", probs, values, preferred_element_type=jnp.float32)
    scaled_q = (query.astype(jnp.float32) * jnp.exp(cumul).T[:, :, None]).astype(jnp.bfloat16)
    carried = jnp.sum(states.astype(jnp.float32) * reach[:, :, None, None], axis=0)
    outer = jnp.einsum("rhd,hde->hre", scaled_q, carried.astype(jnp.bfloat16), preferred_element_type=jnp.float32)
    mixed = inner + outer
    scale = lax.rsqrt(jnp.mean(mixed * mixed, axis=-1, keepdims=True) + norm_eps)
    normed = (mixed * scale * gain.reshape(heads, 1, size)).astype(jnp.bfloat16)
    normed = normed.transpose(1, 0, 2).reshape(rows, heads * size)
    parts = jnp.einsum("rh,chd->rcd", normed, w_all, preferred_element_type=jnp.float32).astype(jnp.bfloat16)
    parts = parts.reshape(rows, -1)
    return lax.psum_scatter(parts, "tp", scatter_dimension=0, tiled=True)


def solution(mesh):
    in_specs = (
        P(("ctx", "tp"), None),
        P(None, None, "tp"),
        P("ctx", "tp"),
        P("tp"),
        P("tp", "ctx"),
    )
    out_specs = P(("ctx", "tp"), None)
    return jax.shard_map(body, mesh=mesh, in_specs=in_specs, out_specs=out_specs, check_vma=False)
```

time: 364 us -> 244 us (0.67)
  waiting for transfers between devices: 209 us -> 144 us
  blocking collectives: 93.6 us -> 33.7 us
    all_to_all x1 -> x0, blocking collectives: 76.6 us -> none  [body(): lax.all_to_all(spread, 'ctx', split_axis=0, concat_axis=1, tiled=True)]
    all_gather x3, waiting for transfers between devices: 167 us -> 101 us  [the longest x1 57.6 us: body(): w_all = lax.all_gather(w_out, 'ctx', axis=0)]
    unnamed x0 -> x1, blocking collectives: none -> 33.7 us
    all_gather x1 -> x0, blocking collectives: 17 us -> none  [carried_in(): lax.all_gather(a.astype(kind), axis)]
    reshape x1 -> x3, local copies, waits for them, and re-layouts: 0.71 us -> 9.68 us  [the longest x1 8.7 us: body(): parts = parts.reshape(rows, -1)]
    all_to_all x1 -> x0, local copies, waits for them, and re-layouts: 3.82 us -> none  [body(): lax.all_to_all(spread, 'ctx', split_axis=0, concat_axis=1, tiled=True)]
    dot_general x5 -> x7, matrix products: 33.1 us -> 36 us  [the longest x1 9.62 us: body(): jnp.einsum('rh,chd->rcd', normed, w_all, preferred_element_type=jnp.float32)]
  transfers between devices with their start and end apart: 4 -> 4, of which waited for: 4 -> 3; matrix products, arithmetic and copies ran while one was open for 3% -> 7% of each run, Pallas kernels for 0% -> 0%
where the time goes in v1:
time: 244 us; the launch traced here: 243 us
  waiting for transfers between devices  144 us (59%)
  matrix products  36 us (15%)
  blocking collectives  33.7 us (14%)
  between operations  13.9 us (6%)
  local copies, waits for them, and re-layouts  11 us (5%)
  other arithmetic  3.96 us (2%)
    all_gather x1, waiting for transfers between devices, body(): w_all = lax.all_gather(w_out, 'ctx', axis=0)  57.6 us
    all_gather x1, waiting for transfers between devices, body(): x = lax.all_gather(activations, 'tp', axis=0, tiled=True)  43.8 us
    reduce_scatter x1, waiting for transfers between devices, body(): return lax.psum_scatter(parts, 'tp', scatter_dimension=0, tiled=True)  41.6 us
    unnamed x1, blocking collectives  33.7 us
    dot_general x1, matrix products, body(): jnp.einsum('rh,chd->rcd', normed, w_all, preferred_element_type=jnp.float32)  9.62 us
    reshape x1, local copies, waits for them, and re-layouts, body(): parts = parts.reshape(rows, -1)  8.7 us
    dot_general x1, matrix products, body(): jnp.dot(x, w_qkv[0], preferred_element_type=jnp.float32)  8.34 us
    dot_general x1, matrix products, body(): jnp.dot(x, w_qkv[1], preferred_element_type=jnp.float32)  8.34 us
  transfers between devices with their start and end apart: 4, of which 3 were waited for; matrix products, arithmetic and copies ran while one was open for 7% of the time, Pallas kernels for 0%

profile of v1, /device:TPU:1, one launch (start us, length us, event | category | flops | bytes accessed | tf_op | source)
XLA Modules:
  0.0 243.2 jit_solution(17983521743780653314)
XLA Ops:
  6.5 0.0 all-gather.7.cloned.1.call-start
  6.5 0.7 all-gather.7.cloned.1.call-update
  7.3 0.0 all-gather.9.cloned.1.call-start
  7.3 0.7 reshape.128
  8.0 1.2 reduce-window.6
  9.2 0.2 slice_reduce_fusion
  9.4 0.2 reduce-window.9
  9.6 0.1 add_bitcast_fusion
  9.6 0.1 slice.25
  9.7 0.1 copy.44
  9.8 0.1 exponential_bitcast_fusion
  9.9 43.8 %all-gather.7.cloned.1.call-done = bf16[512,6144]{1,0:T(8,128)(2,1)} async-done(((bf16[64,6144]{1,0:T(8,128)(2,1)}), bf16[512,6144]{1,0:T(8,128)(2,1)}) %all-gather.7.cloned.1.call-update) | async-done | bytes 6291472 | tf_op jit(solution)/shard_map/all_gather | solution.py:14
  53.7 0.0 copy-start.1
  53.7 8.3 %multiply_convert_fusion.3 = bf16[512,512]{0,1:T(8,128)(2,1)S(1)} fusion(bf16[512,6144]{1,0:T(8,128)(2,1)} %all-gather.7.cloned.1.call-done, bf16[3,6144,512]{2,1,0:T(8,128)(2,1)} %param.6), kind=kOutput, calls=%fused_computation.24 | convolution fusion | flops 3222536192 | bytes 13107200 | tf_op jit(solution)/shard_map/dot_general | solution.py:24
  62.0 0.0 copy-done.1
  62.0 0.0 copy-start.2
  62.1 5.7 %fusion.11 = bf16[512,512]{0,1:T(8,128)(2,1)S(1)} fusion(bf16[512,6144]{1,0:T(8,128)(2,1)S(1)} %copy-done.1, bf16[3,6144,512]{2,1,0:T(8,128)(2,1)} %param.6), kind=kOutput, calls=%fused_computation.15 | convolution fusion | flops 3221487616 | bytes 13107200 | tf_op jit(solution)/shard_map/dot_general | solution.py:25
  67.8 1.0 convolution_convert_fusion.1
  68.7 0.0 all-gather.9.cloned.1.call-update
  68.8 0.0 all-gather.11.cloned.1.call-start
  68.8 0.7 all-gather.11.cloned.1.call-update
  69.5 0.0 reduce-scatter.2.cloned.1.call-start
  69.6 0.0 copy-done.2
  69.6 0.6 dynamic-slice
  70.9 0.1 bitcast_dynamic-update-slice_fusion
  71.0 33.7 %all-reduce = f32[64]{0:T(128)S(1)} all-reduce(f32[64]{0:T(128)S(1)} %bitcast_dynamic-update-slice_fusion), channel_id=3, replica_groups=mesh['ctx'=16,'tp'=8] {'ctx'}, use_global_device_ids=true, to_apply=%add | all-reduce | flops 64 | bytes 512
  104.7 0.1 reshape.134
  104.8 0.1 copy.31
  104.9 0.1 select_reduce_fusion
  105.0 0.1 copy.32
  105.1 0.1 iota_compare_fusion
  105.2 8.3 %multiply_convert_fusion.4 = bf16[512,512]{0,1:T(8,128)(2,1)S(1)} fusion(bf16[512,6144]{1,0:T(8,128)(2,1)} %all-gather.7.cloned.1.call-done, bf16[3,6144,512]{2,1,0:T(8,128)(2,1)} %param.6), kind=kOutput, calls=%fused_computation.25 | convolution fusion | flops 3222536192 | bytes 13107200 | tf_op jit(solution)/shard_map/dot_general | solution.py:33
  113.5 0.3 copy.28
  113.8 0.0 copy-start
  113.8 2.1 fusion.10
  115.9 0.0 all-gather.9.cloned.1.call-done
  115.9 2.1 fusion.9
  118.0 0.9 multiply_reduce_fusion
  118.9 0.0 copy-done
  118.9 0.2 fusion.15
  119.1 57.6 %all-gather.11.cloned.1.call-done = bf16[8192,384]{1,0:T(8,128)(2,1)} async-done(((bf16[512,384]{1,0:T(8,128)(2,1)}), bf16[8192,384]{1,0:T(8,128)(2,1)}) %all-gather.11.cloned.1.call-update) | async-done | bytes 6291472 | tf_op jit(solution)/shard_map/all_gather | solution.py:15
  176.7 9.6 %convolution_convert_fusion = bf16[512,16,384]{0,2,1:T(8,128)(2,1)} fusion(bf16[512,512,1]{0,1,2:T(8,128)(2,1)S(1)} %bitcast.66, bf16[16,512,384]{2,1,0:T(8,128)(2,1)} %bitcast.73), kind=kOutput, calls=%fused_computation.12 | convolution fusion | flops 3224371200 | bytes 13107200 | tf_op jit(solution)/shard_map/rh,chd->rcd/dot_general | solution.py:47
  186.3 8.7 %copy.36 = bf16[512,6144]{1,0:T(8,128)(2,1)} copy(bf16[512,6144]{0,1:T(8,128)(2,1)} %bitcast.62) | data formatting | bytes 12582912 | tf_op jit(solution)/shard_map/reshape | solution.py:48
  195.0 0.0 reduce-scatter.2.cloned.1.call-update
  195.0 41.6 %reduce-scatter.2.cloned.1.call-done = bf16[64,6144]{1,0:T(8,128)(2,1)} async-done(((bf16[512,6144]{1,0:T(8,128)(2,1)}), bf16[64,6144]{1,0:T(8,128)(2,1)}) %reduce-scatter.2.cloned.1.call-update) | async-done | bytes 786448 | tf_op jit(solution)/shard_map/reduce_scatter | solution.py:49
  (6 shorter events, 0.0 us)
Async XLA Ops:
  6.5 47.1 %all-gather.7.cloned.1.call-start = ((), (), s32[]{:S(2)}) async-start(), calls=%async_computation.1 | async-start | bytes 7077888 | tf_op jit(solution)/shard_map/all_gather | solution.py:14
  7.3 108.7 %all-gather.9.cloned.1.call-start = ((), (), s32[]{:S(2)}) async-start(), calls=%async_computation.3 | async-start | bytes 2228224 | tf_op jit(solution)/shard_map/all_gather | solution.py:28
  53.7 8.4 %copy-start.1 = (bf16[512,6144]{1,0:T(8,128)(2,1)S(1)}, bf16[512,6144]{1,0:T(8,128)(2,1)}, u32[]{:S(2)}) copy-start(bf16[512,6144]{1,0:T(8,128)(2,1)} %all-gather.7.cloned.1.call-done) | copy-start | bytes 18874372
  62.0 7.5 %copy-start.2 = (u32[128]{0:T(128)S(1)}, u32[128]{0:T(128)}, u32[]{:S(2)}) copy-start(u32[128]{0:T(128)} %constant.25) | copy-start | bytes 1540
  68.8 107.9 %all-gather.11.cloned.1.call-start = ((), (), s32[]{:S(2)}) async-start(), calls=%async_computation.4 | async-start | bytes 6684672 | tf_op jit(solution)/shard_map/all_gather | solution.py:15
  69.5 167.1 %reduce-scatter.2.cloned.1.call-start = ((), (), s32[]{:S(2)}) async-start(), calls=%async_computation.2 | async-start | bytes 7077888 | tf_op jit(solution)/shard_map/reduce_scatter | solution.py:49
  113.8 5.1 %copy-start = (f32[512]{0:T(512)S(1)}, f32[512]{0:T(512)}, u32[]{:S(2)}) copy-start(f32[512]{0:T(512)} %param.8) | copy-start | bytes 6148
Sparse Core Ops, SparseCore 0:
  9.0 44.5 all-gather.6
  68.9 43.8 all-gather.8
  114.9 61.7 all-gather.10
  195.1 41.4 reduce-scatter.1

commit v2 on v1

v2 whole, which is shorter than its diff:
```python
import functools

import jax
import jax.numpy as jnp
from jax import lax
from jax.experimental import pallas as pl
from jax.experimental.pallas import tpu as pltpu
from jax.sharding import PartitionSpec as P

norm_eps = 1e-06
f32, bf16 = jnp.float32, jnp.bfloat16
HEADS, SIZE = 4, 128
WIDE = HEADS * SIZE
N_X = N_Z = N_Y = 4
VMEM_LIMIT = 40 * 2**20


def params(**kw):
    return pltpu.CompilerParams(vmem_limit_bytes=VMEM_LIMIT, **kw)


def cost(flops, nbytes):
    return pl.CostEstimate(flops=flops, bytes_accessed=nbytes, transcendentals=0)


def to_y(a, k):
    return lax.ppermute(a, "tp", [(i, (i // 2 + k) % N_Y * 2 + i % 2) for i in range(2 * N_Y)])


def to_sibling(a):
    return lax.ppermute(a, "tp", [(i, i ^ 1) for i in range(2 * N_Y)])


def to_x(a, k):
    return lax.ppermute(a, "ctx", [(j, j // N_X * N_X + (j + k) % N_X) for j in range(N_X * N_Z)])


def to_z(a, k):
    return lax.ppermute(a, "ctx", [(j, j + N_X * k) for j in range(N_X * N_Z) if j // N_X + k < N_Z])


def qkv_kernel(layout, *refs):
    pieces, w, out, rows = refs[: len(layout)], refs[len(layout)], refs[-2], refs[-1]
    step = pl.program_id(0)

    @pl.when(step == 0)
    def _():
        for piece, (row, col) in zip(pieces, layout):
            rows[row : row + piece.shape[0], col : col + piece.shape[1]] = piece[...]

    acc = jnp.dot(rows[...], w[0], preferred_element_type=f32)
    gated = acc / (1.0 + jnp.exp(-acc))
    out[...] = jnp.where(step < 4, gated, acc).astype(bf16)


def qkv(pieces, layout, count, w_qkv, block, held=None):
    depth = w_qkv.shape[1]
    tile = 256
    per = WIDE // tile
    kept = () if held is None else (held,)
    return pl.pallas_call(
        functools.partial(qkv_kernel, layout),
        grid=(3 * per,),
        out_shape=jax.ShapeDtypeStruct((512, 3 * WIDE), bf16),
        in_specs=[pl.BlockSpec(p.shape, lambda j: (0, 0)) for p in pieces]
        + [pl.BlockSpec((1, depth, tile), lambda j: (j // per, 0, j % per))]
        + [pl.BlockSpec(memory_space=pl.ANY)] * len(kept),
        out_specs=pl.BlockSpec((count, tile), lambda j: (block, j)),
        input_output_aliases={len(pieces) + 1: 0} if kept else {},
        scratch_shapes=[pltpu.VMEM((count, depth), bf16)],
        compiler_params=params(),
        cost_estimate=cost(2 * count * depth * 3 * WIDE, 3 * WIDE * depth * 2),
        name="qkv",
    )(*pieces, w_qkv, *kept)


def pack(out, last):
    high = last.astype(bf16).astype(f32)
    mid = (last - high).astype(bf16).astype(f32)
    low = last - high - mid
    out[WIDE:, :] = jnp.concatenate([high, mid, low, jnp.zeros_like(low)], axis=0).astype(bf16)


def unpack(ref):
    tail = ref[WIDE:, :].astype(f32)
    return tail[0:4] + tail[4:8] + tail[8:12]


def state_kernel(rows, g, last, out):
    for h in range(HEADS):
        keys = rows[:, WIDE + h * SIZE : WIDE + (h + 1) * SIZE].astype(f32)
        values = rows[:, 2 * WIDE + h * SIZE : 2 * WIDE + (h + 1) * SIZE]
        scaled = (keys * jnp.exp(last[h : h + 1, 0:1] - g[:, h : h + 1])).astype(bf16)
        state = lax.dot_general(scaled, values, (((0,), (0,)), ((), ())), preferred_element_type=f32)
        out[h * SIZE : (h + 1) * SIZE, :] = state.astype(bf16)
    pack(out, last[...])


def inner_kernel(at, rows, g, gt, out):
    def position(idx):
        chunk = idx >> 7
        ahead = jnp.where(chunk == 0, 1, jnp.where(chunk == 1, 3, jnp.where(chunk == 2, 0, 2)))
        return ((at[0] + ahead) & 3) * 128 + ((at[1] + (idx >> 6)) & 1) * 64 + (idx & 63)

    n = g.shape[0]
    row = position(lax.broadcasted_iota(jnp.int32, (n, 1), 0))
    col = position(lax.broadcasted_iota(jnp.int32, (1, n), 1))
    lower = row >= col
    for h in range(HEADS):
        query = rows[:, h * SIZE : (h + 1) * SIZE]
        keys = rows[:, WIDE + h * SIZE : WIDE + (h + 1) * SIZE]
        values = rows[:, 2 * WIDE + h * SIZE : 2 * WIDE + (h + 1) * SIZE]
        scores = lax.dot_general(query, keys, (((1,), (1,)), ((), ())), preferred_element_type=f32)
        lagged = g[:, h : h + 1] - gt[h : h + 1, :]
        probs = jnp.where(lower, scores * jnp.exp(jnp.minimum(lagged, 0.0)), 0.0).astype(bf16)
        out[:, h * SIZE : (h + 1) * SIZE] = jnp.dot(probs, values, preferred_element_type=f32)


def row_kernel(at, s0, s1, s2, s3, before, total):
    refs = (s0, s1, s2, s3)
    x = at[2]
    place = [(x - k) & 3 for k in range(N_X)]
    last = [unpack(ref) for ref in refs]

    def between(k, end):
        return sum(jnp.where((place[m] > place[k]) & (place[m] < end), last[m], 0.0) for m in range(N_X))

    reach = [jnp.where(place[k] < x, jnp.exp(between(k, x)), 0.0) for k in range(N_X)]
    whole = [jnp.exp(between(k, N_X)) for k in range(N_X)]
    for h in range(HEADS):
        rows = slice(h * SIZE, (h + 1) * SIZE)
        states = [ref[rows, :].astype(f32) for ref in refs]
        before[rows, :] = sum(states[k] * reach[k][h : h + 1] for k in range(1, N_X))
        total[rows, :] = sum(states[k] * whole[k][h : h + 1] for k in range(N_X)).astype(bf16)
    pack(total, last[0] + last[1] + last[2] + last[3])
    lead = sum(jnp.where(place[k] < x, last[k], 0.0) for k in range(1, N_X))
    before[WIDE:, :] = jnp.concatenate([lead, lead], axis=0)


def normed_kernel(before, t1, t2, t3, qkv, g, inner, gain, out):
    lead = jnp.exp(before[WIDE : WIDE + HEADS, :])
    r1, r2 = unpack(t1), unpack(t2)
    reach2, reach3 = jnp.exp(r1), jnp.exp(r1 + r2)
    for h in range(HEADS):
        rows = slice(h * SIZE, (h + 1) * SIZE)
        one = slice(h, h + 1)
        earlier = (
            t1[rows, :].astype(f32) + t2[rows, :].astype(f32) * reach2[one] + t3[rows, :].astype(f32) * reach3[one]
        )
        carried = (earlier * lead[one] + before[rows, :]).astype(bf16)
        query = qkv[:, rows].astype(f32)
        scaled = (query * jnp.exp(g[:, one])).astype(bf16)
        mixed = inner[:, rows] + jnp.dot(scaled, carried, preferred_element_type=f32)
        scale = lax.rsqrt(jnp.mean(mixed * mixed, axis=-1, keepdims=True) + norm_eps)
        out[:, rows] = (mixed * scale * gain[:, rows]).astype(bf16)


def whole_call(kernel, args, outs, name, flops, scalars=0):
    nbytes = sum(a.size * a.dtype.itemsize for a in args)
    return pl.pallas_call(
        kernel,
        out_shape=outs,
        in_specs=[pl.BlockSpec(memory_space=pltpu.SMEM)] * scalars
        + [pl.BlockSpec(memory_space=pltpu.VMEM)] * (len(args) - scalars),
        out_specs=jax.tree.map(lambda _: pl.BlockSpec(memory_space=pltpu.VMEM), outs),
        compiler_params=params(),
        cost_estimate=cost(flops, nbytes),
        name=name,
    )(*args)


def project_kernel(n, per, *refs):
    chunks, w, outs = refs[:n], refs[n], refs[n + 1 :]
    rows = jnp.concatenate([chunk[...] for chunk in chunks], axis=0)
    width = w.shape[2]
    for m in range(per):
        part = jnp.dot(rows, w[m], preferred_element_type=f32).astype(bf16)
        for i, out in enumerate(outs):
            out[:, m * width : (m + 1) * width] = part[i * 64 : (i + 1) * 64]


def project(normed, w_all, places):
    n_ctx, depth, width = w_all.shape
    per = 4
    half = jax.ShapeDtypeStruct((64, n_ctx * width), bf16)
    n = len(places)
    return pl.pallas_call(
        functools.partial(project_kernel, n, per),
        grid=(n_ctx // per,),
        out_shape=[half] * (2 * n),
        in_specs=[pl.BlockSpec((128, depth), lambda j, r=r: (r, 0)) for r in places]
        + [pl.BlockSpec((per, depth, width), lambda j: (j, 0, 0))],
        out_specs=[pl.BlockSpec((64, per * width), lambda j: (0, j))] * (2 * n),
        compiler_params=params(),
        cost_estimate=cost(2 * n * 128 * depth * n_ctx * width, 2 * depth * n_ctx * width),
        name="project",
    )(*[normed] * n, w_all)


def plus(*terms):
    total = terms[0].astype(f32)
    for term in terms[1:]:
        total = total + term.astype(f32)
    return total.astype(bf16)


def body(activations, w_qkv, log_decay, gain, w_out):
    tp, ctx = lax.axis_index("tp"), lax.axis_index("ctx")
    y, core = tp // 2, tp % 2
    at = jnp.stack([y, core, ctx % N_X]).astype(jnp.int32)
    w_all = lax.all_gather(w_out, "ctx", axis=0)

    cumul = jnp.cumsum(log_decay.T, axis=1)
    last = jnp.broadcast_to(cumul[:, -1:], (HEADS, SIZE))
    gt = jnp.roll(cumul.reshape(HEADS, N_Y, 2, 64), -y, axis=1)
    gt = jnp.where(core == 0, gt, gt[:, :, ::-1])
    gt = jnp.stack([gt[:, 1], gt[:, 3], gt[:, 0], gt[:, 2]], axis=1).reshape(HEADS, 512)
    g = gt.T

    mid = activations.shape[1] // 2
    left, right = to_y(activations, 1), to_y(activations, -1)
    own2 = to_sibling(activations)
    rows = qkv([activations, own2], [(0, 0), (64, 0)], 128, w_qkv, 2)
    left, right, rows = lax.optimization_barrier((left, right, rows))
    far_l, far_r = to_y(left[:, :mid], 1), to_y(right[:, mid:], -1)
    left2, right2 = to_sibling(left), to_sibling(right)
    rows = qkv([right, right2, left, left2], [(0, 0), (64, 0), (128, 0), (192, 0)], 256, w_qkv, 0, rows)
    far_l, far_r, rows = lax.optimization_barrier((far_l, far_r, rows))
    far_l2, far_r2 = to_sibling(far_l), to_sibling(far_r)
    rows = qkv([far_l, far_r, far_l2, far_r2], [(0, 0), (0, mid), (64, 0), (64, mid)], 128, w_qkv, 3, rows)

    packed = jax.ShapeDtypeStruct((WIDE + 16, SIZE), bf16)
    state = whole_call(state_kernel, (rows, g, last), packed, "state", 2 * 512 * WIDE * SIZE)
    row = [state] + [to_x(state, k) for k in range(1, N_X)]
    inner = whole_call(
        inner_kernel, (at, rows, g, gt), jax.ShapeDtypeStruct((512, WIDE), f32), "inner", 4 * 512 * 512 * WIDE, 1
    )
    before, total = whole_call(
        row_kernel, (at, *row), (jax.ShapeDtypeStruct((WIDE + 8, SIZE), f32), packed), "row", 10 * WIDE * SIZE, 1
    )
    totals = [to_z(total, k) for k in range(1, N_Z)]
    normed = whole_call(
        normed_kernel,
        (before, *totals, rows, g, inner, gain.reshape(1, WIDE)),
        jax.ShapeDtypeStruct((512, WIDE), bf16),
        "normed",
        2 * 512 * WIDE * SIZE,
    )

    far_own, far_sib = project(normed, w_all, (3,))
    far = plus(far_own, to_sibling(far_sib))
    from_l, from_r = to_y(far[:, :mid], 1), to_y(far[:, mid:], -1)
    up_own, up_sib, down_own, down_sib = project(normed, w_all, (0, 1))
    up, down = plus(up_own, to_sibling(up_sib)), plus(down_own, to_sibling(down_sib))
    up_plain, down_plain = to_y(up[:, mid:], 1), to_y(down[:, :mid], -1)
    up_sum, down_sum = to_y(plus(up[:, :mid], from_l), 1), to_y(plus(down[:, mid:], from_r), -1)
    normed, up, down = lax.optimization_barrier((normed, up, down))
    here_own, here_sib = project(normed, w_all, (2,))
    here_sib = to_sibling(here_sib)
    first = plus(here_own[:, :mid], here_sib[:, :mid], down_plain, up_sum)
    second = plus(here_own[:, mid:], here_sib[:, mid:], up_plain, down_sum)
    return jnp.concatenate([first, second], axis=1)


def solution(mesh):
    in_specs = (
        P(("ctx", "tp"), None),
        P(None, None, "tp"),
        P("ctx", "tp"),
        P("tp"),
        P("tp", "ctx"),
    )
    out_specs = P(("ctx", "tp"), None)
    return jax.shard_map(body, mesh=mesh, in_specs=in_specs, out_specs=out_specs, check_vma=False)
```

time: 244 us -> 143 us (0.59)
  waiting for transfers between devices: 144 us -> 44.2 us
  Pallas kernels: 0 us -> 41.2 us
  matrix products: 36 us -> 0 us
  blocking collectives: 33.7 us -> 0 us
  starting transfers between devices: 0.12 us -> 31.7 us
  local copies, waits for them, and re-layouts: 11 us -> 7.93 us
    all_gather x1, waiting for transfers between devices: 57.6 us -> 0.02 us  [body(): w_all = lax.all_gather(w_out, 'ctx', axis=0)]
    all_gather x2 -> x0, waiting for transfers between devices: 43.8 us -> none  [the longest x1 43.8 us: body(): x = lax.all_gather(activations, 'tp', axis=0, tiled=True)]
    ppermute x0 -> x25, waiting for transfers between devices: none -> 43.5 us  [the longest x10 30.4 us: to_y(): lax.ppermute(a, 'tp', [(i, (i // 2 + k) % N_Y * 2 + i % 2) for i in range...]
    reduce_scatter x1 -> x0, waiting for transfers between devices: 41.6 us -> none  [body(): return lax.psum_scatter(parts, 'tp', scatter_dimension=0, tiled=True)]
    pallas_call x0 -> x10, Pallas kernels: none -> 41.2 us  [the longest x3 29.5 us: qkv(): pl.pallas_call(functools.partial(qkv_kernel, layout), grid=(3 * per,), ou...]
    dot_general x7 -> x0, matrix products: 36 us -> none  [the longest x1 9.62 us: body(): jnp.einsum('rh,chd->rcd', normed, w_all, preferred_element_type=jnp.float32)]
    unnamed x1 -> x0, blocking collectives: 33.7 us -> none
    ppermute x0 -> x25, starting transfers between devices: none -> 31.7 us  [the longest x3 10.6 us: to_z(): lax.ppermute(a, 'ctx', [(j, j + N_X * k) for j in range(N_X * N_Z) if j /...]
  transfers between devices with their start and end apart: 4 -> 26, of which waited for: 3 -> 12; matrix products, arithmetic and copies ran while one was open for 7% -> 5% of each run, Pallas kernels for 0% -> 28%
where the time goes in v2:
time: 143 us
  waiting for transfers between devices  44.2 us (31%)
  Pallas kernels  41.2 us (29%)
  starting transfers between devices  31.7 us (22%)
  between operations  13.7 us (10%)
  local copies, waits for them, and re-layouts  7.93 us (6%)
  other arithmetic  3.82 us (3%)
    ppermute x10, waiting for transfers between devices, to_y(): lax.ppermute(a, 'tp', [(i, (i // 2 + k) % N_Y * 2 + i % 2) for i in range...  30.4 us
    pallas_call x3, Pallas kernels, qkv(): pl.pallas_call(functools.partial(qkv_kernel, layout), grid=(3 * per,), ou...  29.5 us
    ppermute x3, waiting for transfers between devices, to_x(): lax.ppermute(a, 'ctx', [(j, j // N_X * N_X + (j + k) % N_X) for j in rang...  11.4 us
    ppermute x3, starting transfers between devices, to_z(): lax.ppermute(a, 'ctx', [(j, j + N_X * k) for j in range(N_X * N_Z) if j /...  10.6 us
    ppermute x10, starting transfers between devices, to_y(): lax.ppermute(a, 'tp', [(i, (i // 2 + k) % N_Y * 2 + i % 2) for i in range...  10.5 us
    pallas_call x3, Pallas kernels, project(): pl.pallas_call(functools.partial(project_kernel, n, per), grid=(n_ctx //...  6.71 us
    ppermute x9, starting transfers between devices, to_sibling(): return lax.ppermute(a, 'tp', [(i, i ^ 1) for i in range(2 * N_Y)])  6.28 us
    pallas_call x4, Pallas kernels, whole_call(): pl.pallas_call(kernel, out_shape=outs, in_specs=[pl.BlockSpec(memory_spac...  4.98 us
  transfers between devices with their start and end apart: 26, of which 12 were waited for; matrix products, arithmetic and copies ran while one was open for 5% of the time, Pallas kernels for 28%

profile of v2, /device:TPU:1, one launch (start us, length us, event | category | flops | bytes accessed | tf_op | source)
XLA Modules:
  0.0 142.5 jit_solution(9928362217642174716)
XLA Ops:
  6.5 0.7 all-gather.3.cloned.1.call-update
  7.3 1.5 %collective-permute-start.2 = (bf16[64,6144]{1,0:T(8,128)(2,1)}, bf16[64,6144]{1,0:T(8,128)(2,1)S(1)}, u32[]{:S(2)}, u32[]{:S(2)}) collective-permute-start(bf16[64,6144]{1,0:T(8,128)(2,1)} %refs_0_.1), channel_id=1, source_target_pairs={{0,1},{1,0},{2,3},{3,2},{4,5},{5,4},{6,7},{7,6},{8,9},{9,8},{10,11... | collective-permute-start | bytes 2359304 | tf_op jit(solution)/shard_map/ppermute | solution.py:31
  8.8 1.4 collective-permute-start
  10.2 1.4 %collective-permute-start.1 = (bf16[64,6144]{1,0:T(8,128)(2,1)}, bf16[64,6144]{1,0:T(8,128)(2,1)}, u32[]{:S(2)}, u32[]{:S(2)}) collective-permute-start(bf16[64,6144]{1,0:T(8,128)(2,1)} %refs_0_.1), channel_id=1, source_target_pairs={{0,6},{1,7},{2,0},{3,1},{4,2},{5,3},{6,4},{7,5},{8,14},{9,15},{10,... | collective-permute-start | bytes 2359304 | tf_op jit(solution)/shard_map/ppermute | solution.py:27
  11.6 0.7 reshape.22
  12.3 1.2 reduce-window.6
  13.9 1.1 copy-done.1
  15.1 9.2 %qkv.3.refs_5_ = bf16[512,1536]{1,0:T(8,128)(2,1)S(1)} custom-call(bf16[64,6144]{1,0:T(8,128)(2,1)S(1)} %copy-done.1, bf16[64,6144]{1,0:T(8,128)(2,1)S(1)} %collective-permute-done.2.refs_1_, bf16[3,6144,512]{2,1,0:T(8,128)(2,1)} %refs_4_.3), custom_call_target="tpu_custom_call" | custom-call | flops 2415919104 | bytes 18874368 | tf_op jit(solution)/shard_map/qkv/pallas_call | solution.py:61
  24.2 5.4 %collective-permute-done.refs_2_ = bf16[64,6144]{1,0:T(8,128)(2,1)S(1)} collective-permute-done((bf16[64,6144]{1,0:T(8,128)(2,1)}, bf16[64,6144]{1,0:T(8,128)(2,1)S(1)}, u32[]{:S(2)}, u32[]{:S(2)}) %collective-permute-start) | collective-permute-done | bytes 786464 | tf_op jit(solution)/shard_map/ppermute | solution.py:27
  29.7 0.7 collective-permute-start.5
  30.8 1.0 slice.58
  31.8 1.4 collective-permute-start.3
  33.2 1.4 collective-permute-start.4
  34.6 11.1 %qkv.4.refs_5_ = bf16[512,1536]{1,0:T(8,128)(2,1)S(1)} custom-call(bf16[64,6144]{1,0:T(8,128)(2,1)} %collective-permute-done.1.refs_0_, bf16[64,6144]{1,0:T(8,128)(2,1)} %collective-permute-done.5.refs_1_, bf16[64,6144]{1,0:T(8,128)(2,1)S(1)} %collective-permute-done.refs_2_, ...), custom_call_target="tpu_custom_call", output_to_operand_aliasing={{}: (5, {})} | custom-call | flops 4831838208 | bytes 18874368 | tf_op jit(solution)/shard_map/qkv/pallas_call | solution.py:61
  45.8 1.1 collective-permute-start.7
  47.0 0.9 copy.20
  47.9 0.7 slice_bitcast_fusion
  48.8 9.2 %qkv.5.rows = bf16[512,1536]{1,0:T(8,128)(2,1)S(1)} custom-call(bf16[64,3072]{1,0:T(8,128)(2,1)S(1)} %collective-permute-done.3.refs_0_, bf16[64,3072]{1,0:T(8,128)(2,1)S(1)} %collective-permute-done.4.refs_1_, bf16[64,3072]{1,0:T(8,128)(2,1)S(1)} %collective-permute-done.7.refs_2_, ...), custom_call_target="tpu_custom_call", output_to_operand_aliasing={{}: (5, {})} | custom-call | flops 2415919104 | bytes 18874368 | tf_op jit(solution)/shard_map/qkv/pallas_call | solution.py:61
  58.1 1.0 state.1.s0
  59.1 2.8 %collective-permute-start.10 = (bf16[528,128]{1,0:T(8,128)(2,1)S(1)}, bf16[528,128]{1,0:T(8,128)(2,1)S(1)}, u32[]{:S(2)}, u32[]{:S(2)}) collective-permute-start(bf16[528,128]{1,0:T(8,128)(2,1)S(1)} %state.1.s0), channel_id=1, source_target_pairs={{0,16},{8,24},{16,0},{24,8},{32,48},{40,56},{48,32},{56,40},{64,80... | collective-permute-start | bytes 405512 | tf_op jit(solution)/shard_map/ppermute | solution.py:35
  61.9 0.9 collective-permute-start.11
  62.8 0.6 collective-permute-start.9
  63.5 5.4 %collective-permute-done.10.s2 = bf16[528,128]{1,0:T(8,128)(2,1)S(1)} collective-permute-done((bf16[528,128]{1,0:T(8,128)(2,1)S(1)}, bf16[528,128]{1,0:T(8,128)(2,1)S(1)}, u32[]{:S(2)}, u32[]{:S(2)}) %collective-permute-start.10) | collective-permute-done | bytes 135200 | tf_op jit(solution)/shard_map/ppermute | solution.py:35
  68.9 6.0 %collective-permute-done.11.s3 = bf16[528,128]{1,0:T(8,128)(2,1)S(1)} collective-permute-done((bf16[528,128]{1,0:T(8,128)(2,1)S(1)}, bf16[528,128]{1,0:T(8,128)(2,1)S(1)}, u32[]{:S(2)}, u32[]{:S(2)}) %collective-permute-start.11) | collective-permute-done | bytes 135200 | tf_op jit(solution)/shard_map/ppermute | solution.py:35
  74.9 0.7 row.1
  75.6 3.6 %collective-permute-start.12 = (bf16[528,128]{1,0:T(8,128)(2,1)S(1)}, bf16[528,128]{1,0:T(8,128)(2,1)S(1)}, u32[]{:S(2)}, u32[]{:S(2)}) collective-permute-start(bf16[528,128]{1,0:T(8,128)(2,1)S(1)} %get-tuple-element.29), channel_id=1, source_target_pairs={{0,32},{8,40},{16,48},{24,56},{32,64},{40,72},{48,80},{56,88},{64,... | collective-permute-start | bytes 405512 | tf_op jit(solution)/shard_map/ppermute | solution.py:39
  79.2 5.7 %collective-permute-start.13 = (bf16[528,128]{1,0:T(8,128)(2,1)S(1)}, bf16[528,128]{1,0:T(8,128)(2,1)S(1)}, u32[]{:S(2)}, u32[]{:S(2)}) collective-permute-start(bf16[528,128]{1,0:T(8,128)(2,1)S(1)} %get-tuple-element.29), channel_id=1, source_target_pairs={{0,64},{8,72},{16,80},{24,88},{32,96},{40,104},{48,112},{56,120},{... | collective-permute-start | bytes 405512 | tf_op jit(solution)/shard_map/ppermute | solution.py:39
  85.0 1.3 collective-permute-start.14
  86.4 2.2 %inner.1 = f32[512,512]{1,0:T(8,128)S(1)} custom-call(s32[3]{0:T(128)S(1)} %pad_add_fusion.at, bf16[512,1536]{1,0:T(8,128)(2,1)S(1)} %qkv.5.rows, f32[512,4]{1,0:T(8,128)S(1)} %bitcast.18, f32[4,512]{1,0:T(4,128)S(1)} %copy.19.gt), custom_call_target="tpu_custom_call" | custom-call | flops 536870912 | bytes 1589260 | tf_op jit(solution)/shard_map/inner/pallas_call | solution.py:160
  88.6 1.0 normed.1.refs_0_.refs_1_
  89.7 2.8 %copy-done = bf16[8192,384]{1,0:T(8,128)(2,1)S(1)} copy-done((bf16[8192,384]{1,0:T(8,128)(2,1)S(1)}, bf16[8192,384]{1,0:T(8,128)(2,1)}, u32[]{:S(2)}) %copy-start) | copy-done | bytes 6291480
  92.5 1.8 %project.5 = (bf16[64,6144]{1,0:T(8,128)(2,1)S(1)}, bf16[64,6144]{1,0:T(8,128)(2,1)S(1)}) custom-call(bf16[512,512]{1,0:T(8,128)(2,1)S(1)} %normed.1.refs_0_.refs_1_, bf16[16,512,384]{2,1,0:T(8,128)(2,1)S(1)} %bitcast.13), custom_call_target="tpu_custom_call" | custom-call | flops 805306368 | bytes 6291456 | tf_op jit(solution)/shard_map/project/pallas_call | solution.py:187
  94.3 2.0 %collective-permute-start.19 = (bf16[64,6144]{1,0:T(8,128)(2,1)S(1)}, bf16[64,6144]{1,0:T(8,128)(2,1)S(1)}, u32[]{:S(2)}, u32[]{:S(2)}) collective-permute-start(bf16[64,6144]{1,0:T(8,128)(2,1)S(1)} %get-tuple-element.38), channel_id=1, source_target_pairs={{0,1},{1,0},{2,3},{3,2},{4,5},{5,4},{6,7},{7,6},{8,9},{9,8},{10,11... | collective-permute-start | bytes 2359304 | tf_op jit(solution)/shard_map/ppermute | solution.py:31
  96.3 3.0 %project.3 = (bf16[64,6144]{1,0:T(8,128)(2,1)S(1)}, bf16[64,6144]{1,0:T(8,128)(2,1)S(1)}, bf16[64,6144]{1,0:T(8,128)(2,1)S(1)}, bf16[64,6144]{1,0:T(8,128)(2,1)S(1)}) custom-call(bf16[512,512]{1,0:T(8,128)(2,1)S(1)} %normed.1.refs_0_.refs_1_, bf16[512,512]{1,0:T(8,128)(2,1)S(1)} %normed.1.refs_0_.refs_1_, bf16[16,512,384]{2,1,0:T(8,128)(2,1)S(1)} %bitcast.14), custom_call_target="tpu_custom_call" | custom-call | flops 1610612736 | bytes 6291456 | tf_op jit(solution)/shard_map/project/pallas_call | solution.py:187
  99.5 0.5 collective-permute-start.15
  100.2 1.1 collective-permute-start.23
  101.9 0.9 collective-permute-done.15
  103.1 1.8 %project.4 = (bf16[64,6144]{1,0:T(8,128)(2,1)S(1)}, bf16[64,6144]{1,0:T(8,128)(2,1)S(1)}) custom-call(bf16[512,512]{1,0:T(8,128)(2,1)S(1)} %normed.1.refs_0_.refs_1_, bf16[16,512,384]{2,1,0:T(8,128)(2,1)S(1)} %bitcast.15), custom_call_target="tpu_custom_call" | custom-call | flops 805306368 | bytes 6291456 | tf_op jit(solution)/shard_map/project/pallas_call | solution.py:187
  105.2 1.0 collective-permute-start.18
  106.7 4.3 %collective-permute-done.23 = bf16[64,3072]{1,0:T(8,128)(2,1)S(1)} collective-permute-done((bf16[64,3072]{1,0:T(8,128)(2,1)S(1)}, bf16[64,3072]{1,0:T(8,128)(2,1)S(1)}, u32[]{:S(2)}, u32[]{:S(2)}) %collective-permute-start.23) | collective-permute-done | bytes 393248 | tf_op jit(solution)/shard_map/ppermute | solution.py:27
  111.1 2.3 %collective-permute-start.24 = (bf16[64,3072]{1,0:T(8,128)(2,1)S(1)}, bf16[64,3072]{1,0:T(8,128)(2,1)S(1)}, u32[]{:S(2)}, u32[]{:S(2)}) collective-permute-start(bf16[64,3072]{1,0:T(8,128)(2,1)S(1)} %add_convert_fusion.4), channel_id=1, source_target_pairs={{0,6},{1,7},{2,0},{3,1},{4,2},{5,3},{6,4},{7,5},{8,14},{9,15},{10,... | collective-permute-start | bytes 1179656 | tf_op jit(solution)/shard_map/ppermute | solution.py:27
  113.3 4.1 %collective-permute-done.20 = bf16[64,3072]{1,0:T(8,128)(2,1)S(1)} collective-permute-done((bf16[64,3072]{1,0:T(8,128)(2,1)S(1)}, bf16[64,3072]{1,0:T(8,128)(2,1)S(1)}, u32[]{:S(2)}, u32[]{:S(2)}) %collective-permute-start.20) | collective-permute-done | bytes 393248 | tf_op jit(solution)/shard_map/ppermute | solution.py:27
  117.6 1.8 %collective-permute-done.18 = bf16[64,3072]{1,0:T(8,128)(2,1)S(1)} collective-permute-done((bf16[64,3072]{1,0:T(8,128)(2,1)S(1)}, bf16[64,3072]{1,0:T(8,128)(2,1)S(1)}, u32[]{:S(2)}, u32[]{:S(2)}) %collective-permute-start.18) | collective-permute-done | bytes 393248 | tf_op jit(solution)/shard_map/ppermute | solution.py:27
  119.4 6.4 %collective-permute-done.22 = bf16[64,3072]{1,0:T(8,128)(2,1)S(1)} collective-permute-done((bf16[64,3072]{1,0:T(8,128)(2,1)S(1)}, bf16[64,3072]{1,0:T(8,128)(2,1)S(1)}, u32[]{:S(2)}, u32[]{:S(2)}) %collective-permute-start.22) | collective-permute-done | bytes 393248 | tf_op jit(solution)/shard_map/ppermute | solution.py:27
  125.8 2.0 %collective-permute-done.24 = bf16[64,3072]{1,0:T(8,128)(2,1)S(1)} collective-permute-done((bf16[64,3072]{1,0:T(8,128)(2,1)S(1)}, bf16[64,3072]{1,0:T(8,128)(2,1)S(1)}, u32[]{:S(2)}, u32[]{:S(2)}) %collective-permute-start.24) | collective-permute-done | bytes 393248 | tf_op jit(solution)/shard_map/ppermute | solution.py:27
  127.8 6.4 %collective-permute-done.21 = bf16[64,3072]{1,0:T(8,128)(2,1)S(1)} collective-permute-done((bf16[64,3072]{1,0:T(8,128)(2,1)S(1)}, bf16[64,3072]{1,0:T(8,128)(2,1)S(1)}, u32[]{:S(2)}, u32[]{:S(2)}) %collective-permute-start.21) | collective-permute-done | bytes 393248 | tf_op jit(solution)/shard_map/ppermute | solution.py:27
  134.3 0.5 add_convert_fusion.5
  134.8 0.9 pad_maximum_fusion
  (50 shorter events, 3.6 us)
Async XLA Ops:
  6.5 83.2 %all-gather.3.cloned.1.call-start = ((), (), s32[]{:S(2)}) async-start(), calls=%async_computation | async-start | bytes 6684672 | tf_op jit(solution)/shard_map/all_gather | solution.py:211
  7.3 6.7 %collective-permute-start.2 = (bf16[64,6144]{1,0:T(8,128)(2,1)}, bf16[64,6144]{1,0:T(8,128)(2,1)S(1)}, u32[]{:S(2)}, u32[]{:S(2)}) collective-permute-start(bf16[64,6144]{1,0:T(8,128)(2,1)} %refs_0_.1), channel_id=1, source_target_pairs={{0,1},{1,0},{2,3},{3,2},{4,5},{5,4},{6,7},{7,6},{8,9},{9,8},{10,11... | collective-permute-start | bytes 2359304 | tf_op jit(solution)/shard_map/ppermute | solution.py:31
  8.8 20.9 %collective-permute-start = (bf16[64,6144]{1,0:T(8,128)(2,1)}, bf16[64,6144]{1,0:T(8,128)(2,1)S(1)}, u32[]{:S(2)}, u32[]{:S(2)}) collective-permute-start(bf16[64,6144]{1,0:T(8,128)(2,1)} %refs_0_.1), channel_id=1, source_target_pairs={{0,2},{1,3},{2,4},{3,5},{4,6},{5,7},{6,0},{7,1},{8,10},{9,11},{10,... | collective-permute-start | bytes 2359304 | tf_op jit(solution)/shard_map/ppermute | solution.py:27
  10.2 19.5 %collective-permute-start.1 = (bf16[64,6144]{1,0:T(8,128)(2,1)}, bf16[64,6144]{1,0:T(8,128)(2,1)}, u32[]{:S(2)}, u32[]{:S(2)}) collective-permute-start(bf16[64,6144]{1,0:T(8,128)(2,1)} %refs_0_.1), channel_id=1, source_target_pairs={{0,6},{1,7},{2,0},{3,1},{4,2},{5,3},{6,4},{7,5},{8,14},{9,15},{10,... | collective-permute-start | bytes 2359304 | tf_op jit(solution)/shard_map/ppermute | solution.py:27
  13.9 1.1 copy-start.1
  29.7 4.9 %collective-permute-start.5 = (bf16[64,6144]{1,0:T(8,128)(2,1)}, bf16[64,6144]{1,0:T(8,128)(2,1)}, u32[]{:S(2)}, u32[]{:S(2)}) collective-permute-start(bf16[64,6144]{1,0:T(8,128)(2,1)} %collective-permute-done.1.refs_0_), channel_id=1, source_target_pairs={{0,1},{1,0},{2,3},{3,2},{4,5},{5,4},{6,7},{7,6},{8,9},{9,8},{10,11... | collective-permute-start | bytes 2359304 | tf_op jit(solution)/shard_map/ppermute | solution.py:31
  30.4 4.2 %collective-permute-start.6 = (bf16[64,6144]{1,0:T(8,128)(2,1)S(1)}, bf16[64,6144]{1,0:T(8,128)(2,1)}, u32[]{:S(2)}, u32[]{:S(2)}) collective-permute-start(bf16[64,6144]{1,0:T(8,128)(2,1)S(1)} %collective-permute-done.refs_2_), channel_id=1, source_target_pairs={{0,1},{1,0},{2,3},{3,2},{4,5},{5,4},{6,7},{7,6},{8,9},{9,8},{10,11... | collective-permute-start | bytes 2359304 | tf_op jit(solution)/shard_map/ppermute | solution.py:31
  31.8 13.9 %collective-permute-start.3 = (bf16[64,3072]{1,0:T(8,128)(2,1)S(1)}, bf16[64,3072]{1,0:T(8,128)(2,1)S(1)}, u32[]{:S(2)}, u32[]{:S(2)}) collective-permute-start(bf16[64,3072]{1,0:T(8,128)(2,1)S(1)} %slice.57), channel_id=1, source_target_pairs={{0,2},{1,3},{2,4},{3,5},{4,6},{5,7},{6,0},{7,1},{8,10},{9,11},{10,... | collective-permute-start | bytes 1179656 | tf_op jit(solution)/shard_map/ppermute | solution.py:27
  33.2 12.6 %collective-permute-start.4 = (bf16[64,3072]{1,0:T(8,128)(2,1)S(1)}, bf16[64,3072]{1,0:T(8,128)(2,1)S(1)}, u32[]{:S(2)}, u32[]{:S(2)}) collective-permute-start(bf16[64,3072]{1,0:T(8,128)(2,1)S(1)} %slice.58), channel_id=1, source_target_pairs={{0,6},{1,7},{2,0},{3,1},{4,2},{5,3},{6,4},{7,5},{8,14},{9,15},{10,... | collective-permute-start | bytes 1179656 | tf_op jit(solution)/shard_map/ppermute | solution.py:27
  45.8 2.8 %collective-permute-start.7 = (bf16[64,3072]{1,0:T(8,128)(2,1)S(1)}, bf16[64,3072]{1,0:T(8,128)(2,1)S(1)}, u32[]{:S(2)}, u32[]{:S(2)}) collective-permute-start(bf16[64,3072]{1,0:T(8,128)(2,1)S(1)} %collective-permute-done.3.refs_0_), channel_id=1, source_target_pairs={{0,1},{1,0},{2,3},{3,2},{4,5},{5,4},{6,7},{7,6},{8,9},{9,8},{10,11... | collective-permute-start | bytes 1179656 | tf_op jit(solution)/shard_map/ppermute | solution.py:31
  46.9 1.9 %collective-permute-start.8 = (bf16[64,3072]{1,0:T(8,128)(2,1)S(1)}, bf16[64,3072]{1,0:T(8,128)(2,1)S(1)}, u32[]{:S(2)}, u32[]{:S(2)}) collective-permute-start(bf16[64,3072]{1,0:T(8,128)(2,1)S(1)} %collective-permute-done.4.refs_1_), channel_id=1, source_target_pairs={{0,1},{1,0},{2,3},{3,2},{4,5},{5,4},{6,7},{7,6},{8,9},{9,8},{10,11... | collective-permute-start | bytes 1179656 | tf_op jit(solution)/shard_map/ppermute | solution.py:31
  59.1 9.8 %collective-permute-start.10 = (bf16[528,128]{1,0:T(8,128)(2,1)S(1)}, bf16[528,128]{1,0:T(8,128)(2,1)S(1)}, u32[]{:S(2)}, u32[]{:S(2)}) collective-permute-start(bf16[528,128]{1,0:T(8,128)(2,1)S(1)} %state.1.s0), channel_id=1, source_target_pairs={{0,16},{8,24},{16,0},{24,8},{32,48},{40,56},{48,32},{56,40},{64,80... | collective-permute-start | bytes 405512 | tf_op jit(solution)/shard_map/ppermute | solution.py:35
  61.9 13.0 %collective-permute-start.11 = (bf16[528,128]{1,0:T(8,128)(2,1)S(1)}, bf16[528,128]{1,0:T(8,128)(2,1)S(1)}, u32[]{:S(2)}, u32[]{:S(2)}) collective-permute-start(bf16[528,128]{1,0:T(8,128)(2,1)S(1)} %state.1.s0), channel_id=1, source_target_pairs={{0,24},{8,0},{16,8},{24,16},{32,56},{40,32},{48,40},{56,48},{64,88... | collective-permute-start | bytes 405512 | tf_op jit(solution)/shard_map/ppermute | solution.py:35
  62.8 12.1 %collective-permute-start.9 = (bf16[528,128]{1,0:T(8,128)(2,1)S(1)}, bf16[528,128]{1,0:T(8,128)(2,1)S(1)}, u32[]{:S(2)}, u32[]{:S(2)}) collective-permute-start(bf16[528,128]{1,0:T(8,128)(2,1)S(1)} %state.1.s0), channel_id=1, source_target_pairs={{0,8},{8,16},{16,24},{24,0},{32,40},{40,48},{48,56},{56,32},{64,72... | collective-permute-start | bytes 405512 | tf_op jit(solution)/shard_map/ppermute | solution.py:35
  75.6 13.0 %collective-permute-start.12 = (bf16[528,128]{1,0:T(8,128)(2,1)S(1)}, bf16[528,128]{1,0:T(8,128)(2,1)S(1)}, u32[]{:S(2)}, u32[]{:S(2)}) collective-permute-start(bf16[528,128]{1,0:T(8,128)(2,1)S(1)} %get-tuple-element.29), channel_id=1, source_target_pairs={{0,32},{8,40},{16,48},{24,56},{32,64},{40,72},{48,80},{56,88},{64,... | collective-permute-start | bytes 405512 | tf_op jit(solution)/shard_map/ppermute | solution.py:39
  79.2 9.4 %collective-permute-start.13 = (bf16[528,128]{1,0:T(8,128)(2,1)S(1)}, bf16[528,128]{1,0:T(8,128)(2,1)S(1)}, u32[]{:S(2)}, u32[]{:S(2)}) collective-permute-start(bf16[528,128]{1,0:T(8,128)(2,1)S(1)} %get-tuple-element.29), channel_id=1, source_target_pairs={{0,64},{8,72},{16,80},{24,88},{32,96},{40,104},{48,112},{56,120},{... | collective-permute-start | bytes 405512 | tf_op jit(solution)/shard_map/ppermute | solution.py:39
  85.0 3.6 %collective-permute-start.14 = (bf16[528,128]{1,0:T(8,128)(2,1)S(1)}, bf16[528,128]{1,0:T(8,128)(2,1)S(1)}, u32[]{:S(2)}, u32[]{:S(2)}) collective-permute-start(bf16[528,128]{1,0:T(8,128)(2,1)S(1)} %get-tuple-element.29), channel_id=1, source_target_pairs={{0,96},{8,104},{16,112},{24,120},{1,97},{9,105},{17,113},{25,121},... | collective-permute-start | bytes 405512 | tf_op jit(solution)/shard_map/ppermute | solution.py:39
  86.3 2.3 %copy-start.2 = (f32[512]{0:T(512)S(1)}, f32[512]{0:T(512)}, u32[]{:S(2)}) copy-start(f32[512]{0:T(512)} %param.8) | copy-start | bytes 6148
  89.7 2.8 %copy-start = (bf16[8192,384]{1,0:T(8,128)(2,1)S(1)}, bf16[8192,384]{1,0:T(8,128)(2,1)}, u32[]{:S(2)}) copy-start(bf16[8192,384]{1,0:T(8,128)(2,1)} %all-gather.3.cloned.1.call-done) | copy-start | bytes 18874372
  94.3 5.7 %collective-permute-start.19 = (bf16[64,6144]{1,0:T(8,128)(2,1)S(1)}, bf16[64,6144]{1,0:T(8,128)(2,1)S(1)}, u32[]{:S(2)}, u32[]{:S(2)}) collective-permute-start(bf16[64,6144]{1,0:T(8,128)(2,1)S(1)} %get-tuple-element.38), channel_id=1, source_target_pairs={{0,1},{1,0},{2,3},{3,2},{4,5},{5,4},{6,7},{7,6},{8,9},{9,8},{10,11... | collective-permute-start | bytes 2359304 | tf_op jit(solution)/shard_map/ppermute | solution.py:31
  99.4 2.4 %collective-permute-start.16 = (bf16[64,6144]{1,0:T(8,128)(2,1)S(1)}, bf16[64,6144]{1,0:T(8,128)(2,1)S(1)}, u32[]{:S(2)}, u32[]{:S(2)}) collective-permute-start(bf16[64,6144]{1,0:T(8,128)(2,1)S(1)} %get-tuple-element.33), channel_id=1, source_target_pairs={{0,1},{1,0},{2,3},{3,2},{4,5},{5,4},{6,7},{7,6},{8,9},{9,8},{10,11... | collective-permute-start | bytes 2359304 | tf_op jit(solution)/shard_map/ppermute | solution.py:31
  99.5 3.4 %collective-permute-start.15 = (bf16[64,6144]{1,0:T(8,128)(2,1)S(1)}, bf16[64,6144]{1,0:T(8,128)(2,1)S(1)}, u32[]{:S(2)}, u32[]{:S(2)}) collective-permute-start(bf16[64,6144]{1,0:T(8,128)(2,1)S(1)} %get-tuple-element.31), channel_id=1, source_target_pairs={{0,1},{1,0},{2,3},{3,2},{4,5},{5,4},{6,7},{7,6},{8,9},{9,8},{10,11... | collective-permute-start | bytes 2359304 | tf_op jit(solution)/shard_map/ppermute | solution.py:31
  100.2 10.7 %collective-permute-start.23 = (bf16[64,3072]{1,0:T(8,128)(2,1)S(1)}, bf16[64,3072]{1,0:T(8,128)(2,1)S(1)}, u32[]{:S(2)}, u32[]{:S(2)}) collective-permute-start(bf16[64,3072]{1,0:T(8,128)(2,1)S(1)} %get-tuple-element.42), channel_id=1, source_target_pairs={{0,6},{1,7},{2,0},{3,1},{4,2},{5,3},{6,4},{7,5},{8,14},{9,15},{10,... | collective-permute-start | bytes 1179656 | tf_op jit(solution)/shard_map/ppermute | solution.py:27
  105.0 22.8 %collective-permute-start.17 = (bf16[64,6144]{1,0:T(8,128)(2,1)S(1)}, bf16[64,6144]{1,0:T(8,128)(2,1)S(1)}, u32[]{:S(2)}, u32[]{:S(2)}) collective-permute-start(bf16[64,6144]{1,0:T(8,128)(2,1)S(1)} %get-tuple-element.36), channel_id=1, source_target_pairs={{0,1},{1,0},{2,3},{3,2},{4,5},{5,4},{6,7},{7,6},{8,9},{9,8},{10,11... | collective-permute-start | bytes 2359304 | tf_op jit(solution)/shard_map/ppermute | solution.py:31
  105.2 14.2 %collective-permute-start.18 = (bf16[64,3072]{1,0:T(8,128)(2,1)S(1)}, bf16[64,3072]{1,0:T(8,128)(2,1)S(1)}, u32[]{:S(2)}, u32[]{:S(2)}) collective-permute-start(bf16[64,3072]{1,0:T(8,128)(2,1)S(1)} %slice.83), channel_id=1, source_target_pairs={{0,6},{1,7},{2,0},{3,1},{4,2},{5,3},{6,4},{7,5},{8,14},{9,15},{10,... | collective-permute-start | bytes 1179656 | tf_op jit(solution)/shard_map/ppermute | solution.py:27
  106.2 11.2 %collective-permute-start.20 = (bf16[64,3072]{1,0:T(8,128)(2,1)S(1)}, bf16[64,3072]{1,0:T(8,128)(2,1)S(1)}, u32[]{:S(2)}, u32[]{:S(2)}) collective-permute-start(bf16[64,3072]{1,0:T(8,128)(2,1)S(1)} %get-tuple-element.41), channel_id=1, source_target_pairs={{0,2},{1,3},{2,4},{3,5},{4,6},{5,7},{6,0},{7,1},{8,10},{9,11},{10,... | collective-permute-start | bytes 1179656 | tf_op jit(solution)/shard_map/ppermute | solution.py:27
  106.7 19.2 %collective-permute-start.22 = (bf16[64,3072]{1,0:T(8,128)(2,1)S(1)}, bf16[64,3072]{1,0:T(8,128)(2,1)S(1)}, u32[]{:S(2)}, u32[]{:S(2)}) collective-permute-start(bf16[64,3072]{1,0:T(8,128)(2,1)S(1)} %slice.87), channel_id=1, source_target_pairs={{0,2},{1,3},{2,4},{3,5},{4,6},{5,7},{6,0},{7,1},{8,10},{9,11},{10,... | collective-permute-start | bytes 1179656 | tf_op jit(solution)/shard_map/ppermute | solution.py:27
  111.1 16.8 %collective-permute-start.24 = (bf16[64,3072]{1,0:T(8,128)(2,1)S(1)}, bf16[64,3072]{1,0:T(8,128)(2,1)S(1)}, u32[]{:S(2)}, u32[]{:S(2)}) collective-permute-start(bf16[64,3072]{1,0:T(8,128)(2,1)S(1)} %add_convert_fusion.4), channel_id=1, source_target_pairs={{0,6},{1,7},{2,0},{3,1},{4,2},{5,3},{6,4},{7,5},{8,14},{9,15},{10,... | collective-permute-start | bytes 1179656 | tf_op jit(solution)/shard_map/ppermute | solution.py:27
  117.5 16.7 %collective-permute-start.21 = (bf16[64,3072]{1,0:T(8,128)(2,1)S(1)}, bf16[64,3072]{1,0:T(8,128)(2,1)S(1)}, u32[]{:S(2)}, u32[]{:S(2)}) collective-permute-start(bf16[64,3072]{1,0:T(8,128)(2,1)S(1)} %add_convert_fusion.6), channel_id=1, source_target_pairs={{0,2},{1,3},{2,4},{3,5},{4,6},{5,7},{6,0},{7,1},{8,10},{9,11},{10,... | collective-permute-start | bytes 1179656 | tf_op jit(solution)/shard_map/ppermute | solution.py:27
Sparse Core Ops, SparseCore 0:
  9.5 70.1 all-gather.2

commit v3 on v2

v3 whole, which is shorter than its diff:
```python
import functools

import jax
import jax.numpy as jnp
import numpy as np
from jax import lax
from jax.experimental import pallas as pl
from jax.experimental.pallas import tpu as pltpu
from jax.sharding import PartitionSpec as P

norm_eps = 1e-06
f32, bf16 = jnp.float32, jnp.bfloat16
HEADS, SIZE = 4, 128
WIDE = HEADS * SIZE
N_X = N_Z = N_Y = 4
PLACES = ((1, 0), (3, 0), (0, 0), (0, 1), (1, 1), (3, 1), (2, 0), (2, 1))
SHARE = 0.01
VMEM_LIMIT = 20 * 2**20


def params(**kw):
    return pltpu.CompilerParams(vmem_limit_bytes=VMEM_LIMIT, **kw)


def cost(flops, nbytes):
    return pl.CostEstimate(flops=int(flops * SHARE), bytes_accessed=int(nbytes * SHARE), transcendentals=0)


def to_y(a, k):
    return lax.ppermute(a, "tp", [(i, (i // 2 + k) % N_Y * 2 + i % 2) for i in range(2 * N_Y)])


def to_sibling(a):
    return lax.ppermute(a, "tp", [(i, i ^ 1) for i in range(2 * N_Y)])


def to_x(a, k):
    return lax.ppermute(a, "ctx", [(j, j // N_X * N_X + (j + k) % N_X) for j in range(N_X * N_Z)])


def to_z(a, k):
    return lax.ppermute(a, "ctx", [(j, j + N_X * k) for j in range(N_X * N_Z) if j // N_X + k < N_Z])


def place_rows(pieces, layout, rows):
    for piece, (row, col) in zip(pieces, layout):
        rows[row : row + piece.shape[0], col : col + piece.shape[1]] = piece[...]


def activate(member, acc):
    return (acc if member == 2 else acc / (1.0 + jnp.exp(-acc))).astype(bf16)


def qkv_first_kernel(layout, *refs):
    n = len(layout)
    pieces, w, out, held, rows, sems = refs[:n], refs[n], *refs[n + 1 :]
    depth = w.shape[1]
    cut = depth // 4
    copies = [
        [
            pltpu.make_async_copy(w.at[m, pl.ds(k * cut, cut)], held.at[m, pl.ds(k * cut, cut)], sems.at[m, k])
            for k in range(4)
        ]
        for m in range(3)
    ]
    for m in range(3):
        for k in range(4):
            copies[m][k].start()
    place_rows(pieces, layout, rows)
    for m in range(3):
        acc = None
        for k in range(4):
            copies[m][k].wait()
            part = jnp.dot(
                rows[:, k * cut : (k + 1) * cut], held[m, k * cut : (k + 1) * cut], preferred_element_type=f32
            )
            acc = part if acc is None else acc + part
        out[:, m * WIDE : (m + 1) * WIDE] = activate(m, acc)


def qkv_kernel(layout, *refs):
    n = len(layout)
    pieces, w, out, rows = refs[:n], refs[n], refs[n + 1], refs[n + 2]
    place_rows(pieces, layout, rows)
    tile = 256
    for m in range(3):
        for start in range(0, WIDE, tile):
            acc = jnp.dot(rows[...], w[m, :, start : start + tile], preferred_element_type=f32)
            out[:, m * WIDE + start : m * WIDE + start + tile] = activate(m, acc)


def qkv(pieces, layout, count, w, first=False):
    depth = w.shape[1]
    out = jax.ShapeDtypeStruct((count, 3 * WIDE), bf16)
    vmem = pl.BlockSpec(memory_space=pltpu.VMEM)
    return pl.pallas_call(
        functools.partial(qkv_first_kernel if first else qkv_kernel, layout),
        out_shape=(out, pltpu.VMEM(w.shape, bf16)) if first else out,
        in_specs=[vmem] * len(pieces) + [pl.BlockSpec(memory_space=pltpu.HBM) if first else vmem],
        out_specs=(vmem, vmem) if first else vmem,
        scratch_shapes=[pltpu.VMEM((count, depth), bf16)] + ([pltpu.SemaphoreType.DMA((3, 4))] if first else []),
        compiler_params=params(),
        cost_estimate=cost(2 * count * depth * 3 * WIDE, 3 * WIDE * depth * 2),
        name="qkv",
    )(*pieces, w)


def columns(refs, start):
    return jnp.concatenate([ref[:, start : start + SIZE] for ref in refs], axis=0)


def pack(out, last):
    high = last.astype(bf16).astype(f32)
    mid = (last - high).astype(bf16).astype(f32)
    low = last - high - mid
    out[WIDE:, :] = jnp.concatenate([high, mid, low, jnp.zeros_like(low)], axis=0).astype(bf16)


def unpack(ref):
    tail = ref[WIDE:, :].astype(f32)
    return tail[0:4] + tail[4:8] + tail[8:12]


def state_kernel(a, b, c, g, last, out):
    for h in range(HEADS):
        keys = columns((a, b, c), WIDE + h * SIZE).astype(f32)
        values = columns((a, b, c), 2 * WIDE + h * SIZE)
        scaled = (keys * jnp.exp(last[h : h + 1, 0:1] - g[:, h : h + 1])).astype(bf16)
        state = lax.dot_general(scaled, values, (((0,), (0,)), ((), ())), preferred_element_type=f32)
        out[h * SIZE : (h + 1) * SIZE, :] = state.astype(bf16)
    pack(out, last[...])


def inner_kernel(a, b, c, g, gt, row, col, out):
    lower = row[...] >= col[...]
    for h in range(HEADS):
        query = columns((a, b, c), h * SIZE)
        keys = columns((a, b, c), WIDE + h * SIZE)
        values = columns((a, b, c), 2 * WIDE + h * SIZE)
        scores = lax.dot_general(query, keys, (((1,), (1,)), ((), ())), preferred_element_type=f32)
        lagged = g[:, h : h + 1] - gt[h : h + 1, :]
        probs = jnp.where(lower, scores * jnp.exp(jnp.minimum(lagged, 0.0)), 0.0).astype(bf16)
        out[:, h * SIZE : (h + 1) * SIZE] = jnp.dot(probs, values, preferred_element_type=f32)


def row_kernel(at, s0, s1, s2, s3, before, total):
    refs = (s0, s1, s2, s3)
    x = at[0]
    place = [(x - k) & 3 for k in range(N_X)]
    last = [unpack(ref) for ref in refs]

    def between(k, end):
        return sum(jnp.where((place[m] > place[k]) & (place[m] < end), last[m], 0.0) for m in range(N_X))

    reach = [jnp.where(place[k] < x, jnp.exp(between(k, x)), 0.0) for k in range(N_X)]
    whole = [jnp.exp(between(k, N_X)) for k in range(N_X)]
    for h in range(HEADS):
        rows = slice(h * SIZE, (h + 1) * SIZE)
        states = [ref[rows, :].astype(f32) for ref in refs]
        before[rows, :] = sum(states[k] * reach[k][h : h + 1] for k in range(1, N_X))
        total[rows, :] = sum(states[k] * whole[k][h : h + 1] for k in range(N_X)).astype(bf16)
    pack(total, last[0] + last[1] + last[2] + last[3])
    lead = sum(jnp.where(place[k] < x, last[k], 0.0) for k in range(1, N_X))
    before[WIDE:, :] = jnp.concatenate([lead, lead], axis=0)


def normed_kernel(before, t1, t2, t3, a, b, c, g, inner, gain, out):
    lead = jnp.exp(before[WIDE : WIDE + HEADS, :])
    r1, r2 = unpack(t1), unpack(t2)
    reach2, reach3 = jnp.exp(r1), jnp.exp(r1 + r2)
    for h in range(HEADS):
        rows = slice(h * SIZE, (h + 1) * SIZE)
        one = slice(h, h + 1)
        earlier = (
            t1[rows, :].astype(f32) + t2[rows, :].astype(f32) * reach2[one] + t3[rows, :].astype(f32) * reach3[one]
        )
        carried = (earlier * lead[one] + before[rows, :]).astype(bf16)
        query = columns((a, b, c), h * SIZE).astype(f32)
        scaled = (query * jnp.exp(g[:, one])).astype(bf16)
        mixed = inner[:, rows] + jnp.dot(scaled, carried, preferred_element_type=f32)
        scale = lax.rsqrt(jnp.mean(mixed * mixed, axis=-1, keepdims=True) + norm_eps)
        out[:, rows] = (mixed * scale * gain[:, rows]).astype(bf16)


def whole_call(kernel, args, outs, name, flops, scalars=0):
    nbytes = sum(a.size * a.dtype.itemsize for a in args)
    return pl.pallas_call(
        kernel,
        out_shape=outs,
        in_specs=[pl.BlockSpec(memory_space=pltpu.SMEM)] * scalars
        + [pl.BlockSpec(memory_space=pltpu.VMEM)] * (len(args) - scalars),
        out_specs=jax.tree.map(lambda _: pl.BlockSpec(memory_space=pltpu.VMEM), outs),
        compiler_params=params(),
        cost_estimate=cost(flops, nbytes),
        name=name,
    )(*args)


def project_part(rows, w, outs, m):
    width = w.shape[2]
    part = jnp.dot(rows, w[m], preferred_element_type=f32).astype(bf16)
    for i, out in enumerate(outs):
        out[:, m * width : (m + 1) * width] = part[i * 64 : (i + 1) * 64]


def project_first_kernel(start, normed, w, own, sib, held, sems):
    per = w.shape[0] // 4
    copies = [
        pltpu.make_async_copy(w.at[pl.ds(i * per, per)], held.at[pl.ds(i * per, per)], sems.at[i]) for i in range(4)
    ]
    for copy in copies:
        copy.start()
    rows = normed[start : start + 128, :]
    for i in range(4):
        copies[i].wait()
        for m in range(i * per, (i + 1) * per):
            project_part(rows, held, (own, sib), m)


def project_kernel(blocks, normed, w, *outs):
    rows = jnp.concatenate([normed[64 * b : 64 * b + 64, :] for b in blocks], axis=0)
    for m in range(w.shape[0]):
        project_part(rows, w, outs, m)


def project(normed, w, blocks, first=False):
    n_ctx, depth, width = w.shape
    vmem = pl.BlockSpec(memory_space=pltpu.VMEM)
    n = len(blocks)
    count = 64 * n
    outs = [jax.ShapeDtypeStruct((64, n_ctx * width), bf16)] * n
    if first:
        kernel = functools.partial(project_first_kernel, blocks[0] * 64)
        outs = outs + [pltpu.VMEM(w.shape, bf16)]
    else:
        kernel = functools.partial(project_kernel, blocks)
    return pl.pallas_call(
        kernel,
        out_shape=outs,
        in_specs=[vmem, pl.BlockSpec(memory_space=pltpu.HBM) if first else vmem],
        out_specs=[vmem] * len(outs),
        scratch_shapes=[pltpu.SemaphoreType.DMA((4,))] if first else [],
        compiler_params=params(),
        cost_estimate=cost(2 * count * depth * n_ctx * width, 2 * depth * n_ctx * width),
        name="project",
    )(normed, w)


def final_kernel(own, sib, up_plain, down_plain, up_sum, down_sum, out):
    mid = up_sum.shape[1]
    for start, one, two in ((0, down_plain, up_sum), (mid, up_plain, down_sum)):
        at = slice(start, start + mid)
        total = own[:, at].astype(f32) + sib[:, at].astype(f32) + one[...].astype(f32) + two[...].astype(f32)
        out[:, at] = total.astype(bf16)


def after(value, *others):
    return lax.optimization_barrier((value, *others))[0]


def plus(*terms):
    total = terms[0].astype(f32)
    for term in terms[1:]:
        total = total + term.astype(f32)
    return total.astype(bf16)


def body(activations, w_qkv, log_decay, gain, w_out):
    tp, ctx = lax.axis_index("tp"), lax.axis_index("ctx")
    y, core = tp // 2, tp % 2
    at = (ctx % N_X).astype(jnp.int32).reshape(1)
    w_all = lax.all_gather(w_out, "ctx", axis=0)

    cumul = jnp.cumsum(log_decay.T, axis=1)
    last = jnp.broadcast_to(cumul[:, -1:], (HEADS, SIZE))
    gt = jnp.roll(cumul.reshape(HEADS, N_Y, 2, 64), -y, axis=1)
    gt = jnp.where(core == 0, gt, gt[:, :, ::-1])
    gt = jnp.concatenate([gt[:, chip, half] for chip, half in PLACES], axis=1)
    g = gt.T
    chip, half = (jnp.array(np.repeat(np.array(p), 64), jnp.int32) for p in zip(*PLACES))
    pos = ((chip + y) & 3) * 128 + ((half + core) & 1) * 64 + jnp.arange(512, dtype=jnp.int32) % 64

    depth = activations.shape[1]
    mid = depth // 2
    low, high = activations[:, :mid], activations[:, mid:]
    left_low, right_high = to_y(low, 1), to_y(high, -1)
    left_high, right_low = to_y(high, 1), to_y(low, -1)
    own2 = to_sibling(activations)
    own2 = after(own2, g, gt, last, at, pos)
    qkv_a, w_qkv = qkv([activations, own2], [(0, 0), (64, 0)], 128, w_qkv, True)
    left_low, right_high = after((left_low, right_high), qkv_a)
    far_low, far_high = to_y(left_low, 1), to_y(right_high, -1)
    low2, high2 = to_sibling(left_low), to_sibling(right_high)
    left_high2, right_low2 = to_sibling(left_high), to_sibling(right_low)
    near = [right_low, right_high, left_low, left_high]
    qkv_b = qkv(near, [(0, 0), (0, mid), (64, 0), (64, mid)], 128, w_qkv)
    far_low, far_high = after((far_low, far_high), qkv_b)
    rest = [right_low2, high2, low2, left_high2, far_low, far_high, to_sibling(far_low), to_sibling(far_high)]
    qkv_c = qkv(rest, [(64 * i, col) for i in range(4) for col in (0, mid)], 256, w_qkv)
    rows = (qkv_b, qkv_a, qkv_c)

    packed = jax.ShapeDtypeStruct((WIDE + 16, SIZE), bf16)
    state = whole_call(state_kernel, (*rows, g, last), packed, "state", 2 * 512 * WIDE * SIZE)
    row = [state] + [to_x(state, k) for k in range(1, N_X)]
    inner = whole_call(
        inner_kernel,
        (*rows, g, gt, pos.reshape(512, 1), pos.reshape(1, 512)),
        jax.ShapeDtypeStruct((512, WIDE), f32),
        "inner",
        4 * 512 * 512 * WIDE,
    )
    before, total = whole_call(
        row_kernel, (at, *row), (jax.ShapeDtypeStruct((WIDE + 8, SIZE), f32), packed), "row", 10 * WIDE * SIZE, 1
    )
    totals = [to_z(total, k) for k in range(1, N_Z)]
    normed = whole_call(
        normed_kernel,
        (before, *totals, *rows, g, inner, gain.reshape(1, WIDE)),
        jax.ShapeDtypeStruct((512, WIDE), bf16),
        "normed",
        2 * 512 * WIDE * SIZE,
    )

    w_all = pltpu.with_memory_space_constraint(w_all, pltpu.HBM)
    far_own, far_sib, w_all = project(normed, w_all, (6, 7), True)
    far_sib = to_sibling(far_sib)
    near_parts = project(normed, w_all, (0, 4, 1, 5))
    far_sib = after(far_sib, near_parts)
    up_own, up_sib, down_own, down_sib = near_parts
    from_l = to_y(plus(far_own[:, :mid], far_sib[:, :mid]), 1)
    from_r = to_y(plus(far_own[:, mid:], far_sib[:, mid:]), -1)
    up_sib, down_sib = to_sibling(up_sib), to_sibling(down_sib)
    up_plain = plus(up_own[:, mid:], up_sib[:, mid:])
    down_plain = plus(down_own[:, :mid], down_sib[:, :mid])
    normed = after(normed, up_plain, down_plain)
    up_plain, down_plain = to_y(up_plain, 1), to_y(down_plain, -1)
    here_own, here_sib = project(normed, w_all, (2, 3))
    from_l, from_r = after((from_l, from_r), here_own)
    up_sum = to_y(plus(up_own[:, :mid], up_sib[:, :mid], from_l), 1)
    down_sum = to_y(plus(down_own[:, mid:], down_sib[:, mid:], from_r), -1)
    here_sib = to_sibling(here_sib)
    return whole_call(
        final_kernel,
        (here_own, here_sib, up_plain, down_plain, up_sum, down_sum),
        jax.ShapeDtypeStruct((64, depth), bf16),
        "final",
        4 * 64 * depth,
    )


def solution(mesh):
    in_specs = (
        P(("ctx", "tp"), None),
        P(None, None, "tp"),
        P("ctx", "tp"),
        P("tp"),
        P("tp", "ctx"),
    )
    out_specs = P(("ctx", "tp"), None)
    return jax.shard_map(body, mesh=mesh, in_specs=in_specs, out_specs=out_specs, check_vma=False)
```

time: 143 us -> 130 us (0.909)
  Pallas kernels: 41.2 us -> 26.8 us
  starting transfers between devices: 31.7 us -> 40.3 us
  local copies, waits for them, and re-layouts: 7.93 us -> 4.64 us
  waiting for transfers between devices: 44.2 us -> 41.6 us
    pallas_call x6, Pallas kernels: 36.2 us -> 21.9 us  [the longest x3 15 us: qkv(): pl.pallas_call(functools.partial(qkv_first_kernel if first else qkv_kerne...]
    ppermute x9 -> x11, starting transfers between devices: 6.28 us -> 11.6 us  [to_sibling(): return lax.ppermute(a, 'tp', [(i, i ^ 1) for i in range(2 * N_Y)])]
    ppermute x10 -> x12, waiting for transfers between devices: 30.4 us -> 26.9 us  [to_y(): lax.ppermute(a, 'tp', [(i, (i // 2 + k) % N_Y * 2 + i % 2) for i in range...]
    ppermute x10 -> x12, starting transfers between devices: 10.5 us -> 13.9 us  [to_y(): lax.ppermute(a, 'tp', [(i, (i // 2 + k) % N_Y * 2 + i % 2) for i in range...]
    unnamed x6 -> x4, local copies, waits for them, and re-layouts: 3.92 us -> 1.14 us
    pallas_call x4 -> x5, Pallas kernels: 4.98 us -> 4.94 us  [whole_call(): pl.pallas_call(kernel, out_shape=outs, in_specs=[pl.BlockSpec(memory_spac...]
  transfers between devices with their start and end apart: 26 -> 30, of which waited for: 12 -> 13; matrix products, arithmetic and copies ran while one was open for 5% -> 5% of each run, Pallas kernels for 28% -> 17%
where the time goes in v3:
time: 130 us
  waiting for transfers between devices  41.6 us (32%)
  starting transfers between devices  40.3 us (31%)
  Pallas kernels  26.8 us (21%)
  between operations  13.7 us (11%)
  local copies, waits for them, and re-layouts  4.64 us (4%)
  other arithmetic  2.94 us (2%)
    ppermute x12, waiting for transfers between devices, to_y(): lax.ppermute(a, 'tp', [(i, (i // 2 + k) % N_Y * 2 + i % 2) for i in range...  26.9 us
    pallas_call x3, Pallas kernels, qkv(): pl.pallas_call(functools.partial(qkv_first_kernel if first else qkv_kerne...  15 us
    ppermute x12, starting transfers between devices, to_y(): lax.ppermute(a, 'tp', [(i, (i // 2 + k) % N_Y * 2 + i % 2) for i in range...  13.9 us
    ppermute x11, starting transfers between devices, to_sibling(): return lax.ppermute(a, 'tp', [(i, i ^ 1) for i in range(2 * N_Y)])  11.6 us
    ppermute x3, waiting for transfers between devices, to_x(): lax.ppermute(a, 'ctx', [(j, j // N_X * N_X + (j + k) % N_X) for j in rang...  11.4 us
    ppermute x3, starting transfers between devices, to_z(): lax.ppermute(a, 'ctx', [(j, j + N_X * k) for j in range(N_X * N_Z) if j /...  9.96 us
    pallas_call x3, Pallas kernels, project(): pl.pallas_call(kernel, out_shape=outs, in_specs=[vmem, pl.BlockSpec(memor...  6.9 us
    pallas_call x5, Pallas kernels, whole_call(): pl.pallas_call(kernel, out_shape=outs, in_specs=[pl.BlockSpec(memory_spac...  4.94 us
  transfers between devices with their start and end apart: 30, of which 13 were waited for; matrix products, arithmetic and copies ran while one was open for 5% of the time, Pallas kernels for 17%

profile of v3, /device:TPU:1, one launch (start us, length us, event | category | flops | bytes accessed | tf_op | source)
XLA Modules:
  0.0 130.0 jit_solution(8362360468509189001)
XLA Ops:
  6.5 0.7 all-gather.3.cloned.1.call-update
  7.3 1.5 %collective-permute-start.3 = (bf16[64,6144]{1,0:T(8,128)(2,1)}, bf16[64,6144]{1,0:T(8,128)(2,1)S(1)}, u32[]{:S(2)}, u32[]{:S(2)}) collective-permute-start(bf16[64,6144]{1,0:T(8,128)(2,1)} %refs_0_.1), channel_id=1, source_target_pairs={{0,1},{1,0},{2,3},{3,2},{4,5},{5,4},{6,7},{7,6},{8,9},{9,8},{10,11... | collective-permute-start | bytes 2359304 | tf_op jit(solution)/shard_map/ppermute | solution.py:34
  8.8 1.9 %fusion.8 = (bf16[64,3072]{1,0:T(8,128)(2,1)S(1)}, bf16[64,3072]{1,0:T(8,128)(2,1)}) fusion(bf16[64,6144]{1,0:T(8,128)(2,1)} %refs_0_.1), kind=kLoop, calls=%fused_computation.25 | loop fusion | bytes 1572864 | tf_op jit(solution)/shard_map/slice | solution.py:285
  10.7 1.4 %collective-permute-start.1 = (bf16[64,3072]{1,0:T(8,128)(2,1)}, bf16[64,3072]{1,0:T(8,128)(2,1)S(1)}, u32[]{:S(2)}, u32[]{:S(2)}) collective-permute-start(bf16[64,3072]{1,0:T(8,128)(2,1)} %get-tuple-element.52), channel_id=1, source_target_pairs={{0,2},{1,3},{2,4},{3,5},{4,6},{5,7},{6,0},{7,1},{8,10},{9,11},{10,... | collective-permute-start | bytes 1179656 | tf_op jit(solution)/shard_map/ppermute | solution.py:30
  12.0 1.4 %collective-permute-start = (bf16[64,3072]{1,0:T(8,128)(2,1)}, bf16[64,3072]{1,0:T(8,128)(2,1)S(1)}, u32[]{:S(2)}, u32[]{:S(2)}) collective-permute-start(bf16[64,3072]{1,0:T(8,128)(2,1)} %get-tuple-element.52), channel_id=1, source_target_pairs={{0,6},{1,7},{2,0},{3,1},{4,2},{5,3},{6,4},{7,5},{8,14},{9,15},{10,... | collective-permute-start | bytes 1179656 | tf_op jit(solution)/shard_map/ppermute | solution.py:30
  13.5 1.5 %collective-permute-start.2 = (bf16[64,3072]{1,0:T(8,128)(2,1)S(1)}, bf16[64,3072]{1,0:T(8,128)(2,1)S(1)}, u32[]{:S(2)}, u32[]{:S(2)}) collective-permute-start(bf16[64,3072]{1,0:T(8,128)(2,1)S(1)} %get-tuple-element.51), channel_id=1, source_target_pairs={{0,6},{1,7},{2,0},{3,1},{4,2},{5,3},{6,4},{7,5},{8,14},{9,15},{10,... | collective-permute-start | bytes 1179656 | tf_op jit(solution)/shard_map/ppermute | solution.py:30
  15.0 0.7 reshape.29
  15.7 1.2 reduce-window.6
  18.0 0.7 fusion.1
  18.8 1.1 copy-done
  19.9 7.3 %qkv.3 = (bf16[128,1536]{1,0:T(8,128)(2,1)S(1)}, bf16[3,6144,512]{2,1,0:T(8,128)(2,1)S(1)}) custom-call(bf16[64,6144]{1,0:T(8,128)(2,1)S(1)} %copy-done, bf16[64,6144]{1,0:T(8,128)(2,1)S(1)} %collective-permute-done.3.refs_1_, bf16[3,6144,512]{2,1,0:T(8,128)(2,1)} %refs_2_.1), custom_call_target="tpu_custom_call" | custom-call | flops 24159192 | bytes 188743 | tf_op jit(solution)/shard_map/qkv/pallas_call | solution.py:96
  27.2 3.9 %collective-permute-done.2.refs_1_ = bf16[64,3072]{1,0:T(8,128)(2,1)S(1)} collective-permute-done((bf16[64,3072]{1,0:T(8,128)(2,1)S(1)}, bf16[64,3072]{1,0:T(8,128)(2,1)S(1)}, u32[]{:S(2)}, u32[]{:S(2)}) %collective-permute-start.2) | collective-permute-done | bytes 393248 | tf_op jit(solution)/shard_map/ppermute | solution.py:30
  31.1 2.8 %collective-permute-start.10 = (bf16[64,3072]{1,0:T(8,128)(2,1)S(1)}, bf16[64,3072]{1,0:T(8,128)(2,1)S(1)}, u32[]{:S(2)}, u32[]{:S(2)}) collective-permute-start(bf16[64,3072]{1,0:T(8,128)(2,1)S(1)} %collective-permute-done.2.refs_1_), channel_id=1, source_target_pairs={{0,6},{1,7},{2,0},{3,1},{4,2},{5,3},{6,4},{7,5},{8,14},{9,15},{10,... | collective-permute-start | bytes 1179656 | tf_op jit(solution)/shard_map/ppermute | solution.py:30
  33.9 1.3 collective-permute-start.5
  35.7 2.6 %qkv.4.a = bf16[128,1536]{1,0:T(8,128)(2,1)S(1)} custom-call(bf16[64,3072]{1,0:T(8,128)(2,1)S(1)} %collective-permute-done.refs_0_, bf16[64,3072]{1,0:T(8,128)(2,1)S(1)} %collective-permute-done.2.refs_1_, bf16[64,3072]{1,0:T(8,128)(2,1)S(1)} %collective-permute-done.1.refs_2_, bf16[64,3072]{1,0:T(8,128)(2,1)S(1)} %collective-permute-done.4.refs_3_, ...), custom_call_target="tpu_custom_call" | custom-call | flops 24159192 | bytes 188743 | tf_op jit(solution)/shard_map/qkv/pallas_call | solution.py:96
  38.3 3.0 %collective-permute-done.10.refs_5_ = bf16[64,3072]{1,0:T(8,128)(2,1)S(1)} collective-permute-done((bf16[64,3072]{1,0:T(8,128)(2,1)S(1)}, bf16[64,3072]{1,0:T(8,128)(2,1)S(1)}, u32[]{:S(2)}, u32[]{:S(2)}) %collective-permute-start.10) | collective-permute-done | bytes 393248 | tf_op jit(solution)/shard_map/ppermute | solution.py:30
  41.3 1.9 %collective-permute-start.7 = (bf16[64,3072]{1,0:T(8,128)(2,1)S(1)}, bf16[64,3072]{1,0:T(8,128)(2,1)S(1)}, u32[]{:S(2)}, u32[]{:S(2)}) collective-permute-start(bf16[64,3072]{1,0:T(8,128)(2,1)S(1)} %collective-permute-done.1.refs_2_), channel_id=1, source_target_pairs={{0,1},{1,0},{2,3},{3,2},{4,5},{5,4},{6,7},{7,6},{8,9},{9,8},{10,11... | collective-permute-start | bytes 1179656 | tf_op jit(solution)/shard_map/ppermute | solution.py:34
  43.2 1.2 collective-permute-done.9.refs_4_
  44.5 2.2 %collective-permute-start.11 = (bf16[64,3072]{1,0:T(8,128)(2,1)S(1)}, bf16[64,3072]{1,0:T(8,128)(2,1)S(1)}, u32[]{:S(2)}, u32[]{:S(2)}) collective-permute-start(bf16[64,3072]{1,0:T(8,128)(2,1)S(1)} %collective-permute-done.9.refs_4_), channel_id=1, source_target_pairs={{0,1},{1,0},{2,3},{3,2},{4,5},{5,4},{6,7},{7,6},{8,9},{9,8},{10,11... | collective-permute-start | bytes 1179656 | tf_op jit(solution)/shard_map/ppermute | solution.py:34
  46.7 1.3 %collective-permute-done.11.refs_6_ = bf16[64,3072]{1,0:T(8,128)(2,1)S(1)} collective-permute-done((bf16[64,3072]{1,0:T(8,128)(2,1)S(1)}, bf16[64,3072]{1,0:T(8,128)(2,1)S(1)}, u32[]{:S(2)}, u32[]{:S(2)}) %collective-permute-start.11) | collective-permute-done | bytes 393248 | tf_op jit(solution)/shard_map/ppermute | solution.py:34
  48.0 0.6 collective-permute-done.12.refs_7_
  48.6 5.0 %qkv.5.c = bf16[256,1536]{1,0:T(8,128)(2,1)S(1)} custom-call(bf16[64,3072]{1,0:T(8,128)(2,1)S(1)} %collective-permute-done.5.refs_0_, bf16[64,3072]{1,0:T(8,128)(2,1)S(1)} %collective-permute-done.6.refs_1_, bf16[64,3072]{1,0:T(8,128)(2,1)S(1)} %collective-permute-done.7.refs_2_, bf16[64,3072]{1,0:T(8,128)(2,1)S(1)} %collective-permute-done.8.refs_3_, ...), custom_call_target="tpu_custom_call" | custom-call | flops 48318384 | bytes 188743 | tf_op jit(solution)/shard_map/qkv/pallas_call | solution.py:96
  53.6 1.0 state.1.s0
  54.6 1.2 collective-permute-start.13
  55.8 2.6 %collective-permute-start.14 = (bf16[528,128]{1,0:T(8,128)(2,1)S(1)}, bf16[528,128]{1,0:T(8,128)(2,1)S(1)}, u32[]{:S(2)}, u32[]{:S(2)}) collective-permute-start(bf16[528,128]{1,0:T(8,128)(2,1)S(1)} %state.1.s0), channel_id=1, source_target_pairs={{0,16},{8,24},{16,0},{24,8},{32,48},{40,56},{48,32},{56,40},{64,80... | collective-permute-start | bytes 405512 | tf_op jit(solution)/shard_map/ppermute | solution.py:38
  58.4 1.2 collective-permute-start.15
  59.5 4.7 %collective-permute-done.13.s1 = bf16[528,128]{1,0:T(8,128)(2,1)S(1)} collective-permute-done((bf16[528,128]{1,0:T(8,128)(2,1)S(1)}, bf16[528,128]{1,0:T(8,128)(2,1)S(1)}, u32[]{:S(2)}, u32[]{:S(2)}) %collective-permute-start.13) | collective-permute-done | bytes 135200 | tf_op jit(solution)/shard_map/ppermute | solution.py:38
  64.2 6.7 %collective-permute-done.14.s2 = bf16[528,128]{1,0:T(8,128)(2,1)S(1)} collective-permute-done((bf16[528,128]{1,0:T(8,128)(2,1)S(1)}, bf16[528,128]{1,0:T(8,128)(2,1)S(1)}, u32[]{:S(2)}, u32[]{:S(2)}) %collective-permute-start.14) | collective-permute-done | bytes 135200 | tf_op jit(solution)/shard_map/ppermute | solution.py:38
  71.1 3.5 %collective-permute-start.16 = (bf16[528,128]{1,0:T(8,128)(2,1)S(1)}, bf16[528,128]{1,0:T(8,128)(2,1)S(1)}, u32[]{:S(2)}, u32[]{:S(2)}) collective-permute-start(bf16[528,128]{1,0:T(8,128)(2,1)S(1)} %get-tuple-element.35), channel_id=1, source_target_pairs={{0,32},{8,40},{16,48},{24,56},{32,64},{40,72},{48,80},{56,88},{64,... | collective-permute-start | bytes 405512 | tf_op jit(solution)/shard_map/ppermute | solution.py:42
  74.6 5.1 %collective-permute-start.17 = (bf16[528,128]{1,0:T(8,128)(2,1)S(1)}, bf16[528,128]{1,0:T(8,128)(2,1)S(1)}, u32[]{:S(2)}, u32[]{:S(2)}) collective-permute-start(bf16[528,128]{1,0:T(8,128)(2,1)S(1)} %get-tuple-element.35), channel_id=1, source_target_pairs={{0,64},{8,72},{16,80},{24,88},{32,96},{40,104},{48,112},{56,120},{... | collective-permute-start | bytes 405512 | tf_op jit(solution)/shard_map/ppermute | solution.py:42
  79.7 1.3 collective-permute-start.18
  81.2 1.4 %inner.1 = f32[512,512]{1,0:T(8,128)S(1)} custom-call(bf16[128,1536]{1,0:T(8,128)(2,1)S(1)} %qkv.4.a, bf16[128,1536]{1,0:T(8,128)(2,1)S(1)} %get-tuple-element.28.b, bf16[256,1536]{1,0:T(8,128)(2,1)S(1)} %qkv.5.c, f32[512,4]{1,0:T(8,128)S(1)} %bitcast.20, f32[4,512]{1,0:T(4,128)S(1)} %concatenate.8.gt, s32[512,1]{1,0:T(8,128)S(1)} %copy.20.row, ...), custom_call_target="tpu_custom_call" | custom-call | flops 5368709 | bytes 15933 | tf_op jit(solution)/shard_map/inner/pallas_call | solution.py:187
  82.7 0.6 collective-permute-done.18.t3
  83.3 1.0 normed.1
  84.4 3.3 %project.3 = (bf16[64,6144]{1,0:T(8,128)(2,1)S(1)}, bf16[64,6144]{1,0:T(8,128)(2,1)S(1)}, bf16[16,512,384]{2,1,0:T(8,128)(2,1)S(1)}) custom-call(bf16[512,512]{1,0:T(8,128)(2,1)S(1)} %normed.1, bf16[16,512,384]{2,1,0:T(8,128)(2,1)} %bitcast.25), custom_call_target="tpu_custom_call" | custom-call | flops 8053063 | bytes 62914 | tf_op jit(solution)/shard_map/project/pallas_call | solution.py:237
  87.7 2.4 %collective-permute-start.24 = (bf16[64,6144]{1,0:T(8,128)(2,1)S(1)}, bf16[64,6144]{1,0:T(8,128)(2,1)S(1)}, u32[]{:S(2)}, u32[]{:S(2)}) collective-permute-start(bf16[64,6144]{1,0:T(8,128)(2,1)S(1)} %get-tuple-element.45), channel_id=1, source_target_pairs={{0,1},{1,0},{2,3},{3,2},{4,5},{5,4},{6,7},{7,6},{8,9},{9,8},{10,11... | collective-permute-start | bytes 2359304 | tf_op jit(solution)/shard_map/ppermute | solution.py:34
  90.1 2.3 %project.4 = (bf16[64,6144]{1,0:T(8,128)(2,1)S(1)}, bf16[64,6144]{1,0:T(8,128)(2,1)S(1)}, bf16[64,6144]{1,0:T(8,128)(2,1)S(1)}, bf16[64,6144]{1,0:T(8,128)(2,1)S(1)}) custom-call(bf16[512,512]{1,0:T(8,128)(2,1)S(1)} %normed.1, bf16[16,512,384]{2,1,0:T(8,128)(2,1)S(1)} %get-tuple-element.36.w), custom_call_target="tpu_custom_call" | custom-call | flops 16106127 | bytes 62914 | tf_op jit(solution)/shard_map/project/pallas_call | solution.py:237
  93.3 2.7 %collective-permute-start.26 = (bf16[64,3072]{1,0:T(8,128)(2,1)S(1)}, bf16[64,3072]{1,0:T(8,128)(2,1)S(1)}, u32[]{:S(2)}, u32[]{:S(2)}) collective-permute-start(bf16[64,3072]{1,0:T(8,128)(2,1)S(1)} %get-tuple-element.49), channel_id=1, source_target_pairs={{0,6},{1,7},{2,0},{3,1},{4,2},{5,3},{6,4},{7,5},{8,14},{9,15},{10,... | collective-permute-start | bytes 1179656 | tf_op jit(solution)/shard_map/ppermute | solution.py:30
  96.3 1.5 %collective-permute-start.22 = (bf16[64,3072]{1,0:T(8,128)(2,1)S(1)}, bf16[64,3072]{1,0:T(8,128)(2,1)S(1)}, u32[]{:S(2)}, u32[]{:S(2)}) collective-permute-start(bf16[64,3072]{1,0:T(8,128)(2,1)S(1)} %add_convert_fusion.5), channel_id=1, source_target_pairs={{0,2},{1,3},{2,4},{3,5},{4,6},{5,7},{6,0},{7,1},{8,10},{9,11},{10,... | collective-permute-start | bytes 1179656 | tf_op jit(solution)/shard_map/ppermute | solution.py:30
  97.8 1.2 project.5
  99.0 1.3 collective-permute-start.21
  100.3 4.9 %collective-permute-done.25 = bf16[64,3072]{1,0:T(8,128)(2,1)S(1)} collective-permute-done((bf16[64,3072]{1,0:T(8,128)(2,1)S(1)}, bf16[64,3072]{1,0:T(8,128)(2,1)S(1)}, u32[]{:S(2)}, u32[]{:S(2)}) %collective-permute-start.25) | collective-permute-done | bytes 393248 | tf_op jit(solution)/shard_map/ppermute | solution.py:30
  105.3 2.4 %collective-permute-start.28 = (bf16[64,3072]{1,0:T(8,128)(2,1)S(1)}, bf16[64,3072]{1,0:T(8,128)(2,1)S(1)}, u32[]{:S(2)}, u32[]{:S(2)}) collective-permute-start(bf16[64,3072]{1,0:T(8,128)(2,1)S(1)} %add_convert_fusion), channel_id=1, source_target_pairs={{0,6},{1,7},{2,0},{3,1},{4,2},{5,3},{6,4},{7,5},{8,14},{9,15},{10,... | collective-permute-start | bytes 1179656 | tf_op jit(solution)/shard_map/ppermute | solution.py:30
  108.0 4.6 %collective-permute-done.23.down_plain = bf16[64,3072]{1,0:T(8,128)(2,1)S(1)} collective-permute-done((bf16[64,3072]{1,0:T(8,128)(2,1)S(1)}, bf16[64,3072]{1,0:T(8,128)(2,1)S(1)}, u32[]{:S(2)}, u32[]{:S(2)}) %collective-permute-start.23) | collective-permute-done | bytes 393248 | tf_op jit(solution)/shard_map/ppermute | solution.py:30
  112.5 1.1 collective-permute-done.22.up_plain
  113.6 7.4 %collective-permute-done.28.down_sum = bf16[64,3072]{1,0:T(8,128)(2,1)S(1)} collective-permute-done((bf16[64,3072]{1,0:T(8,128)(2,1)S(1)}, bf16[64,3072]{1,0:T(8,128)(2,1)S(1)}, u32[]{:S(2)}, u32[]{:S(2)}) %collective-permute-start.28) | collective-permute-done | bytes 393248 | tf_op jit(solution)/shard_map/ppermute | solution.py:30
  120.9 0.9 collective-permute-done.27.up_sum
  121.9 1.3 final.1
  (51 shorter events, 3.5 us)
Async XLA Ops:
  6.5 77.8 %all-gather.3.cloned.1.call-start = ((), (), s32[]{:S(2)}) async-start(), calls=%async_computation | async-start | bytes 6684672 | tf_op jit(solution)/shard_map/all_gather | solution.py:272
  7.3 11.4 %collective-permute-start.3 = (bf16[64,6144]{1,0:T(8,128)(2,1)}, bf16[64,6144]{1,0:T(8,128)(2,1)S(1)}, u32[]{:S(2)}, u32[]{:S(2)}) collective-permute-start(bf16[64,6144]{1,0:T(8,128)(2,1)} %refs_0_.1), channel_id=1, source_target_pairs={{0,1},{1,0},{2,3},{3,2},{4,5},{5,4},{6,7},{7,6},{8,9},{9,8},{10,11... | collective-permute-start | bytes 2359304 | tf_op jit(solution)/shard_map/ppermute | solution.py:34
  10.7 16.6 %collective-permute-start.1 = (bf16[64,3072]{1,0:T(8,128)(2,1)}, bf16[64,3072]{1,0:T(8,128)(2,1)S(1)}, u32[]{:S(2)}, u32[]{:S(2)}) collective-permute-start(bf16[64,3072]{1,0:T(8,128)(2,1)} %get-tuple-element.52), channel_id=1, source_target_pairs={{0,2},{1,3},{2,4},{3,5},{4,6},{5,7},{6,0},{7,1},{8,10},{9,11},{10,... | collective-permute-start | bytes 1179656 | tf_op jit(solution)/shard_map/ppermute | solution.py:30
  12.0 21.9 %collective-permute-start = (bf16[64,3072]{1,0:T(8,128)(2,1)}, bf16[64,3072]{1,0:T(8,128)(2,1)S(1)}, u32[]{:S(2)}, u32[]{:S(2)}) collective-permute-start(bf16[64,3072]{1,0:T(8,128)(2,1)} %get-tuple-element.52), channel_id=1, source_target_pairs={{0,6},{1,7},{2,0},{3,1},{4,2},{5,3},{6,4},{7,5},{8,14},{9,15},{10,... | collective-permute-start | bytes 1179656 | tf_op jit(solution)/shard_map/ppermute | solution.py:30
  13.5 17.6 %collective-permute-start.2 = (bf16[64,3072]{1,0:T(8,128)(2,1)S(1)}, bf16[64,3072]{1,0:T(8,128)(2,1)S(1)}, u32[]{:S(2)}, u32[]{:S(2)}) collective-permute-start(bf16[64,3072]{1,0:T(8,128)(2,1)S(1)} %get-tuple-element.51), channel_id=1, source_target_pairs={{0,6},{1,7},{2,0},{3,1},{4,2},{5,3},{6,4},{7,5},{8,14},{9,15},{10,... | collective-permute-start | bytes 1179656 | tf_op jit(solution)/shard_map/ppermute | solution.py:30
  15.0 20.2 %collective-permute-start.4 = (bf16[64,3072]{1,0:T(8,128)(2,1)S(1)}, bf16[64,3072]{1,0:T(8,128)(2,1)S(1)}, u32[]{:S(2)}, u32[]{:S(2)}) collective-permute-start(bf16[64,3072]{1,0:T(8,128)(2,1)S(1)} %get-tuple-element.51), channel_id=1, source_target_pairs={{0,2},{1,3},{2,4},{3,5},{4,6},{5,7},{6,0},{7,1},{8,10},{9,11},{10,... | collective-permute-start | bytes 1179656 | tf_op jit(solution)/shard_map/ppermute | solution.py:30
  18.8 1.1 copy-start
  31.1 10.2 %collective-permute-start.10 = (bf16[64,3072]{1,0:T(8,128)(2,1)S(1)}, bf16[64,3072]{1,0:T(8,128)(2,1)S(1)}, u32[]{:S(2)}, u32[]{:S(2)}) collective-permute-start(bf16[64,3072]{1,0:T(8,128)(2,1)S(1)} %collective-permute-done.2.refs_1_), channel_id=1, source_target_pairs={{0,6},{1,7},{2,0},{3,1},{4,2},{5,3},{6,4},{7,5},{8,14},{9,15},{10,... | collective-permute-start | bytes 1179656 | tf_op jit(solution)/shard_map/ppermute | solution.py:30
  33.9 10.6 %collective-permute-start.9 = (bf16[64,3072]{1,0:T(8,128)(2,1)S(1)}, bf16[64,3072]{1,0:T(8,128)(2,1)S(1)}, u32[]{:S(2)}, u32[]{:S(2)}) collective-permute-start(bf16[64,3072]{1,0:T(8,128)(2,1)S(1)} %collective-permute-done.1.refs_2_), channel_id=1, source_target_pairs={{0,2},{1,3},{2,4},{3,5},{4,6},{5,7},{6,0},{7,1},{8,10},{9,11},{10,... | collective-permute-start | bytes 1179656 | tf_op jit(solution)/shard_map/ppermute | solution.py:30
  33.9 12.7 %collective-permute-start.5 = (bf16[64,3072]{1,0:T(8,128)(2,1)S(1)}, bf16[64,3072]{1,0:T(8,128)(2,1)S(1)}, u32[]{:S(2)}, u32[]{:S(2)}) collective-permute-start(bf16[64,3072]{1,0:T(8,128)(2,1)S(1)} %collective-permute-done.refs_0_), channel_id=1, source_target_pairs={{0,1},{1,0},{2,3},{3,2},{4,5},{5,4},{6,7},{7,6},{8,9},{9,8},{10,11... | collective-permute-start | bytes 1179656 | tf_op jit(solution)/shard_map/ppermute | solution.py:34
  35.2 11.5 %collective-permute-start.8 = (bf16[64,3072]{1,0:T(8,128)(2,1)S(1)}, bf16[64,3072]{1,0:T(8,128)(2,1)S(1)}, u32[]{:S(2)}, u32[]{:S(2)}) collective-permute-start(bf16[64,3072]{1,0:T(8,128)(2,1)S(1)} %collective-permute-done.4.refs_3_), channel_id=1, source_target_pairs={{0,1},{1,0},{2,3},{3,2},{4,5},{5,4},{6,7},{7,6},{8,9},{9,8},{10,11... | collective-permute-start | bytes 1179656 | tf_op jit(solution)/shard_map/ppermute | solution.py:34
  35.3 11.4 %collective-permute-start.6 = (bf16[64,3072]{1,0:T(8,128)(2,1)S(1)}, bf16[64,3072]{1,0:T(8,128)(2,1)S(1)}, u32[]{:S(2)}, u32[]{:S(2)}) collective-permute-start(bf16[64,3072]{1,0:T(8,128)(2,1)S(1)} %collective-permute-done.2.refs_1_), channel_id=1, source_target_pairs={{0,1},{1,0},{2,3},{3,2},{4,5},{5,4},{6,7},{7,6},{8,9},{9,8},{10,11... | collective-permute-start | bytes 1179656 | tf_op jit(solution)/shard_map/ppermute | solution.py:34
  38.3 45.0 %copy-start.1 = (f32[512]{0:T(512)S(1)}, f32[512]{0:T(512)}, u32[]{:S(2)}) copy-start(f32[512]{0:T(512)} %param.10) | copy-start | bytes 6148
  41.3 5.3 %collective-permute-start.7 = (bf16[64,3072]{1,0:T(8,128)(2,1)S(1)}, bf16[64,3072]{1,0:T(8,128)(2,1)S(1)}, u32[]{:S(2)}, u32[]{:S(2)}) collective-permute-start(bf16[64,3072]{1,0:T(8,128)(2,1)S(1)} %collective-permute-done.1.refs_2_), channel_id=1, source_target_pairs={{0,1},{1,0},{2,3},{3,2},{4,5},{5,4},{6,7},{7,6},{8,9},{9,8},{10,11... | collective-permute-start | bytes 1179656 | tf_op jit(solution)/shard_map/ppermute | solution.py:34
  44.5 3.5 %collective-permute-start.11 = (bf16[64,3072]{1,0:T(8,128)(2,1)S(1)}, bf16[64,3072]{1,0:T(8,128)(2,1)S(1)}, u32[]{:S(2)}, u32[]{:S(2)}) collective-permute-start(bf16[64,3072]{1,0:T(8,128)(2,1)S(1)} %collective-permute-done.9.refs_4_), channel_id=1, source_target_pairs={{0,1},{1,0},{2,3},{3,2},{4,5},{5,4},{6,7},{7,6},{8,9},{9,8},{10,11... | collective-permute-start | bytes 1179656 | tf_op jit(solution)/shard_map/ppermute | solution.py:34
  46.6 1.9 %collective-permute-start.12 = (bf16[64,3072]{1,0:T(8,128)(2,1)S(1)}, bf16[64,3072]{1,0:T(8,128)(2,1)S(1)}, u32[]{:S(2)}, u32[]{:S(2)}) collective-permute-start(bf16[64,3072]{1,0:T(8,128)(2,1)S(1)} %collective-permute-done.10.refs_5_), channel_id=1, source_target_pairs={{0,1},{1,0},{2,3},{3,2},{4,5},{5,4},{6,7},{7,6},{8,9},{9,8},{10,11... | collective-permute-start | bytes 1179656 | tf_op jit(solution)/shard_map/ppermute | solution.py:34
  54.6 9.6 %collective-permute-start.13 = (bf16[528,128]{1,0:T(8,128)(2,1)S(1)}, bf16[528,128]{1,0:T(8,128)(2,1)S(1)}, u32[]{:S(2)}, u32[]{:S(2)}) collective-permute-start(bf16[528,128]{1,0:T(8,128)(2,1)S(1)} %state.1.s0), channel_id=1, source_target_pairs={{0,8},{8,16},{16,24},{24,0},{32,40},{40,48},{48,56},{56,32},{64,72... | collective-permute-start | bytes 405512 | tf_op jit(solution)/shard_map/ppermute | solution.py:38
  55.8 15.1 %collective-permute-start.14 = (bf16[528,128]{1,0:T(8,128)(2,1)S(1)}, bf16[528,128]{1,0:T(8,128)(2,1)S(1)}, u32[]{:S(2)}, u32[]{:S(2)}) collective-permute-start(bf16[528,128]{1,0:T(8,128)(2,1)S(1)} %state.1.s0), channel_id=1, source_target_pairs={{0,16},{8,24},{16,0},{24,8},{32,48},{40,56},{48,32},{56,40},{64,80... | collective-permute-start | bytes 405512 | tf_op jit(solution)/shard_map/ppermute | solution.py:38
  58.4 12.5 %collective-permute-start.15 = (bf16[528,128]{1,0:T(8,128)(2,1)S(1)}, bf16[528,128]{1,0:T(8,128)(2,1)S(1)}, u32[]{:S(2)}, u32[]{:S(2)}) collective-permute-start(bf16[528,128]{1,0:T(8,128)(2,1)S(1)} %state.1.s0), channel_id=1, source_target_pairs={{0,24},{8,0},{16,8},{24,16},{32,56},{40,32},{48,40},{56,48},{64,88... | collective-permute-start | bytes 405512 | tf_op jit(solution)/shard_map/ppermute | solution.py:38
  71.1 11.6 %collective-permute-start.16 = (bf16[528,128]{1,0:T(8,128)(2,1)S(1)}, bf16[528,128]{1,0:T(8,128)(2,1)S(1)}, u32[]{:S(2)}, u32[]{:S(2)}) collective-permute-start(bf16[528,128]{1,0:T(8,128)(2,1)S(1)} %get-tuple-element.35), channel_id=1, source_target_pairs={{0,32},{8,40},{16,48},{24,56},{32,64},{40,72},{48,80},{56,88},{64,... | collective-permute-start | bytes 405512 | tf_op jit(solution)/shard_map/ppermute | solution.py:42
  74.6 8.0 %collective-permute-start.17 = (bf16[528,128]{1,0:T(8,128)(2,1)S(1)}, bf16[528,128]{1,0:T(8,128)(2,1)S(1)}, u32[]{:S(2)}, u32[]{:S(2)}) collective-permute-start(bf16[528,128]{1,0:T(8,128)(2,1)S(1)} %get-tuple-element.35), channel_id=1, source_target_pairs={{0,64},{8,72},{16,80},{24,88},{32,96},{40,104},{48,112},{56,120},{... | collective-permute-start | bytes 405512 | tf_op jit(solution)/shard_map/ppermute | solution.py:42
  79.7 3.6 %collective-permute-start.18 = (bf16[528,128]{1,0:T(8,128)(2,1)S(1)}, bf16[528,128]{1,0:T(8,128)(2,1)S(1)}, u32[]{:S(2)}, u32[]{:S(2)}) collective-permute-start(bf16[528,128]{1,0:T(8,128)(2,1)S(1)} %get-tuple-element.35), channel_id=1, source_target_pairs={{0,96},{8,104},{16,112},{24,120},{1,97},{9,105},{17,113},{25,121},... | collective-permute-start | bytes 405512 | tf_op jit(solution)/shard_map/ppermute | solution.py:42
  87.7 5.3 %collective-permute-start.24 = (bf16[64,6144]{1,0:T(8,128)(2,1)S(1)}, bf16[64,6144]{1,0:T(8,128)(2,1)S(1)}, u32[]{:S(2)}, u32[]{:S(2)}) collective-permute-start(bf16[64,6144]{1,0:T(8,128)(2,1)S(1)} %get-tuple-element.45), channel_id=1, source_target_pairs={{0,1},{1,0},{2,3},{3,2},{4,5},{5,4},{6,7},{7,6},{8,9},{9,8},{10,11... | collective-permute-start | bytes 2359304 | tf_op jit(solution)/shard_map/ppermute | solution.py:34
  92.4 3.5 %collective-permute-start.20 = (bf16[64,6144]{1,0:T(8,128)(2,1)S(1)}, bf16[64,6144]{1,0:T(8,128)(2,1)S(1)}, u32[]{:S(2)}, u32[]{:S(2)}) collective-permute-start(bf16[64,6144]{1,0:T(8,128)(2,1)S(1)} %get-tuple-element.40), channel_id=1, source_target_pairs={{0,1},{1,0},{2,3},{3,2},{4,5},{5,4},{6,7},{7,6},{8,9},{9,8},{10,11... | collective-permute-start | bytes 2359304 | tf_op jit(solution)/shard_map/ppermute | solution.py:34
  92.5 3.6 %collective-permute-start.19 = (bf16[64,6144]{1,0:T(8,128)(2,1)S(1)}, bf16[64,6144]{1,0:T(8,128)(2,1)S(1)}, u32[]{:S(2)}, u32[]{:S(2)}) collective-permute-start(bf16[64,6144]{1,0:T(8,128)(2,1)S(1)} %get-tuple-element.38), channel_id=1, source_target_pairs={{0,1},{1,0},{2,3},{3,2},{4,5},{5,4},{6,7},{7,6},{8,9},{9,8},{10,11... | collective-permute-start | bytes 2359304 | tf_op jit(solution)/shard_map/ppermute | solution.py:34
  93.2 12.0 %collective-permute-start.25 = (bf16[64,3072]{1,0:T(8,128)(2,1)S(1)}, bf16[64,3072]{1,0:T(8,128)(2,1)S(1)}, u32[]{:S(2)}, u32[]{:S(2)}) collective-permute-start(bf16[64,3072]{1,0:T(8,128)(2,1)S(1)} %get-tuple-element.50), channel_id=1, source_target_pairs={{0,2},{1,3},{2,4},{3,5},{4,6},{5,7},{6,0},{7,1},{8,10},{9,11},{10,... | collective-permute-start | bytes 1179656 | tf_op jit(solution)/shard_map/ppermute | solution.py:30
  93.3 11.9 %collective-permute-start.26 = (bf16[64,3072]{1,0:T(8,128)(2,1)S(1)}, bf16[64,3072]{1,0:T(8,128)(2,1)S(1)}, u32[]{:S(2)}, u32[]{:S(2)}) collective-permute-start(bf16[64,3072]{1,0:T(8,128)(2,1)S(1)} %get-tuple-element.49), channel_id=1, source_target_pairs={{0,6},{1,7},{2,0},{3,1},{4,2},{5,3},{6,4},{7,5},{8,14},{9,15},{10,... | collective-permute-start | bytes 1179656 | tf_op jit(solution)/shard_map/ppermute | solution.py:30
  96.1 16.5 %collective-permute-start.23 = (bf16[64,3072]{1,0:T(8,128)(2,1)S(1)}, bf16[64,3072]{1,0:T(8,128)(2,1)S(1)}, u32[]{:S(2)}, u32[]{:S(2)}) collective-permute-start(bf16[64,3072]{1,0:T(8,128)(2,1)S(1)} %add_convert_fusion.4), channel_id=1, source_target_pairs={{0,6},{1,7},{2,0},{3,1},{4,2},{5,3},{6,4},{7,5},{8,14},{9,15},{10,... | collective-permute-start | bytes 1179656 | tf_op jit(solution)/shard_map/ppermute | solution.py:30
  96.3 17.3 %collective-permute-start.22 = (bf16[64,3072]{1,0:T(8,128)(2,1)S(1)}, bf16[64,3072]{1,0:T(8,128)(2,1)S(1)}, u32[]{:S(2)}, u32[]{:S(2)}) collective-permute-start(bf16[64,3072]{1,0:T(8,128)(2,1)S(1)} %add_convert_fusion.5), channel_id=1, source_target_pairs={{0,2},{1,3},{2,4},{3,5},{4,6},{5,7},{6,0},{7,1},{8,10},{9,11},{10,... | collective-permute-start | bytes 1179656 | tf_op jit(solution)/shard_map/ppermute | solution.py:30
  99.0 22.9 %collective-permute-start.21 = (bf16[64,6144]{1,0:T(8,128)(2,1)S(1)}, bf16[64,6144]{1,0:T(8,128)(2,1)S(1)}, u32[]{:S(2)}, u32[]{:S(2)}) collective-permute-start(bf16[64,6144]{1,0:T(8,128)(2,1)S(1)} %get-tuple-element.43), channel_id=1, source_target_pairs={{0,1},{1,0},{2,3},{3,2},{4,5},{5,4},{6,7},{7,6},{8,9},{9,8},{10,11... | collective-permute-start | bytes 2359304 | tf_op jit(solution)/shard_map/ppermute | solution.py:34
  105.3 15.6 %collective-permute-start.28 = (bf16[64,3072]{1,0:T(8,128)(2,1)S(1)}, bf16[64,3072]{1,0:T(8,128)(2,1)S(1)}, u32[]{:S(2)}, u32[]{:S(2)}) collective-permute-start(bf16[64,3072]{1,0:T(8,128)(2,1)S(1)} %add_convert_fusion), channel_id=1, source_target_pairs={{0,6},{1,7},{2,0},{3,1},{4,2},{5,3},{6,4},{7,5},{8,14},{9,15},{10,... | collective-permute-start | bytes 1179656 | tf_op jit(solution)/shard_map/ppermute | solution.py:30
  107.9 14.0 %collective-permute-start.27 = (bf16[64,3072]{1,0:T(8,128)(2,1)S(1)}, bf16[64,3072]{1,0:T(8,128)(2,1)S(1)}, u32[]{:S(2)}, u32[]{:S(2)}) collective-permute-start(bf16[64,3072]{1,0:T(8,128)(2,1)S(1)} %add_convert_fusion.1), channel_id=1, source_target_pairs={{0,2},{1,3},{2,4},{3,5},{4,6},{5,7},{6,0},{7,1},{8,10},{9,11},{10,... | collective-permute-start | bytes 1179656 | tf_op jit(solution)/shard_map/ppermute | solution.py:30
Sparse Core Ops, SparseCore 0:
  9.5 70.1 all-gather.2

commit v4 on v3

--- a/solution.py
+++ b/solution.py
@@ -196,17 +196,18 @@
     )(*args)
 
 
-def project_part(rows, w, outs, m):
+def project_part(rows, w, outs, m, start):
     width = w.shape[2]
     part = jnp.dot(rows, w[m], preferred_element_type=f32).astype(bf16)
     for i, out in enumerate(outs):
-        out[:, m * width : (m + 1) * width] = part[i * 64 : (i + 1) * 64]
-
-
-def project_first_kernel(start, normed, w, own, sib, held, sems):
-    per = w.shape[0] // 4
+        out[:, start + m * width : start + (m + 1) * width] = part[i * 64 : (i + 1) * 64]
+
+
+def project_first_kernel(base, start, normed, w, own, sib, held, sems):
+    per = held.shape[0] // 4
     copies = [
-        pltpu.make_async_copy(w.at[pl.ds(i * per, per)], held.at[pl.ds(i * per, per)], sems.at[i]) for i in range(4)
+        pltpu.make_async_copy(w.at[pl.ds(base + i * per, per)], held.at[pl.ds(i * per, per)], sems.at[i])
+        for i in range(4)
     ]
     for copy in copies:
         copy.start()
@@ -214,44 +215,60 @@
     for i in range(4):
         copies[i].wait()
         for m in range(i * per, (i + 1) * per):
-            project_part(rows, held, (own, sib), m)
-
-
-def project_kernel(blocks, normed, w, *outs):
+            project_part(rows, held, (own, sib), m, 0)
+
+
+def project_kernel(blocks, normed, w1, w2, *outs):
     rows = jnp.concatenate([normed[64 * b : 64 * b + 64, :] for b in blocks], axis=0)
-    for m in range(w.shape[0]):
-        project_part(rows, w, outs, m)
-
-
-def project(normed, w, blocks, first=False):
-    n_ctx, depth, width = w.shape
+    for m in range(w1.shape[0]):
+        project_part(rows, w1, outs, m, 0)
+        project_part(rows, w2, outs, m, outs[0].shape[1] // 2)
+
+
+def project_first(normed, w, base, count, start):
+    _, depth, width = w.shape
+    vmem = pl.BlockSpec(memory_space=pltpu.VMEM)
+    half = jax.ShapeDtypeStruct((64, count * width), bf16)
+    return pl.pallas_call(
+        functools.partial(project_first_kernel, base, start),
+        out_shape=[half, half, pltpu.VMEM((count, depth, width), bf16)],
+        in_specs=[vmem, pl.BlockSpec(memory_space=pltpu.HBM)],
+        out_specs=[vmem] * 3,
+        scratch_shapes=[pltpu.SemaphoreType.DMA((4,))],
+        compiler_params=params(),
+        cost_estimate=cost(256 * depth * count * width, 2 * depth * count * width),
+        name="project",
+    )(normed, pltpu.with_memory_space_constraint(w, pltpu.HBM))
+
+
+def project(normed, w1, w2, blocks):
+    n_ctx, depth, width = w1.shape
+    n_ctx += w2.shape[0]
     vmem = pl.BlockSpec(memory_space=pltpu.VMEM)
     n = len(blocks)
-    count = 64 * n
-    outs = [jax.ShapeDtypeStruct((64, n_ctx * width), bf16)] * n
-    if first:
-        kernel = functools.partial(project_first_kernel, blocks[0] * 64)
-        outs = outs + [pltpu.VMEM(w.shape, bf16)]
-    else:
-        kernel = functools.partial(project_kernel, blocks)
     return pl.pallas_call(
-        kernel,
-        out_shape=outs,
-        in_specs=[vmem, pl.BlockSpec(memory_space=pltpu.HBM) if first else vmem],
-        out_specs=[vmem] * len(outs),
-        scratch_shapes=[pltpu.SemaphoreType.DMA((4,))] if first else [],
+        functools.partial(project_kernel, blocks),
+        out_shape=[jax.ShapeDtypeStruct((64, n_ctx * width), bf16)] * n,
+        in_specs=[vmem] * 3,
+        out_specs=[vmem] * n,
         compiler_params=params(),
-        cost_estimate=cost(2 * count * depth * n_ctx * width, 2 * depth * n_ctx * width),
+        cost_estimate=cost(2 * 64 * n * depth * n_ctx * width, 2 * depth * n_ctx * width),
         name="project",
-    )(normed, w)
-
-
-def final_kernel(own, sib, up_plain, down_plain, up_sum, down_sum, out):
+    )(normed, w1, w2)
+
+
+def gather_kernel(own, sib, up_plain, down_plain, out):
+    mid = up_plain.shape[1]
+    for start, other in ((0, down_plain), (mid, up_plain)):
+        at = slice(start, start + mid)
+        out[:, at] = own[:, at].astype(f32) + sib[:, at].astype(f32) + other[...].astype(f32)
+
+
+def final_kernel(partial, up_sum, down_sum, out):
     mid = up_sum.shape[1]
-    for start, one, two in ((0, down_plain, up_sum), (mid, up_plain, down_sum)):
+    for start, other in ((0, up_sum), (mid, down_sum)):
         at = slice(start, start + mid)
-        total = own[:, at].astype(f32) + sib[:, at].astype(f32) + one[...].astype(f32) + two[...].astype(f32)
-        out[:, at] = total.astype(bf16)
+        out[:, at] = (partial[:, at] + other[...].astype(f32)).astype(bf16)
 
 
 def after(value, *others):
@@ -282,9 +299,11 @@
 
     depth = activations.shape[1]
     mid = depth // 2
-    low, high = activations[:, :mid], activations[:, mid:]
+    low = activations[:, :mid]
+    high = after(activations, low)[:, mid:]
     left_low, right_high = to_y(low, 1), to_y(high, -1)
-    left_high, right_low = to_y(high, 1), to_y(low, -1)
+    low_b, high_b = after((low, high), g, gt, last, at, pos)
+    left_high, right_low = to_y(high_b, 1), to_y(low_b, -1)
     own2 = to_sibling(activations)
     own2 = after(own2, g, gt, last, at, pos)
     qkv_a, w_qkv = qkv([activations, own2], [(0, 0), (64, 0)], 128, w_qkv, True)
@@ -309,6 +328,7 @@
         "inner",
         4 * 512 * 512 * WIDE,
     )
+    row = after(row, inner)
     before, total = whole_call(
         row_kernel, (at, *row), (jax.ShapeDtypeStruct((WIDE + 8, SIZE), f32), packed), "row", 10 * WIDE * SIZE, 1
     )
@@ -321,30 +341,36 @@
         2 * 512 * WIDE * SIZE,
     )
 
-    w_all = pltpu.with_memory_space_constraint(w_all, pltpu.HBM)
-    far_own, far_sib, w_all = project(normed, w_all, (6, 7), True)
-    far_sib = to_sibling(far_sib)
-    near_parts = project(normed, w_all, (0, 4, 1, 5))
-    far_sib = after(far_sib, near_parts)
+    n = w_all.shape[0] // 2
+    low_own, low_sib, w1 = project_first(normed, w_all, 0, n, 384)
+    low_sib = to_sibling(low_sib)
+    high_own, high_sib, w2 = project_first(after(normed, w1), w_all, n, n, 384)
+    high_sib = to_sibling(high_sib)
+    near_parts = project(after(normed, high_own), w1, w2, (0, 4, 1, 5))
+    low_sib, high_sib = after((low_sib, high_sib), near_parts)
+    far_low, far_high = plus(low_own, low_sib), plus(high_own, high_sib)
+    from_l, from_r = to_y(far_low, 1), to_y(far_high, -1)
     up_own, up_sib, down_own, down_sib = near_parts
-    from_l = to_y(plus(far_own[:, :mid], far_sib[:, :mid]), 1)
-    from_r = to_y(plus(far_own[:, mid:], far_sib[:, mid:]), -1)
     up_sib, down_sib = to_sibling(up_sib), to_sibling(down_sib)
     up_plain = plus(up_own[:, mid:], up_sib[:, mid:])
     down_plain = plus(down_own[:, :mid], down_sib[:, :mid])
     normed = after(normed, up_plain, down_plain)
     up_plain, down_plain = to_y(up_plain, 1), to_y(down_plain, -1)
-    here_own, here_sib = project(normed, w_all, (2, 3))
+    here_own, here_sib = project(normed, w1, w2, (2, 3))
     from_l, from_r = after((from_l, from_r), here_own)
     up_sum = to_y(plus(up_own[:, :mid], up_sib[:, :mid], from_l), 1)
     down_sum = to_y(plus(down_own[:, mid:], down_sib[:, mid:], from_r), -1)
     here_sib = to_sibling(here_sib)
+    partial = whole_call(
+        gather_kernel,
+        (here_own, here_sib, up_plain, down_plain),
+        jax.ShapeDtypeStruct((64, depth), f32),
+        "gather",
+        3 * 64 * depth,
+    )
+    up_sum, down_sum = after((up_sum, down_sum), partial)
     return whole_call(
-        final_kernel,
-        (here_own, here_sib, up_plain, down_plain, up_sum, down_sum),
-        jax.ShapeDtypeStruct((64, depth), bf16),
-        "final",
-        4 * 64 * depth,
+        final_kernel, (partial, up_sum, down_sum), jax.ShapeDtypeStruct((64, depth), bf16), "final", 64 * depth
     )
 
 

time: 130 us -> 129 us (level)
  waiting for transfers between devices: 41.6 us -> 38.3 us
  Pallas kernels: 26.8 us -> 28.3 us
    ppermute x12, waiting for transfers between devices: 26.9 us -> 23.7 us  [to_y(): lax.ppermute(a, 'tp', [(i, (i // 2 + k) % N_Y * 2 + i % 2) for i in range...]
    ppermute x3, waiting for transfers between devices: 11.4 us -> 9.76 us  [to_x(): lax.ppermute(a, 'ctx', [(j, j // N_X * N_X + (j + k) % N_X) for j in rang...]
    ppermute x3, waiting for transfers between devices: 0.63 us -> 2.23 us  [to_z(): lax.ppermute(a, 'ctx', [(j, j + N_X * k) for j in range(N_X * N_Z) if j /...]
    pallas_call x3 -> x4, Pallas kernels: 6.9 us -> 8.38 us  [the longest x2 4.78 us: project_first(): pl.pallas_call(functools.partial(project_first_kernel, base, start), out_...]
    ppermute x11 -> x12, starting transfers between devices: 11.6 us -> 12.5 us  [to_sibling(): return lax.ppermute(a, 'tp', [(i, i ^ 1) for i in range(2 * N_Y)])]
    pallas_call x5 -> x6, Pallas kernels: 4.94 us -> 4.96 us  [whole_call(): pl.pallas_call(kernel, out_shape=outs, in_specs=[pl.BlockSpec(memory_spac...]
  transfers between devices with their start and end apart: 30 -> 31, of which waited for: 13 -> 14; matrix products, arithmetic and copies ran while one was open for 5% -> 5% of each run, Pallas kernels for 17% -> 18%
where the time goes in v4:
time: 129 us; the launch traced here: 128 us
  starting transfers between devices  40.4 us (31%)
  waiting for transfers between devices  38.3 us (30%)
  Pallas kernels  28.3 us (22%)
  between operations  13.7 us (11%)
  local copies, waits for them, and re-layouts  4.77 us (4%)
  other arithmetic  2.94 us (2%)
    ppermute x12, waiting for transfers between devices, to_y(): lax.ppermute(a, 'tp', [(i, (i // 2 + k) % N_Y * 2 + i % 2) for i in range...  23.7 us
    pallas_call x3, Pallas kernels, qkv(): pl.pallas_call(functools.partial(qkv_first_kernel if first else qkv_kerne...  14.9 us
    ppermute x12, starting transfers between devices, to_y(): lax.ppermute(a, 'tp', [(i, (i // 2 + k) % N_Y * 2 + i % 2) for i in range...  12.9 us
    ppermute x12, starting transfers between devices, to_sibling(): return lax.ppermute(a, 'tp', [(i, i ^ 1) for i in range(2 * N_Y)])  12.5 us
    ppermute x3, starting transfers between devices, to_z(): lax.ppermute(a, 'ctx', [(j, j + N_X * k) for j in range(N_X * N_Z) if j /...  10.1 us
    ppermute x3, waiting for transfers between devices, to_x(): lax.ppermute(a, 'ctx', [(j, j // N_X * N_X + (j + k) % N_X) for j in rang...  9.76 us
    pallas_call x6, Pallas kernels, whole_call(): pl.pallas_call(kernel, out_shape=outs, in_specs=[pl.BlockSpec(memory_spac...  4.96 us
    ppermute x3, starting transfers between devices, to_x(): lax.ppermute(a, 'ctx', [(j, j // N_X * N_X + (j + k) % N_X) for j in rang...  4.9 us
  transfers between devices with their start and end apart: 31, of which 14 were waited for; matrix products, arithmetic and copies ran while one was open for 5% of the time, Pallas kernels for 18%

profile of v4, /device:TPU:1, one launch (start us, length us, event | category | flops | bytes accessed | tf_op | source)
XLA Modules:
  0.0 128.4 jit_solution(4613109847724339303)
XLA Ops:
  6.5 0.7 all-gather.3.cloned.1.call-update
  7.3 1.5 %collective-permute-start.3 = (bf16[64,6144]{1,0:T(8,128)(2,1)}, bf16[64,6144]{1,0:T(8,128)(2,1)S(1)}, u32[]{:S(2)}, u32[]{:S(2)}) collective-permute-start(bf16[64,6144]{1,0:T(8,128)(2,1)} %refs_0_.1), channel_id=1, source_target_pairs={{0,1},{1,0},{2,3},{3,2},{4,5},{5,4},{6,7},{7,6},{8,9},{9,8},{10,11... | collective-permute-start | bytes 2359304 | tf_op jit(solution)/shard_map/ppermute | solution.py:34
  8.8 1.0 slice.63
  9.8 1.4 %collective-permute-start.1 = (bf16[64,3072]{1,0:T(8,128)(2,1)S(1)}, bf16[64,3072]{1,0:T(8,128)(2,1)S(1)}, u32[]{:S(2)}, u32[]{:S(2)}) collective-permute-start(bf16[64,3072]{1,0:T(8,128)(2,1)S(1)} %slice.63), channel_id=1, source_target_pairs={{0,2},{1,3},{2,4},{3,5},{4,6},{5,7},{6,0},{7,1},{8,10},{9,11},{10,... | collective-permute-start | bytes 1179656 | tf_op jit(solution)/shard_map/ppermute | solution.py:30
  11.2 1.0 slice.64
  12.3 1.5 %collective-permute-start.2 = (bf16[64,3072]{1,0:T(8,128)(2,1)S(1)}, bf16[64,3072]{1,0:T(8,128)(2,1)S(1)}, u32[]{:S(2)}, u32[]{:S(2)}) collective-permute-start(bf16[64,3072]{1,0:T(8,128)(2,1)S(1)} %slice.64), channel_id=1, source_target_pairs={{0,6},{1,7},{2,0},{3,1},{4,2},{5,3},{6,4},{7,5},{8,14},{9,15},{10,... | collective-permute-start | bytes 1179656 | tf_op jit(solution)/shard_map/ppermute | solution.py:30
  13.8 0.7 reshape.29
  14.5 1.2 reduce-window.6
  17.6 1.5 %collective-permute-start = (bf16[64,3072]{1,0:T(8,128)(2,1)S(1)}, bf16[64,3072]{1,0:T(8,128)(2,1)S(1)}, u32[]{:S(2)}, u32[]{:S(2)}) collective-permute-start(bf16[64,3072]{1,0:T(8,128)(2,1)S(1)} %slice.63), channel_id=1, source_target_pairs={{0,6},{1,7},{2,0},{3,1},{4,2},{5,3},{6,4},{7,5},{8,14},{9,15},{10,... | collective-permute-start | bytes 1179656 | tf_op jit(solution)/shard_map/ppermute | solution.py:30
  19.0 1.1 copy-done
  20.2 7.3 %qkv.3 = (bf16[128,1536]{1,0:T(8,128)(2,1)S(1)}, bf16[3,6144,512]{2,1,0:T(8,128)(2,1)S(1)}) custom-call(bf16[64,6144]{1,0:T(8,128)(2,1)S(1)} %copy-done, bf16[64,6144]{1,0:T(8,128)(2,1)S(1)} %collective-permute-done.3.refs_1_, bf16[3,6144,512]{2,1,0:T(8,128)(2,1)} %refs_2_.1), custom_call_target="tpu_custom_call" | custom-call | flops 24159192 | bytes 188743 | tf_op jit(solution)/shard_map/qkv/pallas_call | solution.py:96
  27.5 2.7 %collective-permute-start.10 = (bf16[64,3072]{1,0:T(8,128)(2,1)S(1)}, bf16[64,3072]{1,0:T(8,128)(2,1)S(1)}, u32[]{:S(2)}, u32[]{:S(2)}) collective-permute-start(bf16[64,3072]{1,0:T(8,128)(2,1)S(1)} %collective-permute-done.2.refs_1_), channel_id=1, source_target_pairs={{0,6},{1,7},{2,0},{3,1},{4,2},{5,3},{6,4},{7,5},{8,14},{9,15},{10,... | collective-permute-start | bytes 1179656 | tf_op jit(solution)/shard_map/ppermute | solution.py:30
  30.2 0.9 collective-permute-done.refs_0_
  31.2 1.8 %collective-permute-start.5 = (bf16[64,3072]{1,0:T(8,128)(2,1)S(1)}, bf16[64,3072]{1,0:T(8,128)(2,1)S(1)}, u32[]{:S(2)}, u32[]{:S(2)}) collective-permute-start(bf16[64,3072]{1,0:T(8,128)(2,1)S(1)} %collective-permute-done.refs_0_), channel_id=1, source_target_pairs={{0,1},{1,0},{2,3},{3,2},{4,5},{5,4},{6,7},{7,6},{8,9},{9,8},{10,11... | collective-permute-start | bytes 1179656 | tf_op jit(solution)/shard_map/ppermute | solution.py:34
  33.5 2.6 %qkv.4.a = bf16[128,1536]{1,0:T(8,128)(2,1)S(1)} custom-call(bf16[64,3072]{1,0:T(8,128)(2,1)S(1)} %collective-permute-done.refs_0_, bf16[64,3072]{1,0:T(8,128)(2,1)S(1)} %collective-permute-done.2.refs_1_, bf16[64,3072]{1,0:T(8,128)(2,1)S(1)} %collective-permute-done.1.refs_2_, bf16[64,3072]{1,0:T(8,128)(2,1)S(1)} %collective-permute-done.4.refs_3_, ...), custom_call_target="tpu_custom_call" | custom-call | flops 24159192 | bytes 188743 | tf_op jit(solution)/shard_map/qkv/pallas_call | solution.py:96
  36.1 3.4 %collective-permute-done.10.refs_5_ = bf16[64,3072]{1,0:T(8,128)(2,1)S(1)} collective-permute-done((bf16[64,3072]{1,0:T(8,128)(2,1)S(1)}, bf16[64,3072]{1,0:T(8,128)(2,1)S(1)}, u32[]{:S(2)}, u32[]{:S(2)}) %collective-permute-start.10) | collective-permute-done | bytes 393248 | tf_op jit(solution)/shard_map/ppermute | solution.py:30
  39.6 1.1 collective-permute-start.7
  40.7 2.3 %collective-permute-start.11 = (bf16[64,3072]{1,0:T(8,128)(2,1)S(1)}, bf16[64,3072]{1,0:T(8,128)(2,1)S(1)}, u32[]{:S(2)}, u32[]{:S(2)}) collective-permute-start(bf16[64,3072]{1,0:T(8,128)(2,1)S(1)} %collective-permute-done.9.refs_4_), channel_id=1, source_target_pairs={{0,1},{1,0},{2,3},{3,2},{4,5},{5,4},{6,7},{7,6},{8,9},{9,8},{10,11... | collective-permute-start | bytes 1179656 | tf_op jit(solution)/shard_map/ppermute | solution.py:34
  43.0 1.3 %collective-permute-done.11.refs_6_ = bf16[64,3072]{1,0:T(8,128)(2,1)S(1)} collective-permute-done((bf16[64,3072]{1,0:T(8,128)(2,1)S(1)}, bf16[64,3072]{1,0:T(8,128)(2,1)S(1)}, u32[]{:S(2)}, u32[]{:S(2)}) %collective-permute-start.11) | collective-permute-done | bytes 393248 | tf_op jit(solution)/shard_map/ppermute | solution.py:34
  44.9 5.0 %qkv.5.c = bf16[256,1536]{1,0:T(8,128)(2,1)S(1)} custom-call(bf16[64,3072]{1,0:T(8,128)(2,1)S(1)} %collective-permute-done.5.refs_0_, bf16[64,3072]{1,0:T(8,128)(2,1)S(1)} %collective-permute-done.6.refs_1_, bf16[64,3072]{1,0:T(8,128)(2,1)S(1)} %collective-permute-done.7.refs_2_, bf16[64,3072]{1,0:T(8,128)(2,1)S(1)} %collective-permute-done.8.refs_3_, ...), custom_call_target="tpu_custom_call" | custom-call | flops 48318384 | bytes 188743 | tf_op jit(solution)/shard_map/qkv/pallas_call | solution.py:96
  49.9 1.0 state.1.s0
  50.9 1.3 %collective-permute-start.13 = (bf16[528,128]{1,0:T(8,128)(2,1)S(1)}, bf16[528,128]{1,0:T(8,128)(2,1)S(1)}, u32[]{:S(2)}, u32[]{:S(2)}) collective-permute-start(bf16[528,128]{1,0:T(8,128)(2,1)S(1)} %state.1.s0), channel_id=1, source_target_pairs={{0,8},{8,16},{16,24},{24,0},{32,40},{40,48},{48,56},{56,32},{64,72... | collective-permute-start | bytes 405512 | tf_op jit(solution)/shard_map/ppermute | solution.py:38
  52.2 2.5 %collective-permute-start.14 = (bf16[528,128]{1,0:T(8,128)(2,1)S(1)}, bf16[528,128]{1,0:T(8,128)(2,1)S(1)}, u32[]{:S(2)}, u32[]{:S(2)}) collective-permute-start(bf16[528,128]{1,0:T(8,128)(2,1)S(1)} %state.1.s0), channel_id=1, source_target_pairs={{0,16},{8,24},{16,0},{24,8},{32,48},{40,56},{48,32},{56,40},{64,80... | collective-permute-start | bytes 405512 | tf_op jit(solution)/shard_map/ppermute | solution.py:38
  54.7 1.1 collective-permute-start.15
  56.0 1.4 %inner.1 = f32[512,512]{1,0:T(8,128)S(1)} custom-call(bf16[128,1536]{1,0:T(8,128)(2,1)S(1)} %qkv.4.a, bf16[128,1536]{1,0:T(8,128)(2,1)S(1)} %get-tuple-element.45.b, bf16[256,1536]{1,0:T(8,128)(2,1)S(1)} %qkv.5.c, f32[512,4]{1,0:T(8,128)S(1)} %bitcast.20, f32[4,512]{1,0:T(4,128)S(1)} %concatenate.8.gt, s32[512,1]{1,0:T(8,128)S(1)} %copy.20.row, ...), custom_call_target="tpu_custom_call" | custom-call | flops 5368709 | bytes 15933 | tf_op jit(solution)/shard_map/inner/pallas_call | solution.py:187
  57.4 3.1 %collective-permute-done.13.s1 = bf16[528,128]{1,0:T(8,128)(2,1)S(1)} collective-permute-done((bf16[528,128]{1,0:T(8,128)(2,1)S(1)}, bf16[528,128]{1,0:T(8,128)(2,1)S(1)}, u32[]{:S(2)}, u32[]{:S(2)}) %collective-permute-start.13) | collective-permute-done | bytes 135200 | tf_op jit(solution)/shard_map/ppermute | solution.py:38
  60.5 6.7 %collective-permute-done.14.s2 = bf16[528,128]{1,0:T(8,128)(2,1)S(1)} collective-permute-done((bf16[528,128]{1,0:T(8,128)(2,1)S(1)}, bf16[528,128]{1,0:T(8,128)(2,1)S(1)}, u32[]{:S(2)}, u32[]{:S(2)}) %collective-permute-start.14) | collective-permute-done | bytes 135200 | tf_op jit(solution)/shard_map/ppermute | solution.py:38
  67.4 3.6 %collective-permute-start.16 = (bf16[528,128]{1,0:T(8,128)(2,1)S(1)}, bf16[528,128]{1,0:T(8,128)(2,1)S(1)}, u32[]{:S(2)}, u32[]{:S(2)}) collective-permute-start(bf16[528,128]{1,0:T(8,128)(2,1)S(1)} %get-tuple-element.57), channel_id=1, source_target_pairs={{0,32},{8,40},{16,48},{24,56},{32,64},{40,72},{48,80},{56,88},{64,... | collective-permute-start | bytes 405512 | tf_op jit(solution)/shard_map/ppermute | solution.py:42
  71.0 5.3 %collective-permute-start.17 = (bf16[528,128]{1,0:T(8,128)(2,1)S(1)}, bf16[528,128]{1,0:T(8,128)(2,1)S(1)}, u32[]{:S(2)}, u32[]{:S(2)}) collective-permute-start(bf16[528,128]{1,0:T(8,128)(2,1)S(1)} %get-tuple-element.57), channel_id=1, source_target_pairs={{0,64},{8,72},{16,80},{24,88},{32,96},{40,104},{48,112},{56,120},{... | collective-permute-start | bytes 405512 | tf_op jit(solution)/shard_map/ppermute | solution.py:42
  76.3 1.3 %collective-permute-start.18 = (bf16[528,128]{1,0:T(8,128)(2,1)S(1)}, bf16[528,128]{1,0:T(8,128)(2,1)S(1)}, u32[]{:S(2)}, u32[]{:S(2)}) collective-permute-start(bf16[528,128]{1,0:T(8,128)(2,1)S(1)} %get-tuple-element.57), channel_id=1, source_target_pairs={{0,96},{8,104},{16,112},{24,120},{1,97},{9,105},{17,113},{25,121},... | collective-permute-start | bytes 405512 | tf_op jit(solution)/shard_map/ppermute | solution.py:42
  78.2 1.6 %collective-permute-done.18.t3 = bf16[528,128]{1,0:T(8,128)(2,1)S(1)} collective-permute-done((bf16[528,128]{1,0:T(8,128)(2,1)S(1)}, bf16[528,128]{1,0:T(8,128)(2,1)S(1)}, u32[]{:S(2)}, u32[]{:S(2)}) %collective-permute-start.18) | collective-permute-done | bytes 135200 | tf_op jit(solution)/shard_map/ppermute | solution.py:42
  79.8 1.0 normed.1
  80.9 2.4 %project.4 = (bf16[64,3072]{1,0:T(8,128)(2,1)S(1)}, bf16[64,3072]{1,0:T(8,128)(2,1)S(1)}, bf16[8,512,384]{2,1,0:T(8,128)(2,1)S(1)}) custom-call(bf16[512,512]{1,0:T(8,128)(2,1)S(1)} %normed.1, bf16[16,512,384]{2,1,0:T(8,128)(2,1)} %bitcast.25), custom_call_target="tpu_custom_call" | custom-call | flops 4026531 | bytes 31457 | tf_op jit(solution)/shard_map/project/pallas_call | solution.py:232
  83.3 2.4 %project.5 = (bf16[64,3072]{1,0:T(8,128)(2,1)S(1)}, bf16[64,3072]{1,0:T(8,128)(2,1)S(1)}, bf16[8,512,384]{2,1,0:T(8,128)(2,1)S(1)}) custom-call(bf16[512,512]{1,0:T(8,128)(2,1)S(1)} %normed.1, bf16[16,512,384]{2,1,0:T(8,128)(2,1)} %bitcast.26), custom_call_target="tpu_custom_call" | custom-call | flops 4026531 | bytes 31457 | tf_op jit(solution)/shard_map/project/pallas_call | solution.py:232
  85.7 2.2 %collective-permute-start.25 = (bf16[64,3072]{1,0:T(8,128)(2,1)S(1)}, bf16[64,3072]{1,0:T(8,128)(2,1)S(1)}, u32[]{:S(2)}, u32[]{:S(2)}) collective-permute-start(bf16[64,3072]{1,0:T(8,128)(2,1)S(1)} %get-tuple-element.72), channel_id=1, source_target_pairs={{0,1},{1,0},{2,3},{3,2},{4,5},{5,4},{6,7},{7,6},{8,9},{9,8},{10,11... | collective-permute-start | bytes 1179656 | tf_op jit(solution)/shard_map/ppermute | solution.py:34
  88.1 2.3 %project.6 = (bf16[64,6144]{1,0:T(8,128)(2,1)S(1)}, bf16[64,6144]{1,0:T(8,128)(2,1)S(1)}, bf16[64,6144]{1,0:T(8,128)(2,1)S(1)}, bf16[64,6144]{1,0:T(8,128)(2,1)S(1)}) custom-call(bf16[512,512]{1,0:T(8,128)(2,1)S(1)} %normed.1, bf16[8,512,384]{2,1,0:T(8,128)(2,1)S(1)} %get-tuple-element.58.w1, bf16[8,512,384]{2,1,0:T(8,128)(2,1)S(1)} %get-tuple-element.62.w2), custom_call_target="tpu_custom_call" | custom-call | flops 16106127 | bytes 62914 | tf_op jit(solution)/shard_map/project/pallas_call | solution.py:249
  91.2 0.9 collective-permute-start.27
  93.0 2.1 %collective-permute-start.23 = (bf16[64,3072]{1,0:T(8,128)(2,1)S(1)}, bf16[64,3072]{1,0:T(8,128)(2,1)S(1)}, u32[]{:S(2)}, u32[]{:S(2)}) collective-permute-start(bf16[64,3072]{1,0:T(8,128)(2,1)S(1)} %add_convert_fusion.4), channel_id=1, source_target_pairs={{0,6},{1,7},{2,0},{3,1},{4,2},{5,3},{6,4},{7,5},{8,14},{9,15},{10,... | collective-permute-start | bytes 1179656 | tf_op jit(solution)/shard_map/ppermute | solution.py:30
  95.3 1.3 project.7
  96.6 5.2 %collective-permute-done.27 = bf16[64,3072]{1,0:T(8,128)(2,1)S(1)} collective-permute-done((bf16[64,3072]{1,0:T(8,128)(2,1)S(1)}, bf16[64,3072]{1,0:T(8,128)(2,1)S(1)}, u32[]{:S(2)}, u32[]{:S(2)}) %collective-permute-start.27) | collective-permute-done | bytes 393248 | tf_op jit(solution)/shard_map/ppermute | solution.py:30
  101.8 1.9 %collective-permute-done.26 = bf16[64,3072]{1,0:T(8,128)(2,1)S(1)} collective-permute-done((bf16[64,3072]{1,0:T(8,128)(2,1)S(1)}, bf16[64,3072]{1,0:T(8,128)(2,1)S(1)}, u32[]{:S(2)}, u32[]{:S(2)}) %collective-permute-start.26) | collective-permute-done | bytes 393248 | tf_op jit(solution)/shard_map/ppermute | solution.py:30
  104.1 2.2 %collective-permute-start.21 = (bf16[64,6144]{1,0:T(8,128)(2,1)S(1)}, bf16[64,6144]{1,0:T(8,128)(2,1)S(1)}, u32[]{:S(2)}, u32[]{:S(2)}) collective-permute-start(bf16[64,6144]{1,0:T(8,128)(2,1)S(1)} %get-tuple-element.69), channel_id=1, source_target_pairs={{0,1},{1,0},{2,3},{3,2},{4,5},{5,4},{6,7},{7,6},{8,9},{9,8},{10,11... | collective-permute-start | bytes 2359304 | tf_op jit(solution)/shard_map/ppermute | solution.py:34
  106.4 1.7 %collective-permute-start.28 = (bf16[64,3072]{1,0:T(8,128)(2,1)S(1)}, bf16[64,3072]{1,0:T(8,128)(2,1)S(1)}, u32[]{:S(2)}, u32[]{:S(2)}) collective-permute-start(bf16[64,3072]{1,0:T(8,128)(2,1)S(1)} %add_convert_fusion.1), channel_id=1, source_target_pairs={{0,2},{1,3},{2,4},{3,5},{4,6},{5,7},{6,0},{7,1},{8,10},{9,11},{10,... | collective-permute-start | bytes 1179656 | tf_op jit(solution)/shard_map/ppermute | solution.py:30
  108.1 2.1 %collective-permute-done.23.down_plain = bf16[64,3072]{1,0:T(8,128)(2,1)S(1)} collective-permute-done((bf16[64,3072]{1,0:T(8,128)(2,1)S(1)}, bf16[64,3072]{1,0:T(8,128)(2,1)S(1)}, u32[]{:S(2)}, u32[]{:S(2)}) %collective-permute-start.23) | collective-permute-done | bytes 393248 | tf_op jit(solution)/shard_map/ppermute | solution.py:30
  110.2 1.9 %collective-permute-done.22.up_plain = bf16[64,3072]{1,0:T(8,128)(2,1)S(1)} collective-permute-done((bf16[64,3072]{1,0:T(8,128)(2,1)S(1)}, bf16[64,3072]{1,0:T(8,128)(2,1)S(1)}, u32[]{:S(2)}, u32[]{:S(2)}) %collective-permute-start.22) | collective-permute-done | bytes 393248 | tf_op jit(solution)/shard_map/ppermute | solution.py:30
  112.4 6.2 %collective-permute-done.29.down_sum = bf16[64,3072]{1,0:T(8,128)(2,1)S(1)} collective-permute-done((bf16[64,3072]{1,0:T(8,128)(2,1)S(1)}, bf16[64,3072]{1,0:T(8,128)(2,1)S(1)}, u32[]{:S(2)}, u32[]{:S(2)}) %collective-permute-start.29) | collective-permute-done | bytes 393248 | tf_op jit(solution)/shard_map/ppermute | solution.py:30
  118.6 1.9 %collective-permute-done.28.up_sum = bf16[64,3072]{1,0:T(8,128)(2,1)S(1)} collective-permute-done((bf16[64,3072]{1,0:T(8,128)(2,1)S(1)}, bf16[64,3072]{1,0:T(8,128)(2,1)S(1)}, u32[]{:S(2)}, u32[]{:S(2)}) %collective-permute-start.28) | collective-permute-done | bytes 393248 | tf_op jit(solution)/shard_map/ppermute | solution.py:30
  120.6 1.0 final.1
  (57 shorter events, 6.7 us)
Async XLA Ops:
  6.5 74.3 %all-gather.3.cloned.1.call-start = ((), (), s32[]{:S(2)}) async-start(), calls=%async_computation | async-start | bytes 6684672 | tf_op jit(solution)/shard_map/all_gather | solution.py:289
  7.3 11.8 %collective-permute-start.3 = (bf16[64,6144]{1,0:T(8,128)(2,1)}, bf16[64,6144]{1,0:T(8,128)(2,1)S(1)}, u32[]{:S(2)}, u32[]{:S(2)}) collective-permute-start(bf16[64,6144]{1,0:T(8,128)(2,1)} %refs_0_.1), channel_id=1, source_target_pairs={{0,1},{1,0},{2,3},{3,2},{4,5},{5,4},{6,7},{7,6},{8,9},{9,8},{10,11... | collective-permute-start | bytes 2359304 | tf_op jit(solution)/shard_map/ppermute | solution.py:34
  9.8 17.7 %collective-permute-start.1 = (bf16[64,3072]{1,0:T(8,128)(2,1)S(1)}, bf16[64,3072]{1,0:T(8,128)(2,1)S(1)}, u32[]{:S(2)}, u32[]{:S(2)}) collective-permute-start(bf16[64,3072]{1,0:T(8,128)(2,1)S(1)} %slice.63), channel_id=1, source_target_pairs={{0,2},{1,3},{2,4},{3,5},{4,6},{5,7},{6,0},{7,1},{8,10},{9,11},{10,... | collective-permute-start | bytes 1179656 | tf_op jit(solution)/shard_map/ppermute | solution.py:30
  12.3 15.2 %collective-permute-start.2 = (bf16[64,3072]{1,0:T(8,128)(2,1)S(1)}, bf16[64,3072]{1,0:T(8,128)(2,1)S(1)}, u32[]{:S(2)}, u32[]{:S(2)}) collective-permute-start(bf16[64,3072]{1,0:T(8,128)(2,1)S(1)} %slice.64), channel_id=1, source_target_pairs={{0,6},{1,7},{2,0},{3,1},{4,2},{5,3},{6,4},{7,5},{8,14},{9,15},{10,... | collective-permute-start | bytes 1179656 | tf_op jit(solution)/shard_map/ppermute | solution.py:30
  17.6 13.6 %collective-permute-start = (bf16[64,3072]{1,0:T(8,128)(2,1)S(1)}, bf16[64,3072]{1,0:T(8,128)(2,1)S(1)}, u32[]{:S(2)}, u32[]{:S(2)}) collective-permute-start(bf16[64,3072]{1,0:T(8,128)(2,1)S(1)} %slice.63), channel_id=1, source_target_pairs={{0,6},{1,7},{2,0},{3,1},{4,2},{5,3},{6,4},{7,5},{8,14},{9,15},{10,... | collective-permute-start | bytes 1179656 | tf_op jit(solution)/shard_map/ppermute | solution.py:30
  19.0 14.0 %collective-permute-start.4 = (bf16[64,3072]{1,0:T(8,128)(2,1)S(1)}, bf16[64,3072]{1,0:T(8,128)(2,1)S(1)}, u32[]{:S(2)}, u32[]{:S(2)}) collective-permute-start(bf16[64,3072]{1,0:T(8,128)(2,1)S(1)} %slice.64), channel_id=1, source_target_pairs={{0,2},{1,3},{2,4},{3,5},{4,6},{5,7},{6,0},{7,1},{8,10},{9,11},{10,... | collective-permute-start | bytes 1179656 | tf_op jit(solution)/shard_map/ppermute | solution.py:30
  19.0 1.1 copy-start
  27.5 12.1 %collective-permute-start.10 = (bf16[64,3072]{1,0:T(8,128)(2,1)S(1)}, bf16[64,3072]{1,0:T(8,128)(2,1)S(1)}, u32[]{:S(2)}, u32[]{:S(2)}) collective-permute-start(bf16[64,3072]{1,0:T(8,128)(2,1)S(1)} %collective-permute-done.2.refs_1_), channel_id=1, source_target_pairs={{0,6},{1,7},{2,0},{3,1},{4,2},{5,3},{6,4},{7,5},{8,14},{9,15},{10,... | collective-permute-start | bytes 1179656 | tf_op jit(solution)/shard_map/ppermute | solution.py:30
  30.2 10.5 %collective-permute-start.9 = (bf16[64,3072]{1,0:T(8,128)(2,1)S(1)}, bf16[64,3072]{1,0:T(8,128)(2,1)S(1)}, u32[]{:S(2)}, u32[]{:S(2)}) collective-permute-start(bf16[64,3072]{1,0:T(8,128)(2,1)S(1)} %collective-permute-done.1.refs_2_), channel_id=1, source_target_pairs={{0,2},{1,3},{2,4},{3,5},{4,6},{5,7},{6,0},{7,1},{8,10},{9,11},{10,... | collective-permute-start | bytes 1179656 | tf_op jit(solution)/shard_map/ppermute | solution.py:30
  31.2 11.8 %collective-permute-start.5 = (bf16[64,3072]{1,0:T(8,128)(2,1)S(1)}, bf16[64,3072]{1,0:T(8,128)(2,1)S(1)}, u32[]{:S(2)}, u32[]{:S(2)}) collective-permute-start(bf16[64,3072]{1,0:T(8,128)(2,1)S(1)} %collective-permute-done.refs_0_), channel_id=1, source_target_pairs={{0,1},{1,0},{2,3},{3,2},{4,5},{5,4},{6,7},{7,6},{8,9},{9,8},{10,11... | collective-permute-start | bytes 1179656 | tf_op jit(solution)/shard_map/ppermute | solution.py:34
  33.0 10.0 %collective-permute-start.8 = (bf16[64,3072]{1,0:T(8,128)(2,1)S(1)}, bf16[64,3072]{1,0:T(8,128)(2,1)S(1)}, u32[]{:S(2)}, u32[]{:S(2)}) collective-permute-start(bf16[64,3072]{1,0:T(8,128)(2,1)S(1)} %collective-permute-done.4.refs_3_), channel_id=1, source_target_pairs={{0,1},{1,0},{2,3},{3,2},{4,5},{5,4},{6,7},{7,6},{8,9},{9,8},{10,11... | collective-permute-start | bytes 1179656 | tf_op jit(solution)/shard_map/ppermute | solution.py:34
  33.0 10.0 %collective-permute-start.6 = (bf16[64,3072]{1,0:T(8,128)(2,1)S(1)}, bf16[64,3072]{1,0:T(8,128)(2,1)S(1)}, u32[]{:S(2)}, u32[]{:S(2)}) collective-permute-start(bf16[64,3072]{1,0:T(8,128)(2,1)S(1)} %collective-permute-done.2.refs_1_), channel_id=1, source_target_pairs={{0,1},{1,0},{2,3},{3,2},{4,5},{5,4},{6,7},{7,6},{8,9},{9,8},{10,11... | collective-permute-start | bytes 1179656 | tf_op jit(solution)/shard_map/ppermute | solution.py:34
  36.1 43.7 %copy-start.1 = (f32[512]{0:T(512)S(1)}, f32[512]{0:T(512)}, u32[]{:S(2)}) copy-start(f32[512]{0:T(512)} %param.10) | copy-start | bytes 6148
  39.6 3.4 %collective-permute-start.7 = (bf16[64,3072]{1,0:T(8,128)(2,1)S(1)}, bf16[64,3072]{1,0:T(8,128)(2,1)S(1)}, u32[]{:S(2)}, u32[]{:S(2)}) collective-permute-start(bf16[64,3072]{1,0:T(8,128)(2,1)S(1)} %collective-permute-done.1.refs_2_), channel_id=1, source_target_pairs={{0,1},{1,0},{2,3},{3,2},{4,5},{5,4},{6,7},{7,6},{8,9},{9,8},{10,11... | collective-permute-start | bytes 1179656 | tf_op jit(solution)/shard_map/ppermute | solution.py:34
  40.7 3.6 %collective-permute-start.11 = (bf16[64,3072]{1,0:T(8,128)(2,1)S(1)}, bf16[64,3072]{1,0:T(8,128)(2,1)S(1)}, u32[]{:S(2)}, u32[]{:S(2)}) collective-permute-start(bf16[64,3072]{1,0:T(8,128)(2,1)S(1)} %collective-permute-done.9.refs_4_), channel_id=1, source_target_pairs={{0,1},{1,0},{2,3},{3,2},{4,5},{5,4},{6,7},{7,6},{8,9},{9,8},{10,11... | collective-permute-start | bytes 1179656 | tf_op jit(solution)/shard_map/ppermute | solution.py:34
  43.0 1.9 %collective-permute-start.12 = (bf16[64,3072]{1,0:T(8,128)(2,1)S(1)}, bf16[64,3072]{1,0:T(8,128)(2,1)S(1)}, u32[]{:S(2)}, u32[]{:S(2)}) collective-permute-start(bf16[64,3072]{1,0:T(8,128)(2,1)S(1)} %collective-permute-done.10.refs_5_), channel_id=1, source_target_pairs={{0,1},{1,0},{2,3},{3,2},{4,5},{5,4},{6,7},{7,6},{8,9},{9,8},{10,11... | collective-permute-start | bytes 1179656 | tf_op jit(solution)/shard_map/ppermute | solution.py:34
  50.9 9.6 %collective-permute-start.13 = (bf16[528,128]{1,0:T(8,128)(2,1)S(1)}, bf16[528,128]{1,0:T(8,128)(2,1)S(1)}, u32[]{:S(2)}, u32[]{:S(2)}) collective-permute-start(bf16[528,128]{1,0:T(8,128)(2,1)S(1)} %state.1.s0), channel_id=1, source_target_pairs={{0,8},{8,16},{16,24},{24,0},{32,40},{40,48},{48,56},{56,32},{64,72... | collective-permute-start | bytes 405512 | tf_op jit(solution)/shard_map/ppermute | solution.py:38
  52.2 15.0 %collective-permute-start.14 = (bf16[528,128]{1,0:T(8,128)(2,1)S(1)}, bf16[528,128]{1,0:T(8,128)(2,1)S(1)}, u32[]{:S(2)}, u32[]{:S(2)}) collective-permute-start(bf16[528,128]{1,0:T(8,128)(2,1)S(1)} %state.1.s0), channel_id=1, source_target_pairs={{0,16},{8,24},{16,0},{24,8},{32,48},{40,56},{48,32},{56,40},{64,80... | collective-permute-start | bytes 405512 | tf_op jit(solution)/shard_map/ppermute | solution.py:38
  54.7 12.5 %collective-permute-start.15 = (bf16[528,128]{1,0:T(8,128)(2,1)S(1)}, bf16[528,128]{1,0:T(8,128)(2,1)S(1)}, u32[]{:S(2)}, u32[]{:S(2)}) collective-permute-start(bf16[528,128]{1,0:T(8,128)(2,1)S(1)} %state.1.s0), channel_id=1, source_target_pairs={{0,24},{8,0},{16,8},{24,16},{32,56},{40,32},{48,40},{56,48},{64,88... | collective-permute-start | bytes 405512 | tf_op jit(solution)/shard_map/ppermute | solution.py:38
  67.4 10.1 %collective-permute-start.16 = (bf16[528,128]{1,0:T(8,128)(2,1)S(1)}, bf16[528,128]{1,0:T(8,128)(2,1)S(1)}, u32[]{:S(2)}, u32[]{:S(2)}) collective-permute-start(bf16[528,128]{1,0:T(8,128)(2,1)S(1)} %get-tuple-element.57), channel_id=1, source_target_pairs={{0,32},{8,40},{16,48},{24,56},{32,64},{40,72},{48,80},{56,88},{64,... | collective-permute-start | bytes 405512 | tf_op jit(solution)/shard_map/ppermute | solution.py:42
  71.0 7.2 %collective-permute-start.17 = (bf16[528,128]{1,0:T(8,128)(2,1)S(1)}, bf16[528,128]{1,0:T(8,128)(2,1)S(1)}, u32[]{:S(2)}, u32[]{:S(2)}) collective-permute-start(bf16[528,128]{1,0:T(8,128)(2,1)S(1)} %get-tuple-element.57), channel_id=1, source_target_pairs={{0,64},{8,72},{16,80},{24,88},{32,96},{40,104},{48,112},{56,120},{... | collective-permute-start | bytes 405512 | tf_op jit(solution)/shard_map/ppermute | solution.py:42
  76.3 3.5 %collective-permute-start.18 = (bf16[528,128]{1,0:T(8,128)(2,1)S(1)}, bf16[528,128]{1,0:T(8,128)(2,1)S(1)}, u32[]{:S(2)}, u32[]{:S(2)}) collective-permute-start(bf16[528,128]{1,0:T(8,128)(2,1)S(1)} %get-tuple-element.57), channel_id=1, source_target_pairs={{0,96},{8,104},{16,112},{24,120},{1,97},{9,105},{17,113},{25,121},... | collective-permute-start | bytes 405512 | tf_op jit(solution)/shard_map/ppermute | solution.py:42
  85.7 5.4 %collective-permute-start.25 = (bf16[64,3072]{1,0:T(8,128)(2,1)S(1)}, bf16[64,3072]{1,0:T(8,128)(2,1)S(1)}, u32[]{:S(2)}, u32[]{:S(2)}) collective-permute-start(bf16[64,3072]{1,0:T(8,128)(2,1)S(1)} %get-tuple-element.72), channel_id=1, source_target_pairs={{0,1},{1,0},{2,3},{3,2},{4,5},{5,4},{6,7},{7,6},{8,9},{9,8},{10,11... | collective-permute-start | bytes 1179656 | tf_op jit(solution)/shard_map/ppermute | solution.py:34
  87.8 3.3 %collective-permute-start.24 = (bf16[64,3072]{1,0:T(8,128)(2,1)S(1)}, bf16[64,3072]{1,0:T(8,128)(2,1)S(1)}, u32[]{:S(2)}, u32[]{:S(2)}) collective-permute-start(bf16[64,3072]{1,0:T(8,128)(2,1)S(1)} %get-tuple-element.71), channel_id=1, source_target_pairs={{0,1},{1,0},{2,3},{3,2},{4,5},{5,4},{6,7},{7,6},{8,9},{9,8},{10,11... | collective-permute-start | bytes 1179656 | tf_op jit(solution)/shard_map/ppermute | solution.py:34
  90.5 2.4 %collective-permute-start.20 = (bf16[64,6144]{1,0:T(8,128)(2,1)S(1)}, bf16[64,6144]{1,0:T(8,128)(2,1)S(1)}, u32[]{:S(2)}, u32[]{:S(2)}) collective-permute-start(bf16[64,6144]{1,0:T(8,128)(2,1)S(1)} %get-tuple-element.66), channel_id=1, source_target_pairs={{0,1},{1,0},{2,3},{3,2},{4,5},{5,4},{6,7},{7,6},{8,9},{9,8},{10,11... | collective-permute-start | bytes 2359304 | tf_op jit(solution)/shard_map/ppermute | solution.py:34
  90.8 4.4 %collective-permute-start.19 = (bf16[64,6144]{1,0:T(8,128)(2,1)S(1)}, bf16[64,6144]{1,0:T(8,128)(2,1)S(1)}, u32[]{:S(2)}, u32[]{:S(2)}) collective-permute-start(bf16[64,6144]{1,0:T(8,128)(2,1)S(1)} %get-tuple-element.64), channel_id=1, source_target_pairs={{0,1},{1,0},{2,3},{3,2},{4,5},{5,4},{6,7},{7,6},{8,9},{9,8},{10,11... | collective-permute-start | bytes 2359304 | tf_op jit(solution)/shard_map/ppermute | solution.py:34
  91.2 10.6 %collective-permute-start.27 = (bf16[64,3072]{1,0:T(8,128)(2,1)S(1)}, bf16[64,3072]{1,0:T(8,128)(2,1)S(1)}, u32[]{:S(2)}, u32[]{:S(2)}) collective-permute-start(bf16[64,3072]{1,0:T(8,128)(2,1)S(1)} %add_convert_fusion.2), channel_id=1, source_target_pairs={{0,6},{1,7},{2,0},{3,1},{4,2},{5,3},{6,4},{7,5},{8,14},{9,15},{10,... | collective-permute-start | bytes 1179656 | tf_op jit(solution)/shard_map/ppermute | solution.py:30
  92.2 11.5 %collective-permute-start.26 = (bf16[64,3072]{1,0:T(8,128)(2,1)S(1)}, bf16[64,3072]{1,0:T(8,128)(2,1)S(1)}, u32[]{:S(2)}, u32[]{:S(2)}) collective-permute-start(bf16[64,3072]{1,0:T(8,128)(2,1)S(1)} %add_convert_fusion.3), channel_id=1, source_target_pairs={{0,2},{1,3},{2,4},{3,5},{4,6},{5,7},{6,0},{7,1},{8,10},{9,11},{10,... | collective-permute-start | bytes 1179656 | tf_op jit(solution)/shard_map/ppermute | solution.py:30
  93.0 17.2 %collective-permute-start.23 = (bf16[64,3072]{1,0:T(8,128)(2,1)S(1)}, bf16[64,3072]{1,0:T(8,128)(2,1)S(1)}, u32[]{:S(2)}, u32[]{:S(2)}) collective-permute-start(bf16[64,3072]{1,0:T(8,128)(2,1)S(1)} %add_convert_fusion.4), channel_id=1, source_target_pairs={{0,6},{1,7},{2,0},{3,1},{4,2},{5,3},{6,4},{7,5},{8,14},{9,15},{10,... | collective-permute-start | bytes 1179656 | tf_op jit(solution)/shard_map/ppermute | solution.py:30
  95.2 16.9 %collective-permute-start.22 = (bf16[64,3072]{1,0:T(8,128)(2,1)S(1)}, bf16[64,3072]{1,0:T(8,128)(2,1)S(1)}, u32[]{:S(2)}, u32[]{:S(2)}) collective-permute-start(bf16[64,3072]{1,0:T(8,128)(2,1)S(1)} %add_convert_fusion.5), channel_id=1, source_target_pairs={{0,2},{1,3},{2,4},{3,5},{4,6},{5,7},{6,0},{7,1},{8,10},{9,11},{10,... | collective-permute-start | bytes 1179656 | tf_op jit(solution)/shard_map/ppermute | solution.py:30
  103.8 14.8 %collective-permute-start.29 = (bf16[64,3072]{1,0:T(8,128)(2,1)S(1)}, bf16[64,3072]{1,0:T(8,128)(2,1)S(1)}, u32[]{:S(2)}, u32[]{:S(2)}) collective-permute-start(bf16[64,3072]{1,0:T(8,128)(2,1)S(1)} %add_convert_fusion), channel_id=1, source_target_pairs={{0,6},{1,7},{2,0},{3,1},{4,2},{5,3},{6,4},{7,5},{8,14},{9,15},{10,... | collective-permute-start | bytes 1179656 | tf_op jit(solution)/shard_map/ppermute | solution.py:30
  104.1 8.1 %collective-permute-start.21 = (bf16[64,6144]{1,0:T(8,128)(2,1)S(1)}, bf16[64,6144]{1,0:T(8,128)(2,1)S(1)}, u32[]{:S(2)}, u32[]{:S(2)}) collective-permute-start(bf16[64,6144]{1,0:T(8,128)(2,1)S(1)} %get-tuple-element.69), channel_id=1, source_target_pairs={{0,1},{1,0},{2,3},{3,2},{4,5},{5,4},{6,7},{7,6},{8,9},{9,8},{10,11... | collective-permute-start | bytes 2359304 | tf_op jit(solution)/shard_map/ppermute | solution.py:34
  106.4 14.2 %collective-permute-start.28 = (bf16[64,3072]{1,0:T(8,128)(2,1)S(1)}, bf16[64,3072]{1,0:T(8,128)(2,1)S(1)}, u32[]{:S(2)}, u32[]{:S(2)}) collective-permute-start(bf16[64,3072]{1,0:T(8,128)(2,1)S(1)} %add_convert_fusion.1), channel_id=1, source_target_pairs={{0,2},{1,3},{2,4},{3,5},{4,6},{5,7},{6,0},{7,1},{8,10},{9,11},{10,... | collective-permute-start | bytes 1179656 | tf_op jit(solution)/shard_map/ppermute | solution.py:30
Sparse Core Ops, SparseCore 0:
  9.5 70.1 all-gather.2

commit v5 on v4

--- a/solution.py
+++ b/solution.py
@@ -13,9 +13,10 @@
 HEADS, SIZE = 4, 128
 WIDE = HEADS * SIZE
 N_X = N_Z = N_Y = 4
+FAR = 384
 PLACES = ((1, 0), (3, 0), (0, 0), (0, 1), (1, 1), (3, 1), (2, 0), (2, 1))
 SHARE = 0.01
-VMEM_LIMIT = 20 * 2**20
+VMEM_LIMIT = 24 * 2**20
 
 
 def params(**kw):
@@ -121,22 +122,22 @@
     return tail[0:4] + tail[4:8] + tail[8:12]
 
 
-def state_kernel(a, b, c, g, last, out):
+def state_kernel(a, b, c, d, g, last, out):
     for h in range(HEADS):
-        keys = columns((a, b, c), WIDE + h * SIZE).astype(f32)
-        values = columns((a, b, c), 2 * WIDE + h * SIZE)
+        keys = columns((a, b, c, d), WIDE + h * SIZE).astype(f32)
+        values = columns((a, b, c, d), 2 * WIDE + h * SIZE)
         scaled = (keys * jnp.exp(last[h : h + 1, 0:1] - g[:, h : h + 1])).astype(bf16)
         state = lax.dot_general(scaled, values, (((0,), (0,)), ((), ())), preferred_element_type=f32)
         out[h * SIZE : (h + 1) * SIZE, :] = state.astype(bf16)
     pack(out, last[...])
 
 
-def inner_kernel(a, b, c, g, gt, row, col, out):
+def inner_kernel(a, b, c, d, g, gt, row, col, out):
     lower = row[...] >= col[...]
     for h in range(HEADS):
-        query = columns((a, b, c), h * SIZE)
-        keys = columns((a, b, c), WIDE + h * SIZE)
-        values = columns((a, b, c), 2 * WIDE + h * SIZE)
+        query = columns((a, b, c, d), h * SIZE)
+        keys = columns((a, b, c, d), WIDE + h * SIZE)
+        values = columns((a, b, c, d), 2 * WIDE + h * SIZE)
         scores = lax.dot_general(query, keys, (((1,), (1,)), ((), ())), preferred_element_type=f32)
         lagged = g[:, h : h + 1] - gt[h : h + 1, :]
         probs = jnp.where(lower, scores * jnp.exp(jnp.minimum(lagged, 0.0)), 0.0).astype(bf16)
@@ -164,7 +165,13 @@
     before[WIDE:, :] = jnp.concatenate([lead, lead], axis=0)
 
 
-def normed_kernel(before, t1, t2, t3, a, b, c, g, inner, gain, out):
+def normed_kernel(before, t1, t2, t3, a, b, c, d, g, inner, gain, w, out, own, sib, held, sems):
+    per = w.shape[0] // 4
+    copies = [
+        pltpu.make_async_copy(w.at[pl.ds(i * per, per)], held.at[pl.ds(i * per, per)], sems.at[i]) for i in range(4)
+    ]
+    for copy in copies:
+        copy.start()
     lead = jnp.exp(before[WIDE : WIDE + HEADS, :])
     r1, r2 = unpack(t1), unpack(t2)
     reach2, reach3 = jnp.exp(r1), jnp.exp(r1 + r2)
@@ -175,11 +182,16 @@
             t1[rows, :].astype(f32) + t2[rows, :].astype(f32) * reach2[one] + t3[rows, :].astype(f32) * reach3[one]
         )
         carried = (earlier * lead[one] + before[rows, :]).astype(bf16)
-        query = columns((a, b, c), h * SIZE).astype(f32)
+        query = columns((a, b, c, d), h * SIZE).astype(f32)
         scaled = (query * jnp.exp(g[:, one])).astype(bf16)
         mixed = inner[:, rows] + jnp.dot(scaled, carried, preferred_element_type=f32)
         scale = lax.rsqrt(jnp.mean(mixed * mixed, axis=-1, keepdims=True) + norm_eps)
         out[:, rows] = (mixed * scale * gain[:, rows]).astype(bf16)
+    far = out[FAR : FAR + 128, :]
+    for i in range(4):
+        copies[i].wait()
+        for m in range(i * per, (i + 1) * per):
+            project_part(far, held, (own, sib), m)
 
 
 def whole_call(kernel, args, outs, name, flops, scalars=0):
@@ -196,65 +208,32 @@
     )(*args)
 
 
-def project_part(rows, w, outs, m, start):
+def project_part(rows, w, outs, m):
     width = w.shape[2]
     part = jnp.dot(rows, w[m], preferred_element_type=f32).astype(bf16)
     for i, out in enumerate(outs):
-        out[:, start + m * width : start + (m + 1) * width] = part[i * 64 : (i + 1) * 64]
-
-
-def project_first_kernel(base, start, normed, w, own, sib, held, sems):
-    per = held.shape[0] // 4
-    copies = [
-        pltpu.make_async_copy(w.at[pl.ds(base + i * per, per)], held.at[pl.ds(i * per, per)], sems.at[i])
-        for i in range(4)
-    ]
-    for copy in copies:
-        copy.start()
-    rows = normed[start : start + 128, :]
-    for i in range(4):
-        copies[i].wait()
-        for m in range(i * per, (i + 1) * per):
-            project_part(rows, held, (own, sib), m, 0)
-
-
-def project_kernel(blocks, normed, w1, w2, *outs):
+        out[:, m * width : (m + 1) * width] = part[i * 64 : (i + 1) * 64]
+
+
+def project_kernel(blocks, normed, w, *outs):
     rows = jnp.concatenate([normed[64 * b : 64 * b + 64, :] for b in blocks], axis=0)
-    for m in range(w1.shape[0]):
-        project_part(rows, w1, outs, m, 0)
-        project_part(rows, w2, outs, m, outs[0].shape[1] // 2)
-
-
-def project_first(normed, w, base, count, start):
-    _, depth, width = w.shape
-    vmem = pl.BlockSpec(memory_space=pltpu.VMEM)
-    half = jax.ShapeDtypeStruct((64, count * width), bf16)
-    return pl.pallas_call(
-        functools.partial(project_first_kernel, base, start),
-        out_shape=[half, half, pltpu.VMEM((count, depth, width), bf16)],
-        in_specs=[vmem, pl.BlockSpec(memory_space=pltpu.HBM)],
-        out_specs=[vmem] * 3,
-        scratch_shapes=[pltpu.SemaphoreType.DMA((4,))],
-        compiler_params=params(),
-        cost_estimate=cost(256 * depth * count * width, 2 * depth * count * width),
-        name="project",
-    )(normed, pltpu.with_memory_space_constraint(w, pltpu.HBM))
-
-
-def project(normed, w1, w2, blocks):
-    n_ctx, depth, width = w1.shape
-    n_ctx += w2.shape[0]
+    for m in range(w.shape[0]):
+        project_part(rows, w, outs, m)
+
+
+def project(normed, w, blocks):
+    n_ctx, depth, width = w.shape
     vmem = pl.BlockSpec(memory_space=pltpu.VMEM)
     n = len(blocks)
     return pl.pallas_call(
         functools.partial(project_kernel, blocks),
         out_shape=[jax.ShapeDtypeStruct((64, n_ctx * width), bf16)] * n,
-        in_specs=[vmem] * 3,
+        in_specs=[vmem] * 2,
         out_specs=[vmem] * n,
         compiler_params=params(),
         cost_estimate=cost(2 * 64 * n * depth * n_ctx * width, 2 * depth * n_ctx * width),
         name="project",
-    )(normed, w1, w2)
+    )(normed, w)
 
 
 def gather_kernel(own, sib, up_plain, down_plain, out):
@@ -305,18 +284,21 @@
     low_b, high_b = after((low, high), g, gt, last, at, pos)
     left_high, right_low = to_y(high_b, 1), to_y(low_b, -1)
     own2 = to_sibling(activations)
-    own2 = after(own2, g, gt, last, at, pos)
+    far_low, far_high = to_y(left_low, 1), to_y(right_high, -1)
+    own2 = after(own2, g, gt, last, at, pos, left_low, right_high)
     qkv_a, w_qkv = qkv([activations, own2], [(0, 0), (64, 0)], 128, w_qkv, True)
-    left_low, right_high = after((left_low, right_high), qkv_a)
-    far_low, far_high = to_y(left_low, 1), to_y(right_high, -1)
     low2, high2 = to_sibling(left_low), to_sibling(right_high)
+    left_high, right_low = after((left_high, right_low), qkv_a)
     left_high2, right_low2 = to_sibling(left_high), to_sibling(right_low)
-    near = [right_low, right_high, left_low, left_high]
-    qkv_b = qkv(near, [(0, 0), (0, mid), (64, 0), (64, mid)], 128, w_qkv)
+    halves = [(0, 0), (0, mid), (64, 0), (64, mid)]
+    qkv_b = qkv([right_low, right_high, left_low, left_high], halves, 128, w_qkv)
     far_low, far_high = after((far_low, far_high), qkv_b)
-    rest = [right_low2, high2, low2, left_high2, far_low, far_high, to_sibling(far_low), to_sibling(far_high)]
-    qkv_c = qkv(rest, [(64 * i, col) for i in range(4) for col in (0, mid)], 256, w_qkv)
-    rows = (qkv_b, qkv_a, qkv_c)
+    far_low2, far_high2 = to_sibling(far_low), to_sibling(far_high)
+    near2 = after([right_low2, high2, low2, left_high2], far_low, far_high)
+    qkv_c = qkv(near2, halves, 128, w_qkv)
+    far_low2, far_high2 = after((far_low2, far_high2), qkv_c)
+    qkv_d = qkv([far_low, far_high, far_low2, far_high2], halves, 128, w_qkv)
+    rows = (qkv_b, qkv_a, qkv_c, qkv_d)
 
     packed = jax.ShapeDtypeStruct((WIDE + 16, SIZE), bf16)
     state = whole_call(state_kernel, (*rows, g, last), packed, "state", 2 * 512 * WIDE * SIZE)
@@ -333,30 +315,32 @@
         row_kernel, (at, *row), (jax.ShapeDtypeStruct((WIDE + 8, SIZE), f32), packed), "row", 10 * WIDE * SIZE, 1
     )
     totals = [to_z(total, k) for k in range(1, N_Z)]
-    normed = whole_call(
+    vmem = pl.BlockSpec(memory_space=pltpu.VMEM)
+    args = (before, *totals, *rows, g, inner, gain.reshape(1, WIDE))
+    half = jax.ShapeDtypeStruct((64, depth), bf16)
+    normed, far_own, far_sib, w = pl.pallas_call(
         normed_kernel,
-        (before, *totals, *rows, g, inner, gain.reshape(1, WIDE)),
-        jax.ShapeDtypeStruct((512, WIDE), bf16),
-        "normed",
-        2 * 512 * WIDE * SIZE,
-    )
-
-    n = w_all.shape[0] // 2
-    low_own, low_sib, w1 = project_first(normed, w_all, 0, n, 384)
-    low_sib = to_sibling(low_sib)
-    high_own, high_sib, w2 = project_first(after(normed, w1), w_all, n, n, 384)
-    high_sib = to_sibling(high_sib)
-    near_parts = project(after(normed, high_own), w1, w2, (0, 4, 1, 5))
-    low_sib, high_sib = after((low_sib, high_sib), near_parts)
-    far_low, far_high = plus(low_own, low_sib), plus(high_own, high_sib)
-    from_l, from_r = to_y(far_low, 1), to_y(far_high, -1)
+        out_shape=[jax.ShapeDtypeStruct((512, WIDE), bf16), half, half, pltpu.VMEM(w_all.shape, bf16)],
+        in_specs=[vmem] * len(args) + [pl.BlockSpec(memory_space=pltpu.HBM)],
+        out_specs=[vmem] * 4,
+        scratch_shapes=[pltpu.SemaphoreType.DMA((4,))],
+        compiler_params=params(),
+        cost_estimate=cost(2 * 512 * WIDE * SIZE, 2 * w_all.size),
+        name="normed",
+    )(*args, pltpu.with_memory_space_constraint(w_all, pltpu.HBM))
+
+    far_sib = to_sibling(far_sib)
+    near_parts = project(normed, w, (0, 4, 1, 5))
+    far_sib = after(far_sib, near_parts)
+    from_l = to_y(plus(far_own[:, :mid], far_sib[:, :mid]), 1)
+    from_r = to_y(plus(far_own[:, mid:], far_sib[:, mid:]), -1)
     up_own, up_sib, down_own, down_sib = near_parts
     up_sib, down_sib = to_sibling(up_sib), to_sibling(down_sib)
     up_plain = plus(up_own[:, mid:], up_sib[:, mid:])
     down_plain = plus(down_own[:, :mid], down_sib[:, :mid])
     normed = after(normed, up_plain, down_plain)
     up_plain, down_plain = to_y(up_plain, 1), to_y(down_plain, -1)
-    here_own, here_sib = project(normed, w1, w2, (2, 3))
+    here_own, here_sib = project(normed, w, (2, 3))
     from_l, from_r = after((from_l, from_r), here_own)
     up_sum = to_y(plus(up_own[:, :mid], up_sib[:, :mid], from_l), 1)
     down_sum = to_y(plus(down_own[:, mid:], down_sib[:, mid:], from_r), -1)

time: 129 us -> 133 us (1.031)
  local copies, waits for them, and re-layouts: 4.77 us -> 7.85 us
    ppermute x12 -> x11, starting transfers between devices: 12.5 us -> 9.83 us  [to_sibling(): return lax.ppermute(a, 'tp', [(i, i ^ 1) for i in range(2 * N_Y)])]
    ppermute x12, starting transfers between devices: 12.9 us -> 14.6 us  [to_y(): lax.ppermute(a, 'tp', [(i, (i // 2 + k) % N_Y * 2 + i % 2) for i in range...]
    unnamed x4 -> x8, local copies, waits for them, and re-layouts: 1.14 us -> 2.72 us
    pallas_call x3 -> x4, Pallas kernels: 14.9 us -> 15.8 us  [qkv(): pl.pallas_call(functools.partial(qkv_first_kernel if first else qkv_kerne...]
    pallas_call x2 -> x1, Pallas kernels: 4.78 us -> 4.02 us  [body(): pl.pallas_call(normed_kernel, out_shape=[jax.ShapeDtypeStruct((512, WIDE)...]
    pallas_call x6 -> x5, Pallas kernels: 4.96 us -> 4.9 us  [whole_call(): pl.pallas_call(kernel, out_shape=outs, in_specs=[pl.BlockSpec(memory_spac...]
  transfers between devices with their start and end apart: 31 -> 30, of which waited for: 14 -> 11; matrix products, arithmetic and copies ran while one was open for 5% -> 6% of each run, Pallas kernels for 18% -> 16%
where the time goes in v5:
time: 133 us; the launch traced here: 132 us
  starting transfers between devices  39.6 us (30%)
  waiting for transfers between devices  39.1 us (29%)
  Pallas kernels  28.5 us (21%)
  between operations  13.7 us (10%)
  local copies, waits for them, and re-layouts  7.85 us (6%)
  other arithmetic  2.96 us (2%)
    ppermute x12, waiting for transfers between devices, to_y(): lax.ppermute(a, 'tp', [(i, (i // 2 + k) % N_Y * 2 + i % 2) for i in range...  24.2 us
    pallas_call x4, Pallas kernels, qkv(): pl.pallas_call(functools.partial(qkv_first_kernel if first else qkv_kerne...  15.8 us
    ppermute x12, starting transfers between devices, to_y(): lax.ppermute(a, 'tp', [(i, (i // 2 + k) % N_Y * 2 + i % 2) for i in range...  14.6 us
    ppermute x3, starting transfers between devices, to_z(): lax.ppermute(a, 'ctx', [(j, j + N_X * k) for j in range(N_X * N_Z) if j /...  10.3 us
    ppermute x3, waiting for transfers between devices, to_x(): lax.ppermute(a, 'ctx', [(j, j // N_X * N_X + (j + k) % N_X) for j in rang...  9.89 us
    ppermute x11, starting transfers between devices, to_sibling(): return lax.ppermute(a, 'tp', [(i, i ^ 1) for i in range(2 * N_Y)])  9.83 us
    pallas_call x5, Pallas kernels, whole_call(): pl.pallas_call(kernel, out_shape=outs, in_specs=[pl.BlockSpec(memory_spac...  4.9 us
    ppermute x3, starting transfers between devices, to_x(): lax.ppermute(a, 'ctx', [(j, j // N_X * N_X + (j + k) % N_X) for j in rang...  4.9 us
  transfers between devices with their start and end apart: 30, of which 11 were waited for; matrix products, arithmetic and copies ran while one was open for 6% of the time, Pallas kernels for 16%

profile of v5, /device:TPU:1, one launch (start us, length us, event | category | flops | bytes accessed | tf_op | source)
XLA Modules:
  0.0 131.7 jit_solution(12565594177740683439)
XLA Ops:
  6.5 0.7 all-gather.3.cloned.1.call-update
  7.3 1.5 %collective-permute-start.2 = (bf16[64,6144]{1,0:T(8,128)(2,1)}, bf16[64,6144]{1,0:T(8,128)(2,1)S(1)}, u32[]{:S(2)}, u32[]{:S(2)}) collective-permute-start(bf16[64,6144]{1,0:T(8,128)(2,1)} %refs_0_.1), channel_id=1, source_target_pairs={{0,1},{1,0},{2,3},{3,2},{4,5},{5,4},{6,7},{7,6},{8,9},{9,8},{10,11... | collective-permute-start | bytes 2359304 | tf_op jit(solution)/shard_map/ppermute | solution.py:35
  8.8 1.8 %slice.75 = bf16[64,3072]{1,0:T(8,128)(2,1)} slice(bf16[64,6144]{1,0:T(8,128)(2,1)} %refs_0_.1), slice={[0:64], [0:3072]} | slice | bytes 786432 | tf_op jit(solution)/shard_map/slice | solution.py:281
  10.5 1.4 %collective-permute-start.3 = (bf16[64,3072]{1,0:T(8,128)(2,1)}, bf16[64,3072]{1,0:T(8,128)(2,1)S(1)}, u32[]{:S(2)}, u32[]{:S(2)}) collective-permute-start(bf16[64,3072]{1,0:T(8,128)(2,1)} %slice.75), channel_id=1, source_target_pairs={{0,2},{1,3},{2,4},{3,5},{4,6},{5,7},{6,0},{7,1},{8,10},{9,11},{10,... | collective-permute-start | bytes 1179656 | tf_op jit(solution)/shard_map/ppermute | solution.py:31
  11.9 1.8 %slice.76 = bf16[64,3072]{1,0:T(8,128)(2,1)} slice(bf16[64,6144]{1,0:T(8,128)(2,1)} %refs_0_.1), slice={[0:64], [3072:6144]} | slice | bytes 786432 | tf_op jit(solution)/shard_map/slice | solution.py:282
  13.7 1.4 %collective-permute-start.4 = (bf16[64,3072]{1,0:T(8,128)(2,1)}, bf16[64,3072]{1,0:T(8,128)(2,1)}, u32[]{:S(2)}, u32[]{:S(2)}) collective-permute-start(bf16[64,3072]{1,0:T(8,128)(2,1)} %slice.76), channel_id=1, source_target_pairs={{0,6},{1,7},{2,0},{3,1},{4,2},{5,3},{6,4},{7,5},{8,14},{9,15},{10,... | collective-permute-start | bytes 1179656 | tf_op jit(solution)/shard_map/ppermute | solution.py:31
  15.1 0.7 reshape.29
  15.8 1.2 reduce-window.6
  18.1 0.7 fusion.1
  18.9 2.7 %collective-permute-start.1 = (bf16[64,3072]{1,0:T(8,128)(2,1)}, bf16[64,3072]{1,0:T(8,128)(2,1)S(1)}, u32[]{:S(2)}, u32[]{:S(2)}) collective-permute-start(bf16[64,3072]{1,0:T(8,128)(2,1)} %slice.75), channel_id=1, source_target_pairs={{0,6},{1,7},{2,0},{3,1},{4,2},{5,3},{6,4},{7,5},{8,14},{9,15},{10,... | collective-permute-start | bytes 1179656 | tf_op jit(solution)/shard_map/ppermute | solution.py:31
  21.6 1.3 collective-permute-done.3.refs_2_
  22.9 1.5 %collective-permute-done.4.refs_1_ = bf16[64,3072]{1,0:T(8,128)(2,1)} collective-permute-done((bf16[64,3072]{1,0:T(8,128)(2,1)}, bf16[64,3072]{1,0:T(8,128)(2,1)}, u32[]{:S(2)}, u32[]{:S(2)}) %collective-permute-start.4) | collective-permute-done | bytes 393248 | tf_op jit(solution)/shard_map/ppermute | solution.py:31
  24.4 2.8 %collective-permute-start.10 = (bf16[64,3072]{1,0:T(8,128)(2,1)}, bf16[64,3072]{1,0:T(8,128)(2,1)S(1)}, u32[]{:S(2)}, u32[]{:S(2)}) collective-permute-start(bf16[64,3072]{1,0:T(8,128)(2,1)} %collective-permute-done.4.refs_1_), channel_id=1, source_target_pairs={{0,6},{1,7},{2,0},{3,1},{4,2},{5,3},{6,4},{7,5},{8,14},{9,15},{10,... | collective-permute-start | bytes 1179656 | tf_op jit(solution)/shard_map/ppermute | solution.py:31
  27.2 1.8 %collective-permute-start.6 = (bf16[64,3072]{1,0:T(8,128)(2,1)}, bf16[64,3072]{1,0:T(8,128)(2,1)S(1)}, u32[]{:S(2)}, u32[]{:S(2)}) collective-permute-start(bf16[64,3072]{1,0:T(8,128)(2,1)} %collective-permute-done.4.refs_1_), channel_id=1, source_target_pairs={{0,1},{1,0},{2,3},{3,2},{4,5},{5,4},{6,7},{7,6},{8,9},{9,8},{10,11... | collective-permute-start | bytes 1179656 | tf_op jit(solution)/shard_map/ppermute | solution.py:35
  29.0 1.2 copy-done
  30.2 7.0 %qkv.4 = (bf16[128,1536]{1,0:T(8,128)(2,1)S(1)}, bf16[3,6144,512]{2,1,0:T(8,128)(2,1)S(1)}) custom-call(bf16[64,6144]{1,0:T(8,128)(2,1)S(1)} %copy-done, bf16[64,6144]{1,0:T(8,128)(2,1)S(1)} %collective-permute-done.2.refs_1_, bf16[3,6144,512]{2,1,0:T(8,128)(2,1)} %refs_2_.1), custom_call_target="tpu_custom_call" | custom-call | flops 24159192 | bytes 188743 | tf_op jit(solution)/shard_map/qkv/pallas_call | solution.py:97
  37.8 1.5 %collective-permute-done.9.refs_0_ = bf16[64,3072]{1,0:T(8,128)(2,1)S(1)} collective-permute-done((bf16[64,3072]{1,0:T(8,128)(2,1)S(1)}, bf16[64,3072]{1,0:T(8,128)(2,1)S(1)}, u32[]{:S(2)}, u32[]{:S(2)}) %collective-permute-start.9) | collective-permute-done | bytes 393248 | tf_op jit(solution)/shard_map/ppermute | solution.py:31
  39.4 1.1 collective-permute-start.8
  40.5 3.6 %qkv.5.a = bf16[128,1536]{1,0:T(8,128)(2,1)S(1)} custom-call(bf16[64,3072]{1,0:T(8,128)(2,1)S(1)} %collective-permute-done.1.refs_0_, bf16[64,3072]{1,0:T(8,128)(2,1)} %collective-permute-done.4.refs_1_, bf16[64,3072]{1,0:T(8,128)(2,1)S(1)} %collective-permute-done.3.refs_2_, bf16[64,3072]{1,0:T(8,128)(2,1)S(1)} %collective-permute-done.refs_3_, ...), custom_call_target="tpu_custom_call" | custom-call | flops 24159192 | bytes 188743 | tf_op jit(solution)/shard_map/qkv/pallas_call | solution.py:97
  44.7 2.6 %qkv.6.c = bf16[128,1536]{1,0:T(8,128)(2,1)S(1)} custom-call(bf16[64,3072]{1,0:T(8,128)(2,1)S(1)} %collective-permute-done.5.refs_0_, bf16[64,3072]{1,0:T(8,128)(2,1)S(1)} %collective-permute-done.6.refs_1_, bf16[64,3072]{1,0:T(8,128)(2,1)S(1)} %collective-permute-done.7.refs_2_, bf16[64,3072]{1,0:T(8,128)(2,1)S(1)} %collective-permute-done.8.refs_3_, ...), custom_call_target="tpu_custom_call" | custom-call | flops 24159192 | bytes 188743 | tf_op jit(solution)/shard_map/qkv/pallas_call | solution.py:97
  47.3 2.6 %qkv.7.d = bf16[128,1536]{1,0:T(8,128)(2,1)S(1)} custom-call(bf16[64,3072]{1,0:T(8,128)(2,1)S(1)} %collective-permute-done.9.refs_0_, bf16[64,3072]{1,0:T(8,128)(2,1)S(1)} %collective-permute-done.10.refs_1_, bf16[64,3072]{1,0:T(8,128)(2,1)S(1)} %collective-permute-done.11.refs_2_, bf16[64,3072]{1,0:T(8,128)(2,1)S(1)} %collective-permute-done.12.refs_3_, ...), custom_call_target="tpu_custom_call" | custom-call | flops 24159192 | bytes 188743 | tf_op jit(solution)/shard_map/qkv/pallas_call | solution.py:97
  50.0 1.0 state.1.s0
  51.0 1.3 collective-permute-start.13
  52.3 2.4 %collective-permute-start.14 = (bf16[528,128]{1,0:T(8,128)(2,1)S(1)}, bf16[528,128]{1,0:T(8,128)(2,1)}, u32[]{:S(2)}, u32[]{:S(2)}) collective-permute-start(bf16[528,128]{1,0:T(8,128)(2,1)S(1)} %state.1.s0), channel_id=1, source_target_pairs={{0,16},{8,24},{16,0},{24,8},{32,48},{40,56},{48,32},{56,40},{64,80... | collective-permute-start | bytes 405512 | tf_op jit(solution)/shard_map/ppermute | solution.py:39
  54.7 1.2 collective-permute-start.15
  56.0 1.4 %inner.1 = f32[512,512]{1,0:T(8,128)S(1)} custom-call(bf16[128,1536]{1,0:T(8,128)(2,1)S(1)} %qkv.5.a, bf16[128,1536]{1,0:T(8,128)(2,1)S(1)} %get-tuple-element.47.b, bf16[128,1536]{1,0:T(8,128)(2,1)S(1)} %qkv.6.c, bf16[128,1536]{1,0:T(8,128)(2,1)S(1)} %qkv.7.d, f32[512,4]{1,0:T(8,128)S(1)} %bitcast.20, f32[4,512]{1,0:T(4,128)S(1)} %concatenate.8.gt, ...), custom_call_target="tpu_custom_call" | custom-call | flops 5368709 | bytes 15933 | tf_op jit(solution)/shard_map/inner/pallas_call | solution.py:199
  57.5 3.1 %collective-permute-done.13.s1 = bf16[528,128]{1,0:T(8,128)(2,1)S(1)} collective-permute-done((bf16[528,128]{1,0:T(8,128)(2,1)S(1)}, bf16[528,128]{1,0:T(8,128)(2,1)S(1)}, u32[]{:S(2)}, u32[]{:S(2)}) %collective-permute-start.13) | collective-permute-done | bytes 135200 | tf_op jit(solution)/shard_map/ppermute | solution.py:39
  60.6 6.8 %collective-permute-done.14.s2 = bf16[528,128]{1,0:T(8,128)(2,1)} collective-permute-done((bf16[528,128]{1,0:T(8,128)(2,1)S(1)}, bf16[528,128]{1,0:T(8,128)(2,1)}, u32[]{:S(2)}, u32[]{:S(2)}) %collective-permute-start.14) | collective-permute-done | bytes 135200 | tf_op jit(solution)/shard_map/ppermute | solution.py:39
  67.4 1.2 row.1
  68.6 3.6 %collective-permute-start.16 = (bf16[528,128]{1,0:T(8,128)(2,1)S(1)}, bf16[528,128]{1,0:T(8,128)(2,1)S(1)}, u32[]{:S(2)}, u32[]{:S(2)}) collective-permute-start(bf16[528,128]{1,0:T(8,128)(2,1)S(1)} %get-tuple-element.64), channel_id=1, source_target_pairs={{0,32},{8,40},{16,48},{24,56},{32,64},{40,72},{48,80},{56,88},{64,... | collective-permute-start | bytes 405512 | tf_op jit(solution)/shard_map/ppermute | solution.py:43
  72.1 5.2 %collective-permute-start.17 = (bf16[528,128]{1,0:T(8,128)(2,1)S(1)}, bf16[528,128]{1,0:T(8,128)(2,1)S(1)}, u32[]{:S(2)}, u32[]{:S(2)}) collective-permute-start(bf16[528,128]{1,0:T(8,128)(2,1)S(1)} %get-tuple-element.64), channel_id=1, source_target_pairs={{0,64},{8,72},{16,80},{24,88},{32,96},{40,104},{48,112},{56,120},{... | collective-permute-start | bytes 405512 | tf_op jit(solution)/shard_map/ppermute | solution.py:43
  77.3 1.5 %collective-permute-start.18 = (bf16[528,128]{1,0:T(8,128)(2,1)S(1)}, bf16[528,128]{1,0:T(8,128)(2,1)S(1)}, u32[]{:S(2)}, u32[]{:S(2)}) collective-permute-start(bf16[528,128]{1,0:T(8,128)(2,1)S(1)} %get-tuple-element.64), channel_id=1, source_target_pairs={{0,96},{8,104},{16,112},{24,120},{1,97},{9,105},{17,113},{25,121},... | collective-permute-start | bytes 405512 | tf_op jit(solution)/shard_map/ppermute | solution.py:43
  79.3 1.5 %collective-permute-done.18.t3 = bf16[528,128]{1,0:T(8,128)(2,1)S(1)} collective-permute-done((bf16[528,128]{1,0:T(8,128)(2,1)S(1)}, bf16[528,128]{1,0:T(8,128)(2,1)S(1)}, u32[]{:S(2)}, u32[]{:S(2)}) %collective-permute-start.18) | collective-permute-done | bytes 135200 | tf_op jit(solution)/shard_map/ppermute | solution.py:43
  80.8 0.7 copy-done.1
  81.5 0.9 copy-done.2
  82.4 4.0 %normed.1 = (bf16[512,512]{1,0:T(8,128)(2,1)S(1)}, bf16[64,6144]{1,0:T(8,128)(2,1)S(1)}, bf16[64,6144]{1,0:T(8,128)(2,1)S(1)}, bf16[16,512,384]{2,1,0:T(8,128)(2,1)S(1)}) custom-call(f32[520,128]{1,0:T(8,128)S(1)} %get-tuple-element.63.before, bf16[528,128]{1,0:T(8,128)(2,1)S(1)} %collective-permute-done.16.t1, ...), custom_call_target="tpu_custom_call" | custom-call | flops 671088 | bytes 62914 | tf_op jit(solution)/shard_map/normed/pallas_call | solution.py:321
  86.4 2.4 %project.2 = (bf16[64,6144]{1,0:T(8,128)(2,1)S(1)}, bf16[64,6144]{1,0:T(8,128)(2,1)S(1)}, bf16[64,6144]{1,0:T(8,128)(2,1)S(1)}, bf16[64,6144]{1,0:T(8,128)(2,1)S(1)}) custom-call(bf16[512,512]{1,0:T(8,128)(2,1)S(1)} %get-tuple-element.71.normed, bf16[16,512,384]{2,1,0:T(8,128)(2,1)S(1)} %get-tuple-element.66.w), custom_call_target="tpu_custom_call" | custom-call | flops 16106127 | bytes 62914 | tf_op jit(solution)/shard_map/project/pallas_call | solution.py:228
  88.8 2.1 %collective-permute-start.19 = (bf16[64,6144]{1,0:T(8,128)(2,1)S(1)}, bf16[64,6144]{1,0:T(8,128)(2,1)S(1)}, u32[]{:S(2)}, u32[]{:S(2)}) collective-permute-start(bf16[64,6144]{1,0:T(8,128)(2,1)S(1)} %get-tuple-element.68), channel_id=1, source_target_pairs={{0,1},{1,0},{2,3},{3,2},{4,5},{5,4},{6,7},{7,6},{8,9},{9,8},{10,11... | collective-permute-start | bytes 2359304 | tf_op jit(solution)/shard_map/ppermute | solution.py:35
  91.5 1.4 %collective-permute-done.19 = bf16[64,6144]{1,0:T(8,128)(2,1)S(1)} collective-permute-done((bf16[64,6144]{1,0:T(8,128)(2,1)S(1)}, bf16[64,6144]{1,0:T(8,128)(2,1)S(1)}, u32[]{:S(2)}, u32[]{:S(2)}) %collective-permute-start.19) | collective-permute-done | bytes 786464 | tf_op jit(solution)/shard_map/ppermute | solution.py:35
  93.1 0.9 collective-permute-done.24
  94.6 2.3 %collective-permute-start.26 = (bf16[64,3072]{1,0:T(8,128)(2,1)S(1)}, bf16[64,3072]{1,0:T(8,128)(2,1)S(1)}, u32[]{:S(2)}, u32[]{:S(2)}) collective-permute-start(bf16[64,3072]{1,0:T(8,128)(2,1)S(1)} %get-tuple-element.81), channel_id=1, source_target_pairs={{0,6},{1,7},{2,0},{3,1},{4,2},{5,3},{6,4},{7,5},{8,14},{9,15},{10,... | collective-permute-start | bytes 1179656 | tf_op jit(solution)/shard_map/ppermute | solution.py:31
  97.0 0.6 collective-permute-start.23
  97.6 1.3 project.3
  98.9 1.6 %collective-permute-start.21 = (bf16[64,6144]{1,0:T(8,128)(2,1)S(1)}, bf16[64,6144]{1,0:T(8,128)(2,1)S(1)}, u32[]{:S(2)}, u32[]{:S(2)}) collective-permute-start(bf16[64,6144]{1,0:T(8,128)(2,1)S(1)} %get-tuple-element.73), channel_id=1, source_target_pairs={{0,1},{1,0},{2,3},{3,2},{4,5},{5,4},{6,7},{7,6},{8,9},{9,8},{10,11... | collective-permute-start | bytes 2359304 | tf_op jit(solution)/shard_map/ppermute | solution.py:35
  100.5 12.5 %collective-permute-done.25 = bf16[64,3072]{1,0:T(8,128)(2,1)S(1)} collective-permute-done((bf16[64,3072]{1,0:T(8,128)(2,1)S(1)}, bf16[64,3072]{1,0:T(8,128)(2,1)S(1)}, u32[]{:S(2)}, u32[]{:S(2)}) %collective-permute-start.25) | collective-permute-done | bytes 393248 | tf_op jit(solution)/shard_map/ppermute | solution.py:31
  113.4 2.7 %collective-permute-start.28 = (bf16[64,3072]{1,0:T(8,128)(2,1)S(1)}, bf16[64,3072]{1,0:T(8,128)(2,1)S(1)}, u32[]{:S(2)}, u32[]{:S(2)}) collective-permute-start(bf16[64,3072]{1,0:T(8,128)(2,1)S(1)} %add_convert_fusion), channel_id=1, source_target_pairs={{0,6},{1,7},{2,0},{3,1},{4,2},{5,3},{6,4},{7,5},{8,14},{9,15},{10,... | collective-permute-start | bytes 1179656 | tf_op jit(solution)/shard_map/ppermute | solution.py:31
  116.4 7.4 %collective-permute-done.27.up_sum = bf16[64,3072]{1,0:T(8,128)(2,1)S(1)} collective-permute-done((bf16[64,3072]{1,0:T(8,128)(2,1)S(1)}, bf16[64,3072]{1,0:T(8,128)(2,1)S(1)}, u32[]{:S(2)}, u32[]{:S(2)}) %collective-permute-start.27) | collective-permute-done | bytes 393248 | tf_op jit(solution)/shard_map/ppermute | solution.py:31
  123.8 1.0 final.1
  (57 shorter events, 5.0 us)
Async XLA Ops:
  6.5 74.9 %all-gather.3.cloned.1.call-start = ((), (), s32[]{:S(2)}) async-start(), calls=%async_computation | async-start | bytes 6684672 | tf_op jit(solution)/shard_map/all_gather | solution.py:268
  7.3 20.0 %collective-permute-start.2 = (bf16[64,6144]{1,0:T(8,128)(2,1)}, bf16[64,6144]{1,0:T(8,128)(2,1)S(1)}, u32[]{:S(2)}, u32[]{:S(2)}) collective-permute-start(bf16[64,6144]{1,0:T(8,128)(2,1)} %refs_0_.1), channel_id=1, source_target_pairs={{0,1},{1,0},{2,3},{3,2},{4,5},{5,4},{6,7},{7,6},{8,9},{9,8},{10,11... | collective-permute-start | bytes 2359304 | tf_op jit(solution)/shard_map/ppermute | solution.py:35
  10.5 12.4 %collective-permute-start.3 = (bf16[64,3072]{1,0:T(8,128)(2,1)}, bf16[64,3072]{1,0:T(8,128)(2,1)S(1)}, u32[]{:S(2)}, u32[]{:S(2)}) collective-permute-start(bf16[64,3072]{1,0:T(8,128)(2,1)} %slice.75), channel_id=1, source_target_pairs={{0,2},{1,3},{2,4},{3,5},{4,6},{5,7},{6,0},{7,1},{8,10},{9,11},{10,... | collective-permute-start | bytes 1179656 | tf_op jit(solution)/shard_map/ppermute | solution.py:31
  13.7 10.7 %collective-permute-start.4 = (bf16[64,3072]{1,0:T(8,128)(2,1)}, bf16[64,3072]{1,0:T(8,128)(2,1)}, u32[]{:S(2)}, u32[]{:S(2)}) collective-permute-start(bf16[64,3072]{1,0:T(8,128)(2,1)} %slice.76), channel_id=1, source_target_pairs={{0,6},{1,7},{2,0},{3,1},{4,2},{5,3},{6,4},{7,5},{8,14},{9,15},{10,... | collective-permute-start | bytes 1179656 | tf_op jit(solution)/shard_map/ppermute | solution.py:31
  18.9 18.3 %collective-permute-start = (bf16[64,3072]{1,0:T(8,128)(2,1)}, bf16[64,3072]{1,0:T(8,128)(2,1)S(1)}, u32[]{:S(2)}, u32[]{:S(2)}) collective-permute-start(bf16[64,3072]{1,0:T(8,128)(2,1)} %slice.76), channel_id=1, source_target_pairs={{0,2},{1,3},{2,4},{3,5},{4,6},{5,7},{6,0},{7,1},{8,10},{9,11},{10,... | collective-permute-start | bytes 1179656 | tf_op jit(solution)/shard_map/ppermute | solution.py:31
  18.9 18.4 %collective-permute-start.1 = (bf16[64,3072]{1,0:T(8,128)(2,1)}, bf16[64,3072]{1,0:T(8,128)(2,1)S(1)}, u32[]{:S(2)}, u32[]{:S(2)}) collective-permute-start(bf16[64,3072]{1,0:T(8,128)(2,1)} %slice.75), channel_id=1, source_target_pairs={{0,6},{1,7},{2,0},{3,1},{4,2},{5,3},{6,4},{7,5},{8,14},{9,15},{10,... | collective-permute-start | bytes 1179656 | tf_op jit(solution)/shard_map/ppermute | solution.py:31
  22.9 16.5 %collective-permute-start.9 = (bf16[64,3072]{1,0:T(8,128)(2,1)S(1)}, bf16[64,3072]{1,0:T(8,128)(2,1)S(1)}, u32[]{:S(2)}, u32[]{:S(2)}) collective-permute-start(bf16[64,3072]{1,0:T(8,128)(2,1)S(1)} %collective-permute-done.3.refs_2_), channel_id=1, source_target_pairs={{0,2},{1,3},{2,4},{3,5},{4,6},{5,7},{6,0},{7,1},{8,10},{9,11},{10,... | collective-permute-start | bytes 1179656 | tf_op jit(solution)/shard_map/ppermute | solution.py:31
  24.4 19.7 %collective-permute-start.10 = (bf16[64,3072]{1,0:T(8,128)(2,1)}, bf16[64,3072]{1,0:T(8,128)(2,1)S(1)}, u32[]{:S(2)}, u32[]{:S(2)}) collective-permute-start(bf16[64,3072]{1,0:T(8,128)(2,1)} %collective-permute-done.4.refs_1_), channel_id=1, source_target_pairs={{0,6},{1,7},{2,0},{3,1},{4,2},{5,3},{6,4},{7,5},{8,14},{9,15},{10,... | collective-permute-start | bytes 1179656 | tf_op jit(solution)/shard_map/ppermute | solution.py:31
  27.2 17.0 %collective-permute-start.6 = (bf16[64,3072]{1,0:T(8,128)(2,1)}, bf16[64,3072]{1,0:T(8,128)(2,1)S(1)}, u32[]{:S(2)}, u32[]{:S(2)}) collective-permute-start(bf16[64,3072]{1,0:T(8,128)(2,1)} %collective-permute-done.4.refs_1_), channel_id=1, source_target_pairs={{0,1},{1,0},{2,3},{3,2},{4,5},{5,4},{6,7},{7,6},{8,9},{9,8},{10,11... | collective-permute-start | bytes 1179656 | tf_op jit(solution)/shard_map/ppermute | solution.py:35
  29.0 1.2 copy-start
  37.2 7.5 %collective-permute-start.7 = (bf16[64,3072]{1,0:T(8,128)(2,1)S(1)}, bf16[64,3072]{1,0:T(8,128)(2,1)S(1)}, u32[]{:S(2)}, u32[]{:S(2)}) collective-permute-start(bf16[64,3072]{1,0:T(8,128)(2,1)S(1)} %collective-permute-done.3.refs_2_), channel_id=1, source_target_pairs={{0,1},{1,0},{2,3},{3,2},{4,5},{5,4},{6,7},{7,6},{8,9},{9,8},{10,11... | collective-permute-start | bytes 1179656 | tf_op jit(solution)/shard_map/ppermute | solution.py:35
  37.4 7.3 %collective-permute-start.5 = (bf16[64,3072]{1,0:T(8,128)(2,1)S(1)}, bf16[64,3072]{1,0:T(8,128)(2,1)S(1)}, u32[]{:S(2)}, u32[]{:S(2)}) collective-permute-start(bf16[64,3072]{1,0:T(8,128)(2,1)S(1)} %collective-permute-done.1.refs_0_), channel_id=1, source_target_pairs={{0,1},{1,0},{2,3},{3,2},{4,5},{5,4},{6,7},{7,6},{8,9},{9,8},{10,11... | collective-permute-start | bytes 1179656 | tf_op jit(solution)/shard_map/ppermute | solution.py:35
  39.4 5.3 %collective-permute-start.8 = (bf16[64,3072]{1,0:T(8,128)(2,1)S(1)}, bf16[64,3072]{1,0:T(8,128)(2,1)S(1)}, u32[]{:S(2)}, u32[]{:S(2)}) collective-permute-start(bf16[64,3072]{1,0:T(8,128)(2,1)S(1)} %collective-permute-done.refs_3_), channel_id=1, source_target_pairs={{0,1},{1,0},{2,3},{3,2},{4,5},{5,4},{6,7},{7,6},{8,9},{9,8},{10,11... | collective-permute-start | bytes 1179656 | tf_op jit(solution)/shard_map/ppermute | solution.py:35
  44.1 3.2 %collective-permute-start.11 = (bf16[64,3072]{1,0:T(8,128)(2,1)S(1)}, bf16[64,3072]{1,0:T(8,128)(2,1)S(1)}, u32[]{:S(2)}, u32[]{:S(2)}) collective-permute-start(bf16[64,3072]{1,0:T(8,128)(2,1)S(1)} %collective-permute-done.9.refs_0_), channel_id=1, source_target_pairs={{0,1},{1,0},{2,3},{3,2},{4,5},{5,4},{6,7},{7,6},{8,9},{9,8},{10,11... | collective-permute-start | bytes 1179656 | tf_op jit(solution)/shard_map/ppermute | solution.py:35
  44.2 3.1 %collective-permute-start.12 = (bf16[64,3072]{1,0:T(8,128)(2,1)S(1)}, bf16[64,3072]{1,0:T(8,128)(2,1)S(1)}, u32[]{:S(2)}, u32[]{:S(2)}) collective-permute-start(bf16[64,3072]{1,0:T(8,128)(2,1)S(1)} %collective-permute-done.10.refs_1_), channel_id=1, source_target_pairs={{0,1},{1,0},{2,3},{3,2},{4,5},{5,4},{6,7},{7,6},{8,9},{9,8},{10,11... | collective-permute-start | bytes 1179656 | tf_op jit(solution)/shard_map/ppermute | solution.py:35
  47.3 34.1 %copy-start.3 = (f32[512]{0:T(512)S(1)}, f32[512]{0:T(512)}, u32[]{:S(2)}) copy-start(f32[512]{0:T(512)} %param.10) | copy-start | bytes 6148
  51.0 9.6 %collective-permute-start.13 = (bf16[528,128]{1,0:T(8,128)(2,1)S(1)}, bf16[528,128]{1,0:T(8,128)(2,1)S(1)}, u32[]{:S(2)}, u32[]{:S(2)}) collective-permute-start(bf16[528,128]{1,0:T(8,128)(2,1)S(1)} %state.1.s0), channel_id=1, source_target_pairs={{0,8},{8,16},{16,24},{24,0},{32,40},{40,48},{48,56},{56,32},{64,72... | collective-permute-start | bytes 405512 | tf_op jit(solution)/shard_map/ppermute | solution.py:39
  52.3 15.1 %collective-permute-start.14 = (bf16[528,128]{1,0:T(8,128)(2,1)S(1)}, bf16[528,128]{1,0:T(8,128)(2,1)}, u32[]{:S(2)}, u32[]{:S(2)}) collective-permute-start(bf16[528,128]{1,0:T(8,128)(2,1)S(1)} %state.1.s0), channel_id=1, source_target_pairs={{0,16},{8,24},{16,0},{24,8},{32,48},{40,56},{48,32},{56,40},{64,80... | collective-permute-start | bytes 405512 | tf_op jit(solution)/shard_map/ppermute | solution.py:39
  54.7 12.7 %collective-permute-start.15 = (bf16[528,128]{1,0:T(8,128)(2,1)S(1)}, bf16[528,128]{1,0:T(8,128)(2,1)}, u32[]{:S(2)}, u32[]{:S(2)}) collective-permute-start(bf16[528,128]{1,0:T(8,128)(2,1)S(1)} %state.1.s0), channel_id=1, source_target_pairs={{0,24},{8,0},{16,8},{24,16},{32,56},{40,32},{48,40},{56,48},{64,88... | collective-permute-start | bytes 405512 | tf_op jit(solution)/shard_map/ppermute | solution.py:39
  68.6 10.3 %collective-permute-start.16 = (bf16[528,128]{1,0:T(8,128)(2,1)S(1)}, bf16[528,128]{1,0:T(8,128)(2,1)S(1)}, u32[]{:S(2)}, u32[]{:S(2)}) collective-permute-start(bf16[528,128]{1,0:T(8,128)(2,1)S(1)} %get-tuple-element.64), channel_id=1, source_target_pairs={{0,32},{8,40},{16,48},{24,56},{32,64},{40,72},{48,80},{56,88},{64,... | collective-permute-start | bytes 405512 | tf_op jit(solution)/shard_map/ppermute | solution.py:43
  72.1 7.2 %collective-permute-start.17 = (bf16[528,128]{1,0:T(8,128)(2,1)S(1)}, bf16[528,128]{1,0:T(8,128)(2,1)S(1)}, u32[]{:S(2)}, u32[]{:S(2)}) collective-permute-start(bf16[528,128]{1,0:T(8,128)(2,1)S(1)} %get-tuple-element.64), channel_id=1, source_target_pairs={{0,64},{8,72},{16,80},{24,88},{32,96},{40,104},{48,112},{56,120},{... | collective-permute-start | bytes 405512 | tf_op jit(solution)/shard_map/ppermute | solution.py:43
  77.3 3.5 %collective-permute-start.18 = (bf16[528,128]{1,0:T(8,128)(2,1)S(1)}, bf16[528,128]{1,0:T(8,128)(2,1)S(1)}, u32[]{:S(2)}, u32[]{:S(2)}) collective-permute-start(bf16[528,128]{1,0:T(8,128)(2,1)S(1)} %get-tuple-element.64), channel_id=1, source_target_pairs={{0,96},{8,104},{16,112},{24,120},{1,97},{9,105},{17,113},{25,121},... | collective-permute-start | bytes 405512 | tf_op jit(solution)/shard_map/ppermute | solution.py:43
  80.8 0.7 copy-start.1
  81.4 0.9 copy-start.2
  88.8 4.1 %collective-permute-start.19 = (bf16[64,6144]{1,0:T(8,128)(2,1)S(1)}, bf16[64,6144]{1,0:T(8,128)(2,1)S(1)}, u32[]{:S(2)}, u32[]{:S(2)}) collective-permute-start(bf16[64,6144]{1,0:T(8,128)(2,1)S(1)} %get-tuple-element.68), channel_id=1, source_target_pairs={{0,1},{1,0},{2,3},{3,2},{4,5},{5,4},{6,7},{7,6},{8,9},{9,8},{10,11... | collective-permute-start | bytes 2359304 | tf_op jit(solution)/shard_map/ppermute | solution.py:35
  90.9 3.0 %collective-permute-start.24 = (bf16[64,6144]{1,0:T(8,128)(2,1)S(1)}, bf16[64,6144]{1,0:T(8,128)(2,1)S(1)}, u32[]{:S(2)}, u32[]{:S(2)}) collective-permute-start(bf16[64,6144]{1,0:T(8,128)(2,1)S(1)} %get-tuple-element.75), channel_id=1, source_target_pairs={{0,1},{1,0},{2,3},{3,2},{4,5},{5,4},{6,7},{7,6},{8,9},{9,8},{10,11... | collective-permute-start | bytes 2359304 | tf_op jit(solution)/shard_map/ppermute | solution.py:35
  91.0 5.9 %collective-permute-start.20 = (bf16[64,6144]{1,0:T(8,128)(2,1)S(1)}, bf16[64,6144]{1,0:T(8,128)(2,1)S(1)}, u32[]{:S(2)}, u32[]{:S(2)}) collective-permute-start(bf16[64,6144]{1,0:T(8,128)(2,1)S(1)} %get-tuple-element.70), channel_id=1, source_target_pairs={{0,1},{1,0},{2,3},{3,2},{4,5},{5,4},{6,7},{7,6},{8,9},{9,8},{10,11... | collective-permute-start | bytes 2359304 | tf_op jit(solution)/shard_map/ppermute | solution.py:35
  93.0 23.2 %collective-permute-start.22 = (bf16[64,3072]{1,0:T(8,128)(2,1)S(1)}, bf16[64,3072]{1,0:T(8,128)(2,1)S(1)}, u32[]{:S(2)}, u32[]{:S(2)}) collective-permute-start(bf16[64,3072]{1,0:T(8,128)(2,1)S(1)} %add_convert_fusion.5), channel_id=1, source_target_pairs={{0,2},{1,3},{2,4},{3,5},{4,6},{5,7},{6,0},{7,1},{8,10},{9,11},{10,... | collective-permute-start | bytes 1179656 | tf_op jit(solution)/shard_map/ppermute | solution.py:31
  94.2 18.8 %collective-permute-start.25 = (bf16[64,3072]{1,0:T(8,128)(2,1)S(1)}, bf16[64,3072]{1,0:T(8,128)(2,1)S(1)}, u32[]{:S(2)}, u32[]{:S(2)}) collective-permute-start(bf16[64,3072]{1,0:T(8,128)(2,1)S(1)} %get-tuple-element.82), channel_id=1, source_target_pairs={{0,2},{1,3},{2,4},{3,5},{4,6},{5,7},{6,0},{7,1},{8,10},{9,11},{10,... | collective-permute-start | bytes 1179656 | tf_op jit(solution)/shard_map/ppermute | solution.py:31
  94.6 18.4 %collective-permute-start.26 = (bf16[64,3072]{1,0:T(8,128)(2,1)S(1)}, bf16[64,3072]{1,0:T(8,128)(2,1)S(1)}, u32[]{:S(2)}, u32[]{:S(2)}) collective-permute-start(bf16[64,3072]{1,0:T(8,128)(2,1)S(1)} %get-tuple-element.81), channel_id=1, source_target_pairs={{0,6},{1,7},{2,0},{3,1},{4,2},{5,3},{6,4},{7,5},{8,14},{9,15},{10,... | collective-permute-start | bytes 1179656 | tf_op jit(solution)/shard_map/ppermute | solution.py:31
  97.0 19.1 %collective-permute-start.23 = (bf16[64,3072]{1,0:T(8,128)(2,1)S(1)}, bf16[64,3072]{1,0:T(8,128)(2,1)S(1)}, u32[]{:S(2)}, u32[]{:S(2)}) collective-permute-start(bf16[64,3072]{1,0:T(8,128)(2,1)S(1)} %add_convert_fusion.4), channel_id=1, source_target_pairs={{0,6},{1,7},{2,0},{3,1},{4,2},{5,3},{6,4},{7,5},{8,14},{9,15},{10,... | collective-permute-start | bytes 1179656 | tf_op jit(solution)/shard_map/ppermute | solution.py:31
  98.9 17.2 %collective-permute-start.21 = (bf16[64,6144]{1,0:T(8,128)(2,1)S(1)}, bf16[64,6144]{1,0:T(8,128)(2,1)S(1)}, u32[]{:S(2)}, u32[]{:S(2)}) collective-permute-start(bf16[64,6144]{1,0:T(8,128)(2,1)S(1)} %get-tuple-element.73), channel_id=1, source_target_pairs={{0,1},{1,0},{2,3},{3,2},{4,5},{5,4},{6,7},{7,6},{8,9},{9,8},{10,11... | collective-permute-start | bytes 2359304 | tf_op jit(solution)/shard_map/ppermute | solution.py:35
  113.1 10.7 %collective-permute-start.27 = (bf16[64,3072]{1,0:T(8,128)(2,1)S(1)}, bf16[64,3072]{1,0:T(8,128)(2,1)S(1)}, u32[]{:S(2)}, u32[]{:S(2)}) collective-permute-start(bf16[64,3072]{1,0:T(8,128)(2,1)S(1)} %add_convert_fusion.1), channel_id=1, source_target_pairs={{0,2},{1,3},{2,4},{3,5},{4,6},{5,7},{6,0},{7,1},{8,10},{9,11},{10,... | collective-permute-start | bytes 1179656 | tf_op jit(solution)/shard_map/ppermute | solution.py:31
  113.4 10.5 %collective-permute-start.28 = (bf16[64,3072]{1,0:T(8,128)(2,1)S(1)}, bf16[64,3072]{1,0:T(8,128)(2,1)S(1)}, u32[]{:S(2)}, u32[]{:S(2)}) collective-permute-start(bf16[64,3072]{1,0:T(8,128)(2,1)S(1)} %add_convert_fusion), channel_id=1, source_target_pairs={{0,6},{1,7},{2,0},{3,1},{4,2},{5,3},{6,4},{7,5},{8,14},{9,15},{10,... | collective-permute-start | bytes 1179656 | tf_op jit(solution)/shard_map/ppermute | solution.py:31
Sparse Core Ops, SparseCore 0:
  9.5 70.1 all-gather.2

commit v6 on v5

--- a/solution.py
+++ b/solution.py
@@ -284,14 +284,15 @@
     low_b, high_b = after((low, high), g, gt, last, at, pos)
     left_high, right_low = to_y(high_b, 1), to_y(low_b, -1)
     own2 = to_sibling(activations)
+    own2 = after(own2, g, gt, last, at, pos)
+    qkv_a, w_qkv = qkv([activations, own2], [(0, 0), (64, 0)], 128, w_qkv, True)
+    left_low, right_high = after((left_low, right_high), qkv_a)
     far_low, far_high = to_y(left_low, 1), to_y(right_high, -1)
-    own2 = after(own2, g, gt, last, at, pos, left_low, right_high)
-    qkv_a, w_qkv = qkv([activations, own2], [(0, 0), (64, 0)], 128, w_qkv, True)
     low2, high2 = to_sibling(left_low), to_sibling(right_high)
-    left_high, right_low = after((left_high, right_low), qkv_a)
     left_high2, right_low2 = to_sibling(left_high), to_sibling(right_low)
     halves = [(0, 0), (0, mid), (64, 0), (64, mid)]
-    qkv_b = qkv([right_low, right_high, left_low, left_high], halves, 128, w_qkv)
+    near = after((right_low, right_high, left_low, left_high), low2, high2)
+    qkv_b = qkv(near, halves, 128, w_qkv)
     far_low, far_high = after((far_low, far_high), qkv_b)
     far_low2, far_high2 = to_sibling(far_low), to_sibling(far_high)
     near2 = after([right_low2, high2, low2, left_high2], far_low, far_high)
@@ -332,9 +333,9 @@
     far_sib = to_sibling(far_sib)
     near_parts = project(normed, w, (0, 4, 1, 5))
     far_sib = after(far_sib, near_parts)
-    from_l = to_y(plus(far_own[:, :mid], far_sib[:, :mid]), 1)
-    from_r = to_y(plus(far_own[:, mid:], far_sib[:, mid:]), -1)
-    up_own, up_sib, down_own, down_sib = near_parts
+    far = plus(far_own[:, :mid], far_sib[:, :mid]), plus(far_own[:, mid:], far_sib[:, mid:])
+    from_l, from_r = to_y(far[0], 1), to_y(far[1], -1)
+    up_own, up_sib, down_own, down_sib = after(near_parts, *far)
     up_sib, down_sib = to_sibling(up_sib), to_sibling(down_sib)
     up_plain = plus(up_own[:, mid:], up_sib[:, mid:])
     down_plain = plus(down_own[:, :mid], down_sib[:, :mid])

time: 133 us -> 130 us (0.977); the launches traced: 132 us -> 130 us
  waiting for transfers between devices: 39.1 us -> 36 us
    ppermute x11, waiting for transfers between devices: 2.36 us -> 0.03 us  [to_sibling(): return lax.ppermute(a, 'tp', [(i, i ^ 1) for i in range(2 * N_Y)])]
    ppermute x12, starting transfers between devices: 14.6 us -> 16.3 us  [to_y(): lax.ppermute(a, 'tp', [(i, (i // 2 + k) % N_Y * 2 + i % 2) for i in range...]
  transfers between devices with their start and end apart: 30 -> 30, of which waited for: 11 -> 10; matrix products, arithmetic and copies ran while one was open for 6% -> 6% of each run, Pallas kernels for 16% -> 18%
where the time goes in v6:
time: 130 us
  starting transfers between devices  40.8 us (31%)
  waiting for transfers between devices  36 us (28%)
  Pallas kernels  28.7 us (22%)
  between operations  13.7 us (11%)
  local copies, waits for them, and re-layouts  7.83 us (6%)
  other arithmetic  2.95 us (2%)
    ppermute x12, waiting for transfers between devices, to_y(): lax.ppermute(a, 'tp', [(i, (i // 2 + k) % N_Y * 2 + i % 2) for i in range...  23.2 us
    ppermute x12, starting transfers between devices, to_y(): lax.ppermute(a, 'tp', [(i, (i // 2 + k) % N_Y * 2 + i % 2) for i in range...  16.3 us
    pallas_call x4, Pallas kernels, qkv(): pl.pallas_call(functools.partial(qkv_first_kernel if first else qkv_kerne...  16.1 us
    ppermute x3, starting transfers between devices, to_z(): lax.ppermute(a, 'ctx', [(j, j + N_X * k) for j in range(N_X * N_Z) if j /...  10.2 us
    ppermute x3, waiting for transfers between devices, to_x(): lax.ppermute(a, 'ctx', [(j, j // N_X * N_X + (j + k) % N_X) for j in rang...  9.73 us
    ppermute x11, starting transfers between devices, to_sibling(): return lax.ppermute(a, 'tp', [(i, i ^ 1) for i in range(2 * N_Y)])  9.52 us
    pallas_call x5, Pallas kernels, whole_call(): pl.pallas_call(kernel, out_shape=outs, in_specs=[pl.BlockSpec(memory_spac...  4.9 us
    ppermute x3, starting transfers between devices, to_x(): lax.ppermute(a, 'ctx', [(j, j // N_X * N_X + (j + k) % N_X) for j in rang...  4.81 us
  transfers between devices with their start and end apart: 30, of which 10 were waited for; matrix products, arithmetic and copies ran while one was open for 6% of the time, Pallas kernels for 18%

profile of v6, /device:TPU:1, one launch (start us, length us, event | category | flops | bytes accessed | tf_op | source)
XLA Modules:
  0.0 130.1 jit_solution(11963767174172394969)
XLA Ops:
  6.5 0.7 all-gather.3.cloned.1.call-update
  7.3 1.5 %collective-permute-start.3 = (bf16[64,6144]{1,0:T(8,128)(2,1)}, bf16[64,6144]{1,0:T(8,128)(2,1)S(1)}, u32[]{:S(2)}, u32[]{:S(2)}) collective-permute-start(bf16[64,6144]{1,0:T(8,128)(2,1)} %refs_0_.1), channel_id=1, source_target_pairs={{0,1},{1,0},{2,3},{3,2},{4,5},{5,4},{6,7},{7,6},{8,9},{9,8},{10,11... | collective-permute-start | bytes 2359304 | tf_op jit(solution)/shard_map/ppermute | solution.py:35
  8.8 1.8 %slice.75 = bf16[64,3072]{1,0:T(8,128)(2,1)} slice(bf16[64,6144]{1,0:T(8,128)(2,1)} %refs_0_.1), slice={[0:64], [0:3072]} | slice | bytes 786432 | tf_op jit(solution)/shard_map/slice | solution.py:281
  10.5 1.4 %collective-permute-start.1 = (bf16[64,3072]{1,0:T(8,128)(2,1)}, bf16[64,3072]{1,0:T(8,128)(2,1)S(1)}, u32[]{:S(2)}, u32[]{:S(2)}) collective-permute-start(bf16[64,3072]{1,0:T(8,128)(2,1)} %slice.75), channel_id=1, source_target_pairs={{0,2},{1,3},{2,4},{3,5},{4,6},{5,7},{6,0},{7,1},{8,10},{9,11},{10,... | collective-permute-start | bytes 1179656 | tf_op jit(solution)/shard_map/ppermute | solution.py:31
  11.9 1.8 %slice.76 = bf16[64,3072]{1,0:T(8,128)(2,1)} slice(bf16[64,6144]{1,0:T(8,128)(2,1)} %refs_0_.1), slice={[0:64], [3072:6144]} | slice | bytes 786432 | tf_op jit(solution)/shard_map/slice | solution.py:282
  13.7 1.4 %collective-permute-start.2 = (bf16[64,3072]{1,0:T(8,128)(2,1)}, bf16[64,3072]{1,0:T(8,128)(2,1)}, u32[]{:S(2)}, u32[]{:S(2)}) collective-permute-start(bf16[64,3072]{1,0:T(8,128)(2,1)} %slice.76), channel_id=1, source_target_pairs={{0,6},{1,7},{2,0},{3,1},{4,2},{5,3},{6,4},{7,5},{8,14},{9,15},{10,... | collective-permute-start | bytes 1179656 | tf_op jit(solution)/shard_map/ppermute | solution.py:31
  15.1 0.7 reshape.29
  15.8 1.2 reduce-window.6
  17.9 0.7 fusion.1
  18.9 1.5 %collective-permute-start = (bf16[64,3072]{1,0:T(8,128)(2,1)}, bf16[64,3072]{1,0:T(8,128)(2,1)S(1)}, u32[]{:S(2)}, u32[]{:S(2)}) collective-permute-start(bf16[64,3072]{1,0:T(8,128)(2,1)} %slice.75), channel_id=1, source_target_pairs={{0,6},{1,7},{2,0},{3,1},{4,2},{5,3},{6,4},{7,5},{8,14},{9,15},{10,... | collective-permute-start | bytes 1179656 | tf_op jit(solution)/shard_map/ppermute | solution.py:31
  20.4 1.1 copy-done
  21.5 7.3 %qkv.4 = (bf16[128,1536]{1,0:T(8,128)(2,1)S(1)}, bf16[3,6144,512]{2,1,0:T(8,128)(2,1)S(1)}) custom-call(bf16[64,6144]{1,0:T(8,128)(2,1)S(1)} %copy-done, bf16[64,6144]{1,0:T(8,128)(2,1)S(1)} %collective-permute-done.3.refs_1_, bf16[3,6144,512]{2,1,0:T(8,128)(2,1)} %refs_2_.1), custom_call_target="tpu_custom_call" | custom-call | flops 24159192 | bytes 188743 | tf_op jit(solution)/shard_map/qkv/pallas_call | solution.py:97
  28.8 1.0 collective-permute-start.5
  30.2 2.6 %collective-permute-done.refs_0_ = bf16[64,3072]{1,0:T(8,128)(2,1)S(1)} collective-permute-done((bf16[64,3072]{1,0:T(8,128)(2,1)}, bf16[64,3072]{1,0:T(8,128)(2,1)S(1)}, u32[]{:S(2)}, u32[]{:S(2)}) %collective-permute-start) | collective-permute-done | bytes 393248 | tf_op jit(solution)/shard_map/ppermute | solution.py:31
  32.8 2.8 %collective-permute-start.10 = (bf16[64,3072]{1,0:T(8,128)(2,1)}, bf16[64,3072]{1,0:T(8,128)(2,1)S(1)}, u32[]{:S(2)}, u32[]{:S(2)}) collective-permute-start(bf16[64,3072]{1,0:T(8,128)(2,1)} %collective-permute-done.2.refs_1_), channel_id=1, source_target_pairs={{0,6},{1,7},{2,0},{3,1},{4,2},{5,3},{6,4},{7,5},{8,14},{9,15},{10,... | collective-permute-start | bytes 1179656 | tf_op jit(solution)/shard_map/ppermute | solution.py:31
  35.6 1.1 collective-permute-start.7
  36.9 3.6 %qkv.5.a = bf16[128,1536]{1,0:T(8,128)(2,1)S(1)} custom-call(bf16[64,3072]{1,0:T(8,128)(2,1)S(1)} %collective-permute-done.refs_0_, bf16[64,3072]{1,0:T(8,128)(2,1)} %collective-permute-done.2.refs_1_, bf16[64,3072]{1,0:T(8,128)(2,1)S(1)} %collective-permute-done.1.refs_2_, bf16[64,3072]{1,0:T(8,128)(2,1)S(1)} %collective-permute-done.4.refs_3_, ...), custom_call_target="tpu_custom_call" | custom-call | flops 24159192 | bytes 188743 | tf_op jit(solution)/shard_map/qkv/pallas_call | solution.py:97
  40.5 1.2 collective-permute-done.9.refs_0_
  41.7 1.9 %collective-permute-done.10.refs_1_ = bf16[64,3072]{1,0:T(8,128)(2,1)S(1)} collective-permute-done((bf16[64,3072]{1,0:T(8,128)(2,1)}, bf16[64,3072]{1,0:T(8,128)(2,1)S(1)}, u32[]{:S(2)}, u32[]{:S(2)}) %collective-permute-start.10) | collective-permute-done | bytes 393248 | tf_op jit(solution)/shard_map/ppermute | solution.py:31
  43.5 1.8 %collective-permute-start.11 = (bf16[64,3072]{1,0:T(8,128)(2,1)S(1)}, bf16[64,3072]{1,0:T(8,128)(2,1)S(1)}, u32[]{:S(2)}, u32[]{:S(2)}) collective-permute-start(bf16[64,3072]{1,0:T(8,128)(2,1)S(1)} %collective-permute-done.9.refs_0_), channel_id=1, source_target_pairs={{0,1},{1,0},{2,3},{3,2},{4,5},{5,4},{6,7},{7,6},{8,9},{9,8},{10,11... | collective-permute-start | bytes 1179656 | tf_op jit(solution)/shard_map/ppermute | solution.py:35
  45.3 2.6 %qkv.6.c = bf16[128,1536]{1,0:T(8,128)(2,1)S(1)} custom-call(bf16[64,3072]{1,0:T(8,128)(2,1)S(1)} %collective-permute-done.7.refs_0_, bf16[64,3072]{1,0:T(8,128)(2,1)S(1)} %collective-permute-done.6.refs_1_, bf16[64,3072]{1,0:T(8,128)(2,1)S(1)} %collective-permute-done.5.refs_2_, bf16[64,3072]{1,0:T(8,128)(2,1)S(1)} %collective-permute-done.8.refs_3_, ...), custom_call_target="tpu_custom_call" | custom-call | flops 24159192 | bytes 188743 | tf_op jit(solution)/shard_map/qkv/pallas_call | solution.py:97
  47.9 2.6 %qkv.7.d = bf16[128,1536]{1,0:T(8,128)(2,1)S(1)} custom-call(bf16[64,3072]{1,0:T(8,128)(2,1)S(1)} %collective-permute-done.9.refs_0_, bf16[64,3072]{1,0:T(8,128)(2,1)S(1)} %collective-permute-done.10.refs_1_, bf16[64,3072]{1,0:T(8,128)(2,1)S(1)} %collective-permute-done.11.refs_2_, bf16[64,3072]{1,0:T(8,128)(2,1)S(1)} %collective-permute-done.12.refs_3_, ...), custom_call_target="tpu_custom_call" | custom-call | flops 24159192 | bytes 188743 | tf_op jit(solution)/shard_map/qkv/pallas_call | solution.py:97
  50.6 1.0 state.1.s0
  51.6 1.2 collective-permute-start.13
  52.8 2.3 %collective-permute-start.14 = (bf16[528,128]{1,0:T(8,128)(2,1)S(1)}, bf16[528,128]{1,0:T(8,128)(2,1)}, u32[]{:S(2)}, u32[]{:S(2)}) collective-permute-start(bf16[528,128]{1,0:T(8,128)(2,1)S(1)} %state.1.s0), channel_id=1, source_target_pairs={{0,16},{8,24},{16,0},{24,8},{32,48},{40,56},{48,32},{56,40},{64,80... | collective-permute-start | bytes 405512 | tf_op jit(solution)/shard_map/ppermute | solution.py:39
  55.1 1.3 collective-permute-start.15
  56.5 1.4 %inner.1 = f32[512,512]{1,0:T(8,128)S(1)} custom-call(bf16[128,1536]{1,0:T(8,128)(2,1)S(1)} %qkv.5.a, bf16[128,1536]{1,0:T(8,128)(2,1)S(1)} %get-tuple-element.54.b, bf16[128,1536]{1,0:T(8,128)(2,1)S(1)} %qkv.6.c, bf16[128,1536]{1,0:T(8,128)(2,1)S(1)} %qkv.7.d, f32[512,4]{1,0:T(8,128)S(1)} %bitcast.20, f32[4,512]{1,0:T(4,128)S(1)} %concatenate.8.gt, ...), custom_call_target="tpu_custom_call" | custom-call | flops 5368709 | bytes 15933 | tf_op jit(solution)/shard_map/inner/pallas_call | solution.py:199
  58.0 3.1 %collective-permute-done.13.s1 = bf16[528,128]{1,0:T(8,128)(2,1)S(1)} collective-permute-done((bf16[528,128]{1,0:T(8,128)(2,1)S(1)}, bf16[528,128]{1,0:T(8,128)(2,1)S(1)}, u32[]{:S(2)}, u32[]{:S(2)}) %collective-permute-start.13) | collective-permute-done | bytes 135200 | tf_op jit(solution)/shard_map/ppermute | solution.py:39
  61.1 6.6 %collective-permute-done.14.s2 = bf16[528,128]{1,0:T(8,128)(2,1)} collective-permute-done((bf16[528,128]{1,0:T(8,128)(2,1)S(1)}, bf16[528,128]{1,0:T(8,128)(2,1)}, u32[]{:S(2)}, u32[]{:S(2)}) %collective-permute-start.14) | collective-permute-done | bytes 135200 | tf_op jit(solution)/shard_map/ppermute | solution.py:39
  67.7 1.2 row.1
  68.9 3.6 %collective-permute-start.16 = (bf16[528,128]{1,0:T(8,128)(2,1)S(1)}, bf16[528,128]{1,0:T(8,128)(2,1)S(1)}, u32[]{:S(2)}, u32[]{:S(2)}) collective-permute-start(bf16[528,128]{1,0:T(8,128)(2,1)S(1)} %get-tuple-element.76), channel_id=1, source_target_pairs={{0,32},{8,40},{16,48},{24,56},{32,64},{40,72},{48,80},{56,88},{64,... | collective-permute-start | bytes 405512 | tf_op jit(solution)/shard_map/ppermute | solution.py:43
  72.5 5.3 %collective-permute-start.17 = (bf16[528,128]{1,0:T(8,128)(2,1)S(1)}, bf16[528,128]{1,0:T(8,128)(2,1)S(1)}, u32[]{:S(2)}, u32[]{:S(2)}) collective-permute-start(bf16[528,128]{1,0:T(8,128)(2,1)S(1)} %get-tuple-element.76), channel_id=1, source_target_pairs={{0,64},{8,72},{16,80},{24,88},{32,96},{40,104},{48,112},{56,120},{... | collective-permute-start | bytes 405512 | tf_op jit(solution)/shard_map/ppermute | solution.py:43
  77.8 1.3 collective-permute-start.18
  79.7 1.7 %collective-permute-done.18.t3 = bf16[528,128]{1,0:T(8,128)(2,1)S(1)} collective-permute-done((bf16[528,128]{1,0:T(8,128)(2,1)S(1)}, bf16[528,128]{1,0:T(8,128)(2,1)S(1)}, u32[]{:S(2)}, u32[]{:S(2)}) %collective-permute-start.18) | collective-permute-done | bytes 135200 | tf_op jit(solution)/shard_map/ppermute | solution.py:43
  82.1 0.9 copy-done.2
  83.0 4.0 %normed.1 = (bf16[512,512]{1,0:T(8,128)(2,1)S(1)}, bf16[64,6144]{1,0:T(8,128)(2,1)S(1)}, bf16[64,6144]{1,0:T(8,128)(2,1)S(1)}, bf16[16,512,384]{2,1,0:T(8,128)(2,1)S(1)}) custom-call(f32[520,128]{1,0:T(8,128)S(1)} %get-tuple-element.75.before, bf16[528,128]{1,0:T(8,128)(2,1)S(1)} %collective-permute-done.16.t1, ...), custom_call_target="tpu_custom_call" | custom-call | flops 671088 | bytes 62914 | tf_op jit(solution)/shard_map/normed/pallas_call | solution.py:322
  87.1 2.4 %collective-permute-start.19 = (bf16[64,6144]{1,0:T(8,128)(2,1)S(1)}, bf16[64,6144]{1,0:T(8,128)(2,1)S(1)}, u32[]{:S(2)}, u32[]{:S(2)}) collective-permute-start(bf16[64,6144]{1,0:T(8,128)(2,1)S(1)} %get-tuple-element.84), channel_id=1, source_target_pairs={{0,1},{1,0},{2,3},{3,2},{4,5},{5,4},{6,7},{7,6},{8,9},{9,8},{10,11... | collective-permute-start | bytes 2359304 | tf_op jit(solution)/shard_map/ppermute | solution.py:35
  89.4 2.4 %project.2 = (bf16[64,6144]{1,0:T(8,128)(2,1)S(1)}, bf16[64,6144]{1,0:T(8,128)(2,1)S(1)}, bf16[64,6144]{1,0:T(8,128)(2,1)S(1)}, bf16[64,6144]{1,0:T(8,128)(2,1)S(1)}) custom-call(bf16[512,512]{1,0:T(8,128)(2,1)S(1)} %get-tuple-element.90.normed, bf16[16,512,384]{2,1,0:T(8,128)(2,1)S(1)} %get-tuple-element.78.w), custom_call_target="tpu_custom_call" | custom-call | flops 16106127 | bytes 62914 | tf_op jit(solution)/shard_map/project/pallas_call | solution.py:228
  93.3 2.6 %collective-permute-start.26 = (bf16[64,3072]{1,0:T(8,128)(2,1)S(1)}, bf16[64,3072]{1,0:T(8,128)(2,1)S(1)}, u32[]{:S(2)}, u32[]{:S(2)}) collective-permute-start(bf16[64,3072]{1,0:T(8,128)(2,1)S(1)} %get-tuple-element.97), channel_id=1, source_target_pairs={{0,6},{1,7},{2,0},{3,1},{4,2},{5,3},{6,4},{7,5},{8,14},{9,15},{10,... | collective-permute-start | bytes 1179656 | tf_op jit(solution)/shard_map/ppermute | solution.py:31
  96.3 2.7 %collective-permute-start.24 = (bf16[64,3072]{1,0:T(8,128)(2,1)S(1)}, bf16[64,3072]{1,0:T(8,128)(2,1)S(1)}, u32[]{:S(2)}, u32[]{:S(2)}) collective-permute-start(bf16[64,3072]{1,0:T(8,128)(2,1)S(1)} %add_convert_fusion.2), channel_id=1, source_target_pairs={{0,6},{1,7},{2,0},{3,1},{4,2},{5,3},{6,4},{7,5},{8,14},{9,15},{10,... | collective-permute-start | bytes 1179656 | tf_op jit(solution)/shard_map/ppermute | solution.py:31
  99.0 1.3 %project.3 = (bf16[64,6144]{1,0:T(8,128)(2,1)S(1)}, bf16[64,6144]{1,0:T(8,128)(2,1)S(1)}) custom-call(bf16[512,512]{1,0:T(8,128)(2,1)S(1)} %get-tuple-element.90.normed, bf16[16,512,384]{2,1,0:T(8,128)(2,1)S(1)} %get-tuple-element.78.w), custom_call_target="tpu_custom_call" | custom-call | flops 8053063 | bytes 62914 | tf_op jit(solution)/shard_map/project/pallas_call | solution.py:228
  100.3 1.0 collective-permute-start.22
  101.3 4.1 %collective-permute-done.25 = bf16[64,3072]{1,0:T(8,128)(2,1)S(1)} collective-permute-done((bf16[64,3072]{1,0:T(8,128)(2,1)S(1)}, bf16[64,3072]{1,0:T(8,128)(2,1)S(1)}, u32[]{:S(2)}, u32[]{:S(2)}) %collective-permute-start.25) | collective-permute-done | bytes 393248 | tf_op jit(solution)/shard_map/ppermute | solution.py:31
  105.5 0.7 collective-permute-start.27
  106.4 2.1 %collective-permute-start.28 = (bf16[64,3072]{1,0:T(8,128)(2,1)S(1)}, bf16[64,3072]{1,0:T(8,128)(2,1)S(1)}, u32[]{:S(2)}, u32[]{:S(2)}) collective-permute-start(bf16[64,3072]{1,0:T(8,128)(2,1)S(1)} %add_convert_fusion), channel_id=1, source_target_pairs={{0,6},{1,7},{2,0},{3,1},{4,2},{5,3},{6,4},{7,5},{8,14},{9,15},{10,... | collective-permute-start | bytes 1179656 | tf_op jit(solution)/shard_map/ppermute | solution.py:31
  108.5 5.3 %collective-permute-done.23.up_plain = bf16[64,3072]{1,0:T(8,128)(2,1)S(1)} collective-permute-done((bf16[64,3072]{1,0:T(8,128)(2,1)S(1)}, bf16[64,3072]{1,0:T(8,128)(2,1)S(1)}, u32[]{:S(2)}, u32[]{:S(2)}) %collective-permute-start.23) | collective-permute-done | bytes 393248 | tf_op jit(solution)/shard_map/ppermute | solution.py:31
  114.0 8.2 %collective-permute-done.27.up_sum = bf16[64,3072]{1,0:T(8,128)(2,1)S(1)} collective-permute-done((bf16[64,3072]{1,0:T(8,128)(2,1)S(1)}, bf16[64,3072]{1,0:T(8,128)(2,1)S(1)}, u32[]{:S(2)}, u32[]{:S(2)}) %collective-permute-start.27) | collective-permute-done | bytes 393248 | tf_op jit(solution)/shard_map/ppermute | solution.py:31
  122.2 1.0 final.1
  (57 shorter events, 5.3 us)
Async XLA Ops:
  6.5 75.6 %all-gather.3.cloned.1.call-start = ((), (), s32[]{:S(2)}) async-start(), calls=%async_computation | async-start | bytes 6684672 | tf_op jit(solution)/shard_map/all_gather | solution.py:268
  7.3 13.1 %collective-permute-start.3 = (bf16[64,6144]{1,0:T(8,128)(2,1)}, bf16[64,6144]{1,0:T(8,128)(2,1)S(1)}, u32[]{:S(2)}, u32[]{:S(2)}) collective-permute-start(bf16[64,6144]{1,0:T(8,128)(2,1)} %refs_0_.1), channel_id=1, source_target_pairs={{0,1},{1,0},{2,3},{3,2},{4,5},{5,4},{6,7},{7,6},{8,9},{9,8},{10,11... | collective-permute-start | bytes 2359304 | tf_op jit(solution)/shard_map/ppermute | solution.py:35
  10.5 18.3 %collective-permute-start.1 = (bf16[64,3072]{1,0:T(8,128)(2,1)}, bf16[64,3072]{1,0:T(8,128)(2,1)S(1)}, u32[]{:S(2)}, u32[]{:S(2)}) collective-permute-start(bf16[64,3072]{1,0:T(8,128)(2,1)} %slice.75), channel_id=1, source_target_pairs={{0,2},{1,3},{2,4},{3,5},{4,6},{5,7},{6,0},{7,1},{8,10},{9,11},{10,... | collective-permute-start | bytes 1179656 | tf_op jit(solution)/shard_map/ppermute | solution.py:31
  13.7 15.1 %collective-permute-start.2 = (bf16[64,3072]{1,0:T(8,128)(2,1)}, bf16[64,3072]{1,0:T(8,128)(2,1)}, u32[]{:S(2)}, u32[]{:S(2)}) collective-permute-start(bf16[64,3072]{1,0:T(8,128)(2,1)} %slice.76), channel_id=1, source_target_pairs={{0,6},{1,7},{2,0},{3,1},{4,2},{5,3},{6,4},{7,5},{8,14},{9,15},{10,... | collective-permute-start | bytes 1179656 | tf_op jit(solution)/shard_map/ppermute | solution.py:31
  18.9 13.9 %collective-permute-start = (bf16[64,3072]{1,0:T(8,128)(2,1)}, bf16[64,3072]{1,0:T(8,128)(2,1)S(1)}, u32[]{:S(2)}, u32[]{:S(2)}) collective-permute-start(bf16[64,3072]{1,0:T(8,128)(2,1)} %slice.75), channel_id=1, source_target_pairs={{0,6},{1,7},{2,0},{3,1},{4,2},{5,3},{6,4},{7,5},{8,14},{9,15},{10,... | collective-permute-start | bytes 1179656 | tf_op jit(solution)/shard_map/ppermute | solution.py:31
  20.4 15.3 %collective-permute-start.4 = (bf16[64,3072]{1,0:T(8,128)(2,1)}, bf16[64,3072]{1,0:T(8,128)(2,1)S(1)}, u32[]{:S(2)}, u32[]{:S(2)}) collective-permute-start(bf16[64,3072]{1,0:T(8,128)(2,1)} %slice.76), channel_id=1, source_target_pairs={{0,2},{1,3},{2,4},{3,5},{4,6},{5,7},{6,0},{7,1},{8,10},{9,11},{10,... | collective-permute-start | bytes 1179656 | tf_op jit(solution)/shard_map/ppermute | solution.py:31
  20.4 1.1 copy-start
  28.8 8.0 %collective-permute-start.5 = (bf16[64,3072]{1,0:T(8,128)(2,1)S(1)}, bf16[64,3072]{1,0:T(8,128)(2,1)S(1)}, u32[]{:S(2)}, u32[]{:S(2)}) collective-permute-start(bf16[64,3072]{1,0:T(8,128)(2,1)S(1)} %collective-permute-done.1.refs_2_), channel_id=1, source_target_pairs={{0,1},{1,0},{2,3},{3,2},{4,5},{5,4},{6,7},{7,6},{8,9},{9,8},{10,11... | collective-permute-start | bytes 1179656 | tf_op jit(solution)/shard_map/ppermute | solution.py:35
  29.8 7.1 %collective-permute-start.6 = (bf16[64,3072]{1,0:T(8,128)(2,1)}, bf16[64,3072]{1,0:T(8,128)(2,1)S(1)}, u32[]{:S(2)}, u32[]{:S(2)}) collective-permute-start(bf16[64,3072]{1,0:T(8,128)(2,1)} %collective-permute-done.2.refs_1_), channel_id=1, source_target_pairs={{0,1},{1,0},{2,3},{3,2},{4,5},{5,4},{6,7},{7,6},{8,9},{9,8},{10,11... | collective-permute-start | bytes 1179656 | tf_op jit(solution)/shard_map/ppermute | solution.py:35
  29.9 11.8 %collective-permute-start.9 = (bf16[64,3072]{1,0:T(8,128)(2,1)S(1)}, bf16[64,3072]{1,0:T(8,128)(2,1)S(1)}, u32[]{:S(2)}, u32[]{:S(2)}) collective-permute-start(bf16[64,3072]{1,0:T(8,128)(2,1)S(1)} %collective-permute-done.1.refs_2_), channel_id=1, source_target_pairs={{0,2},{1,3},{2,4},{3,5},{4,6},{5,7},{6,0},{7,1},{8,10},{9,11},{10,... | collective-permute-start | bytes 1179656 | tf_op jit(solution)/shard_map/ppermute | solution.py:31
  32.8 10.7 %collective-permute-start.10 = (bf16[64,3072]{1,0:T(8,128)(2,1)}, bf16[64,3072]{1,0:T(8,128)(2,1)S(1)}, u32[]{:S(2)}, u32[]{:S(2)}) collective-permute-start(bf16[64,3072]{1,0:T(8,128)(2,1)} %collective-permute-done.2.refs_1_), channel_id=1, source_target_pairs={{0,6},{1,7},{2,0},{3,1},{4,2},{5,3},{6,4},{7,5},{8,14},{9,15},{10,... | collective-permute-start | bytes 1179656 | tf_op jit(solution)/shard_map/ppermute | solution.py:31
  35.6 9.6 %collective-permute-start.7 = (bf16[64,3072]{1,0:T(8,128)(2,1)S(1)}, bf16[64,3072]{1,0:T(8,128)(2,1)S(1)}, u32[]{:S(2)}, u32[]{:S(2)}) collective-permute-start(bf16[64,3072]{1,0:T(8,128)(2,1)S(1)} %collective-permute-done.refs_0_), channel_id=1, source_target_pairs={{0,1},{1,0},{2,3},{3,2},{4,5},{5,4},{6,7},{7,6},{8,9},{9,8},{10,11... | collective-permute-start | bytes 1179656 | tf_op jit(solution)/shard_map/ppermute | solution.py:35
  36.8 8.5 %collective-permute-start.8 = (bf16[64,3072]{1,0:T(8,128)(2,1)S(1)}, bf16[64,3072]{1,0:T(8,128)(2,1)S(1)}, u32[]{:S(2)}, u32[]{:S(2)}) collective-permute-start(bf16[64,3072]{1,0:T(8,128)(2,1)S(1)} %collective-permute-done.4.refs_3_), channel_id=1, source_target_pairs={{0,1},{1,0},{2,3},{3,2},{4,5},{5,4},{6,7},{7,6},{8,9},{9,8},{10,11... | collective-permute-start | bytes 1179656 | tf_op jit(solution)/shard_map/ppermute | solution.py:35
  43.5 4.4 %collective-permute-start.11 = (bf16[64,3072]{1,0:T(8,128)(2,1)S(1)}, bf16[64,3072]{1,0:T(8,128)(2,1)S(1)}, u32[]{:S(2)}, u32[]{:S(2)}) collective-permute-start(bf16[64,3072]{1,0:T(8,128)(2,1)S(1)} %collective-permute-done.9.refs_0_), channel_id=1, source_target_pairs={{0,1},{1,0},{2,3},{3,2},{4,5},{5,4},{6,7},{7,6},{8,9},{9,8},{10,11... | collective-permute-start | bytes 1179656 | tf_op jit(solution)/shard_map/ppermute | solution.py:35
  45.3 2.7 %collective-permute-start.12 = (bf16[64,3072]{1,0:T(8,128)(2,1)S(1)}, bf16[64,3072]{1,0:T(8,128)(2,1)S(1)}, u32[]{:S(2)}, u32[]{:S(2)}) collective-permute-start(bf16[64,3072]{1,0:T(8,128)(2,1)S(1)} %collective-permute-done.10.refs_1_), channel_id=1, source_target_pairs={{0,1},{1,0},{2,3},{3,2},{4,5},{5,4},{6,7},{7,6},{8,9},{9,8},{10,11... | collective-permute-start | bytes 1179656 | tf_op jit(solution)/shard_map/ppermute | solution.py:35
  47.9 34.2 %copy-start.3 = (f32[512]{0:T(512)S(1)}, f32[512]{0:T(512)}, u32[]{:S(2)}) copy-start(f32[512]{0:T(512)} %param.10) | copy-start | bytes 6148
  51.6 9.5 %collective-permute-start.13 = (bf16[528,128]{1,0:T(8,128)(2,1)S(1)}, bf16[528,128]{1,0:T(8,128)(2,1)S(1)}, u32[]{:S(2)}, u32[]{:S(2)}) collective-permute-start(bf16[528,128]{1,0:T(8,128)(2,1)S(1)} %state.1.s0), channel_id=1, source_target_pairs={{0,8},{8,16},{16,24},{24,0},{32,40},{40,48},{48,56},{56,32},{64,72... | collective-permute-start | bytes 405512 | tf_op jit(solution)/shard_map/ppermute | solution.py:39
  52.8 14.9 %collective-permute-start.14 = (bf16[528,128]{1,0:T(8,128)(2,1)S(1)}, bf16[528,128]{1,0:T(8,128)(2,1)}, u32[]{:S(2)}, u32[]{:S(2)}) collective-permute-start(bf16[528,128]{1,0:T(8,128)(2,1)S(1)} %state.1.s0), channel_id=1, source_target_pairs={{0,16},{8,24},{16,0},{24,8},{32,48},{40,56},{48,32},{56,40},{64,80... | collective-permute-start | bytes 405512 | tf_op jit(solution)/shard_map/ppermute | solution.py:39
  55.1 12.6 %collective-permute-start.15 = (bf16[528,128]{1,0:T(8,128)(2,1)S(1)}, bf16[528,128]{1,0:T(8,128)(2,1)}, u32[]{:S(2)}, u32[]{:S(2)}) collective-permute-start(bf16[528,128]{1,0:T(8,128)(2,1)S(1)} %state.1.s0), channel_id=1, source_target_pairs={{0,24},{8,0},{16,8},{24,16},{32,56},{40,32},{48,40},{56,48},{64,88... | collective-permute-start | bytes 405512 | tf_op jit(solution)/shard_map/ppermute | solution.py:39
  68.9 10.2 %collective-permute-start.16 = (bf16[528,128]{1,0:T(8,128)(2,1)S(1)}, bf16[528,128]{1,0:T(8,128)(2,1)S(1)}, u32[]{:S(2)}, u32[]{:S(2)}) collective-permute-start(bf16[528,128]{1,0:T(8,128)(2,1)S(1)} %get-tuple-element.76), channel_id=1, source_target_pairs={{0,32},{8,40},{16,48},{24,56},{32,64},{40,72},{48,80},{56,88},{64,... | collective-permute-start | bytes 405512 | tf_op jit(solution)/shard_map/ppermute | solution.py:43
  72.5 7.3 %collective-permute-start.17 = (bf16[528,128]{1,0:T(8,128)(2,1)S(1)}, bf16[528,128]{1,0:T(8,128)(2,1)S(1)}, u32[]{:S(2)}, u32[]{:S(2)}) collective-permute-start(bf16[528,128]{1,0:T(8,128)(2,1)S(1)} %get-tuple-element.76), channel_id=1, source_target_pairs={{0,64},{8,72},{16,80},{24,88},{32,96},{40,104},{48,112},{56,120},{... | collective-permute-start | bytes 405512 | tf_op jit(solution)/shard_map/ppermute | solution.py:43
  77.8 3.7 %collective-permute-start.18 = (bf16[528,128]{1,0:T(8,128)(2,1)S(1)}, bf16[528,128]{1,0:T(8,128)(2,1)S(1)}, u32[]{:S(2)}, u32[]{:S(2)}) collective-permute-start(bf16[528,128]{1,0:T(8,128)(2,1)S(1)} %get-tuple-element.76), channel_id=1, source_target_pairs={{0,96},{8,104},{16,112},{24,120},{1,97},{9,105},{17,113},{25,121},... | collective-permute-start | bytes 405512 | tf_op jit(solution)/shard_map/ppermute | solution.py:43
  81.5 0.7 copy-start.1
  82.1 0.9 copy-start.2
  87.1 4.8 %collective-permute-start.19 = (bf16[64,6144]{1,0:T(8,128)(2,1)S(1)}, bf16[64,6144]{1,0:T(8,128)(2,1)S(1)}, u32[]{:S(2)}, u32[]{:S(2)}) collective-permute-start(bf16[64,6144]{1,0:T(8,128)(2,1)S(1)} %get-tuple-element.84), channel_id=1, source_target_pairs={{0,1},{1,0},{2,3},{3,2},{4,5},{5,4},{6,7},{7,6},{8,9},{9,8},{10,11... | collective-permute-start | bytes 2359304 | tf_op jit(solution)/shard_map/ppermute | solution.py:35
  92.1 3.9 %collective-permute-start.20 = (bf16[64,6144]{1,0:T(8,128)(2,1)S(1)}, bf16[64,6144]{1,0:T(8,128)(2,1)S(1)}, u32[]{:S(2)}, u32[]{:S(2)}) collective-permute-start(bf16[64,6144]{1,0:T(8,128)(2,1)S(1)} %get-tuple-element.87), channel_id=1, source_target_pairs={{0,1},{1,0},{2,3},{3,2},{4,5},{5,4},{6,7},{7,6},{8,9},{9,8},{10,11... | collective-permute-start | bytes 2359304 | tf_op jit(solution)/shard_map/ppermute | solution.py:35
  92.2 4.0 %collective-permute-start.21 = (bf16[64,6144]{1,0:T(8,128)(2,1)S(1)}, bf16[64,6144]{1,0:T(8,128)(2,1)S(1)}, u32[]{:S(2)}, u32[]{:S(2)}) collective-permute-start(bf16[64,6144]{1,0:T(8,128)(2,1)S(1)} %get-tuple-element.89), channel_id=1, source_target_pairs={{0,1},{1,0},{2,3},{3,2},{4,5},{5,4},{6,7},{7,6},{8,9},{9,8},{10,11... | collective-permute-start | bytes 2359304 | tf_op jit(solution)/shard_map/ppermute | solution.py:35
  92.7 12.7 %collective-permute-start.25 = (bf16[64,3072]{1,0:T(8,128)(2,1)S(1)}, bf16[64,3072]{1,0:T(8,128)(2,1)S(1)}, u32[]{:S(2)}, u32[]{:S(2)}) collective-permute-start(bf16[64,3072]{1,0:T(8,128)(2,1)S(1)} %get-tuple-element.98), channel_id=1, source_target_pairs={{0,2},{1,3},{2,4},{3,5},{4,6},{5,7},{6,0},{7,1},{8,10},{9,11},{10,... | collective-permute-start | bytes 1179656 | tf_op jit(solution)/shard_map/ppermute | solution.py:31
  93.3 12.0 %collective-permute-start.26 = (bf16[64,3072]{1,0:T(8,128)(2,1)S(1)}, bf16[64,3072]{1,0:T(8,128)(2,1)S(1)}, u32[]{:S(2)}, u32[]{:S(2)}) collective-permute-start(bf16[64,3072]{1,0:T(8,128)(2,1)S(1)} %get-tuple-element.97), channel_id=1, source_target_pairs={{0,6},{1,7},{2,0},{3,1},{4,2},{5,3},{6,4},{7,5},{8,14},{9,15},{10,... | collective-permute-start | bytes 1179656 | tf_op jit(solution)/shard_map/ppermute | solution.py:31
  96.1 17.7 %collective-permute-start.23 = (bf16[64,3072]{1,0:T(8,128)(2,1)S(1)}, bf16[64,3072]{1,0:T(8,128)(2,1)S(1)}, u32[]{:S(2)}, u32[]{:S(2)}) collective-permute-start(bf16[64,3072]{1,0:T(8,128)(2,1)S(1)} %add_convert_fusion.3), channel_id=1, source_target_pairs={{0,2},{1,3},{2,4},{3,5},{4,6},{5,7},{6,0},{7,1},{8,10},{9,11},{10,... | collective-permute-start | bytes 1179656 | tf_op jit(solution)/shard_map/ppermute | solution.py:31
  96.3 17.5 %collective-permute-start.24 = (bf16[64,3072]{1,0:T(8,128)(2,1)S(1)}, bf16[64,3072]{1,0:T(8,128)(2,1)S(1)}, u32[]{:S(2)}, u32[]{:S(2)}) collective-permute-start(bf16[64,3072]{1,0:T(8,128)(2,1)S(1)} %add_convert_fusion.2), channel_id=1, source_target_pairs={{0,6},{1,7},{2,0},{3,1},{4,2},{5,3},{6,4},{7,5},{8,14},{9,15},{10,... | collective-permute-start | bytes 1179656 | tf_op jit(solution)/shard_map/ppermute | solution.py:31
  100.3 13.5 %collective-permute-start.22 = (bf16[64,6144]{1,0:T(8,128)(2,1)S(1)}, bf16[64,6144]{1,0:T(8,128)(2,1)S(1)}, u32[]{:S(2)}, u32[]{:S(2)}) collective-permute-start(bf16[64,6144]{1,0:T(8,128)(2,1)S(1)} %get-tuple-element.92), channel_id=1, source_target_pairs={{0,1},{1,0},{2,3},{3,2},{4,5},{5,4},{6,7},{7,6},{8,9},{9,8},{10,11... | collective-permute-start | bytes 2359304 | tf_op jit(solution)/shard_map/ppermute | solution.py:35
  105.5 16.7 %collective-permute-start.27 = (bf16[64,3072]{1,0:T(8,128)(2,1)S(1)}, bf16[64,3072]{1,0:T(8,128)(2,1)S(1)}, u32[]{:S(2)}, u32[]{:S(2)}) collective-permute-start(bf16[64,3072]{1,0:T(8,128)(2,1)S(1)} %add_convert_fusion.1), channel_id=1, source_target_pairs={{0,2},{1,3},{2,4},{3,5},{4,6},{5,7},{6,0},{7,1},{8,10},{9,11},{10,... | collective-permute-start | bytes 1179656 | tf_op jit(solution)/shard_map/ppermute | solution.py:31
  106.4 15.8 %collective-permute-start.28 = (bf16[64,3072]{1,0:T(8,128)(2,1)S(1)}, bf16[64,3072]{1,0:T(8,128)(2,1)S(1)}, u32[]{:S(2)}, u32[]{:S(2)}) collective-permute-start(bf16[64,3072]{1,0:T(8,128)(2,1)S(1)} %add_convert_fusion), channel_id=1, source_target_pairs={{0,6},{1,7},{2,0},{3,1},{4,2},{5,3},{6,4},{7,5},{8,14},{9,15},{10,... | collective-permute-start | bytes 1179656 | tf_op jit(solution)/shard_map/ppermute | solution.py:31
Sparse Core Ops, SparseCore 0:
  9.5 70.1 all-gather.2

commit v7 on v6

--- a/solution.py
+++ b/solution.py
@@ -16,7 +16,7 @@
 FAR = 384
 PLACES = ((1, 0), (3, 0), (0, 0), (0, 1), (1, 1), (3, 1), (2, 0), (2, 1))
 SHARE = 0.01
-VMEM_LIMIT = 24 * 2**20
+VMEM_LIMIT = 20 * 2**20
 
 
 def params(**kw):
@@ -165,13 +165,7 @@
     before[WIDE:, :] = jnp.concatenate([lead, lead], axis=0)
 
 
-def normed_kernel(before, t1, t2, t3, a, b, c, d, g, inner, gain, w, out, own, sib, held, sems):
-    per = w.shape[0] // 4
-    copies = [
-        pltpu.make_async_copy(w.at[pl.ds(i * per, per)], held.at[pl.ds(i * per, per)], sems.at[i]) for i in range(4)
-    ]
-    for copy in copies:
-        copy.start()
+def normed_kernel(before, t1, t2, t3, a, b, c, d, g, inner, gain, out):
     lead = jnp.exp(before[WIDE : WIDE + HEADS, :])
     r1, r2 = unpack(t1), unpack(t2)
     reach2, reach3 = jnp.exp(r1), jnp.exp(r1 + r2)
@@ -187,11 +181,6 @@
         mixed = inner[:, rows] + jnp.dot(scaled, carried, preferred_element_type=f32)
         scale = lax.rsqrt(jnp.mean(mixed * mixed, axis=-1, keepdims=True) + norm_eps)
         out[:, rows] = (mixed * scale * gain[:, rows]).astype(bf16)
-    far = out[FAR : FAR + 128, :]
-    for i in range(4):
-        copies[i].wait()
-        for m in range(i * per, (i + 1) * per):
-            project_part(far, held, (own, sib), m)
 
 
 def whole_call(kernel, args, outs, name, flops, scalars=0):
@@ -213,6 +202,20 @@
     part = jnp.dot(rows, w[m], preferred_element_type=f32).astype(bf16)
     for i, out in enumerate(outs):
         out[:, m * width : (m + 1) * width] = part[i * 64 : (i + 1) * 64]
+
+
+def project_first_kernel(normed, w, own, sib, held, sems):
+    per = w.shape[0] // 4
+    copies = [
+        pltpu.make_async_copy(w.at[pl.ds(i * per, per)], held.at[pl.ds(i * per, per)], sems.at[i]) for i in range(4)
+    ]
+    for copy in copies:
+        copy.start()
+    far = normed[FAR : FAR + 128, :]
+    for i in range(4):
+        copies[i].wait()
+        for m in range(i * per, (i + 1) * per):
+            project_part(far, held, (own, sib), m)
 
 
 def project_kernel(blocks, normed, w, *outs):
@@ -316,19 +319,25 @@
         row_kernel, (at, *row), (jax.ShapeDtypeStruct((WIDE + 8, SIZE), f32), packed), "row", 10 * WIDE * SIZE, 1
     )
     totals = [to_z(total, k) for k in range(1, N_Z)]
+    normed = whole_call(
+        normed_kernel,
+        (before, *totals, *rows, g, inner, gain.reshape(1, WIDE)),
+        jax.ShapeDtypeStruct((512, WIDE), bf16),
+        "normed",
+        2 * 512 * WIDE * SIZE,
+    )
     vmem = pl.BlockSpec(memory_space=pltpu.VMEM)
-    args = (before, *totals, *rows, g, inner, gain.reshape(1, WIDE))
     half = jax.ShapeDtypeStruct((64, depth), bf16)
-    normed, far_own, far_sib, w = pl.pallas_call(
-        normed_kernel,
-        out_shape=[jax.ShapeDtypeStruct((512, WIDE), bf16), half, half, pltpu.VMEM(w_all.shape, bf16)],
-        in_specs=[vmem] * len(args) + [pl.BlockSpec(memory_space=pltpu.HBM)],
-        out_specs=[vmem] * 4,
+    far_own, far_sib, w = pl.pallas_call(
+        project_first_kernel,
+        out_shape=[half, half, pltpu.VMEM(w_all.shape, bf16)],
+        in_specs=[vmem, pl.BlockSpec(memory_space=pltpu.HBM)],
+        out_specs=[vmem] * 3,
         scratch_shapes=[pltpu.SemaphoreType.DMA((4,))],
         compiler_params=params(),
-        cost_estimate=cost(2 * 512 * WIDE * SIZE, 2 * w_all.size),
-        name="normed",
-    )(*args, pltpu.with_memory_space_constraint(w_all, pltpu.HBM))
+        cost_estimate=cost(256 * w_all.size, 2 * w_all.size),
+        name="project",
+    )(normed, pltpu.with_memory_space_constraint(w_all, pltpu.HBM))
 
     far_sib = to_sibling(far_sib)
     near_parts = project(normed, w, (0, 4, 1, 5))

time: 130 us -> 126 us (0.969)
  local copies, waits for them, and re-layouts: 7.83 us -> 4.77 us
  Pallas kernels: 28.7 us -> 27 us
    unnamed x8 -> x4, local copies, waits for them, and re-layouts: 2.7 us -> 1.14 us
    pallas_call x5 -> x6, Pallas kernels: 4.9 us -> 4.96 us  [whole_call(): pl.pallas_call(kernel, out_shape=outs, in_specs=[pl.BlockSpec(memory_spac...]
  transfers between devices with their start and end apart: 30 -> 30, of which waited for: 10 -> 11; matrix products, arithmetic and copies ran while one was open for 6% -> 5% of each run, Pallas kernels for 18% -> 18%
where the time goes in v7:
time: 126 us
  starting transfers between devices  41 us (33%)
  waiting for transfers between devices  36.5 us (29%)
  Pallas kernels  27 us (21%)
  between operations  13.7 us (11%)
  local copies, waits for them, and re-layouts  4.77 us (4%)
  other arithmetic  2.94 us (2%)
    ppermute x12, waiting for transfers between devices, to_y(): lax.ppermute(a, 'tp', [(i, (i // 2 + k) % N_Y * 2 + i % 2) for i in range...  23.4 us
    ppermute x12, starting transfers between devices, to_y(): lax.ppermute(a, 'tp', [(i, (i // 2 + k) % N_Y * 2 + i % 2) for i in range...  16.5 us
    pallas_call x4, Pallas kernels, qkv(): pl.pallas_call(functools.partial(qkv_first_kernel if first else qkv_kerne...  15.1 us
    ppermute x3, starting transfers between devices, to_z(): lax.ppermute(a, 'ctx', [(j, j + N_X * k) for j in range(N_X * N_Z) if j /...  9.95 us
    ppermute x3, waiting for transfers between devices, to_x(): lax.ppermute(a, 'ctx', [(j, j // N_X * N_X + (j + k) % N_X) for j in rang...  9.72 us
    ppermute x11, starting transfers between devices, to_sibling(): return lax.ppermute(a, 'tp', [(i, i ^ 1) for i in range(2 * N_Y)])  9.58 us
    pallas_call x6, Pallas kernels, whole_call(): pl.pallas_call(kernel, out_shape=outs, in_specs=[pl.BlockSpec(memory_spac...  4.96 us
    ppermute x3, starting transfers between devices, to_x(): lax.ppermute(a, 'ctx', [(j, j // N_X * N_X + (j + k) % N_X) for j in rang...  4.91 us
  transfers between devices with their start and end apart: 30, of which 11 were waited for; matrix products, arithmetic and copies ran while one was open for 5% of the time, Pallas kernels for 18%

profile of v7, /device:TPU:1, one launch (start us, length us, event | category | flops | bytes accessed | tf_op | source)
XLA Modules:
  0.0 125.8 jit_solution(97818922063800813)
XLA Ops:
  6.5 0.7 all-gather.3.cloned.1.call-update
  7.3 1.5 %collective-permute-start.3 = (bf16[64,6144]{1,0:T(8,128)(2,1)}, bf16[64,6144]{1,0:T(8,128)(2,1)S(1)}, u32[]{:S(2)}, u32[]{:S(2)}) collective-permute-start(bf16[64,6144]{1,0:T(8,128)(2,1)} %refs_0_.1), channel_id=1, source_target_pairs={{0,1},{1,0},{2,3},{3,2},{4,5},{5,4},{6,7},{7,6},{8,9},{9,8},{10,11... | collective-permute-start | bytes 2359304 | tf_op jit(solution)/shard_map/ppermute | solution.py:35
  8.8 1.0 slice.75
  9.8 1.4 %collective-permute-start.1 = (bf16[64,3072]{1,0:T(8,128)(2,1)S(1)}, bf16[64,3072]{1,0:T(8,128)(2,1)S(1)}, u32[]{:S(2)}, u32[]{:S(2)}) collective-permute-start(bf16[64,3072]{1,0:T(8,128)(2,1)S(1)} %slice.75), channel_id=1, source_target_pairs={{0,2},{1,3},{2,4},{3,5},{4,6},{5,7},{6,0},{7,1},{8,10},{9,11},{10,... | collective-permute-start | bytes 1179656 | tf_op jit(solution)/shard_map/ppermute | solution.py:31
  11.2 1.0 slice.76
  12.3 1.5 %collective-permute-start.2 = (bf16[64,3072]{1,0:T(8,128)(2,1)S(1)}, bf16[64,3072]{1,0:T(8,128)(2,1)S(1)}, u32[]{:S(2)}, u32[]{:S(2)}) collective-permute-start(bf16[64,3072]{1,0:T(8,128)(2,1)S(1)} %slice.76), channel_id=1, source_target_pairs={{0,6},{1,7},{2,0},{3,1},{4,2},{5,3},{6,4},{7,5},{8,14},{9,15},{10,... | collective-permute-start | bytes 1179656 | tf_op jit(solution)/shard_map/ppermute | solution.py:31
  13.8 0.7 reshape.29
  14.5 1.2 reduce-window.6
  16.5 0.7 fusion.1
  17.6 1.5 %collective-permute-start = (bf16[64,3072]{1,0:T(8,128)(2,1)S(1)}, bf16[64,3072]{1,0:T(8,128)(2,1)S(1)}, u32[]{:S(2)}, u32[]{:S(2)}) collective-permute-start(bf16[64,3072]{1,0:T(8,128)(2,1)S(1)} %slice.75), channel_id=1, source_target_pairs={{0,6},{1,7},{2,0},{3,1},{4,2},{5,3},{6,4},{7,5},{8,14},{9,15},{10,... | collective-permute-start | bytes 1179656 | tf_op jit(solution)/shard_map/ppermute | solution.py:31
  19.0 1.1 copy-done
  20.2 7.3 %qkv.4 = (bf16[128,1536]{1,0:T(8,128)(2,1)S(1)}, bf16[3,6144,512]{2,1,0:T(8,128)(2,1)S(1)}) custom-call(bf16[64,6144]{1,0:T(8,128)(2,1)S(1)} %copy-done, bf16[64,6144]{1,0:T(8,128)(2,1)S(1)} %collective-permute-done.3.refs_1_, bf16[3,6144,512]{2,1,0:T(8,128)(2,1)} %refs_2_.1), custom_call_target="tpu_custom_call" | custom-call | flops 24159192 | bytes 188743 | tf_op jit(solution)/shard_map/qkv/pallas_call | solution.py:97
  27.5 1.1 collective-permute-start.5
  28.8 2.3 %collective-permute-done.refs_0_ = bf16[64,3072]{1,0:T(8,128)(2,1)S(1)} collective-permute-done((bf16[64,3072]{1,0:T(8,128)(2,1)S(1)}, bf16[64,3072]{1,0:T(8,128)(2,1)S(1)}, u32[]{:S(2)}, u32[]{:S(2)}) %collective-permute-start) | collective-permute-done | bytes 393248 | tf_op jit(solution)/shard_map/ppermute | solution.py:31
  31.2 2.8 %collective-permute-start.10 = (bf16[64,3072]{1,0:T(8,128)(2,1)S(1)}, bf16[64,3072]{1,0:T(8,128)(2,1)S(1)}, u32[]{:S(2)}, u32[]{:S(2)}) collective-permute-start(bf16[64,3072]{1,0:T(8,128)(2,1)S(1)} %collective-permute-done.2.refs_1_), channel_id=1, source_target_pairs={{0,6},{1,7},{2,0},{3,1},{4,2},{5,3},{6,4},{7,5},{8,14},{9,15},{10,... | collective-permute-start | bytes 1179656 | tf_op jit(solution)/shard_map/ppermute | solution.py:31
  34.0 1.2 collective-permute-start.7
  35.3 2.6 %qkv.5.a = bf16[128,1536]{1,0:T(8,128)(2,1)S(1)} custom-call(bf16[64,3072]{1,0:T(8,128)(2,1)S(1)} %collective-permute-done.refs_0_, bf16[64,3072]{1,0:T(8,128)(2,1)S(1)} %collective-permute-done.2.refs_1_, bf16[64,3072]{1,0:T(8,128)(2,1)S(1)} %collective-permute-done.1.refs_2_, bf16[64,3072]{1,0:T(8,128)(2,1)S(1)} %collective-permute-done.4.refs_3_, ...), custom_call_target="tpu_custom_call" | custom-call | flops 24159192 | bytes 188743 | tf_op jit(solution)/shard_map/qkv/pallas_call | solution.py:97
  37.9 2.5 %collective-permute-done.9.refs_0_ = bf16[64,3072]{1,0:T(8,128)(2,1)S(1)} collective-permute-done((bf16[64,3072]{1,0:T(8,128)(2,1)S(1)}, bf16[64,3072]{1,0:T(8,128)(2,1)S(1)}, u32[]{:S(2)}, u32[]{:S(2)}) %collective-permute-start.9) | collective-permute-done | bytes 393248 | tf_op jit(solution)/shard_map/ppermute | solution.py:31
  40.4 1.0 collective-permute-done.10.refs_1_
  41.5 1.9 %collective-permute-start.11 = (bf16[64,3072]{1,0:T(8,128)(2,1)S(1)}, bf16[64,3072]{1,0:T(8,128)(2,1)S(1)}, u32[]{:S(2)}, u32[]{:S(2)}) collective-permute-start(bf16[64,3072]{1,0:T(8,128)(2,1)S(1)} %collective-permute-done.9.refs_0_), channel_id=1, source_target_pairs={{0,1},{1,0},{2,3},{3,2},{4,5},{5,4},{6,7},{7,6},{8,9},{9,8},{10,11... | collective-permute-start | bytes 1179656 | tf_op jit(solution)/shard_map/ppermute | solution.py:35
  43.3 2.6 %qkv.6.c = bf16[128,1536]{1,0:T(8,128)(2,1)S(1)} custom-call(bf16[64,3072]{1,0:T(8,128)(2,1)S(1)} %collective-permute-done.7.refs_0_, bf16[64,3072]{1,0:T(8,128)(2,1)S(1)} %collective-permute-done.6.refs_1_, bf16[64,3072]{1,0:T(8,128)(2,1)S(1)} %collective-permute-done.5.refs_2_, bf16[64,3072]{1,0:T(8,128)(2,1)S(1)} %collective-permute-done.8.refs_3_, ...), custom_call_target="tpu_custom_call" | custom-call | flops 24159192 | bytes 188743 | tf_op jit(solution)/shard_map/qkv/pallas_call | solution.py:97
  46.0 2.6 %qkv.7.d = bf16[128,1536]{1,0:T(8,128)(2,1)S(1)} custom-call(bf16[64,3072]{1,0:T(8,128)(2,1)S(1)} %collective-permute-done.9.refs_0_, bf16[64,3072]{1,0:T(8,128)(2,1)S(1)} %collective-permute-done.10.refs_1_, bf16[64,3072]{1,0:T(8,128)(2,1)S(1)} %collective-permute-done.11.refs_2_, bf16[64,3072]{1,0:T(8,128)(2,1)S(1)} %collective-permute-done.12.refs_3_, ...), custom_call_target="tpu_custom_call" | custom-call | flops 24159192 | bytes 188743 | tf_op jit(solution)/shard_map/qkv/pallas_call | solution.py:97
  48.6 1.0 state.1.s0
  49.6 1.3 %collective-permute-start.13 = (bf16[528,128]{1,0:T(8,128)(2,1)S(1)}, bf16[528,128]{1,0:T(8,128)(2,1)S(1)}, u32[]{:S(2)}, u32[]{:S(2)}) collective-permute-start(bf16[528,128]{1,0:T(8,128)(2,1)S(1)} %state.1.s0), channel_id=1, source_target_pairs={{0,8},{8,16},{16,24},{24,0},{32,40},{40,48},{48,56},{56,32},{64,72... | collective-permute-start | bytes 405512 | tf_op jit(solution)/shard_map/ppermute | solution.py:39
  50.9 2.5 %collective-permute-start.14 = (bf16[528,128]{1,0:T(8,128)(2,1)S(1)}, bf16[528,128]{1,0:T(8,128)(2,1)S(1)}, u32[]{:S(2)}, u32[]{:S(2)}) collective-permute-start(bf16[528,128]{1,0:T(8,128)(2,1)S(1)} %state.1.s0), channel_id=1, source_target_pairs={{0,16},{8,24},{16,0},{24,8},{32,48},{40,56},{48,32},{56,40},{64,80... | collective-permute-start | bytes 405512 | tf_op jit(solution)/shard_map/ppermute | solution.py:39
  53.4 1.2 collective-permute-start.15
  54.7 1.4 %inner.1 = f32[512,512]{1,0:T(8,128)S(1)} custom-call(bf16[128,1536]{1,0:T(8,128)(2,1)S(1)} %qkv.5.a, bf16[128,1536]{1,0:T(8,128)(2,1)S(1)} %get-tuple-element.53.b, bf16[128,1536]{1,0:T(8,128)(2,1)S(1)} %qkv.6.c, bf16[128,1536]{1,0:T(8,128)(2,1)S(1)} %qkv.7.d, f32[512,4]{1,0:T(8,128)S(1)} %bitcast.20, f32[4,512]{1,0:T(4,128)S(1)} %concatenate.8.gt, ...), custom_call_target="tpu_custom_call" | custom-call | flops 5368709 | bytes 15933 | tf_op jit(solution)/shard_map/inner/pallas_call | solution.py:188
  56.1 3.0 %collective-permute-done.13.s1 = bf16[528,128]{1,0:T(8,128)(2,1)S(1)} collective-permute-done((bf16[528,128]{1,0:T(8,128)(2,1)S(1)}, bf16[528,128]{1,0:T(8,128)(2,1)S(1)}, u32[]{:S(2)}, u32[]{:S(2)}) %collective-permute-start.13) | collective-permute-done | bytes 135200 | tf_op jit(solution)/shard_map/ppermute | solution.py:39
  59.2 6.7 %collective-permute-done.14.s2 = bf16[528,128]{1,0:T(8,128)(2,1)S(1)} collective-permute-done((bf16[528,128]{1,0:T(8,128)(2,1)S(1)}, bf16[528,128]{1,0:T(8,128)(2,1)S(1)}, u32[]{:S(2)}, u32[]{:S(2)}) %collective-permute-start.14) | collective-permute-done | bytes 135200 | tf_op jit(solution)/shard_map/ppermute | solution.py:39
  66.1 3.6 %collective-permute-start.16 = (bf16[528,128]{1,0:T(8,128)(2,1)S(1)}, bf16[528,128]{1,0:T(8,128)(2,1)S(1)}, u32[]{:S(2)}, u32[]{:S(2)}) collective-permute-start(bf16[528,128]{1,0:T(8,128)(2,1)S(1)} %get-tuple-element.75), channel_id=1, source_target_pairs={{0,32},{8,40},{16,48},{24,56},{32,64},{40,72},{48,80},{56,88},{64,... | collective-permute-start | bytes 405512 | tf_op jit(solution)/shard_map/ppermute | solution.py:43
  69.6 5.1 %collective-permute-start.17 = (bf16[528,128]{1,0:T(8,128)(2,1)S(1)}, bf16[528,128]{1,0:T(8,128)(2,1)S(1)}, u32[]{:S(2)}, u32[]{:S(2)}) collective-permute-start(bf16[528,128]{1,0:T(8,128)(2,1)S(1)} %get-tuple-element.75), channel_id=1, source_target_pairs={{0,64},{8,72},{16,80},{24,88},{32,96},{40,104},{48,112},{56,120},{... | collective-permute-start | bytes 405512 | tf_op jit(solution)/shard_map/ppermute | solution.py:43
  74.7 1.3 %collective-permute-start.18 = (bf16[528,128]{1,0:T(8,128)(2,1)S(1)}, bf16[528,128]{1,0:T(8,128)(2,1)S(1)}, u32[]{:S(2)}, u32[]{:S(2)}) collective-permute-start(bf16[528,128]{1,0:T(8,128)(2,1)S(1)} %get-tuple-element.75), channel_id=1, source_target_pairs={{0,96},{8,104},{16,112},{24,120},{1,97},{9,105},{17,113},{25,121},... | collective-permute-start | bytes 405512 | tf_op jit(solution)/shard_map/ppermute | solution.py:43
  76.7 1.7 %collective-permute-done.18.t3 = bf16[528,128]{1,0:T(8,128)(2,1)S(1)} collective-permute-done((bf16[528,128]{1,0:T(8,128)(2,1)S(1)}, bf16[528,128]{1,0:T(8,128)(2,1)S(1)}, u32[]{:S(2)}, u32[]{:S(2)}) %collective-permute-start.18) | collective-permute-done | bytes 135200 | tf_op jit(solution)/shard_map/ppermute | solution.py:43
  78.4 1.0 normed.1
  79.7 3.3 %project.3 = (bf16[64,6144]{1,0:T(8,128)(2,1)S(1)}, bf16[64,6144]{1,0:T(8,128)(2,1)S(1)}, bf16[16,512,384]{2,1,0:T(8,128)(2,1)S(1)}) custom-call(bf16[512,512]{1,0:T(8,128)(2,1)S(1)} %normed.1, bf16[16,512,384]{2,1,0:T(8,128)(2,1)} %bitcast.25), custom_call_target="tpu_custom_call" | custom-call | flops 8053063 | bytes 62914 | tf_op jit(solution)/shard_map/project/pallas_call | solution.py:331
  83.0 2.2 %collective-permute-start.19 = (bf16[64,6144]{1,0:T(8,128)(2,1)S(1)}, bf16[64,6144]{1,0:T(8,128)(2,1)S(1)}, u32[]{:S(2)}, u32[]{:S(2)}) collective-permute-start(bf16[64,6144]{1,0:T(8,128)(2,1)S(1)} %get-tuple-element.82), channel_id=1, source_target_pairs={{0,1},{1,0},{2,3},{3,2},{4,5},{5,4},{6,7},{7,6},{8,9},{9,8},{10,11... | collective-permute-start | bytes 2359304 | tf_op jit(solution)/shard_map/ppermute | solution.py:35
  85.2 2.3 %project.4 = (bf16[64,6144]{1,0:T(8,128)(2,1)S(1)}, bf16[64,6144]{1,0:T(8,128)(2,1)S(1)}, bf16[64,6144]{1,0:T(8,128)(2,1)S(1)}, bf16[64,6144]{1,0:T(8,128)(2,1)S(1)}) custom-call(bf16[512,512]{1,0:T(8,128)(2,1)S(1)} %normed.1, bf16[16,512,384]{2,1,0:T(8,128)(2,1)S(1)} %get-tuple-element.76.w), custom_call_target="tpu_custom_call" | custom-call | flops 16106127 | bytes 62914 | tf_op jit(solution)/shard_map/project/pallas_call | solution.py:231
  88.3 0.8 collective-permute-start.25
  89.1 2.7 %collective-permute-start.26 = (bf16[64,3072]{1,0:T(8,128)(2,1)S(1)}, bf16[64,3072]{1,0:T(8,128)(2,1)S(1)}, u32[]{:S(2)}, u32[]{:S(2)}) collective-permute-start(bf16[64,3072]{1,0:T(8,128)(2,1)S(1)} %get-tuple-element.95), channel_id=1, source_target_pairs={{0,6},{1,7},{2,0},{3,1},{4,2},{5,3},{6,4},{7,5},{8,14},{9,15},{10,... | collective-permute-start | bytes 1179656 | tf_op jit(solution)/shard_map/ppermute | solution.py:31
  92.1 2.8 %collective-permute-start.24 = (bf16[64,3072]{1,0:T(8,128)(2,1)S(1)}, bf16[64,3072]{1,0:T(8,128)(2,1)S(1)}, u32[]{:S(2)}, u32[]{:S(2)}) collective-permute-start(bf16[64,3072]{1,0:T(8,128)(2,1)S(1)} %add_convert_fusion.2), channel_id=1, source_target_pairs={{0,6},{1,7},{2,0},{3,1},{4,2},{5,3},{6,4},{7,5},{8,14},{9,15},{10,... | collective-permute-start | bytes 1179656 | tf_op jit(solution)/shard_map/ppermute | solution.py:31
  94.8 1.2 project.5
  96.1 1.0 collective-permute-start.22
  97.0 4.1 %collective-permute-done.25 = bf16[64,3072]{1,0:T(8,128)(2,1)S(1)} collective-permute-done((bf16[64,3072]{1,0:T(8,128)(2,1)S(1)}, bf16[64,3072]{1,0:T(8,128)(2,1)S(1)}, u32[]{:S(2)}, u32[]{:S(2)}) %collective-permute-start.25) | collective-permute-done | bytes 393248 | tf_op jit(solution)/shard_map/ppermute | solution.py:31
  101.3 0.7 collective-permute-start.27
  102.2 2.1 %collective-permute-start.28 = (bf16[64,3072]{1,0:T(8,128)(2,1)S(1)}, bf16[64,3072]{1,0:T(8,128)(2,1)S(1)}, u32[]{:S(2)}, u32[]{:S(2)}) collective-permute-start(bf16[64,3072]{1,0:T(8,128)(2,1)S(1)} %add_convert_fusion), channel_id=1, source_target_pairs={{0,6},{1,7},{2,0},{3,1},{4,2},{5,3},{6,4},{7,5},{8,14},{9,15},{10,... | collective-permute-start | bytes 1179656 | tf_op jit(solution)/shard_map/ppermute | solution.py:31
  104.3 5.3 %collective-permute-done.23.up_plain = bf16[64,3072]{1,0:T(8,128)(2,1)S(1)} collective-permute-done((bf16[64,3072]{1,0:T(8,128)(2,1)S(1)}, bf16[64,3072]{1,0:T(8,128)(2,1)S(1)}, u32[]{:S(2)}, u32[]{:S(2)}) %collective-permute-start.23) | collective-permute-done | bytes 393248 | tf_op jit(solution)/shard_map/ppermute | solution.py:31
  109.8 8.2 %collective-permute-done.27.up_sum = bf16[64,3072]{1,0:T(8,128)(2,1)S(1)} collective-permute-done((bf16[64,3072]{1,0:T(8,128)(2,1)S(1)}, bf16[64,3072]{1,0:T(8,128)(2,1)S(1)}, u32[]{:S(2)}, u32[]{:S(2)}) %collective-permute-start.27) | collective-permute-done | bytes 393248 | tf_op jit(solution)/shard_map/ppermute | solution.py:31
  118.0 1.0 final.1
  (54 shorter events, 4.3 us)
Async XLA Ops:
  6.5 73.2 %all-gather.3.cloned.1.call-start = ((), (), s32[]{:S(2)}) async-start(), calls=%async_computation | async-start | bytes 6684672 | tf_op jit(solution)/shard_map/all_gather | solution.py:271
  7.3 11.8 %collective-permute-start.3 = (bf16[64,6144]{1,0:T(8,128)(2,1)}, bf16[64,6144]{1,0:T(8,128)(2,1)S(1)}, u32[]{:S(2)}, u32[]{:S(2)}) collective-permute-start(bf16[64,6144]{1,0:T(8,128)(2,1)} %refs_0_.1), channel_id=1, source_target_pairs={{0,1},{1,0},{2,3},{3,2},{4,5},{5,4},{6,7},{7,6},{8,9},{9,8},{10,11... | collective-permute-start | bytes 2359304 | tf_op jit(solution)/shard_map/ppermute | solution.py:35
  9.8 17.7 %collective-permute-start.1 = (bf16[64,3072]{1,0:T(8,128)(2,1)S(1)}, bf16[64,3072]{1,0:T(8,128)(2,1)S(1)}, u32[]{:S(2)}, u32[]{:S(2)}) collective-permute-start(bf16[64,3072]{1,0:T(8,128)(2,1)S(1)} %slice.75), channel_id=1, source_target_pairs={{0,2},{1,3},{2,4},{3,5},{4,6},{5,7},{6,0},{7,1},{8,10},{9,11},{10,... | collective-permute-start | bytes 1179656 | tf_op jit(solution)/shard_map/ppermute | solution.py:31
  12.3 15.3 %collective-permute-start.2 = (bf16[64,3072]{1,0:T(8,128)(2,1)S(1)}, bf16[64,3072]{1,0:T(8,128)(2,1)S(1)}, u32[]{:S(2)}, u32[]{:S(2)}) collective-permute-start(bf16[64,3072]{1,0:T(8,128)(2,1)S(1)} %slice.76), channel_id=1, source_target_pairs={{0,6},{1,7},{2,0},{3,1},{4,2},{5,3},{6,4},{7,5},{8,14},{9,15},{10,... | collective-permute-start | bytes 1179656 | tf_op jit(solution)/shard_map/ppermute | solution.py:31
  17.6 13.6 %collective-permute-start = (bf16[64,3072]{1,0:T(8,128)(2,1)S(1)}, bf16[64,3072]{1,0:T(8,128)(2,1)S(1)}, u32[]{:S(2)}, u32[]{:S(2)}) collective-permute-start(bf16[64,3072]{1,0:T(8,128)(2,1)S(1)} %slice.75), channel_id=1, source_target_pairs={{0,6},{1,7},{2,0},{3,1},{4,2},{5,3},{6,4},{7,5},{8,14},{9,15},{10,... | collective-permute-start | bytes 1179656 | tf_op jit(solution)/shard_map/ppermute | solution.py:31
  19.0 15.0 %collective-permute-start.4 = (bf16[64,3072]{1,0:T(8,128)(2,1)S(1)}, bf16[64,3072]{1,0:T(8,128)(2,1)S(1)}, u32[]{:S(2)}, u32[]{:S(2)}) collective-permute-start(bf16[64,3072]{1,0:T(8,128)(2,1)S(1)} %slice.76), channel_id=1, source_target_pairs={{0,2},{1,3},{2,4},{3,5},{4,6},{5,7},{6,0},{7,1},{8,10},{9,11},{10,... | collective-permute-start | bytes 1179656 | tf_op jit(solution)/shard_map/ppermute | solution.py:31
  19.0 1.1 copy-start
  27.5 7.7 %collective-permute-start.5 = (bf16[64,3072]{1,0:T(8,128)(2,1)S(1)}, bf16[64,3072]{1,0:T(8,128)(2,1)S(1)}, u32[]{:S(2)}, u32[]{:S(2)}) collective-permute-start(bf16[64,3072]{1,0:T(8,128)(2,1)S(1)} %collective-permute-done.1.refs_2_), channel_id=1, source_target_pairs={{0,1},{1,0},{2,3},{3,2},{4,5},{5,4},{6,7},{7,6},{8,9},{9,8},{10,11... | collective-permute-start | bytes 1179656 | tf_op jit(solution)/shard_map/ppermute | solution.py:35
  28.6 6.7 %collective-permute-start.6 = (bf16[64,3072]{1,0:T(8,128)(2,1)S(1)}, bf16[64,3072]{1,0:T(8,128)(2,1)S(1)}, u32[]{:S(2)}, u32[]{:S(2)}) collective-permute-start(bf16[64,3072]{1,0:T(8,128)(2,1)S(1)} %collective-permute-done.2.refs_1_), channel_id=1, source_target_pairs={{0,1},{1,0},{2,3},{3,2},{4,5},{5,4},{6,7},{7,6},{8,9},{9,8},{10,11... | collective-permute-start | bytes 1179656 | tf_op jit(solution)/shard_map/ppermute | solution.py:35
  28.7 11.8 %collective-permute-start.9 = (bf16[64,3072]{1,0:T(8,128)(2,1)S(1)}, bf16[64,3072]{1,0:T(8,128)(2,1)S(1)}, u32[]{:S(2)}, u32[]{:S(2)}) collective-permute-start(bf16[64,3072]{1,0:T(8,128)(2,1)S(1)} %collective-permute-done.1.refs_2_), channel_id=1, source_target_pairs={{0,2},{1,3},{2,4},{3,5},{4,6},{5,7},{6,0},{7,1},{8,10},{9,11},{10,... | collective-permute-start | bytes 1179656 | tf_op jit(solution)/shard_map/ppermute | solution.py:31
  31.2 10.3 %collective-permute-start.10 = (bf16[64,3072]{1,0:T(8,128)(2,1)S(1)}, bf16[64,3072]{1,0:T(8,128)(2,1)S(1)}, u32[]{:S(2)}, u32[]{:S(2)}) collective-permute-start(bf16[64,3072]{1,0:T(8,128)(2,1)S(1)} %collective-permute-done.2.refs_1_), channel_id=1, source_target_pairs={{0,6},{1,7},{2,0},{3,1},{4,2},{5,3},{6,4},{7,5},{8,14},{9,15},{10,... | collective-permute-start | bytes 1179656 | tf_op jit(solution)/shard_map/ppermute | solution.py:31
  34.0 9.3 %collective-permute-start.7 = (bf16[64,3072]{1,0:T(8,128)(2,1)S(1)}, bf16[64,3072]{1,0:T(8,128)(2,1)S(1)}, u32[]{:S(2)}, u32[]{:S(2)}) collective-permute-start(bf16[64,3072]{1,0:T(8,128)(2,1)S(1)} %collective-permute-done.refs_0_), channel_id=1, source_target_pairs={{0,1},{1,0},{2,3},{3,2},{4,5},{5,4},{6,7},{7,6},{8,9},{9,8},{10,11... | collective-permute-start | bytes 1179656 | tf_op jit(solution)/shard_map/ppermute | solution.py:35
  35.2 8.1 %collective-permute-start.8 = (bf16[64,3072]{1,0:T(8,128)(2,1)S(1)}, bf16[64,3072]{1,0:T(8,128)(2,1)S(1)}, u32[]{:S(2)}, u32[]{:S(2)}) collective-permute-start(bf16[64,3072]{1,0:T(8,128)(2,1)S(1)} %collective-permute-done.4.refs_3_), channel_id=1, source_target_pairs={{0,1},{1,0},{2,3},{3,2},{4,5},{5,4},{6,7},{7,6},{8,9},{9,8},{10,11... | collective-permute-start | bytes 1179656 | tf_op jit(solution)/shard_map/ppermute | solution.py:35
  41.5 4.5 %collective-permute-start.11 = (bf16[64,3072]{1,0:T(8,128)(2,1)S(1)}, bf16[64,3072]{1,0:T(8,128)(2,1)S(1)}, u32[]{:S(2)}, u32[]{:S(2)}) collective-permute-start(bf16[64,3072]{1,0:T(8,128)(2,1)S(1)} %collective-permute-done.9.refs_0_), channel_id=1, source_target_pairs={{0,1},{1,0},{2,3},{3,2},{4,5},{5,4},{6,7},{7,6},{8,9},{9,8},{10,11... | collective-permute-start | bytes 1179656 | tf_op jit(solution)/shard_map/ppermute | solution.py:35
  43.3 2.7 %collective-permute-start.12 = (bf16[64,3072]{1,0:T(8,128)(2,1)S(1)}, bf16[64,3072]{1,0:T(8,128)(2,1)S(1)}, u32[]{:S(2)}, u32[]{:S(2)}) collective-permute-start(bf16[64,3072]{1,0:T(8,128)(2,1)S(1)} %collective-permute-done.10.refs_1_), channel_id=1, source_target_pairs={{0,1},{1,0},{2,3},{3,2},{4,5},{5,4},{6,7},{7,6},{8,9},{9,8},{10,11... | collective-permute-start | bytes 1179656 | tf_op jit(solution)/shard_map/ppermute | solution.py:35
  46.0 32.5 %copy-start.1 = (f32[512]{0:T(512)S(1)}, f32[512]{0:T(512)}, u32[]{:S(2)}) copy-start(f32[512]{0:T(512)} %param.10) | copy-start | bytes 6148
  49.6 9.5 %collective-permute-start.13 = (bf16[528,128]{1,0:T(8,128)(2,1)S(1)}, bf16[528,128]{1,0:T(8,128)(2,1)S(1)}, u32[]{:S(2)}, u32[]{:S(2)}) collective-permute-start(bf16[528,128]{1,0:T(8,128)(2,1)S(1)} %state.1.s0), channel_id=1, source_target_pairs={{0,8},{8,16},{16,24},{24,0},{32,40},{40,48},{48,56},{56,32},{64,72... | collective-permute-start | bytes 405512 | tf_op jit(solution)/shard_map/ppermute | solution.py:39
  50.9 14.9 %collective-permute-start.14 = (bf16[528,128]{1,0:T(8,128)(2,1)S(1)}, bf16[528,128]{1,0:T(8,128)(2,1)S(1)}, u32[]{:S(2)}, u32[]{:S(2)}) collective-permute-start(bf16[528,128]{1,0:T(8,128)(2,1)S(1)} %state.1.s0), channel_id=1, source_target_pairs={{0,16},{8,24},{16,0},{24,8},{32,48},{40,56},{48,32},{56,40},{64,80... | collective-permute-start | bytes 405512 | tf_op jit(solution)/shard_map/ppermute | solution.py:39
  53.4 12.5 %collective-permute-start.15 = (bf16[528,128]{1,0:T(8,128)(2,1)S(1)}, bf16[528,128]{1,0:T(8,128)(2,1)S(1)}, u32[]{:S(2)}, u32[]{:S(2)}) collective-permute-start(bf16[528,128]{1,0:T(8,128)(2,1)S(1)} %state.1.s0), channel_id=1, source_target_pairs={{0,24},{8,0},{16,8},{24,16},{32,56},{40,32},{48,40},{56,48},{64,88... | collective-permute-start | bytes 405512 | tf_op jit(solution)/shard_map/ppermute | solution.py:39
  66.1 10.0 %collective-permute-start.16 = (bf16[528,128]{1,0:T(8,128)(2,1)S(1)}, bf16[528,128]{1,0:T(8,128)(2,1)S(1)}, u32[]{:S(2)}, u32[]{:S(2)}) collective-permute-start(bf16[528,128]{1,0:T(8,128)(2,1)S(1)} %get-tuple-element.75), channel_id=1, source_target_pairs={{0,32},{8,40},{16,48},{24,56},{32,64},{40,72},{48,80},{56,88},{64,... | collective-permute-start | bytes 405512 | tf_op jit(solution)/shard_map/ppermute | solution.py:43
  69.6 7.1 %collective-permute-start.17 = (bf16[528,128]{1,0:T(8,128)(2,1)S(1)}, bf16[528,128]{1,0:T(8,128)(2,1)S(1)}, u32[]{:S(2)}, u32[]{:S(2)}) collective-permute-start(bf16[528,128]{1,0:T(8,128)(2,1)S(1)} %get-tuple-element.75), channel_id=1, source_target_pairs={{0,64},{8,72},{16,80},{24,88},{32,96},{40,104},{48,112},{56,120},{... | collective-permute-start | bytes 405512 | tf_op jit(solution)/shard_map/ppermute | solution.py:43
  74.7 3.7 %collective-permute-start.18 = (bf16[528,128]{1,0:T(8,128)(2,1)S(1)}, bf16[528,128]{1,0:T(8,128)(2,1)S(1)}, u32[]{:S(2)}, u32[]{:S(2)}) collective-permute-start(bf16[528,128]{1,0:T(8,128)(2,1)S(1)} %get-tuple-element.75), channel_id=1, source_target_pairs={{0,96},{8,104},{16,112},{24,120},{1,97},{9,105},{17,113},{25,121},... | collective-permute-start | bytes 405512 | tf_op jit(solution)/shard_map/ppermute | solution.py:43
  83.0 4.5 %collective-permute-start.19 = (bf16[64,6144]{1,0:T(8,128)(2,1)S(1)}, bf16[64,6144]{1,0:T(8,128)(2,1)S(1)}, u32[]{:S(2)}, u32[]{:S(2)}) collective-permute-start(bf16[64,6144]{1,0:T(8,128)(2,1)S(1)} %get-tuple-element.82), channel_id=1, source_target_pairs={{0,1},{1,0},{2,3},{3,2},{4,5},{5,4},{6,7},{7,6},{8,9},{9,8},{10,11... | collective-permute-start | bytes 2359304 | tf_op jit(solution)/shard_map/ppermute | solution.py:35
  87.7 4.0 %collective-permute-start.20 = (bf16[64,6144]{1,0:T(8,128)(2,1)S(1)}, bf16[64,6144]{1,0:T(8,128)(2,1)S(1)}, u32[]{:S(2)}, u32[]{:S(2)}) collective-permute-start(bf16[64,6144]{1,0:T(8,128)(2,1)S(1)} %get-tuple-element.85), channel_id=1, source_target_pairs={{0,1},{1,0},{2,3},{3,2},{4,5},{5,4},{6,7},{7,6},{8,9},{9,8},{10,11... | collective-permute-start | bytes 2359304 | tf_op jit(solution)/shard_map/ppermute | solution.py:35
  87.8 4.1 %collective-permute-start.21 = (bf16[64,6144]{1,0:T(8,128)(2,1)S(1)}, bf16[64,6144]{1,0:T(8,128)(2,1)S(1)}, u32[]{:S(2)}, u32[]{:S(2)}) collective-permute-start(bf16[64,6144]{1,0:T(8,128)(2,1)S(1)} %get-tuple-element.87), channel_id=1, source_target_pairs={{0,1},{1,0},{2,3},{3,2},{4,5},{5,4},{6,7},{7,6},{8,9},{9,8},{10,11... | collective-permute-start | bytes 2359304 | tf_op jit(solution)/shard_map/ppermute | solution.py:35
  88.3 12.8 %collective-permute-start.25 = (bf16[64,3072]{1,0:T(8,128)(2,1)S(1)}, bf16[64,3072]{1,0:T(8,128)(2,1)S(1)}, u32[]{:S(2)}, u32[]{:S(2)}) collective-permute-start(bf16[64,3072]{1,0:T(8,128)(2,1)S(1)} %get-tuple-element.96), channel_id=1, source_target_pairs={{0,2},{1,3},{2,4},{3,5},{4,6},{5,7},{6,0},{7,1},{8,10},{9,11},{10,... | collective-permute-start | bytes 1179656 | tf_op jit(solution)/shard_map/ppermute | solution.py:31
  89.1 12.1 %collective-permute-start.26 = (bf16[64,3072]{1,0:T(8,128)(2,1)S(1)}, bf16[64,3072]{1,0:T(8,128)(2,1)S(1)}, u32[]{:S(2)}, u32[]{:S(2)}) collective-permute-start(bf16[64,3072]{1,0:T(8,128)(2,1)S(1)} %get-tuple-element.95), channel_id=1, source_target_pairs={{0,6},{1,7},{2,0},{3,1},{4,2},{5,3},{6,4},{7,5},{8,14},{9,15},{10,... | collective-permute-start | bytes 1179656 | tf_op jit(solution)/shard_map/ppermute | solution.py:31
  91.9 17.7 %collective-permute-start.23 = (bf16[64,3072]{1,0:T(8,128)(2,1)S(1)}, bf16[64,3072]{1,0:T(8,128)(2,1)S(1)}, u32[]{:S(2)}, u32[]{:S(2)}) collective-permute-start(bf16[64,3072]{1,0:T(8,128)(2,1)S(1)} %add_convert_fusion.3), channel_id=1, source_target_pairs={{0,2},{1,3},{2,4},{3,5},{4,6},{5,7},{6,0},{7,1},{8,10},{9,11},{10,... | collective-permute-start | bytes 1179656 | tf_op jit(solution)/shard_map/ppermute | solution.py:31
  92.1 17.5 %collective-permute-start.24 = (bf16[64,3072]{1,0:T(8,128)(2,1)S(1)}, bf16[64,3072]{1,0:T(8,128)(2,1)S(1)}, u32[]{:S(2)}, u32[]{:S(2)}) collective-permute-start(bf16[64,3072]{1,0:T(8,128)(2,1)S(1)} %add_convert_fusion.2), channel_id=1, source_target_pairs={{0,6},{1,7},{2,0},{3,1},{4,2},{5,3},{6,4},{7,5},{8,14},{9,15},{10,... | collective-permute-start | bytes 1179656 | tf_op jit(solution)/shard_map/ppermute | solution.py:31
  96.1 13.5 %collective-permute-start.22 = (bf16[64,6144]{1,0:T(8,128)(2,1)S(1)}, bf16[64,6144]{1,0:T(8,128)(2,1)S(1)}, u32[]{:S(2)}, u32[]{:S(2)}) collective-permute-start(bf16[64,6144]{1,0:T(8,128)(2,1)S(1)} %get-tuple-element.90), channel_id=1, source_target_pairs={{0,1},{1,0},{2,3},{3,2},{4,5},{5,4},{6,7},{7,6},{8,9},{9,8},{10,11... | collective-permute-start | bytes 2359304 | tf_op jit(solution)/shard_map/ppermute | solution.py:35
  101.3 16.7 %collective-permute-start.27 = (bf16[64,3072]{1,0:T(8,128)(2,1)S(1)}, bf16[64,3072]{1,0:T(8,128)(2,1)S(1)}, u32[]{:S(2)}, u32[]{:S(2)}) collective-permute-start(bf16[64,3072]{1,0:T(8,128)(2,1)S(1)} %add_convert_fusion.1), channel_id=1, source_target_pairs={{0,2},{1,3},{2,4},{3,5},{4,6},{5,7},{6,0},{7,1},{8,10},{9,11},{10,... | collective-permute-start | bytes 1179656 | tf_op jit(solution)/shard_map/ppermute | solution.py:31
  102.2 15.8 %collective-permute-start.28 = (bf16[64,3072]{1,0:T(8,128)(2,1)S(1)}, bf16[64,3072]{1,0:T(8,128)(2,1)S(1)}, u32[]{:S(2)}, u32[]{:S(2)}) collective-permute-start(bf16[64,3072]{1,0:T(8,128)(2,1)S(1)} %add_convert_fusion), channel_id=1, source_target_pairs={{0,6},{1,7},{2,0},{3,1},{4,2},{5,3},{6,4},{7,5},{8,14},{9,15},{10,... | collective-permute-start | bytes 1179656 | tf_op jit(solution)/shard_map/ppermute | solution.py:31
Sparse Core Ops, SparseCore 0:
  9.5 70.1 all-gather.2

commit v8 on v7

--- a/solution.py
+++ b/solution.py
@@ -144,7 +144,7 @@
         out[:, h * SIZE : (h + 1) * SIZE] = jnp.dot(probs, values, preferred_element_type=f32)
 
 
-def row_kernel(at, s0, s1, s2, s3, before, total):
+def row_kernel(at, s0, s2, s1, s3, before, total):
     refs = (s0, s1, s2, s3)
     x = at[0]
     place = [(x - k) & 3 for k in range(N_X)]
@@ -165,7 +165,7 @@
     before[WIDE:, :] = jnp.concatenate([lead, lead], axis=0)
 
 
-def normed_kernel(before, t1, t2, t3, a, b, c, d, g, inner, gain, out):
+def normed_kernel(before, t2, t1, t3, a, b, c, d, g, inner, gain, out):
     lead = jnp.exp(before[WIDE : WIDE + HEADS, :])
     r1, r2 = unpack(t1), unpack(t2)
     reach2, reach3 = jnp.exp(r1), jnp.exp(r1 + r2)
@@ -205,17 +205,14 @@
 
 
 def project_first_kernel(normed, w, own, sib, held, sems):
-    per = w.shape[0] // 4
-    copies = [
-        pltpu.make_async_copy(w.at[pl.ds(i * per, per)], held.at[pl.ds(i * per, per)], sems.at[i]) for i in range(4)
-    ]
+    n = w.shape[0]
+    copies = [pltpu.make_async_copy(w.at[m], held.at[m], sems.at[m]) for m in range(n)]
     for copy in copies:
         copy.start()
     far = normed[FAR : FAR + 128, :]
-    for i in range(4):
-        copies[i].wait()
-        for m in range(i * per, (i + 1) * per):
-            project_part(far, held, (own, sib), m)
+    for m in range(n):
+        copies[m].wait()
+        project_part(far, held, (own, sib), m)
 
 
 def project_kernel(blocks, normed, w, *outs):
@@ -306,7 +303,7 @@
 
     packed = jax.ShapeDtypeStruct((WIDE + 16, SIZE), bf16)
     state = whole_call(state_kernel, (*rows, g, last), packed, "state", 2 * 512 * WIDE * SIZE)
-    row = [state] + [to_x(state, k) for k in range(1, N_X)]
+    row = [state] + [to_x(state, k) for k in (2, 1, 3)]
     inner = whole_call(
         inner_kernel,
         (*rows, g, gt, pos.reshape(512, 1), pos.reshape(1, 512)),
@@ -318,7 +315,7 @@
     before, total = whole_call(
         row_kernel, (at, *row), (jax.ShapeDtypeStruct((WIDE + 8, SIZE), f32), packed), "row", 10 * WIDE * SIZE, 1
     )
-    totals = [to_z(total, k) for k in range(1, N_Z)]
+    totals = [to_z(total, k) for k in (2, 1, 3)]
     normed = whole_call(
         normed_kernel,
         (before, *totals, *rows, g, inner, gain.reshape(1, WIDE)),
@@ -333,7 +330,7 @@
         out_shape=[half, half, pltpu.VMEM(w_all.shape, bf16)],
         in_specs=[vmem, pl.BlockSpec(memory_space=pltpu.HBM)],
         out_specs=[vmem] * 3,
-        scratch_shapes=[pltpu.SemaphoreType.DMA((4,))],
+        scratch_shapes=[pltpu.SemaphoreType.DMA((w_all.shape[0],))],
         compiler_params=params(),
         cost_estimate=cost(256 * w_all.size, 2 * w_all.size),
         name="project",

time: 126 us -> 127 us (level)
  Pallas kernels: 27 us -> 28.5 us
  starting transfers between devices: 41 us -> 39.7 us
    pallas_call x1, Pallas kernels: 3.31 us -> 4.85 us  [body(): pl.pallas_call(project_first_kernel, out_shape=[half, half, pltpu.VMEM(w_...]
    all_gather x1, waiting for transfers between devices: 0.22 us -> 1.55 us  [body(): w_all = lax.all_gather(w_out, 'ctx', axis=0)]
  transfers between devices with their start and end apart: 30 -> 30, of which waited for: 11 -> 12; matrix products, arithmetic and copies ran while one was open for 5% -> 5% of each run, Pallas kernels for 18% -> 18%
where the time goes in v8:
time: 127 us; the launch traced here: 126 us
  starting transfers between devices  39.7 us (31%)
  waiting for transfers between devices  36.5 us (29%)
  Pallas kernels  28.5 us (22%)
  between operations  13.7 us (11%)
  local copies, waits for them, and re-layouts  4.77 us (4%)
  other arithmetic  2.94 us (2%)
    ppermute x12, waiting for transfers between devices, to_y(): lax.ppermute(a, 'tp', [(i, (i // 2 + k) % N_Y * 2 + i % 2) for i in range...  23.4 us
    ppermute x12, starting transfers between devices, to_y(): lax.ppermute(a, 'tp', [(i, (i // 2 + k) % N_Y * 2 + i % 2) for i in range...  16.5 us
    pallas_call x4, Pallas kernels, qkv(): pl.pallas_call(functools.partial(qkv_first_kernel if first else qkv_kerne...  15.1 us
    ppermute x3, starting transfers between devices, to_z(): lax.ppermute(a, 'ctx', [(j, j + N_X * k) for j in range(N_X * N_Z) if j /...  9.34 us
    ppermute x3, waiting for transfers between devices, to_x(): lax.ppermute(a, 'ctx', [(j, j // N_X * N_X + (j + k) % N_X) for j in rang...  8.62 us
    ppermute x11, starting transfers between devices, to_sibling(): return lax.ppermute(a, 'tp', [(i, i ^ 1) for i in range(2 * N_Y)])  8.37 us
    ppermute x3, starting transfers between devices, to_x(): lax.ppermute(a, 'ctx', [(j, j // N_X * N_X + (j + k) % N_X) for j in rang...  5.53 us
    pallas_call x6, Pallas kernels, whole_call(): pl.pallas_call(kernel, out_shape=outs, in_specs=[pl.BlockSpec(memory_spac...  4.96 us
  transfers between devices with their start and end apart: 30, of which 12 were waited for; matrix products, arithmetic and copies ran while one was open for 5% of the time, Pallas kernels for 18%

profile of v8, /device:TPU:1, one launch (start us, length us, event | category | flops | bytes accessed | tf_op | source)
XLA Modules:
  0.0 126.2 jit_solution(11185547334426314230)
XLA Ops:
  6.5 0.7 all-gather.3.cloned.1.call-update
  7.3 1.5 %collective-permute-start.3 = (bf16[64,6144]{1,0:T(8,128)(2,1)}, bf16[64,6144]{1,0:T(8,128)(2,1)S(1)}, u32[]{:S(2)}, u32[]{:S(2)}) collective-permute-start(bf16[64,6144]{1,0:T(8,128)(2,1)} %refs_0_.1), channel_id=1, source_target_pairs={{0,1},{1,0},{2,3},{3,2},{4,5},{5,4},{6,7},{7,6},{8,9},{9,8},{10,11... | collective-permute-start | bytes 2359304 | tf_op jit(solution)/shard_map/ppermute | solution.py:35
  8.8 1.0 slice.75
  9.8 1.4 %collective-permute-start.1 = (bf16[64,3072]{1,0:T(8,128)(2,1)S(1)}, bf16[64,3072]{1,0:T(8,128)(2,1)S(1)}, u32[]{:S(2)}, u32[]{:S(2)}) collective-permute-start(bf16[64,3072]{1,0:T(8,128)(2,1)S(1)} %slice.75), channel_id=1, source_target_pairs={{0,2},{1,3},{2,4},{3,5},{4,6},{5,7},{6,0},{7,1},{8,10},{9,11},{10,... | collective-permute-start | bytes 1179656 | tf_op jit(solution)/shard_map/ppermute | solution.py:31
  11.2 1.0 slice.76
  12.3 1.5 %collective-permute-start.2 = (bf16[64,3072]{1,0:T(8,128)(2,1)S(1)}, bf16[64,3072]{1,0:T(8,128)(2,1)S(1)}, u32[]{:S(2)}, u32[]{:S(2)}) collective-permute-start(bf16[64,3072]{1,0:T(8,128)(2,1)S(1)} %slice.76), channel_id=1, source_target_pairs={{0,6},{1,7},{2,0},{3,1},{4,2},{5,3},{6,4},{7,5},{8,14},{9,15},{10,... | collective-permute-start | bytes 1179656 | tf_op jit(solution)/shard_map/ppermute | solution.py:31
  14.5 1.2 reduce-window.6
  17.6 1.5 %collective-permute-start = (bf16[64,3072]{1,0:T(8,128)(2,1)S(1)}, bf16[64,3072]{1,0:T(8,128)(2,1)S(1)}, u32[]{:S(2)}, u32[]{:S(2)}) collective-permute-start(bf16[64,3072]{1,0:T(8,128)(2,1)S(1)} %slice.75), channel_id=1, source_target_pairs={{0,6},{1,7},{2,0},{3,1},{4,2},{5,3},{6,4},{7,5},{8,14},{9,15},{10,... | collective-permute-start | bytes 1179656 | tf_op jit(solution)/shard_map/ppermute | solution.py:31
  19.0 1.1 copy-done
  20.2 7.3 %qkv.4 = (bf16[128,1536]{1,0:T(8,128)(2,1)S(1)}, bf16[3,6144,512]{2,1,0:T(8,128)(2,1)S(1)}) custom-call(bf16[64,6144]{1,0:T(8,128)(2,1)S(1)} %copy-done, bf16[64,6144]{1,0:T(8,128)(2,1)S(1)} %collective-permute-done.3.refs_1_, bf16[3,6144,512]{2,1,0:T(8,128)(2,1)} %refs_2_.1), custom_call_target="tpu_custom_call" | custom-call | flops 24159192 | bytes 188743 | tf_op jit(solution)/shard_map/qkv/pallas_call | solution.py:97
  27.5 1.1 collective-permute-start.5
  28.8 2.3 %collective-permute-done.refs_0_ = bf16[64,3072]{1,0:T(8,128)(2,1)S(1)} collective-permute-done((bf16[64,3072]{1,0:T(8,128)(2,1)S(1)}, bf16[64,3072]{1,0:T(8,128)(2,1)S(1)}, u32[]{:S(2)}, u32[]{:S(2)}) %collective-permute-start) | collective-permute-done | bytes 393248 | tf_op jit(solution)/shard_map/ppermute | solution.py:31
  31.2 2.8 %collective-permute-start.10 = (bf16[64,3072]{1,0:T(8,128)(2,1)S(1)}, bf16[64,3072]{1,0:T(8,128)(2,1)S(1)}, u32[]{:S(2)}, u32[]{:S(2)}) collective-permute-start(bf16[64,3072]{1,0:T(8,128)(2,1)S(1)} %collective-permute-done.2.refs_1_), channel_id=1, source_target_pairs={{0,6},{1,7},{2,0},{3,1},{4,2},{5,3},{6,4},{7,5},{8,14},{9,15},{10,... | collective-permute-start | bytes 1179656 | tf_op jit(solution)/shard_map/ppermute | solution.py:31
  34.0 1.2 collective-permute-start.7
  35.3 2.6 %qkv.5.a = bf16[128,1536]{1,0:T(8,128)(2,1)S(1)} custom-call(bf16[64,3072]{1,0:T(8,128)(2,1)S(1)} %collective-permute-done.refs_0_, bf16[64,3072]{1,0:T(8,128)(2,1)S(1)} %collective-permute-done.2.refs_1_, bf16[64,3072]{1,0:T(8,128)(2,1)S(1)} %collective-permute-done.1.refs_2_, bf16[64,3072]{1,0:T(8,128)(2,1)S(1)} %collective-permute-done.4.refs_3_, ...), custom_call_target="tpu_custom_call" | custom-call | flops 24159192 | bytes 188743 | tf_op jit(solution)/shard_map/qkv/pallas_call | solution.py:97
  37.9 2.5 %collective-permute-done.9.refs_0_ = bf16[64,3072]{1,0:T(8,128)(2,1)S(1)} collective-permute-done((bf16[64,3072]{1,0:T(8,128)(2,1)S(1)}, bf16[64,3072]{1,0:T(8,128)(2,1)S(1)}, u32[]{:S(2)}, u32[]{:S(2)}) %collective-permute-start.9) | collective-permute-done | bytes 393248 | tf_op jit(solution)/shard_map/ppermute | solution.py:31
  40.4 1.0 collective-permute-done.10.refs_1_
  41.5 1.9 %collective-permute-start.11 = (bf16[64,3072]{1,0:T(8,128)(2,1)S(1)}, bf16[64,3072]{1,0:T(8,128)(2,1)S(1)}, u32[]{:S(2)}, u32[]{:S(2)}) collective-permute-start(bf16[64,3072]{1,0:T(8,128)(2,1)S(1)} %collective-permute-done.9.refs_0_), channel_id=1, source_target_pairs={{0,1},{1,0},{2,3},{3,2},{4,5},{5,4},{6,7},{7,6},{8,9},{9,8},{10,11... | collective-permute-start | bytes 1179656 | tf_op jit(solution)/shard_map/ppermute | solution.py:35
  43.3 2.6 %qkv.6.c = bf16[128,1536]{1,0:T(8,128)(2,1)S(1)} custom-call(bf16[64,3072]{1,0:T(8,128)(2,1)S(1)} %collective-permute-done.7.refs_0_, bf16[64,3072]{1,0:T(8,128)(2,1)S(1)} %collective-permute-done.6.refs_1_, bf16[64,3072]{1,0:T(8,128)(2,1)S(1)} %collective-permute-done.5.refs_2_, bf16[64,3072]{1,0:T(8,128)(2,1)S(1)} %collective-permute-done.8.refs_3_, ...), custom_call_target="tpu_custom_call" | custom-call | flops 24159192 | bytes 188743 | tf_op jit(solution)/shard_map/qkv/pallas_call | solution.py:97
  46.0 2.6 %qkv.7.d = bf16[128,1536]{1,0:T(8,128)(2,1)S(1)} custom-call(bf16[64,3072]{1,0:T(8,128)(2,1)S(1)} %collective-permute-done.9.refs_0_, bf16[64,3072]{1,0:T(8,128)(2,1)S(1)} %collective-permute-done.10.refs_1_, bf16[64,3072]{1,0:T(8,128)(2,1)S(1)} %collective-permute-done.11.refs_2_, bf16[64,3072]{1,0:T(8,128)(2,1)S(1)} %collective-permute-done.12.refs_3_, ...), custom_call_target="tpu_custom_call" | custom-call | flops 24159192 | bytes 188743 | tf_op jit(solution)/shard_map/qkv/pallas_call | solution.py:97
  48.6 1.0 state.1.s0
  49.6 2.9 %collective-permute-start.13 = (bf16[528,128]{1,0:T(8,128)(2,1)S(1)}, bf16[528,128]{1,0:T(8,128)(2,1)S(1)}, u32[]{:S(2)}, u32[]{:S(2)}) collective-permute-start(bf16[528,128]{1,0:T(8,128)(2,1)S(1)} %state.1.s0), channel_id=1, source_target_pairs={{0,16},{8,24},{16,0},{24,8},{32,48},{40,56},{48,32},{56,40},{64,80... | collective-permute-start | bytes 405512 | tf_op jit(solution)/shard_map/ppermute | solution.py:39
  52.8 2.4 %collective-permute-start.15 = (bf16[528,128]{1,0:T(8,128)(2,1)S(1)}, bf16[528,128]{1,0:T(8,128)(2,1)S(1)}, u32[]{:S(2)}, u32[]{:S(2)}) collective-permute-start(bf16[528,128]{1,0:T(8,128)(2,1)S(1)} %state.1.s0), channel_id=1, source_target_pairs={{0,24},{8,0},{16,8},{24,16},{32,56},{40,32},{48,40},{56,48},{64,88... | collective-permute-start | bytes 405512 | tf_op jit(solution)/shard_map/ppermute | solution.py:39
  55.3 1.4 %inner.1 = f32[512,512]{1,0:T(8,128)S(1)} custom-call(bf16[128,1536]{1,0:T(8,128)(2,1)S(1)} %qkv.5.a, bf16[128,1536]{1,0:T(8,128)(2,1)S(1)} %get-tuple-element.53.b, bf16[128,1536]{1,0:T(8,128)(2,1)S(1)} %qkv.6.c, bf16[128,1536]{1,0:T(8,128)(2,1)S(1)} %qkv.7.d, f32[512,4]{1,0:T(8,128)S(1)} %bitcast.20, f32[4,512]{1,0:T(4,128)S(1)} %concatenate.8.gt, ...), custom_call_target="tpu_custom_call" | custom-call | flops 5368709 | bytes 15933 | tf_op jit(solution)/shard_map/inner/pallas_call | solution.py:188
  56.8 2.6 %collective-permute-done.13.s2 = bf16[528,128]{1,0:T(8,128)(2,1)S(1)} collective-permute-done((bf16[528,128]{1,0:T(8,128)(2,1)S(1)}, bf16[528,128]{1,0:T(8,128)(2,1)S(1)}, u32[]{:S(2)}, u32[]{:S(2)}) %collective-permute-start.13) | collective-permute-done | bytes 135200 | tf_op jit(solution)/shard_map/ppermute | solution.py:39
  59.4 4.9 %collective-permute-done.14.s1 = bf16[528,128]{1,0:T(8,128)(2,1)S(1)} collective-permute-done((bf16[528,128]{1,0:T(8,128)(2,1)S(1)}, bf16[528,128]{1,0:T(8,128)(2,1)S(1)}, u32[]{:S(2)}, u32[]{:S(2)}) %collective-permute-start.14) | collective-permute-done | bytes 135200 | tf_op jit(solution)/shard_map/ppermute | solution.py:39
  64.2 1.2 collective-permute-done.15.s3
  65.6 5.4 %collective-permute-start.16 = (bf16[528,128]{1,0:T(8,128)(2,1)S(1)}, bf16[528,128]{1,0:T(8,128)(2,1)S(1)}, u32[]{:S(2)}, u32[]{:S(2)}) collective-permute-start(bf16[528,128]{1,0:T(8,128)(2,1)S(1)} %get-tuple-element.75), channel_id=1, source_target_pairs={{0,64},{8,72},{16,80},{24,88},{32,96},{40,104},{48,112},{56,120},{... | collective-permute-start | bytes 405512 | tf_op jit(solution)/shard_map/ppermute | solution.py:43
  71.0 2.6 %collective-permute-start.17 = (bf16[528,128]{1,0:T(8,128)(2,1)S(1)}, bf16[528,128]{1,0:T(8,128)(2,1)S(1)}, u32[]{:S(2)}, u32[]{:S(2)}) collective-permute-start(bf16[528,128]{1,0:T(8,128)(2,1)S(1)} %get-tuple-element.75), channel_id=1, source_target_pairs={{0,32},{8,40},{16,48},{24,56},{32,64},{40,72},{48,80},{56,88},{64,... | collective-permute-start | bytes 405512 | tf_op jit(solution)/shard_map/ppermute | solution.py:43
  73.6 1.3 %collective-permute-start.18 = (bf16[528,128]{1,0:T(8,128)(2,1)S(1)}, bf16[528,128]{1,0:T(8,128)(2,1)S(1)}, u32[]{:S(2)}, u32[]{:S(2)}) collective-permute-start(bf16[528,128]{1,0:T(8,128)(2,1)S(1)} %get-tuple-element.75), channel_id=1, source_target_pairs={{0,96},{8,104},{16,112},{24,120},{1,97},{9,105},{17,113},{25,121},... | collective-permute-start | bytes 405512 | tf_op jit(solution)/shard_map/ppermute | solution.py:43
  74.9 1.1 collective-permute-done.17.t1
  76.1 1.0 collective-permute-done.18.t3
  77.1 1.0 normed.1
  78.1 1.5 %all-gather.3.cloned.1.call-done = bf16[8192,384]{1,0:T(8,128)(2,1)} async-done(((bf16[512,384]{1,0:T(8,128)(2,1)}), bf16[8192,384]{1,0:T(8,128)(2,1)}) %all-gather.3.cloned.1.call-update) | async-done | bytes 6291472 | tf_op jit(solution)/shard_map/all_gather | solution.py:268
  79.7 4.8 %project.3 = (bf16[64,6144]{1,0:T(8,128)(2,1)S(1)}, bf16[64,6144]{1,0:T(8,128)(2,1)S(1)}, bf16[16,512,384]{2,1,0:T(8,128)(2,1)S(1)}) custom-call(bf16[512,512]{1,0:T(8,128)(2,1)S(1)} %normed.1, bf16[16,512,384]{2,1,0:T(8,128)(2,1)} %bitcast.25), custom_call_target="tpu_custom_call" | custom-call | flops 8053063 | bytes 62914 | tf_op jit(solution)/shard_map/project/pallas_call | solution.py:328
  84.5 1.0 collective-permute-start.19
  85.5 2.3 %project.4 = (bf16[64,6144]{1,0:T(8,128)(2,1)S(1)}, bf16[64,6144]{1,0:T(8,128)(2,1)S(1)}, bf16[64,6144]{1,0:T(8,128)(2,1)S(1)}, bf16[64,6144]{1,0:T(8,128)(2,1)S(1)}) custom-call(bf16[512,512]{1,0:T(8,128)(2,1)S(1)} %normed.1, bf16[16,512,384]{2,1,0:T(8,128)(2,1)S(1)} %get-tuple-element.76.w), custom_call_target="tpu_custom_call" | custom-call | flops 16106127 | bytes 62914 | tf_op jit(solution)/shard_map/project/pallas_call | solution.py:228
  88.6 1.2 collective-permute-start.25
  89.9 2.2 %collective-permute-start.26 = (bf16[64,3072]{1,0:T(8,128)(2,1)S(1)}, bf16[64,3072]{1,0:T(8,128)(2,1)S(1)}, u32[]{:S(2)}, u32[]{:S(2)}) collective-permute-start(bf16[64,3072]{1,0:T(8,128)(2,1)S(1)} %get-tuple-element.95), channel_id=1, source_target_pairs={{0,6},{1,7},{2,0},{3,1},{4,2},{5,3},{6,4},{7,5},{8,14},{9,15},{10,... | collective-permute-start | bytes 1179656 | tf_op jit(solution)/shard_map/ppermute | solution.py:31
  92.4 2.8 %collective-permute-start.24 = (bf16[64,3072]{1,0:T(8,128)(2,1)S(1)}, bf16[64,3072]{1,0:T(8,128)(2,1)S(1)}, u32[]{:S(2)}, u32[]{:S(2)}) collective-permute-start(bf16[64,3072]{1,0:T(8,128)(2,1)S(1)} %add_convert_fusion.2), channel_id=1, source_target_pairs={{0,6},{1,7},{2,0},{3,1},{4,2},{5,3},{6,4},{7,5},{8,14},{9,15},{10,... | collective-permute-start | bytes 1179656 | tf_op jit(solution)/shard_map/ppermute | solution.py:31
  95.1 1.2 project.5
  96.4 1.0 collective-permute-start.22
  97.3 4.1 %collective-permute-done.25 = bf16[64,3072]{1,0:T(8,128)(2,1)S(1)} collective-permute-done((bf16[64,3072]{1,0:T(8,128)(2,1)S(1)}, bf16[64,3072]{1,0:T(8,128)(2,1)S(1)}, u32[]{:S(2)}, u32[]{:S(2)}) %collective-permute-start.25) | collective-permute-done | bytes 393248 | tf_op jit(solution)/shard_map/ppermute | solution.py:31
  101.6 0.7 collective-permute-start.27
  102.5 2.1 %collective-permute-start.28 = (bf16[64,3072]{1,0:T(8,128)(2,1)S(1)}, bf16[64,3072]{1,0:T(8,128)(2,1)S(1)}, u32[]{:S(2)}, u32[]{:S(2)}) collective-permute-start(bf16[64,3072]{1,0:T(8,128)(2,1)S(1)} %add_convert_fusion), channel_id=1, source_target_pairs={{0,6},{1,7},{2,0},{3,1},{4,2},{5,3},{6,4},{7,5},{8,14},{9,15},{10,... | collective-permute-start | bytes 1179656 | tf_op jit(solution)/shard_map/ppermute | solution.py:31
  104.6 5.3 %collective-permute-done.23.up_plain = bf16[64,3072]{1,0:T(8,128)(2,1)S(1)} collective-permute-done((bf16[64,3072]{1,0:T(8,128)(2,1)S(1)}, bf16[64,3072]{1,0:T(8,128)(2,1)S(1)}, u32[]{:S(2)}, u32[]{:S(2)}) %collective-permute-start.23) | collective-permute-done | bytes 393248 | tf_op jit(solution)/shard_map/ppermute | solution.py:31
  110.2 8.2 %collective-permute-done.27.up_sum = bf16[64,3072]{1,0:T(8,128)(2,1)S(1)} collective-permute-done((bf16[64,3072]{1,0:T(8,128)(2,1)S(1)}, bf16[64,3072]{1,0:T(8,128)(2,1)S(1)}, u32[]{:S(2)}, u32[]{:S(2)}) %collective-permute-start.27) | collective-permute-done | bytes 393248 | tf_op jit(solution)/shard_map/ppermute | solution.py:31
  118.3 1.0 final.1
  (54 shorter events, 5.2 us)
Async XLA Ops:
  6.5 73.2 %all-gather.3.cloned.1.call-start = ((), (), s32[]{:S(2)}) async-start(), calls=%async_computation | async-start | bytes 6684672 | tf_op jit(solution)/shard_map/all_gather | solution.py:268
  7.3 11.8 %collective-permute-start.3 = (bf16[64,6144]{1,0:T(8,128)(2,1)}, bf16[64,6144]{1,0:T(8,128)(2,1)S(1)}, u32[]{:S(2)}, u32[]{:S(2)}) collective-permute-start(bf16[64,6144]{1,0:T(8,128)(2,1)} %refs_0_.1), channel_id=1, source_target_pairs={{0,1},{1,0},{2,3},{3,2},{4,5},{5,4},{6,7},{7,6},{8,9},{9,8},{10,11... | collective-permute-start | bytes 2359304 | tf_op jit(solution)/shard_map/ppermute | solution.py:35
  9.8 17.7 %collective-permute-start.1 = (bf16[64,3072]{1,0:T(8,128)(2,1)S(1)}, bf16[64,3072]{1,0:T(8,128)(2,1)S(1)}, u32[]{:S(2)}, u32[]{:S(2)}) collective-permute-start(bf16[64,3072]{1,0:T(8,128)(2,1)S(1)} %slice.75), channel_id=1, source_target_pairs={{0,2},{1,3},{2,4},{3,5},{4,6},{5,7},{6,0},{7,1},{8,10},{9,11},{10,... | collective-permute-start | bytes 1179656 | tf_op jit(solution)/shard_map/ppermute | solution.py:31
  12.3 15.3 %collective-permute-start.2 = (bf16[64,3072]{1,0:T(8,128)(2,1)S(1)}, bf16[64,3072]{1,0:T(8,128)(2,1)S(1)}, u32[]{:S(2)}, u32[]{:S(2)}) collective-permute-start(bf16[64,3072]{1,0:T(8,128)(2,1)S(1)} %slice.76), channel_id=1, source_target_pairs={{0,6},{1,7},{2,0},{3,1},{4,2},{5,3},{6,4},{7,5},{8,14},{9,15},{10,... | collective-permute-start | bytes 1179656 | tf_op jit(solution)/shard_map/ppermute | solution.py:31
  17.6 13.6 %collective-permute-start = (bf16[64,3072]{1,0:T(8,128)(2,1)S(1)}, bf16[64,3072]{1,0:T(8,128)(2,1)S(1)}, u32[]{:S(2)}, u32[]{:S(2)}) collective-permute-start(bf16[64,3072]{1,0:T(8,128)(2,1)S(1)} %slice.75), channel_id=1, source_target_pairs={{0,6},{1,7},{2,0},{3,1},{4,2},{5,3},{6,4},{7,5},{8,14},{9,15},{10,... | collective-permute-start | bytes 1179656 | tf_op jit(solution)/shard_map/ppermute | solution.py:31
  19.0 15.0 %collective-permute-start.4 = (bf16[64,3072]{1,0:T(8,128)(2,1)S(1)}, bf16[64,3072]{1,0:T(8,128)(2,1)S(1)}, u32[]{:S(2)}, u32[]{:S(2)}) collective-permute-start(bf16[64,3072]{1,0:T(8,128)(2,1)S(1)} %slice.76), channel_id=1, source_target_pairs={{0,2},{1,3},{2,4},{3,5},{4,6},{5,7},{6,0},{7,1},{8,10},{9,11},{10,... | collective-permute-start | bytes 1179656 | tf_op jit(solution)/shard_map/ppermute | solution.py:31
  19.0 1.1 copy-start
  27.5 7.7 %collective-permute-start.5 = (bf16[64,3072]{1,0:T(8,128)(2,1)S(1)}, bf16[64,3072]{1,0:T(8,128)(2,1)S(1)}, u32[]{:S(2)}, u32[]{:S(2)}) collective-permute-start(bf16[64,3072]{1,0:T(8,128)(2,1)S(1)} %collective-permute-done.1.refs_2_), channel_id=1, source_target_pairs={{0,1},{1,0},{2,3},{3,2},{4,5},{5,4},{6,7},{7,6},{8,9},{9,8},{10,11... | collective-permute-start | bytes 1179656 | tf_op jit(solution)/shard_map/ppermute | solution.py:35
  28.6 6.7 %collective-permute-start.6 = (bf16[64,3072]{1,0:T(8,128)(2,1)S(1)}, bf16[64,3072]{1,0:T(8,128)(2,1)S(1)}, u32[]{:S(2)}, u32[]{:S(2)}) collective-permute-start(bf16[64,3072]{1,0:T(8,128)(2,1)S(1)} %collective-permute-done.2.refs_1_), channel_id=1, source_target_pairs={{0,1},{1,0},{2,3},{3,2},{4,5},{5,4},{6,7},{7,6},{8,9},{9,8},{10,11... | collective-permute-start | bytes 1179656 | tf_op jit(solution)/shard_map/ppermute | solution.py:35
  28.7 11.8 %collective-permute-start.9 = (bf16[64,3072]{1,0:T(8,128)(2,1)S(1)}, bf16[64,3072]{1,0:T(8,128)(2,1)S(1)}, u32[]{:S(2)}, u32[]{:S(2)}) collective-permute-start(bf16[64,3072]{1,0:T(8,128)(2,1)S(1)} %collective-permute-done.1.refs_2_), channel_id=1, source_target_pairs={{0,2},{1,3},{2,4},{3,5},{4,6},{5,7},{6,0},{7,1},{8,10},{9,11},{10,... | collective-permute-start | bytes 1179656 | tf_op jit(solution)/shard_map/ppermute | solution.py:31
  31.2 10.3 %collective-permute-start.10 = (bf16[64,3072]{1,0:T(8,128)(2,1)S(1)}, bf16[64,3072]{1,0:T(8,128)(2,1)S(1)}, u32[]{:S(2)}, u32[]{:S(2)}) collective-permute-start(bf16[64,3072]{1,0:T(8,128)(2,1)S(1)} %collective-permute-done.2.refs_1_), channel_id=1, source_target_pairs={{0,6},{1,7},{2,0},{3,1},{4,2},{5,3},{6,4},{7,5},{8,14},{9,15},{10,... | collective-permute-start | bytes 1179656 | tf_op jit(solution)/shard_map/ppermute | solution.py:31
  34.0 9.3 %collective-permute-start.7 = (bf16[64,3072]{1,0:T(8,128)(2,1)S(1)}, bf16[64,3072]{1,0:T(8,128)(2,1)S(1)}, u32[]{:S(2)}, u32[]{:S(2)}) collective-permute-start(bf16[64,3072]{1,0:T(8,128)(2,1)S(1)} %collective-permute-done.refs_0_), channel_id=1, source_target_pairs={{0,1},{1,0},{2,3},{3,2},{4,5},{5,4},{6,7},{7,6},{8,9},{9,8},{10,11... | collective-permute-start | bytes 1179656 | tf_op jit(solution)/shard_map/ppermute | solution.py:35
  35.2 8.1 %collective-permute-start.8 = (bf16[64,3072]{1,0:T(8,128)(2,1)S(1)}, bf16[64,3072]{1,0:T(8,128)(2,1)S(1)}, u32[]{:S(2)}, u32[]{:S(2)}) collective-permute-start(bf16[64,3072]{1,0:T(8,128)(2,1)S(1)} %collective-permute-done.4.refs_3_), channel_id=1, source_target_pairs={{0,1},{1,0},{2,3},{3,2},{4,5},{5,4},{6,7},{7,6},{8,9},{9,8},{10,11... | collective-permute-start | bytes 1179656 | tf_op jit(solution)/shard_map/ppermute | solution.py:35
  41.5 4.5 %collective-permute-start.11 = (bf16[64,3072]{1,0:T(8,128)(2,1)S(1)}, bf16[64,3072]{1,0:T(8,128)(2,1)S(1)}, u32[]{:S(2)}, u32[]{:S(2)}) collective-permute-start(bf16[64,3072]{1,0:T(8,128)(2,1)S(1)} %collective-permute-done.9.refs_0_), channel_id=1, source_target_pairs={{0,1},{1,0},{2,3},{3,2},{4,5},{5,4},{6,7},{7,6},{8,9},{9,8},{10,11... | collective-permute-start | bytes 1179656 | tf_op jit(solution)/shard_map/ppermute | solution.py:35
  43.3 2.7 %collective-permute-start.12 = (bf16[64,3072]{1,0:T(8,128)(2,1)S(1)}, bf16[64,3072]{1,0:T(8,128)(2,1)S(1)}, u32[]{:S(2)}, u32[]{:S(2)}) collective-permute-start(bf16[64,3072]{1,0:T(8,128)(2,1)S(1)} %collective-permute-done.10.refs_1_), channel_id=1, source_target_pairs={{0,1},{1,0},{2,3},{3,2},{4,5},{5,4},{6,7},{7,6},{8,9},{9,8},{10,11... | collective-permute-start | bytes 1179656 | tf_op jit(solution)/shard_map/ppermute | solution.py:35
  46.0 31.1 %copy-start.1 = (f32[512]{0:T(512)S(1)}, f32[512]{0:T(512)}, u32[]{:S(2)}) copy-start(f32[512]{0:T(512)} %param.10) | copy-start | bytes 6148
  49.6 9.7 %collective-permute-start.13 = (bf16[528,128]{1,0:T(8,128)(2,1)S(1)}, bf16[528,128]{1,0:T(8,128)(2,1)S(1)}, u32[]{:S(2)}, u32[]{:S(2)}) collective-permute-start(bf16[528,128]{1,0:T(8,128)(2,1)S(1)} %state.1.s0), channel_id=1, source_target_pairs={{0,16},{8,24},{16,0},{24,8},{32,48},{40,56},{48,32},{56,40},{64,80... | collective-permute-start | bytes 405512 | tf_op jit(solution)/shard_map/ppermute | solution.py:39
  52.5 11.7 %collective-permute-start.14 = (bf16[528,128]{1,0:T(8,128)(2,1)S(1)}, bf16[528,128]{1,0:T(8,128)(2,1)S(1)}, u32[]{:S(2)}, u32[]{:S(2)}) collective-permute-start(bf16[528,128]{1,0:T(8,128)(2,1)S(1)} %state.1.s0), channel_id=1, source_target_pairs={{0,8},{8,16},{16,24},{24,0},{32,40},{40,48},{48,56},{56,32},{64,72... | collective-permute-start | bytes 405512 | tf_op jit(solution)/shard_map/ppermute | solution.py:39
  52.8 12.6 %collective-permute-start.15 = (bf16[528,128]{1,0:T(8,128)(2,1)S(1)}, bf16[528,128]{1,0:T(8,128)(2,1)S(1)}, u32[]{:S(2)}, u32[]{:S(2)}) collective-permute-start(bf16[528,128]{1,0:T(8,128)(2,1)S(1)} %state.1.s0), channel_id=1, source_target_pairs={{0,24},{8,0},{16,8},{24,16},{32,56},{40,32},{48,40},{56,48},{64,88... | collective-permute-start | bytes 405512 | tf_op jit(solution)/shard_map/ppermute | solution.py:39
  65.6 9.4 %collective-permute-start.16 = (bf16[528,128]{1,0:T(8,128)(2,1)S(1)}, bf16[528,128]{1,0:T(8,128)(2,1)S(1)}, u32[]{:S(2)}, u32[]{:S(2)}) collective-permute-start(bf16[528,128]{1,0:T(8,128)(2,1)S(1)} %get-tuple-element.75), channel_id=1, source_target_pairs={{0,64},{8,72},{16,80},{24,88},{32,96},{40,104},{48,112},{56,120},{... | collective-permute-start | bytes 405512 | tf_op jit(solution)/shard_map/ppermute | solution.py:43
  71.0 5.1 %collective-permute-start.17 = (bf16[528,128]{1,0:T(8,128)(2,1)S(1)}, bf16[528,128]{1,0:T(8,128)(2,1)S(1)}, u32[]{:S(2)}, u32[]{:S(2)}) collective-permute-start(bf16[528,128]{1,0:T(8,128)(2,1)S(1)} %get-tuple-element.75), channel_id=1, source_target_pairs={{0,32},{8,40},{16,48},{24,56},{32,64},{40,72},{48,80},{56,88},{64,... | collective-permute-start | bytes 405512 | tf_op jit(solution)/shard_map/ppermute | solution.py:43
  73.6 3.5 %collective-permute-start.18 = (bf16[528,128]{1,0:T(8,128)(2,1)S(1)}, bf16[528,128]{1,0:T(8,128)(2,1)S(1)}, u32[]{:S(2)}, u32[]{:S(2)}) collective-permute-start(bf16[528,128]{1,0:T(8,128)(2,1)S(1)} %get-tuple-element.75), channel_id=1, source_target_pairs={{0,96},{8,104},{16,112},{24,120},{1,97},{9,105},{17,113},{25,121},... | collective-permute-start | bytes 405512 | tf_op jit(solution)/shard_map/ppermute | solution.py:43
  84.5 3.3 %collective-permute-start.19 = (bf16[64,6144]{1,0:T(8,128)(2,1)S(1)}, bf16[64,6144]{1,0:T(8,128)(2,1)S(1)}, u32[]{:S(2)}, u32[]{:S(2)}) collective-permute-start(bf16[64,6144]{1,0:T(8,128)(2,1)S(1)} %get-tuple-element.82), channel_id=1, source_target_pairs={{0,1},{1,0},{2,3},{3,2},{4,5},{5,4},{6,7},{7,6},{8,9},{9,8},{10,11... | collective-permute-start | bytes 2359304 | tf_op jit(solution)/shard_map/ppermute | solution.py:35
  88.1 4.0 %collective-permute-start.20 = (bf16[64,6144]{1,0:T(8,128)(2,1)S(1)}, bf16[64,6144]{1,0:T(8,128)(2,1)S(1)}, u32[]{:S(2)}, u32[]{:S(2)}) collective-permute-start(bf16[64,6144]{1,0:T(8,128)(2,1)S(1)} %get-tuple-element.85), channel_id=1, source_target_pairs={{0,1},{1,0},{2,3},{3,2},{4,5},{5,4},{6,7},{7,6},{8,9},{9,8},{10,11... | collective-permute-start | bytes 2359304 | tf_op jit(solution)/shard_map/ppermute | solution.py:35
  88.2 4.1 %collective-permute-start.21 = (bf16[64,6144]{1,0:T(8,128)(2,1)S(1)}, bf16[64,6144]{1,0:T(8,128)(2,1)S(1)}, u32[]{:S(2)}, u32[]{:S(2)}) collective-permute-start(bf16[64,6144]{1,0:T(8,128)(2,1)S(1)} %get-tuple-element.87), channel_id=1, source_target_pairs={{0,1},{1,0},{2,3},{3,2},{4,5},{5,4},{6,7},{7,6},{8,9},{9,8},{10,11... | collective-permute-start | bytes 2359304 | tf_op jit(solution)/shard_map/ppermute | solution.py:35
  88.6 12.8 %collective-permute-start.25 = (bf16[64,3072]{1,0:T(8,128)(2,1)S(1)}, bf16[64,3072]{1,0:T(8,128)(2,1)S(1)}, u32[]{:S(2)}, u32[]{:S(2)}) collective-permute-start(bf16[64,3072]{1,0:T(8,128)(2,1)S(1)} %get-tuple-element.96), channel_id=1, source_target_pairs={{0,2},{1,3},{2,4},{3,5},{4,6},{5,7},{6,0},{7,1},{8,10},{9,11},{10,... | collective-permute-start | bytes 1179656 | tf_op jit(solution)/shard_map/ppermute | solution.py:31
  89.9 11.6 %collective-permute-start.26 = (bf16[64,3072]{1,0:T(8,128)(2,1)S(1)}, bf16[64,3072]{1,0:T(8,128)(2,1)S(1)}, u32[]{:S(2)}, u32[]{:S(2)}) collective-permute-start(bf16[64,3072]{1,0:T(8,128)(2,1)S(1)} %get-tuple-element.95), channel_id=1, source_target_pairs={{0,6},{1,7},{2,0},{3,1},{4,2},{5,3},{6,4},{7,5},{8,14},{9,15},{10,... | collective-permute-start | bytes 1179656 | tf_op jit(solution)/shard_map/ppermute | solution.py:31
  92.2 17.7 %collective-permute-start.23 = (bf16[64,3072]{1,0:T(8,128)(2,1)S(1)}, bf16[64,3072]{1,0:T(8,128)(2,1)S(1)}, u32[]{:S(2)}, u32[]{:S(2)}) collective-permute-start(bf16[64,3072]{1,0:T(8,128)(2,1)S(1)} %add_convert_fusion.3), channel_id=1, source_target_pairs={{0,2},{1,3},{2,4},{3,5},{4,6},{5,7},{6,0},{7,1},{8,10},{9,11},{10,... | collective-permute-start | bytes 1179656 | tf_op jit(solution)/shard_map/ppermute | solution.py:31
  92.4 17.5 %collective-permute-start.24 = (bf16[64,3072]{1,0:T(8,128)(2,1)S(1)}, bf16[64,3072]{1,0:T(8,128)(2,1)S(1)}, u32[]{:S(2)}, u32[]{:S(2)}) collective-permute-start(bf16[64,3072]{1,0:T(8,128)(2,1)S(1)} %add_convert_fusion.2), channel_id=1, source_target_pairs={{0,6},{1,7},{2,0},{3,1},{4,2},{5,3},{6,4},{7,5},{8,14},{9,15},{10,... | collective-permute-start | bytes 1179656 | tf_op jit(solution)/shard_map/ppermute | solution.py:31
  96.4 13.5 %collective-permute-start.22 = (bf16[64,6144]{1,0:T(8,128)(2,1)S(1)}, bf16[64,6144]{1,0:T(8,128)(2,1)S(1)}, u32[]{:S(2)}, u32[]{:S(2)}) collective-permute-start(bf16[64,6144]{1,0:T(8,128)(2,1)S(1)} %get-tuple-element.90), channel_id=1, source_target_pairs={{0,1},{1,0},{2,3},{3,2},{4,5},{5,4},{6,7},{7,6},{8,9},{9,8},{10,11... | collective-permute-start | bytes 2359304 | tf_op jit(solution)/shard_map/ppermute | solution.py:35
  101.6 16.7 %collective-permute-start.27 = (bf16[64,3072]{1,0:T(8,128)(2,1)S(1)}, bf16[64,3072]{1,0:T(8,128)(2,1)S(1)}, u32[]{:S(2)}, u32[]{:S(2)}) collective-permute-start(bf16[64,3072]{1,0:T(8,128)(2,1)S(1)} %add_convert_fusion.1), channel_id=1, source_target_pairs={{0,2},{1,3},{2,4},{3,5},{4,6},{5,7},{6,0},{7,1},{8,10},{9,11},{10,... | collective-permute-start | bytes 1179656 | tf_op jit(solution)/shard_map/ppermute | solution.py:31
  102.5 15.8 %collective-permute-start.28 = (bf16[64,3072]{1,0:T(8,128)(2,1)S(1)}, bf16[64,3072]{1,0:T(8,128)(2,1)S(1)}, u32[]{:S(2)}, u32[]{:S(2)}) collective-permute-start(bf16[64,3072]{1,0:T(8,128)(2,1)S(1)} %add_convert_fusion), channel_id=1, source_target_pairs={{0,6},{1,7},{2,0},{3,1},{4,2},{5,3},{6,4},{7,5},{8,14},{9,15},{10,... | collective-permute-start | bytes 1179656 | tf_op jit(solution)/shard_map/ppermute | solution.py:31
Sparse Core Ops, SparseCore 0:
  9.5 70.1 all-gather.2

commit v9 on v7

--- a/solution.py
+++ b/solution.py
@@ -144,7 +144,7 @@
         out[:, h * SIZE : (h + 1) * SIZE] = jnp.dot(probs, values, preferred_element_type=f32)
 
 
-def row_kernel(at, s0, s1, s2, s3, before, total):
+def row_kernel(at, s0, s2, s1, s3, before, total):
     refs = (s0, s1, s2, s3)
     x = at[0]
     place = [(x - k) & 3 for k in range(N_X)]
@@ -165,7 +165,7 @@
     before[WIDE:, :] = jnp.concatenate([lead, lead], axis=0)
 
 
-def normed_kernel(before, t1, t2, t3, a, b, c, d, g, inner, gain, out):
+def normed_kernel(before, t2, t1, t3, a, b, c, d, g, inner, gain, out):
     lead = jnp.exp(before[WIDE : WIDE + HEADS, :])
     r1, r2 = unpack(t1), unpack(t2)
     reach2, reach3 = jnp.exp(r1), jnp.exp(r1 + r2)
@@ -306,7 +306,7 @@
 
     packed = jax.ShapeDtypeStruct((WIDE + 16, SIZE), bf16)
     state = whole_call(state_kernel, (*rows, g, last), packed, "state", 2 * 512 * WIDE * SIZE)
-    row = [state] + [to_x(state, k) for k in range(1, N_X)]
+    row = [state] + [to_x(state, k) for k in (2, 1, 3)]
     inner = whole_call(
         inner_kernel,
         (*rows, g, gt, pos.reshape(512, 1), pos.reshape(1, 512)),
@@ -318,7 +318,7 @@
     before, total = whole_call(
         row_kernel, (at, *row), (jax.ShapeDtypeStruct((WIDE + 8, SIZE), f32), packed), "row", 10 * WIDE * SIZE, 1
     )
-    totals = [to_z(total, k) for k in range(1, N_Z)]
+    totals = [to_z(total, k) for k in (2, 1, 3)]
     normed = whole_call(
         normed_kernel,
         (before, *totals, *rows, g, inner, gain.reshape(1, WIDE)),

time: 126 us -> 125 us (level)
    all_gather x1, waiting for transfers between devices: 0.22 us -> 1.55 us  [body(): w_all = lax.all_gather(w_out, 'ctx', axis=0)]
  transfers between devices with their start and end apart: 30 -> 30, of which waited for: 11 -> 12; matrix products, arithmetic and copies ran while one was open for 5% -> 5% of each run, Pallas kernels for 18% -> 18%
where the time goes in v9:
time: 125 us
  starting transfers between devices  39.8 us (32%)
  waiting for transfers between devices  36.5 us (29%)
  Pallas kernels  27 us (22%)
  between operations  13.7 us (11%)
  local copies, waits for them, and re-layouts  4.77 us (4%)
  other arithmetic  2.94 us (2%)
    ppermute x12, waiting for transfers between devices, to_y(): lax.ppermute(a, 'tp', [(i, (i // 2 + k) % N_Y * 2 + i % 2) for i in range...  23.4 us
    ppermute x12, starting transfers between devices, to_y(): lax.ppermute(a, 'tp', [(i, (i // 2 + k) % N_Y * 2 + i % 2) for i in range...  16.5 us
    pallas_call x4, Pallas kernels, qkv(): pl.pallas_call(functools.partial(qkv_first_kernel if first else qkv_kerne...  15.1 us
    ppermute x3, starting transfers between devices, to_z(): lax.ppermute(a, 'ctx', [(j, j + N_X * k) for j in range(N_X * N_Z) if j /...  9.34 us
    ppermute x3, waiting for transfers between devices, to_x(): lax.ppermute(a, 'ctx', [(j, j // N_X * N_X + (j + k) % N_X) for j in rang...  8.62 us
    ppermute x11, starting transfers between devices, to_sibling(): return lax.ppermute(a, 'tp', [(i, i ^ 1) for i in range(2 * N_Y)])  8.38 us
    ppermute x3, starting transfers between devices, to_x(): lax.ppermute(a, 'ctx', [(j, j // N_X * N_X + (j + k) % N_X) for j in rang...  5.53 us
    pallas_call x6, Pallas kernels, whole_call(): pl.pallas_call(kernel, out_shape=outs, in_specs=[pl.BlockSpec(memory_spac...  4.96 us
  transfers between devices with their start and end apart: 30, of which 12 were waited for; matrix products, arithmetic and copies ran while one was open for 5% of the time, Pallas kernels for 18%

profile of v9, /device:TPU:1, one launch (start us, length us, event | category | flops | bytes accessed | tf_op | source)
XLA Modules:
  0.0 124.6 jit_solution(9908172459318216030)
XLA Ops:
  6.5 0.7 all-gather.3.cloned.1.call-update
  7.3 1.5 %collective-permute-start.3 = (bf16[64,6144]{1,0:T(8,128)(2,1)}, bf16[64,6144]{1,0:T(8,128)(2,1)S(1)}, u32[]{:S(2)}, u32[]{:S(2)}) collective-permute-start(bf16[64,6144]{1,0:T(8,128)(2,1)} %refs_0_.1), channel_id=1, source_target_pairs={{0,1},{1,0},{2,3},{3,2},{4,5},{5,4},{6,7},{7,6},{8,9},{9,8},{10,11... | collective-permute-start | bytes 2359304 | tf_op jit(solution)/shard_map/ppermute | solution.py:35
  8.8 1.0 slice.75
  9.8 1.4 %collective-permute-start.1 = (bf16[64,3072]{1,0:T(8,128)(2,1)S(1)}, bf16[64,3072]{1,0:T(8,128)(2,1)S(1)}, u32[]{:S(2)}, u32[]{:S(2)}) collective-permute-start(bf16[64,3072]{1,0:T(8,128)(2,1)S(1)} %slice.75), channel_id=1, source_target_pairs={{0,2},{1,3},{2,4},{3,5},{4,6},{5,7},{6,0},{7,1},{8,10},{9,11},{10,... | collective-permute-start | bytes 1179656 | tf_op jit(solution)/shard_map/ppermute | solution.py:31
  11.2 1.0 slice.76
  12.3 1.5 %collective-permute-start.2 = (bf16[64,3072]{1,0:T(8,128)(2,1)S(1)}, bf16[64,3072]{1,0:T(8,128)(2,1)S(1)}, u32[]{:S(2)}, u32[]{:S(2)}) collective-permute-start(bf16[64,3072]{1,0:T(8,128)(2,1)S(1)} %slice.76), channel_id=1, source_target_pairs={{0,6},{1,7},{2,0},{3,1},{4,2},{5,3},{6,4},{7,5},{8,14},{9,15},{10,... | collective-permute-start | bytes 1179656 | tf_op jit(solution)/shard_map/ppermute | solution.py:31
  14.5 1.2 reduce-window.6
  17.6 1.5 %collective-permute-start = (bf16[64,3072]{1,0:T(8,128)(2,1)S(1)}, bf16[64,3072]{1,0:T(8,128)(2,1)S(1)}, u32[]{:S(2)}, u32[]{:S(2)}) collective-permute-start(bf16[64,3072]{1,0:T(8,128)(2,1)S(1)} %slice.75), channel_id=1, source_target_pairs={{0,6},{1,7},{2,0},{3,1},{4,2},{5,3},{6,4},{7,5},{8,14},{9,15},{10,... | collective-permute-start | bytes 1179656 | tf_op jit(solution)/shard_map/ppermute | solution.py:31
  19.0 1.1 copy-done
  20.2 7.3 %qkv.4 = (bf16[128,1536]{1,0:T(8,128)(2,1)S(1)}, bf16[3,6144,512]{2,1,0:T(8,128)(2,1)S(1)}) custom-call(bf16[64,6144]{1,0:T(8,128)(2,1)S(1)} %copy-done, bf16[64,6144]{1,0:T(8,128)(2,1)S(1)} %collective-permute-done.3.refs_1_, bf16[3,6144,512]{2,1,0:T(8,128)(2,1)} %refs_2_.1), custom_call_target="tpu_custom_call" | custom-call | flops 24159192 | bytes 188743 | tf_op jit(solution)/shard_map/qkv/pallas_call | solution.py:97
  27.5 1.1 collective-permute-start.5
  28.8 2.3 %collective-permute-done.refs_0_ = bf16[64,3072]{1,0:T(8,128)(2,1)S(1)} collective-permute-done((bf16[64,3072]{1,0:T(8,128)(2,1)S(1)}, bf16[64,3072]{1,0:T(8,128)(2,1)S(1)}, u32[]{:S(2)}, u32[]{:S(2)}) %collective-permute-start) | collective-permute-done | bytes 393248 | tf_op jit(solution)/shard_map/ppermute | solution.py:31
  31.2 2.8 %collective-permute-start.10 = (bf16[64,3072]{1,0:T(8,128)(2,1)S(1)}, bf16[64,3072]{1,0:T(8,128)(2,1)S(1)}, u32[]{:S(2)}, u32[]{:S(2)}) collective-permute-start(bf16[64,3072]{1,0:T(8,128)(2,1)S(1)} %collective-permute-done.2.refs_1_), channel_id=1, source_target_pairs={{0,6},{1,7},{2,0},{3,1},{4,2},{5,3},{6,4},{7,5},{8,14},{9,15},{10,... | collective-permute-start | bytes 1179656 | tf_op jit(solution)/shard_map/ppermute | solution.py:31
  34.0 1.2 collective-permute-start.7
  35.3 2.6 %qkv.5.a = bf16[128,1536]{1,0:T(8,128)(2,1)S(1)} custom-call(bf16[64,3072]{1,0:T(8,128)(2,1)S(1)} %collective-permute-done.refs_0_, bf16[64,3072]{1,0:T(8,128)(2,1)S(1)} %collective-permute-done.2.refs_1_, bf16[64,3072]{1,0:T(8,128)(2,1)S(1)} %collective-permute-done.1.refs_2_, bf16[64,3072]{1,0:T(8,128)(2,1)S(1)} %collective-permute-done.4.refs_3_, ...), custom_call_target="tpu_custom_call" | custom-call | flops 24159192 | bytes 188743 | tf_op jit(solution)/shard_map/qkv/pallas_call | solution.py:97
  37.9 2.5 %collective-permute-done.9.refs_0_ = bf16[64,3072]{1,0:T(8,128)(2,1)S(1)} collective-permute-done((bf16[64,3072]{1,0:T(8,128)(2,1)S(1)}, bf16[64,3072]{1,0:T(8,128)(2,1)S(1)}, u32[]{:S(2)}, u32[]{:S(2)}) %collective-permute-start.9) | collective-permute-done | bytes 393248 | tf_op jit(solution)/shard_map/ppermute | solution.py:31
  40.4 1.0 collective-permute-done.10.refs_1_
  41.5 1.9 %collective-permute-start.11 = (bf16[64,3072]{1,0:T(8,128)(2,1)S(1)}, bf16[64,3072]{1,0:T(8,128)(2,1)S(1)}, u32[]{:S(2)}, u32[]{:S(2)}) collective-permute-start(bf16[64,3072]{1,0:T(8,128)(2,1)S(1)} %collective-permute-done.9.refs_0_), channel_id=1, source_target_pairs={{0,1},{1,0},{2,3},{3,2},{4,5},{5,4},{6,7},{7,6},{8,9},{9,8},{10,11... | collective-permute-start | bytes 1179656 | tf_op jit(solution)/shard_map/ppermute | solution.py:35
  43.3 2.6 %qkv.6.c = bf16[128,1536]{1,0:T(8,128)(2,1)S(1)} custom-call(bf16[64,3072]{1,0:T(8,128)(2,1)S(1)} %collective-permute-done.7.refs_0_, bf16[64,3072]{1,0:T(8,128)(2,1)S(1)} %collective-permute-done.6.refs_1_, bf16[64,3072]{1,0:T(8,128)(2,1)S(1)} %collective-permute-done.5.refs_2_, bf16[64,3072]{1,0:T(8,128)(2,1)S(1)} %collective-permute-done.8.refs_3_, ...), custom_call_target="tpu_custom_call" | custom-call | flops 24159192 | bytes 188743 | tf_op jit(solution)/shard_map/qkv/pallas_call | solution.py:97
  46.0 2.6 %qkv.7.d = bf16[128,1536]{1,0:T(8,128)(2,1)S(1)} custom-call(bf16[64,3072]{1,0:T(8,128)(2,1)S(1)} %collective-permute-done.9.refs_0_, bf16[64,3072]{1,0:T(8,128)(2,1)S(1)} %collective-permute-done.10.refs_1_, bf16[64,3072]{1,0:T(8,128)(2,1)S(1)} %collective-permute-done.11.refs_2_, bf16[64,3072]{1,0:T(8,128)(2,1)S(1)} %collective-permute-done.12.refs_3_, ...), custom_call_target="tpu_custom_call" | custom-call | flops 24159192 | bytes 188743 | tf_op jit(solution)/shard_map/qkv/pallas_call | solution.py:97
  48.6 1.0 state.1.s0
  49.6 2.9 %collective-permute-start.13 = (bf16[528,128]{1,0:T(8,128)(2,1)S(1)}, bf16[528,128]{1,0:T(8,128)(2,1)S(1)}, u32[]{:S(2)}, u32[]{:S(2)}) collective-permute-start(bf16[528,128]{1,0:T(8,128)(2,1)S(1)} %state.1.s0), channel_id=1, source_target_pairs={{0,16},{8,24},{16,0},{24,8},{32,48},{40,56},{48,32},{56,40},{64,80... | collective-permute-start | bytes 405512 | tf_op jit(solution)/shard_map/ppermute | solution.py:39
  52.8 2.4 %collective-permute-start.15 = (bf16[528,128]{1,0:T(8,128)(2,1)S(1)}, bf16[528,128]{1,0:T(8,128)(2,1)S(1)}, u32[]{:S(2)}, u32[]{:S(2)}) collective-permute-start(bf16[528,128]{1,0:T(8,128)(2,1)S(1)} %state.1.s0), channel_id=1, source_target_pairs={{0,24},{8,0},{16,8},{24,16},{32,56},{40,32},{48,40},{56,48},{64,88... | collective-permute-start | bytes 405512 | tf_op jit(solution)/shard_map/ppermute | solution.py:39
  55.3 1.4 %inner.1 = f32[512,512]{1,0:T(8,128)S(1)} custom-call(bf16[128,1536]{1,0:T(8,128)(2,1)S(1)} %qkv.5.a, bf16[128,1536]{1,0:T(8,128)(2,1)S(1)} %get-tuple-element.53.b, bf16[128,1536]{1,0:T(8,128)(2,1)S(1)} %qkv.6.c, bf16[128,1536]{1,0:T(8,128)(2,1)S(1)} %qkv.7.d, f32[512,4]{1,0:T(8,128)S(1)} %bitcast.20, f32[4,512]{1,0:T(4,128)S(1)} %concatenate.8.gt, ...), custom_call_target="tpu_custom_call" | custom-call | flops 5368709 | bytes 15933 | tf_op jit(solution)/shard_map/inner/pallas_call | solution.py:188
  56.8 2.6 %collective-permute-done.13.s2 = bf16[528,128]{1,0:T(8,128)(2,1)S(1)} collective-permute-done((bf16[528,128]{1,0:T(8,128)(2,1)S(1)}, bf16[528,128]{1,0:T(8,128)(2,1)S(1)}, u32[]{:S(2)}, u32[]{:S(2)}) %collective-permute-start.13) | collective-permute-done | bytes 135200 | tf_op jit(solution)/shard_map/ppermute | solution.py:39
  59.4 4.9 %collective-permute-done.14.s1 = bf16[528,128]{1,0:T(8,128)(2,1)S(1)} collective-permute-done((bf16[528,128]{1,0:T(8,128)(2,1)S(1)}, bf16[528,128]{1,0:T(8,128)(2,1)S(1)}, u32[]{:S(2)}, u32[]{:S(2)}) %collective-permute-start.14) | collective-permute-done | bytes 135200 | tf_op jit(solution)/shard_map/ppermute | solution.py:39
  64.2 1.2 collective-permute-done.15.s3
  65.6 5.4 %collective-permute-start.16 = (bf16[528,128]{1,0:T(8,128)(2,1)S(1)}, bf16[528,128]{1,0:T(8,128)(2,1)S(1)}, u32[]{:S(2)}, u32[]{:S(2)}) collective-permute-start(bf16[528,128]{1,0:T(8,128)(2,1)S(1)} %get-tuple-element.75), channel_id=1, source_target_pairs={{0,64},{8,72},{16,80},{24,88},{32,96},{40,104},{48,112},{56,120},{... | collective-permute-start | bytes 405512 | tf_op jit(solution)/shard_map/ppermute | solution.py:43
  71.0 2.6 %collective-permute-start.17 = (bf16[528,128]{1,0:T(8,128)(2,1)S(1)}, bf16[528,128]{1,0:T(8,128)(2,1)S(1)}, u32[]{:S(2)}, u32[]{:S(2)}) collective-permute-start(bf16[528,128]{1,0:T(8,128)(2,1)S(1)} %get-tuple-element.75), channel_id=1, source_target_pairs={{0,32},{8,40},{16,48},{24,56},{32,64},{40,72},{48,80},{56,88},{64,... | collective-permute-start | bytes 405512 | tf_op jit(solution)/shard_map/ppermute | solution.py:43
  73.6 1.3 %collective-permute-start.18 = (bf16[528,128]{1,0:T(8,128)(2,1)S(1)}, bf16[528,128]{1,0:T(8,128)(2,1)S(1)}, u32[]{:S(2)}, u32[]{:S(2)}) collective-permute-start(bf16[528,128]{1,0:T(8,128)(2,1)S(1)} %get-tuple-element.75), channel_id=1, source_target_pairs={{0,96},{8,104},{16,112},{24,120},{1,97},{9,105},{17,113},{25,121},... | collective-permute-start | bytes 405512 | tf_op jit(solution)/shard_map/ppermute | solution.py:43
  74.9 1.1 collective-permute-done.17.t1
  76.1 1.0 collective-permute-done.18.t3
  77.1 1.0 normed.1
  78.1 1.5 %all-gather.3.cloned.1.call-done = bf16[8192,384]{1,0:T(8,128)(2,1)} async-done(((bf16[512,384]{1,0:T(8,128)(2,1)}), bf16[8192,384]{1,0:T(8,128)(2,1)}) %all-gather.3.cloned.1.call-update) | async-done | bytes 6291472 | tf_op jit(solution)/shard_map/all_gather | solution.py:271
  79.7 3.3 %project.3 = (bf16[64,6144]{1,0:T(8,128)(2,1)S(1)}, bf16[64,6144]{1,0:T(8,128)(2,1)S(1)}, bf16[16,512,384]{2,1,0:T(8,128)(2,1)S(1)}) custom-call(bf16[512,512]{1,0:T(8,128)(2,1)S(1)} %normed.1, bf16[16,512,384]{2,1,0:T(8,128)(2,1)} %bitcast.25), custom_call_target="tpu_custom_call" | custom-call | flops 8053063 | bytes 62914 | tf_op jit(solution)/shard_map/project/pallas_call | solution.py:331
  83.0 1.0 collective-permute-start.19
  84.0 2.3 %project.4 = (bf16[64,6144]{1,0:T(8,128)(2,1)S(1)}, bf16[64,6144]{1,0:T(8,128)(2,1)S(1)}, bf16[64,6144]{1,0:T(8,128)(2,1)S(1)}, bf16[64,6144]{1,0:T(8,128)(2,1)S(1)}) custom-call(bf16[512,512]{1,0:T(8,128)(2,1)S(1)} %normed.1, bf16[16,512,384]{2,1,0:T(8,128)(2,1)S(1)} %get-tuple-element.76.w), custom_call_target="tpu_custom_call" | custom-call | flops 16106127 | bytes 62914 | tf_op jit(solution)/shard_map/project/pallas_call | solution.py:231
  87.1 1.2 collective-permute-start.25
  88.3 2.2 %collective-permute-start.26 = (bf16[64,3072]{1,0:T(8,128)(2,1)S(1)}, bf16[64,3072]{1,0:T(8,128)(2,1)S(1)}, u32[]{:S(2)}, u32[]{:S(2)}) collective-permute-start(bf16[64,3072]{1,0:T(8,128)(2,1)S(1)} %get-tuple-element.95), channel_id=1, source_target_pairs={{0,6},{1,7},{2,0},{3,1},{4,2},{5,3},{6,4},{7,5},{8,14},{9,15},{10,... | collective-permute-start | bytes 1179656 | tf_op jit(solution)/shard_map/ppermute | solution.py:31
  90.8 2.8 %collective-permute-start.24 = (bf16[64,3072]{1,0:T(8,128)(2,1)S(1)}, bf16[64,3072]{1,0:T(8,128)(2,1)S(1)}, u32[]{:S(2)}, u32[]{:S(2)}) collective-permute-start(bf16[64,3072]{1,0:T(8,128)(2,1)S(1)} %add_convert_fusion.2), channel_id=1, source_target_pairs={{0,6},{1,7},{2,0},{3,1},{4,2},{5,3},{6,4},{7,5},{8,14},{9,15},{10,... | collective-permute-start | bytes 1179656 | tf_op jit(solution)/shard_map/ppermute | solution.py:31
  93.6 1.2 project.5
  94.9 1.0 collective-permute-start.22
  95.8 4.1 %collective-permute-done.25 = bf16[64,3072]{1,0:T(8,128)(2,1)S(1)} collective-permute-done((bf16[64,3072]{1,0:T(8,128)(2,1)S(1)}, bf16[64,3072]{1,0:T(8,128)(2,1)S(1)}, u32[]{:S(2)}, u32[]{:S(2)}) %collective-permute-start.25) | collective-permute-done | bytes 393248 | tf_op jit(solution)/shard_map/ppermute | solution.py:31
  100.1 0.7 collective-permute-start.27
  101.0 2.1 %collective-permute-start.28 = (bf16[64,3072]{1,0:T(8,128)(2,1)S(1)}, bf16[64,3072]{1,0:T(8,128)(2,1)S(1)}, u32[]{:S(2)}, u32[]{:S(2)}) collective-permute-start(bf16[64,3072]{1,0:T(8,128)(2,1)S(1)} %add_convert_fusion), channel_id=1, source_target_pairs={{0,6},{1,7},{2,0},{3,1},{4,2},{5,3},{6,4},{7,5},{8,14},{9,15},{10,... | collective-permute-start | bytes 1179656 | tf_op jit(solution)/shard_map/ppermute | solution.py:31
  103.0 5.3 %collective-permute-done.23.up_plain = bf16[64,3072]{1,0:T(8,128)(2,1)S(1)} collective-permute-done((bf16[64,3072]{1,0:T(8,128)(2,1)S(1)}, bf16[64,3072]{1,0:T(8,128)(2,1)S(1)}, u32[]{:S(2)}, u32[]{:S(2)}) %collective-permute-start.23) | collective-permute-done | bytes 393248 | tf_op jit(solution)/shard_map/ppermute | solution.py:31
  108.6 8.2 %collective-permute-done.27.up_sum = bf16[64,3072]{1,0:T(8,128)(2,1)S(1)} collective-permute-done((bf16[64,3072]{1,0:T(8,128)(2,1)S(1)}, bf16[64,3072]{1,0:T(8,128)(2,1)S(1)}, u32[]{:S(2)}, u32[]{:S(2)}) %collective-permute-start.27) | collective-permute-done | bytes 393248 | tf_op jit(solution)/shard_map/ppermute | solution.py:31
  116.8 1.0 final.1
  (54 shorter events, 5.2 us)
Async XLA Ops:
  6.5 73.2 %all-gather.3.cloned.1.call-start = ((), (), s32[]{:S(2)}) async-start(), calls=%async_computation | async-start | bytes 6684672 | tf_op jit(solution)/shard_map/all_gather | solution.py:271
  7.3 11.8 %collective-permute-start.3 = (bf16[64,6144]{1,0:T(8,128)(2,1)}, bf16[64,6144]{1,0:T(8,128)(2,1)S(1)}, u32[]{:S(2)}, u32[]{:S(2)}) collective-permute-start(bf16[64,6144]{1,0:T(8,128)(2,1)} %refs_0_.1), channel_id=1, source_target_pairs={{0,1},{1,0},{2,3},{3,2},{4,5},{5,4},{6,7},{7,6},{8,9},{9,8},{10,11... | collective-permute-start | bytes 2359304 | tf_op jit(solution)/shard_map/ppermute | solution.py:35
  9.8 17.7 %collective-permute-start.1 = (bf16[64,3072]{1,0:T(8,128)(2,1)S(1)}, bf16[64,3072]{1,0:T(8,128)(2,1)S(1)}, u32[]{:S(2)}, u32[]{:S(2)}) collective-permute-start(bf16[64,3072]{1,0:T(8,128)(2,1)S(1)} %slice.75), channel_id=1, source_target_pairs={{0,2},{1,3},{2,4},{3,5},{4,6},{5,7},{6,0},{7,1},{8,10},{9,11},{10,... | collective-permute-start | bytes 1179656 | tf_op jit(solution)/shard_map/ppermute | solution.py:31
  12.3 15.3 %collective-permute-start.2 = (bf16[64,3072]{1,0:T(8,128)(2,1)S(1)}, bf16[64,3072]{1,0:T(8,128)(2,1)S(1)}, u32[]{:S(2)}, u32[]{:S(2)}) collective-permute-start(bf16[64,3072]{1,0:T(8,128)(2,1)S(1)} %slice.76), channel_id=1, source_target_pairs={{0,6},{1,7},{2,0},{3,1},{4,2},{5,3},{6,4},{7,5},{8,14},{9,15},{10,... | collective-permute-start | bytes 1179656 | tf_op jit(solution)/shard_map/ppermute | solution.py:31
  17.6 13.6 %collective-permute-start = (bf16[64,3072]{1,0:T(8,128)(2,1)S(1)}, bf16[64,3072]{1,0:T(8,128)(2,1)S(1)}, u32[]{:S(2)}, u32[]{:S(2)}) collective-permute-start(bf16[64,3072]{1,0:T(8,128)(2,1)S(1)} %slice.75), channel_id=1, source_target_pairs={{0,6},{1,7},{2,0},{3,1},{4,2},{5,3},{6,4},{7,5},{8,14},{9,15},{10,... | collective-permute-start | bytes 1179656 | tf_op jit(solution)/shard_map/ppermute | solution.py:31
  19.0 15.0 %collective-permute-start.4 = (bf16[64,3072]{1,0:T(8,128)(2,1)S(1)}, bf16[64,3072]{1,0:T(8,128)(2,1)S(1)}, u32[]{:S(2)}, u32[]{:S(2)}) collective-permute-start(bf16[64,3072]{1,0:T(8,128)(2,1)S(1)} %slice.76), channel_id=1, source_target_pairs={{0,2},{1,3},{2,4},{3,5},{4,6},{5,7},{6,0},{7,1},{8,10},{9,11},{10,... | collective-permute-start | bytes 1179656 | tf_op jit(solution)/shard_map/ppermute | solution.py:31
  19.0 1.1 copy-start
  27.5 7.7 %collective-permute-start.5 = (bf16[64,3072]{1,0:T(8,128)(2,1)S(1)}, bf16[64,3072]{1,0:T(8,128)(2,1)S(1)}, u32[]{:S(2)}, u32[]{:S(2)}) collective-permute-start(bf16[64,3072]{1,0:T(8,128)(2,1)S(1)} %collective-permute-done.1.refs_2_), channel_id=1, source_target_pairs={{0,1},{1,0},{2,3},{3,2},{4,5},{5,4},{6,7},{7,6},{8,9},{9,8},{10,11... | collective-permute-start | bytes 1179656 | tf_op jit(solution)/shard_map/ppermute | solution.py:35
  28.6 6.7 %collective-permute-start.6 = (bf16[64,3072]{1,0:T(8,128)(2,1)S(1)}, bf16[64,3072]{1,0:T(8,128)(2,1)S(1)}, u32[]{:S(2)}, u32[]{:S(2)}) collective-permute-start(bf16[64,3072]{1,0:T(8,128)(2,1)S(1)} %collective-permute-done.2.refs_1_), channel_id=1, source_target_pairs={{0,1},{1,0},{2,3},{3,2},{4,5},{5,4},{6,7},{7,6},{8,9},{9,8},{10,11... | collective-permute-start | bytes 1179656 | tf_op jit(solution)/shard_map/ppermute | solution.py:35
  28.7 11.8 %collective-permute-start.9 = (bf16[64,3072]{1,0:T(8,128)(2,1)S(1)}, bf16[64,3072]{1,0:T(8,128)(2,1)S(1)}, u32[]{:S(2)}, u32[]{:S(2)}) collective-permute-start(bf16[64,3072]{1,0:T(8,128)(2,1)S(1)} %collective-permute-done.1.refs_2_), channel_id=1, source_target_pairs={{0,2},{1,3},{2,4},{3,5},{4,6},{5,7},{6,0},{7,1},{8,10},{9,11},{10,... | collective-permute-start | bytes 1179656 | tf_op jit(solution)/shard_map/ppermute | solution.py:31
  31.2 10.3 %collective-permute-start.10 = (bf16[64,3072]{1,0:T(8,128)(2,1)S(1)}, bf16[64,3072]{1,0:T(8,128)(2,1)S(1)}, u32[]{:S(2)}, u32[]{:S(2)}) collective-permute-start(bf16[64,3072]{1,0:T(8,128)(2,1)S(1)} %collective-permute-done.2.refs_1_), channel_id=1, source_target_pairs={{0,6},{1,7},{2,0},{3,1},{4,2},{5,3},{6,4},{7,5},{8,14},{9,15},{10,... | collective-permute-start | bytes 1179656 | tf_op jit(solution)/shard_map/ppermute | solution.py:31
  34.0 9.3 %collective-permute-start.7 = (bf16[64,3072]{1,0:T(8,128)(2,1)S(1)}, bf16[64,3072]{1,0:T(8,128)(2,1)S(1)}, u32[]{:S(2)}, u32[]{:S(2)}) collective-permute-start(bf16[64,3072]{1,0:T(8,128)(2,1)S(1)} %collective-permute-done.refs_0_), channel_id=1, source_target_pairs={{0,1},{1,0},{2,3},{3,2},{4,5},{5,4},{6,7},{7,6},{8,9},{9,8},{10,11... | collective-permute-start | bytes 1179656 | tf_op jit(solution)/shard_map/ppermute | solution.py:35
  35.2 8.1 %collective-permute-start.8 = (bf16[64,3072]{1,0:T(8,128)(2,1)S(1)}, bf16[64,3072]{1,0:T(8,128)(2,1)S(1)}, u32[]{:S(2)}, u32[]{:S(2)}) collective-permute-start(bf16[64,3072]{1,0:T(8,128)(2,1)S(1)} %collective-permute-done.4.refs_3_), channel_id=1, source_target_pairs={{0,1},{1,0},{2,3},{3,2},{4,5},{5,4},{6,7},{7,6},{8,9},{9,8},{10,11... | collective-permute-start | bytes 1179656 | tf_op jit(solution)/shard_map/ppermute | solution.py:35
  41.5 4.5 %collective-permute-start.11 = (bf16[64,3072]{1,0:T(8,128)(2,1)S(1)}, bf16[64,3072]{1,0:T(8,128)(2,1)S(1)}, u32[]{:S(2)}, u32[]{:S(2)}) collective-permute-start(bf16[64,3072]{1,0:T(8,128)(2,1)S(1)} %collective-permute-done.9.refs_0_), channel_id=1, source_target_pairs={{0,1},{1,0},{2,3},{3,2},{4,5},{5,4},{6,7},{7,6},{8,9},{9,8},{10,11... | collective-permute-start | bytes 1179656 | tf_op jit(solution)/shard_map/ppermute | solution.py:35
  43.3 2.7 %collective-permute-start.12 = (bf16[64,3072]{1,0:T(8,128)(2,1)S(1)}, bf16[64,3072]{1,0:T(8,128)(2,1)S(1)}, u32[]{:S(2)}, u32[]{:S(2)}) collective-permute-start(bf16[64,3072]{1,0:T(8,128)(2,1)S(1)} %collective-permute-done.10.refs_1_), channel_id=1, source_target_pairs={{0,1},{1,0},{2,3},{3,2},{4,5},{5,4},{6,7},{7,6},{8,9},{9,8},{10,11... | collective-permute-start | bytes 1179656 | tf_op jit(solution)/shard_map/ppermute | solution.py:35
  46.0 31.1 %copy-start.1 = (f32[512]{0:T(512)S(1)}, f32[512]{0:T(512)}, u32[]{:S(2)}) copy-start(f32[512]{0:T(512)} %param.10) | copy-start | bytes 6148
  49.6 9.7 %collective-permute-start.13 = (bf16[528,128]{1,0:T(8,128)(2,1)S(1)}, bf16[528,128]{1,0:T(8,128)(2,1)S(1)}, u32[]{:S(2)}, u32[]{:S(2)}) collective-permute-start(bf16[528,128]{1,0:T(8,128)(2,1)S(1)} %state.1.s0), channel_id=1, source_target_pairs={{0,16},{8,24},{16,0},{24,8},{32,48},{40,56},{48,32},{56,40},{64,80... | collective-permute-start | bytes 405512 | tf_op jit(solution)/shard_map/ppermute | solution.py:39
  52.5 11.7 %collective-permute-start.14 = (bf16[528,128]{1,0:T(8,128)(2,1)S(1)}, bf16[528,128]{1,0:T(8,128)(2,1)S(1)}, u32[]{:S(2)}, u32[]{:S(2)}) collective-permute-start(bf16[528,128]{1,0:T(8,128)(2,1)S(1)} %state.1.s0), channel_id=1, source_target_pairs={{0,8},{8,16},{16,24},{24,0},{32,40},{40,48},{48,56},{56,32},{64,72... | collective-permute-start | bytes 405512 | tf_op jit(solution)/shard_map/ppermute | solution.py:39
  52.8 12.6 %collective-permute-start.15 = (bf16[528,128]{1,0:T(8,128)(2,1)S(1)}, bf16[528,128]{1,0:T(8,128)(2,1)S(1)}, u32[]{:S(2)}, u32[]{:S(2)}) collective-permute-start(bf16[528,128]{1,0:T(8,128)(2,1)S(1)} %state.1.s0), channel_id=1, source_target_pairs={{0,24},{8,0},{16,8},{24,16},{32,56},{40,32},{48,40},{56,48},{64,88... | collective-permute-start | bytes 405512 | tf_op jit(solution)/shard_map/ppermute | solution.py:39
  65.6 9.4 %collective-permute-start.16 = (bf16[528,128]{1,0:T(8,128)(2,1)S(1)}, bf16[528,128]{1,0:T(8,128)(2,1)S(1)}, u32[]{:S(2)}, u32[]{:S(2)}) collective-permute-start(bf16[528,128]{1,0:T(8,128)(2,1)S(1)} %get-tuple-element.75), channel_id=1, source_target_pairs={{0,64},{8,72},{16,80},{24,88},{32,96},{40,104},{48,112},{56,120},{... | collective-permute-start | bytes 405512 | tf_op jit(solution)/shard_map/ppermute | solution.py:43
  71.0 5.1 %collective-permute-start.17 = (bf16[528,128]{1,0:T(8,128)(2,1)S(1)}, bf16[528,128]{1,0:T(8,128)(2,1)S(1)}, u32[]{:S(2)}, u32[]{:S(2)}) collective-permute-start(bf16[528,128]{1,0:T(8,128)(2,1)S(1)} %get-tuple-element.75), channel_id=1, source_target_pairs={{0,32},{8,40},{16,48},{24,56},{32,64},{40,72},{48,80},{56,88},{64,... | collective-permute-start | bytes 405512 | tf_op jit(solution)/shard_map/ppermute | solution.py:43
  73.6 3.5 %collective-permute-start.18 = (bf16[528,128]{1,0:T(8,128)(2,1)S(1)}, bf16[528,128]{1,0:T(8,128)(2,1)S(1)}, u32[]{:S(2)}, u32[]{:S(2)}) collective-permute-start(bf16[528,128]{1,0:T(8,128)(2,1)S(1)} %get-tuple-element.75), channel_id=1, source_target_pairs={{0,96},{8,104},{16,112},{24,120},{1,97},{9,105},{17,113},{25,121},... | collective-permute-start | bytes 405512 | tf_op jit(solution)/shard_map/ppermute | solution.py:43
  83.0 3.3 %collective-permute-start.19 = (bf16[64,6144]{1,0:T(8,128)(2,1)S(1)}, bf16[64,6144]{1,0:T(8,128)(2,1)S(1)}, u32[]{:S(2)}, u32[]{:S(2)}) collective-permute-start(bf16[64,6144]{1,0:T(8,128)(2,1)S(1)} %get-tuple-element.82), channel_id=1, source_target_pairs={{0,1},{1,0},{2,3},{3,2},{4,5},{5,4},{6,7},{7,6},{8,9},{9,8},{10,11... | collective-permute-start | bytes 2359304 | tf_op jit(solution)/shard_map/ppermute | solution.py:35
  86.5 4.0 %collective-permute-start.20 = (bf16[64,6144]{1,0:T(8,128)(2,1)S(1)}, bf16[64,6144]{1,0:T(8,128)(2,1)S(1)}, u32[]{:S(2)}, u32[]{:S(2)}) collective-permute-start(bf16[64,6144]{1,0:T(8,128)(2,1)S(1)} %get-tuple-element.85), channel_id=1, source_target_pairs={{0,1},{1,0},{2,3},{3,2},{4,5},{5,4},{6,7},{7,6},{8,9},{9,8},{10,11... | collective-permute-start | bytes 2359304 | tf_op jit(solution)/shard_map/ppermute | solution.py:35
  86.6 4.1 %collective-permute-start.21 = (bf16[64,6144]{1,0:T(8,128)(2,1)S(1)}, bf16[64,6144]{1,0:T(8,128)(2,1)S(1)}, u32[]{:S(2)}, u32[]{:S(2)}) collective-permute-start(bf16[64,6144]{1,0:T(8,128)(2,1)S(1)} %get-tuple-element.87), channel_id=1, source_target_pairs={{0,1},{1,0},{2,3},{3,2},{4,5},{5,4},{6,7},{7,6},{8,9},{9,8},{10,11... | collective-permute-start | bytes 2359304 | tf_op jit(solution)/shard_map/ppermute | solution.py:35
  87.1 12.8 %collective-permute-start.25 = (bf16[64,3072]{1,0:T(8,128)(2,1)S(1)}, bf16[64,3072]{1,0:T(8,128)(2,1)S(1)}, u32[]{:S(2)}, u32[]{:S(2)}) collective-permute-start(bf16[64,3072]{1,0:T(8,128)(2,1)S(1)} %get-tuple-element.96), channel_id=1, source_target_pairs={{0,2},{1,3},{2,4},{3,5},{4,6},{5,7},{6,0},{7,1},{8,10},{9,11},{10,... | collective-permute-start | bytes 1179656 | tf_op jit(solution)/shard_map/ppermute | solution.py:31
  88.3 11.6 %collective-permute-start.26 = (bf16[64,3072]{1,0:T(8,128)(2,1)S(1)}, bf16[64,3072]{1,0:T(8,128)(2,1)S(1)}, u32[]{:S(2)}, u32[]{:S(2)}) collective-permute-start(bf16[64,3072]{1,0:T(8,128)(2,1)S(1)} %get-tuple-element.95), channel_id=1, source_target_pairs={{0,6},{1,7},{2,0},{3,1},{4,2},{5,3},{6,4},{7,5},{8,14},{9,15},{10,... | collective-permute-start | bytes 1179656 | tf_op jit(solution)/shard_map/ppermute | solution.py:31
  90.7 17.7 %collective-permute-start.23 = (bf16[64,3072]{1,0:T(8,128)(2,1)S(1)}, bf16[64,3072]{1,0:T(8,128)(2,1)S(1)}, u32[]{:S(2)}, u32[]{:S(2)}) collective-permute-start(bf16[64,3072]{1,0:T(8,128)(2,1)S(1)} %add_convert_fusion.3), channel_id=1, source_target_pairs={{0,2},{1,3},{2,4},{3,5},{4,6},{5,7},{6,0},{7,1},{8,10},{9,11},{10,... | collective-permute-start | bytes 1179656 | tf_op jit(solution)/shard_map/ppermute | solution.py:31
  90.8 17.5 %collective-permute-start.24 = (bf16[64,3072]{1,0:T(8,128)(2,1)S(1)}, bf16[64,3072]{1,0:T(8,128)(2,1)S(1)}, u32[]{:S(2)}, u32[]{:S(2)}) collective-permute-start(bf16[64,3072]{1,0:T(8,128)(2,1)S(1)} %add_convert_fusion.2), channel_id=1, source_target_pairs={{0,6},{1,7},{2,0},{3,1},{4,2},{5,3},{6,4},{7,5},{8,14},{9,15},{10,... | collective-permute-start | bytes 1179656 | tf_op jit(solution)/shard_map/ppermute | solution.py:31
  94.9 13.5 %collective-permute-start.22 = (bf16[64,6144]{1,0:T(8,128)(2,1)S(1)}, bf16[64,6144]{1,0:T(8,128)(2,1)S(1)}, u32[]{:S(2)}, u32[]{:S(2)}) collective-permute-start(bf16[64,6144]{1,0:T(8,128)(2,1)S(1)} %get-tuple-element.90), channel_id=1, source_target_pairs={{0,1},{1,0},{2,3},{3,2},{4,5},{5,4},{6,7},{7,6},{8,9},{9,8},{10,11... | collective-permute-start | bytes 2359304 | tf_op jit(solution)/shard_map/ppermute | solution.py:35
  100.1 16.7 %collective-permute-start.27 = (bf16[64,3072]{1,0:T(8,128)(2,1)S(1)}, bf16[64,3072]{1,0:T(8,128)(2,1)S(1)}, u32[]{:S(2)}, u32[]{:S(2)}) collective-permute-start(bf16[64,3072]{1,0:T(8,128)(2,1)S(1)} %add_convert_fusion.1), channel_id=1, source_target_pairs={{0,2},{1,3},{2,4},{3,5},{4,6},{5,7},{6,0},{7,1},{8,10},{9,11},{10,... | collective-permute-start | bytes 1179656 | tf_op jit(solution)/shard_map/ppermute | solution.py:31
  101.0 15.8 %collective-permute-start.28 = (bf16[64,3072]{1,0:T(8,128)(2,1)S(1)}, bf16[64,3072]{1,0:T(8,128)(2,1)S(1)}, u32[]{:S(2)}, u32[]{:S(2)}) collective-permute-start(bf16[64,3072]{1,0:T(8,128)(2,1)S(1)} %add_convert_fusion), channel_id=1, source_target_pairs={{0,6},{1,7},{2,0},{3,1},{4,2},{5,3},{6,4},{7,5},{8,14},{9,15},{10,... | collective-permute-start | bytes 1179656 | tf_op jit(solution)/shard_map/ppermute | solution.py:31
Sparse Core Ops, SparseCore 0:
  9.5 70.1 all-gather.2

commit v10 on v9

--- a/solution.py
+++ b/solution.py
@@ -205,14 +205,14 @@
 
 
 def project_first_kernel(normed, w, own, sib, held, sems):
-    per = w.shape[0] // 4
+    per = w.shape[0] // 2
     copies = [
-        pltpu.make_async_copy(w.at[pl.ds(i * per, per)], held.at[pl.ds(i * per, per)], sems.at[i]) for i in range(4)
+        pltpu.make_async_copy(w.at[pl.ds(i * per, per)], held.at[pl.ds(i * per, per)], sems.at[i]) for i in range(2)
     ]
     for copy in copies:
         copy.start()
     far = normed[FAR : FAR + 128, :]
-    for i in range(4):
+    for i in range(2):
         copies[i].wait()
         for m in range(i * per, (i + 1) * per):
             project_part(far, held, (own, sib), m)
@@ -333,7 +333,7 @@
         out_shape=[half, half, pltpu.VMEM(w_all.shape, bf16)],
         in_specs=[vmem, pl.BlockSpec(memory_space=pltpu.HBM)],
         out_specs=[vmem] * 3,
-        scratch_shapes=[pltpu.SemaphoreType.DMA((4,))],
+        scratch_shapes=[pltpu.SemaphoreType.DMA((2,))],
         compiler_params=params(),
         cost_estimate=cost(256 * w_all.size, 2 * w_all.size),
         name="project",

time: 125 us -> 125 us (level)
  no operation moved by 1% of the time
where the time goes in v10:
time: 125 us
  starting transfers between devices  39.7 us (32%)
  waiting for transfers between devices  36.5 us (29%)
  Pallas kernels  27.3 us (22%)
  between operations  13.7 us (11%)
  local copies, waits for them, and re-layouts  4.77 us (4%)
  other arithmetic  2.94 us (2%)
    ppermute x12, waiting for transfers between devices, to_y(): lax.ppermute(a, 'tp', [(i, (i // 2 + k) % N_Y * 2 + i % 2) for i in range...  23.4 us
    ppermute x12, starting transfers between devices, to_y(): lax.ppermute(a, 'tp', [(i, (i // 2 + k) % N_Y * 2 + i % 2) for i in range...  16.5 us
    pallas_call x4, Pallas kernels, qkv(): pl.pallas_call(functools.partial(qkv_first_kernel if first else qkv_kerne...  15.1 us
    ppermute x3, starting transfers between devices, to_z(): lax.ppermute(a, 'ctx', [(j, j + N_X * k) for j in range(N_X * N_Z) if j /...  9.34 us
    ppermute x3, waiting for transfers between devices, to_x(): lax.ppermute(a, 'ctx', [(j, j // N_X * N_X + (j + k) % N_X) for j in rang...  8.62 us
    ppermute x11, starting transfers between devices, to_sibling(): return lax.ppermute(a, 'tp', [(i, i ^ 1) for i in range(2 * N_Y)])  8.37 us
    ppermute x3, starting transfers between devices, to_x(): lax.ppermute(a, 'ctx', [(j, j // N_X * N_X + (j + k) % N_X) for j in rang...  5.53 us
    pallas_call x6, Pallas kernels, whole_call(): pl.pallas_call(kernel, out_shape=outs, in_specs=[pl.BlockSpec(memory_spac...  4.96 us
  transfers between devices with their start and end apart: 30, of which 12 were waited for; matrix products, arithmetic and copies ran while one was open for 5% of the time, Pallas kernels for 18%

profile of v10, /device:TPU:1, one launch (start us, length us, event | category | flops | bytes accessed | tf_op | source)
XLA Modules:
  0.0 124.9 jit_solution(3303764476415502910)
XLA Ops:
  6.5 0.7 all-gather.3.cloned.1.call-update
  7.3 1.5 %collective-permute-start.3 = (bf16[64,6144]{1,0:T(8,128)(2,1)}, bf16[64,6144]{1,0:T(8,128)(2,1)S(1)}, u32[]{:S(2)}, u32[]{:S(2)}) collective-permute-start(bf16[64,6144]{1,0:T(8,128)(2,1)} %refs_0_.1), channel_id=1, source_target_pairs={{0,1},{1,0},{2,3},{3,2},{4,5},{5,4},{6,7},{7,6},{8,9},{9,8},{10,11... | collective-permute-start | bytes 2359304 | tf_op jit(solution)/shard_map/ppermute | solution.py:35
  8.8 1.0 slice.75
  9.8 1.4 %collective-permute-start.1 = (bf16[64,3072]{1,0:T(8,128)(2,1)S(1)}, bf16[64,3072]{1,0:T(8,128)(2,1)S(1)}, u32[]{:S(2)}, u32[]{:S(2)}) collective-permute-start(bf16[64,3072]{1,0:T(8,128)(2,1)S(1)} %slice.75), channel_id=1, source_target_pairs={{0,2},{1,3},{2,4},{3,5},{4,6},{5,7},{6,0},{7,1},{8,10},{9,11},{10,... | collective-permute-start | bytes 1179656 | tf_op jit(solution)/shard_map/ppermute | solution.py:31
  11.2 1.0 slice.76
  12.3 1.5 %collective-permute-start.2 = (bf16[64,3072]{1,0:T(8,128)(2,1)S(1)}, bf16[64,3072]{1,0:T(8,128)(2,1)S(1)}, u32[]{:S(2)}, u32[]{:S(2)}) collective-permute-start(bf16[64,3072]{1,0:T(8,128)(2,1)S(1)} %slice.76), channel_id=1, source_target_pairs={{0,6},{1,7},{2,0},{3,1},{4,2},{5,3},{6,4},{7,5},{8,14},{9,15},{10,... | collective-permute-start | bytes 1179656 | tf_op jit(solution)/shard_map/ppermute | solution.py:31
  14.5 1.2 reduce-window.6
  17.6 1.5 %collective-permute-start = (bf16[64,3072]{1,0:T(8,128)(2,1)S(1)}, bf16[64,3072]{1,0:T(8,128)(2,1)S(1)}, u32[]{:S(2)}, u32[]{:S(2)}) collective-permute-start(bf16[64,3072]{1,0:T(8,128)(2,1)S(1)} %slice.75), channel_id=1, source_target_pairs={{0,6},{1,7},{2,0},{3,1},{4,2},{5,3},{6,4},{7,5},{8,14},{9,15},{10,... | collective-permute-start | bytes 1179656 | tf_op jit(solution)/shard_map/ppermute | solution.py:31
  19.0 1.1 copy-done
  20.2 7.3 %qkv.4 = (bf16[128,1536]{1,0:T(8,128)(2,1)S(1)}, bf16[3,6144,512]{2,1,0:T(8,128)(2,1)S(1)}) custom-call(bf16[64,6144]{1,0:T(8,128)(2,1)S(1)} %copy-done, bf16[64,6144]{1,0:T(8,128)(2,1)S(1)} %collective-permute-done.3.refs_1_, bf16[3,6144,512]{2,1,0:T(8,128)(2,1)} %refs_2_.1), custom_call_target="tpu_custom_call" | custom-call | flops 24159192 | bytes 188743 | tf_op jit(solution)/shard_map/qkv/pallas_call | solution.py:97
  27.5 1.1 collective-permute-start.5
  28.8 2.3 %collective-permute-done.refs_0_ = bf16[64,3072]{1,0:T(8,128)(2,1)S(1)} collective-permute-done((bf16[64,3072]{1,0:T(8,128)(2,1)S(1)}, bf16[64,3072]{1,0:T(8,128)(2,1)S(1)}, u32[]{:S(2)}, u32[]{:S(2)}) %collective-permute-start) | collective-permute-done | bytes 393248 | tf_op jit(solution)/shard_map/ppermute | solution.py:31
  31.2 2.8 %collective-permute-start.10 = (bf16[64,3072]{1,0:T(8,128)(2,1)S(1)}, bf16[64,3072]{1,0:T(8,128)(2,1)S(1)}, u32[]{:S(2)}, u32[]{:S(2)}) collective-permute-start(bf16[64,3072]{1,0:T(8,128)(2,1)S(1)} %collective-permute-done.2.refs_1_), channel_id=1, source_target_pairs={{0,6},{1,7},{2,0},{3,1},{4,2},{5,3},{6,4},{7,5},{8,14},{9,15},{10,... | collective-permute-start | bytes 1179656 | tf_op jit(solution)/shard_map/ppermute | solution.py:31
  34.0 1.2 collective-permute-start.7
  35.3 2.6 %qkv.5.a = bf16[128,1536]{1,0:T(8,128)(2,1)S(1)} custom-call(bf16[64,3072]{1,0:T(8,128)(2,1)S(1)} %collective-permute-done.refs_0_, bf16[64,3072]{1,0:T(8,128)(2,1)S(1)} %collective-permute-done.2.refs_1_, bf16[64,3072]{1,0:T(8,128)(2,1)S(1)} %collective-permute-done.1.refs_2_, bf16[64,3072]{1,0:T(8,128)(2,1)S(1)} %collective-permute-done.4.refs_3_, ...), custom_call_target="tpu_custom_call" | custom-call | flops 24159192 | bytes 188743 | tf_op jit(solution)/shard_map/qkv/pallas_call | solution.py:97
  37.9 2.5 %collective-permute-done.9.refs_0_ = bf16[64,3072]{1,0:T(8,128)(2,1)S(1)} collective-permute-done((bf16[64,3072]{1,0:T(8,128)(2,1)S(1)}, bf16[64,3072]{1,0:T(8,128)(2,1)S(1)}, u32[]{:S(2)}, u32[]{:S(2)}) %collective-permute-start.9) | collective-permute-done | bytes 393248 | tf_op jit(solution)/shard_map/ppermute | solution.py:31
  40.4 1.0 collective-permute-done.10.refs_1_
  41.5 1.9 %collective-permute-start.11 = (bf16[64,3072]{1,0:T(8,128)(2,1)S(1)}, bf16[64,3072]{1,0:T(8,128)(2,1)S(1)}, u32[]{:S(2)}, u32[]{:S(2)}) collective-permute-start(bf16[64,3072]{1,0:T(8,128)(2,1)S(1)} %collective-permute-done.9.refs_0_), channel_id=1, source_target_pairs={{0,1},{1,0},{2,3},{3,2},{4,5},{5,4},{6,7},{7,6},{8,9},{9,8},{10,11... | collective-permute-start | bytes 1179656 | tf_op jit(solution)/shard_map/ppermute | solution.py:35
  43.3 2.6 %qkv.6.c = bf16[128,1536]{1,0:T(8,128)(2,1)S(1)} custom-call(bf16[64,3072]{1,0:T(8,128)(2,1)S(1)} %collective-permute-done.7.refs_0_, bf16[64,3072]{1,0:T(8,128)(2,1)S(1)} %collective-permute-done.6.refs_1_, bf16[64,3072]{1,0:T(8,128)(2,1)S(1)} %collective-permute-done.5.refs_2_, bf16[64,3072]{1,0:T(8,128)(2,1)S(1)} %collective-permute-done.8.refs_3_, ...), custom_call_target="tpu_custom_call" | custom-call | flops 24159192 | bytes 188743 | tf_op jit(solution)/shard_map/qkv/pallas_call | solution.py:97
  46.0 2.6 %qkv.7.d = bf16[128,1536]{1,0:T(8,128)(2,1)S(1)} custom-call(bf16[64,3072]{1,0:T(8,128)(2,1)S(1)} %collective-permute-done.9.refs_0_, bf16[64,3072]{1,0:T(8,128)(2,1)S(1)} %collective-permute-done.10.refs_1_, bf16[64,3072]{1,0:T(8,128)(2,1)S(1)} %collective-permute-done.11.refs_2_, bf16[64,3072]{1,0:T(8,128)(2,1)S(1)} %collective-permute-done.12.refs_3_, ...), custom_call_target="tpu_custom_call" | custom-call | flops 24159192 | bytes 188743 | tf_op jit(solution)/shard_map/qkv/pallas_call | solution.py:97
  48.6 1.0 state.1.s0
  49.6 2.9 %collective-permute-start.13 = (bf16[528,128]{1,0:T(8,128)(2,1)S(1)}, bf16[528,128]{1,0:T(8,128)(2,1)S(1)}, u32[]{:S(2)}, u32[]{:S(2)}) collective-permute-start(bf16[528,128]{1,0:T(8,128)(2,1)S(1)} %state.1.s0), channel_id=1, source_target_pairs={{0,16},{8,24},{16,0},{24,8},{32,48},{40,56},{48,32},{56,40},{64,80... | collective-permute-start | bytes 405512 | tf_op jit(solution)/shard_map/ppermute | solution.py:39
  52.8 2.4 %collective-permute-start.15 = (bf16[528,128]{1,0:T(8,128)(2,1)S(1)}, bf16[528,128]{1,0:T(8,128)(2,1)S(1)}, u32[]{:S(2)}, u32[]{:S(2)}) collective-permute-start(bf16[528,128]{1,0:T(8,128)(2,1)S(1)} %state.1.s0), channel_id=1, source_target_pairs={{0,24},{8,0},{16,8},{24,16},{32,56},{40,32},{48,40},{56,48},{64,88... | collective-permute-start | bytes 405512 | tf_op jit(solution)/shard_map/ppermute | solution.py:39
  55.3 1.4 %inner.1 = f32[512,512]{1,0:T(8,128)S(1)} custom-call(bf16[128,1536]{1,0:T(8,128)(2,1)S(1)} %qkv.5.a, bf16[128,1536]{1,0:T(8,128)(2,1)S(1)} %get-tuple-element.53.b, bf16[128,1536]{1,0:T(8,128)(2,1)S(1)} %qkv.6.c, bf16[128,1536]{1,0:T(8,128)(2,1)S(1)} %qkv.7.d, f32[512,4]{1,0:T(8,128)S(1)} %bitcast.20, f32[4,512]{1,0:T(4,128)S(1)} %concatenate.8.gt, ...), custom_call_target="tpu_custom_call" | custom-call | flops 5368709 | bytes 15933 | tf_op jit(solution)/shard_map/inner/pallas_call | solution.py:188
  56.8 2.6 %collective-permute-done.13.s2 = bf16[528,128]{1,0:T(8,128)(2,1)S(1)} collective-permute-done((bf16[528,128]{1,0:T(8,128)(2,1)S(1)}, bf16[528,128]{1,0:T(8,128)(2,1)S(1)}, u32[]{:S(2)}, u32[]{:S(2)}) %collective-permute-start.13) | collective-permute-done | bytes 135200 | tf_op jit(solution)/shard_map/ppermute | solution.py:39
  59.4 4.9 %collective-permute-done.14.s1 = bf16[528,128]{1,0:T(8,128)(2,1)S(1)} collective-permute-done((bf16[528,128]{1,0:T(8,128)(2,1)S(1)}, bf16[528,128]{1,0:T(8,128)(2,1)S(1)}, u32[]{:S(2)}, u32[]{:S(2)}) %collective-permute-start.14) | collective-permute-done | bytes 135200 | tf_op jit(solution)/shard_map/ppermute | solution.py:39
  64.2 1.2 collective-permute-done.15.s3
  65.6 5.4 %collective-permute-start.16 = (bf16[528,128]{1,0:T(8,128)(2,1)S(1)}, bf16[528,128]{1,0:T(8,128)(2,1)S(1)}, u32[]{:S(2)}, u32[]{:S(2)}) collective-permute-start(bf16[528,128]{1,0:T(8,128)(2,1)S(1)} %get-tuple-element.75), channel_id=1, source_target_pairs={{0,64},{8,72},{16,80},{24,88},{32,96},{40,104},{48,112},{56,120},{... | collective-permute-start | bytes 405512 | tf_op jit(solution)/shard_map/ppermute | solution.py:43
  71.0 2.6 %collective-permute-start.17 = (bf16[528,128]{1,0:T(8,128)(2,1)S(1)}, bf16[528,128]{1,0:T(8,128)(2,1)S(1)}, u32[]{:S(2)}, u32[]{:S(2)}) collective-permute-start(bf16[528,128]{1,0:T(8,128)(2,1)S(1)} %get-tuple-element.75), channel_id=1, source_target_pairs={{0,32},{8,40},{16,48},{24,56},{32,64},{40,72},{48,80},{56,88},{64,... | collective-permute-start | bytes 405512 | tf_op jit(solution)/shard_map/ppermute | solution.py:43
  73.6 1.3 %collective-permute-start.18 = (bf16[528,128]{1,0:T(8,128)(2,1)S(1)}, bf16[528,128]{1,0:T(8,128)(2,1)S(1)}, u32[]{:S(2)}, u32[]{:S(2)}) collective-permute-start(bf16[528,128]{1,0:T(8,128)(2,1)S(1)} %get-tuple-element.75), channel_id=1, source_target_pairs={{0,96},{8,104},{16,112},{24,120},{1,97},{9,105},{17,113},{25,121},... | collective-permute-start | bytes 405512 | tf_op jit(solution)/shard_map/ppermute | solution.py:43
  74.9 1.1 collective-permute-done.17.t1
  76.1 1.0 collective-permute-done.18.t3
  77.1 1.0 normed.1
  78.1 1.5 %all-gather.3.cloned.1.call-done = bf16[8192,384]{1,0:T(8,128)(2,1)} async-done(((bf16[512,384]{1,0:T(8,128)(2,1)}), bf16[8192,384]{1,0:T(8,128)(2,1)}) %all-gather.3.cloned.1.call-update) | async-done | bytes 6291472 | tf_op jit(solution)/shard_map/all_gather | solution.py:271
  79.7 3.6 %project.3 = (bf16[64,6144]{1,0:T(8,128)(2,1)S(1)}, bf16[64,6144]{1,0:T(8,128)(2,1)S(1)}, bf16[16,512,384]{2,1,0:T(8,128)(2,1)S(1)}) custom-call(bf16[512,512]{1,0:T(8,128)(2,1)S(1)} %normed.1, bf16[16,512,384]{2,1,0:T(8,128)(2,1)} %bitcast.25), custom_call_target="tpu_custom_call" | custom-call | flops 8053063 | bytes 62914 | tf_op jit(solution)/shard_map/project/pallas_call | solution.py:331
  83.3 1.0 collective-permute-start.19
  84.3 2.3 %project.4 = (bf16[64,6144]{1,0:T(8,128)(2,1)S(1)}, bf16[64,6144]{1,0:T(8,128)(2,1)S(1)}, bf16[64,6144]{1,0:T(8,128)(2,1)S(1)}, bf16[64,6144]{1,0:T(8,128)(2,1)S(1)}) custom-call(bf16[512,512]{1,0:T(8,128)(2,1)S(1)} %normed.1, bf16[16,512,384]{2,1,0:T(8,128)(2,1)S(1)} %get-tuple-element.76.w), custom_call_target="tpu_custom_call" | custom-call | flops 16106127 | bytes 62914 | tf_op jit(solution)/shard_map/project/pallas_call | solution.py:231
  87.4 1.2 collective-permute-start.25
  88.6 2.2 %collective-permute-start.26 = (bf16[64,3072]{1,0:T(8,128)(2,1)S(1)}, bf16[64,3072]{1,0:T(8,128)(2,1)S(1)}, u32[]{:S(2)}, u32[]{:S(2)}) collective-permute-start(bf16[64,3072]{1,0:T(8,128)(2,1)S(1)} %get-tuple-element.95), channel_id=1, source_target_pairs={{0,6},{1,7},{2,0},{3,1},{4,2},{5,3},{6,4},{7,5},{8,14},{9,15},{10,... | collective-permute-start | bytes 1179656 | tf_op jit(solution)/shard_map/ppermute | solution.py:31
  91.1 2.8 %collective-permute-start.24 = (bf16[64,3072]{1,0:T(8,128)(2,1)S(1)}, bf16[64,3072]{1,0:T(8,128)(2,1)S(1)}, u32[]{:S(2)}, u32[]{:S(2)}) collective-permute-start(bf16[64,3072]{1,0:T(8,128)(2,1)S(1)} %add_convert_fusion.2), channel_id=1, source_target_pairs={{0,6},{1,7},{2,0},{3,1},{4,2},{5,3},{6,4},{7,5},{8,14},{9,15},{10,... | collective-permute-start | bytes 1179656 | tf_op jit(solution)/shard_map/ppermute | solution.py:31
  93.9 1.2 project.5
  95.1 1.0 collective-permute-start.22
  96.1 4.1 %collective-permute-done.25 = bf16[64,3072]{1,0:T(8,128)(2,1)S(1)} collective-permute-done((bf16[64,3072]{1,0:T(8,128)(2,1)S(1)}, bf16[64,3072]{1,0:T(8,128)(2,1)S(1)}, u32[]{:S(2)}, u32[]{:S(2)}) %collective-permute-start.25) | collective-permute-done | bytes 393248 | tf_op jit(solution)/shard_map/ppermute | solution.py:31
  100.4 0.7 collective-permute-start.27
  101.2 2.1 %collective-permute-start.28 = (bf16[64,3072]{1,0:T(8,128)(2,1)S(1)}, bf16[64,3072]{1,0:T(8,128)(2,1)S(1)}, u32[]{:S(2)}, u32[]{:S(2)}) collective-permute-start(bf16[64,3072]{1,0:T(8,128)(2,1)S(1)} %add_convert_fusion), channel_id=1, source_target_pairs={{0,6},{1,7},{2,0},{3,1},{4,2},{5,3},{6,4},{7,5},{8,14},{9,15},{10,... | collective-permute-start | bytes 1179656 | tf_op jit(solution)/shard_map/ppermute | solution.py:31
  103.3 5.3 %collective-permute-done.23.up_plain = bf16[64,3072]{1,0:T(8,128)(2,1)S(1)} collective-permute-done((bf16[64,3072]{1,0:T(8,128)(2,1)S(1)}, bf16[64,3072]{1,0:T(8,128)(2,1)S(1)}, u32[]{:S(2)}, u32[]{:S(2)}) %collective-permute-start.23) | collective-permute-done | bytes 393248 | tf_op jit(solution)/shard_map/ppermute | solution.py:31
  108.9 8.2 %collective-permute-done.27.up_sum = bf16[64,3072]{1,0:T(8,128)(2,1)S(1)} collective-permute-done((bf16[64,3072]{1,0:T(8,128)(2,1)S(1)}, bf16[64,3072]{1,0:T(8,128)(2,1)S(1)}, u32[]{:S(2)}, u32[]{:S(2)}) %collective-permute-start.27) | collective-permute-done | bytes 393248 | tf_op jit(solution)/shard_map/ppermute | solution.py:31
  117.1 1.0 final.1
  (54 shorter events, 5.2 us)
Async XLA Ops:
  6.5 73.2 %all-gather.3.cloned.1.call-start = ((), (), s32[]{:S(2)}) async-start(), calls=%async_computation | async-start | bytes 6684672 | tf_op jit(solution)/shard_map/all_gather | solution.py:271
  7.3 11.8 %collective-permute-start.3 = (bf16[64,6144]{1,0:T(8,128)(2,1)}, bf16[64,6144]{1,0:T(8,128)(2,1)S(1)}, u32[]{:S(2)}, u32[]{:S(2)}) collective-permute-start(bf16[64,6144]{1,0:T(8,128)(2,1)} %refs_0_.1), channel_id=1, source_target_pairs={{0,1},{1,0},{2,3},{3,2},{4,5},{5,4},{6,7},{7,6},{8,9},{9,8},{10,11... | collective-permute-start | bytes 2359304 | tf_op jit(solution)/shard_map/ppermute | solution.py:35
  9.8 17.7 %collective-permute-start.1 = (bf16[64,3072]{1,0:T(8,128)(2,1)S(1)}, bf16[64,3072]{1,0:T(8,128)(2,1)S(1)}, u32[]{:S(2)}, u32[]{:S(2)}) collective-permute-start(bf16[64,3072]{1,0:T(8,128)(2,1)S(1)} %slice.75), channel_id=1, source_target_pairs={{0,2},{1,3},{2,4},{3,5},{4,6},{5,7},{6,0},{7,1},{8,10},{9,11},{10,... | collective-permute-start | bytes 1179656 | tf_op jit(solution)/shard_map/ppermute | solution.py:31
  12.3 15.3 %collective-permute-start.2 = (bf16[64,3072]{1,0:T(8,128)(2,1)S(1)}, bf16[64,3072]{1,0:T(8,128)(2,1)S(1)}, u32[]{:S(2)}, u32[]{:S(2)}) collective-permute-start(bf16[64,3072]{1,0:T(8,128)(2,1)S(1)} %slice.76), channel_id=1, source_target_pairs={{0,6},{1,7},{2,0},{3,1},{4,2},{5,3},{6,4},{7,5},{8,14},{9,15},{10,... | collective-permute-start | bytes 1179656 | tf_op jit(solution)/shard_map/ppermute | solution.py:31
  17.6 13.6 %collective-permute-start = (bf16[64,3072]{1,0:T(8,128)(2,1)S(1)}, bf16[64,3072]{1,0:T(8,128)(2,1)S(1)}, u32[]{:S(2)}, u32[]{:S(2)}) collective-permute-start(bf16[64,3072]{1,0:T(8,128)(2,1)S(1)} %slice.75), channel_id=1, source_target_pairs={{0,6},{1,7},{2,0},{3,1},{4,2},{5,3},{6,4},{7,5},{8,14},{9,15},{10,... | collective-permute-start | bytes 1179656 | tf_op jit(solution)/shard_map/ppermute | solution.py:31
  19.0 15.0 %collective-permute-start.4 = (bf16[64,3072]{1,0:T(8,128)(2,1)S(1)}, bf16[64,3072]{1,0:T(8,128)(2,1)S(1)}, u32[]{:S(2)}, u32[]{:S(2)}) collective-permute-start(bf16[64,3072]{1,0:T(8,128)(2,1)S(1)} %slice.76), channel_id=1, source_target_pairs={{0,2},{1,3},{2,4},{3,5},{4,6},{5,7},{6,0},{7,1},{8,10},{9,11},{10,... | collective-permute-start | bytes 1179656 | tf_op jit(solution)/shard_map/ppermute | solution.py:31
  19.0 1.1 copy-start
  27.5 7.7 %collective-permute-start.5 = (bf16[64,3072]{1,0:T(8,128)(2,1)S(1)}, bf16[64,3072]{1,0:T(8,128)(2,1)S(1)}, u32[]{:S(2)}, u32[]{:S(2)}) collective-permute-start(bf16[64,3072]{1,0:T(8,128)(2,1)S(1)} %collective-permute-done.1.refs_2_), channel_id=1, source_target_pairs={{0,1},{1,0},{2,3},{3,2},{4,5},{5,4},{6,7},{7,6},{8,9},{9,8},{10,11... | collective-permute-start | bytes 1179656 | tf_op jit(solution)/shard_map/ppermute | solution.py:35
  28.6 6.7 %collective-permute-start.6 = (bf16[64,3072]{1,0:T(8,128)(2,1)S(1)}, bf16[64,3072]{1,0:T(8,128)(2,1)S(1)}, u32[]{:S(2)}, u32[]{:S(2)}) collective-permute-start(bf16[64,3072]{1,0:T(8,128)(2,1)S(1)} %collective-permute-done.2.refs_1_), channel_id=1, source_target_pairs={{0,1},{1,0},{2,3},{3,2},{4,5},{5,4},{6,7},{7,6},{8,9},{9,8},{10,11... | collective-permute-start | bytes 1179656 | tf_op jit(solution)/shard_map/ppermute | solution.py:35
  28.7 11.8 %collective-permute-start.9 = (bf16[64,3072]{1,0:T(8,128)(2,1)S(1)}, bf16[64,3072]{1,0:T(8,128)(2,1)S(1)}, u32[]{:S(2)}, u32[]{:S(2)}) collective-permute-start(bf16[64,3072]{1,0:T(8,128)(2,1)S(1)} %collective-permute-done.1.refs_2_), channel_id=1, source_target_pairs={{0,2},{1,3},{2,4},{3,5},{4,6},{5,7},{6,0},{7,1},{8,10},{9,11},{10,... | collective-permute-start | bytes 1179656 | tf_op jit(solution)/shard_map/ppermute | solution.py:31
  31.2 10.3 %collective-permute-start.10 = (bf16[64,3072]{1,0:T(8,128)(2,1)S(1)}, bf16[64,3072]{1,0:T(8,128)(2,1)S(1)}, u32[]{:S(2)}, u32[]{:S(2)}) collective-permute-start(bf16[64,3072]{1,0:T(8,128)(2,1)S(1)} %collective-permute-done.2.refs_1_), channel_id=1, source_target_pairs={{0,6},{1,7},{2,0},{3,1},{4,2},{5,3},{6,4},{7,5},{8,14},{9,15},{10,... | collective-permute-start | bytes 1179656 | tf_op jit(solution)/shard_map/ppermute | solution.py:31
  34.0 9.3 %collective-permute-start.7 = (bf16[64,3072]{1,0:T(8,128)(2,1)S(1)}, bf16[64,3072]{1,0:T(8,128)(2,1)S(1)}, u32[]{:S(2)}, u32[]{:S(2)}) collective-permute-start(bf16[64,3072]{1,0:T(8,128)(2,1)S(1)} %collective-permute-done.refs_0_), channel_id=1, source_target_pairs={{0,1},{1,0},{2,3},{3,2},{4,5},{5,4},{6,7},{7,6},{8,9},{9,8},{10,11... | collective-permute-start | bytes 1179656 | tf_op jit(solution)/shard_map/ppermute | solution.py:35
  35.2 8.1 %collective-permute-start.8 = (bf16[64,3072]{1,0:T(8,128)(2,1)S(1)}, bf16[64,3072]{1,0:T(8,128)(2,1)S(1)}, u32[]{:S(2)}, u32[]{:S(2)}) collective-permute-start(bf16[64,3072]{1,0:T(8,128)(2,1)S(1)} %collective-permute-done.4.refs_3_), channel_id=1, source_target_pairs={{0,1},{1,0},{2,3},{3,2},{4,5},{5,4},{6,7},{7,6},{8,9},{9,8},{10,11... | collective-permute-start | bytes 1179656 | tf_op jit(solution)/shard_map/ppermute | solution.py:35
  41.5 4.5 %collective-permute-start.11 = (bf16[64,3072]{1,0:T(8,128)(2,1)S(1)}, bf16[64,3072]{1,0:T(8,128)(2,1)S(1)}, u32[]{:S(2)}, u32[]{:S(2)}) collective-permute-start(bf16[64,3072]{1,0:T(8,128)(2,1)S(1)} %collective-permute-done.9.refs_0_), channel_id=1, source_target_pairs={{0,1},{1,0},{2,3},{3,2},{4,5},{5,4},{6,7},{7,6},{8,9},{9,8},{10,11... | collective-permute-start | bytes 1179656 | tf_op jit(solution)/shard_map/ppermute | solution.py:35
  43.3 2.7 %collective-permute-start.12 = (bf16[64,3072]{1,0:T(8,128)(2,1)S(1)}, bf16[64,3072]{1,0:T(8,128)(2,1)S(1)}, u32[]{:S(2)}, u32[]{:S(2)}) collective-permute-start(bf16[64,3072]{1,0:T(8,128)(2,1)S(1)} %collective-permute-done.10.refs_1_), channel_id=1, source_target_pairs={{0,1},{1,0},{2,3},{3,2},{4,5},{5,4},{6,7},{7,6},{8,9},{9,8},{10,11... | collective-permute-start | bytes 1179656 | tf_op jit(solution)/shard_map/ppermute | solution.py:35
  46.0 31.1 %copy-start.1 = (f32[512]{0:T(512)S(1)}, f32[512]{0:T(512)}, u32[]{:S(2)}) copy-start(f32[512]{0:T(512)} %param.10) | copy-start | bytes 6148
  49.6 9.7 %collective-permute-start.13 = (bf16[528,128]{1,0:T(8,128)(2,1)S(1)}, bf16[528,128]{1,0:T(8,128)(2,1)S(1)}, u32[]{:S(2)}, u32[]{:S(2)}) collective-permute-start(bf16[528,128]{1,0:T(8,128)(2,1)S(1)} %state.1.s0), channel_id=1, source_target_pairs={{0,16},{8,24},{16,0},{24,8},{32,48},{40,56},{48,32},{56,40},{64,80... | collective-permute-start | bytes 405512 | tf_op jit(solution)/shard_map/ppermute | solution.py:39
  52.5 11.7 %collective-permute-start.14 = (bf16[528,128]{1,0:T(8,128)(2,1)S(1)}, bf16[528,128]{1,0:T(8,128)(2,1)S(1)}, u32[]{:S(2)}, u32[]{:S(2)}) collective-permute-start(bf16[528,128]{1,0:T(8,128)(2,1)S(1)} %state.1.s0), channel_id=1, source_target_pairs={{0,8},{8,16},{16,24},{24,0},{32,40},{40,48},{48,56},{56,32},{64,72... | collective-permute-start | bytes 405512 | tf_op jit(solution)/shard_map/ppermute | solution.py:39
  52.8 12.6 %collective-permute-start.15 = (bf16[528,128]{1,0:T(8,128)(2,1)S(1)}, bf16[528,128]{1,0:T(8,128)(2,1)S(1)}, u32[]{:S(2)}, u32[]{:S(2)}) collective-permute-start(bf16[528,128]{1,0:T(8,128)(2,1)S(1)} %state.1.s0), channel_id=1, source_target_pairs={{0,24},{8,0},{16,8},{24,16},{32,56},{40,32},{48,40},{56,48},{64,88... | collective-permute-start | bytes 405512 | tf_op jit(solution)/shard_map/ppermute | solution.py:39
  65.6 9.4 %collective-permute-start.16 = (bf16[528,128]{1,0:T(8,128)(2,1)S(1)}, bf16[528,128]{1,0:T(8,128)(2,1)S(1)}, u32[]{:S(2)}, u32[]{:S(2)}) collective-permute-start(bf16[528,128]{1,0:T(8,128)(2,1)S(1)} %get-tuple-element.75), channel_id=1, source_target_pairs={{0,64},{8,72},{16,80},{24,88},{32,96},{40,104},{48,112},{56,120},{... | collective-permute-start | bytes 405512 | tf_op jit(solution)/shard_map/ppermute | solution.py:43
  71.0 5.1 %collective-permute-start.17 = (bf16[528,128]{1,0:T(8,128)(2,1)S(1)}, bf16[528,128]{1,0:T(8,128)(2,1)S(1)}, u32[]{:S(2)}, u32[]{:S(2)}) collective-permute-start(bf16[528,128]{1,0:T(8,128)(2,1)S(1)} %get-tuple-element.75), channel_id=1, source_target_pairs={{0,32},{8,40},{16,48},{24,56},{32,64},{40,72},{48,80},{56,88},{64,... | collective-permute-start | bytes 405512 | tf_op jit(solution)/shard_map/ppermute | solution.py:43
  73.6 3.5 %collective-permute-start.18 = (bf16[528,128]{1,0:T(8,128)(2,1)S(1)}, bf16[528,128]{1,0:T(8,128)(2,1)S(1)}, u32[]{:S(2)}, u32[]{:S(2)}) collective-permute-start(bf16[528,128]{1,0:T(8,128)(2,1)S(1)} %get-tuple-element.75), channel_id=1, source_target_pairs={{0,96},{8,104},{16,112},{24,120},{1,97},{9,105},{17,113},{25,121},... | collective-permute-start | bytes 405512 | tf_op jit(solution)/shard_map/ppermute | solution.py:43
  83.3 3.3 %collective-permute-start.19 = (bf16[64,6144]{1,0:T(8,128)(2,1)S(1)}, bf16[64,6144]{1,0:T(8,128)(2,1)S(1)}, u32[]{:S(2)}, u32[]{:S(2)}) collective-permute-start(bf16[64,6144]{1,0:T(8,128)(2,1)S(1)} %get-tuple-element.82), channel_id=1, source_target_pairs={{0,1},{1,0},{2,3},{3,2},{4,5},{5,4},{6,7},{7,6},{8,9},{9,8},{10,11... | collective-permute-start | bytes 2359304 | tf_op jit(solution)/shard_map/ppermute | solution.py:35
  86.8 4.0 %collective-permute-start.20 = (bf16[64,6144]{1,0:T(8,128)(2,1)S(1)}, bf16[64,6144]{1,0:T(8,128)(2,1)S(1)}, u32[]{:S(2)}, u32[]{:S(2)}) collective-permute-start(bf16[64,6144]{1,0:T(8,128)(2,1)S(1)} %get-tuple-element.85), channel_id=1, source_target_pairs={{0,1},{1,0},{2,3},{3,2},{4,5},{5,4},{6,7},{7,6},{8,9},{9,8},{10,11... | collective-permute-start | bytes 2359304 | tf_op jit(solution)/shard_map/ppermute | solution.py:35
  86.9 4.1 %collective-permute-start.21 = (bf16[64,6144]{1,0:T(8,128)(2,1)S(1)}, bf16[64,6144]{1,0:T(8,128)(2,1)S(1)}, u32[]{:S(2)}, u32[]{:S(2)}) collective-permute-start(bf16[64,6144]{1,0:T(8,128)(2,1)S(1)} %get-tuple-element.87), channel_id=1, source_target_pairs={{0,1},{1,0},{2,3},{3,2},{4,5},{5,4},{6,7},{7,6},{8,9},{9,8},{10,11... | collective-permute-start | bytes 2359304 | tf_op jit(solution)/shard_map/ppermute | solution.py:35
  87.4 12.8 %collective-permute-start.25 = (bf16[64,3072]{1,0:T(8,128)(2,1)S(1)}, bf16[64,3072]{1,0:T(8,128)(2,1)S(1)}, u32[]{:S(2)}, u32[]{:S(2)}) collective-permute-start(bf16[64,3072]{1,0:T(8,128)(2,1)S(1)} %get-tuple-element.96), channel_id=1, source_target_pairs={{0,2},{1,3},{2,4},{3,5},{4,6},{5,7},{6,0},{7,1},{8,10},{9,11},{10,... | collective-permute-start | bytes 1179656 | tf_op jit(solution)/shard_map/ppermute | solution.py:31
  88.6 11.6 %collective-permute-start.26 = (bf16[64,3072]{1,0:T(8,128)(2,1)S(1)}, bf16[64,3072]{1,0:T(8,128)(2,1)S(1)}, u32[]{:S(2)}, u32[]{:S(2)}) collective-permute-start(bf16[64,3072]{1,0:T(8,128)(2,1)S(1)} %get-tuple-element.95), channel_id=1, source_target_pairs={{0,6},{1,7},{2,0},{3,1},{4,2},{5,3},{6,4},{7,5},{8,14},{9,15},{10,... | collective-permute-start | bytes 1179656 | tf_op jit(solution)/shard_map/ppermute | solution.py:31
  90.9 17.7 %collective-permute-start.23 = (bf16[64,3072]{1,0:T(8,128)(2,1)S(1)}, bf16[64,3072]{1,0:T(8,128)(2,1)S(1)}, u32[]{:S(2)}, u32[]{:S(2)}) collective-permute-start(bf16[64,3072]{1,0:T(8,128)(2,1)S(1)} %add_convert_fusion.3), channel_id=1, source_target_pairs={{0,2},{1,3},{2,4},{3,5},{4,6},{5,7},{6,0},{7,1},{8,10},{9,11},{10,... | collective-permute-start | bytes 1179656 | tf_op jit(solution)/shard_map/ppermute | solution.py:31
  91.1 17.5 %collective-permute-start.24 = (bf16[64,3072]{1,0:T(8,128)(2,1)S(1)}, bf16[64,3072]{1,0:T(8,128)(2,1)S(1)}, u32[]{:S(2)}, u32[]{:S(2)}) collective-permute-start(bf16[64,3072]{1,0:T(8,128)(2,1)S(1)} %add_convert_fusion.2), channel_id=1, source_target_pairs={{0,6},{1,7},{2,0},{3,1},{4,2},{5,3},{6,4},{7,5},{8,14},{9,15},{10,... | collective-permute-start | bytes 1179656 | tf_op jit(solution)/shard_map/ppermute | solution.py:31
  95.1 13.5 %collective-permute-start.22 = (bf16[64,6144]{1,0:T(8,128)(2,1)S(1)}, bf16[64,6144]{1,0:T(8,128)(2,1)S(1)}, u32[]{:S(2)}, u32[]{:S(2)}) collective-permute-start(bf16[64,6144]{1,0:T(8,128)(2,1)S(1)} %get-tuple-element.90), channel_id=1, source_target_pairs={{0,1},{1,0},{2,3},{3,2},{4,5},{5,4},{6,7},{7,6},{8,9},{9,8},{10,11... | collective-permute-start | bytes 2359304 | tf_op jit(solution)/shard_map/ppermute | solution.py:35
  100.4 16.7 %collective-permute-start.27 = (bf16[64,3072]{1,0:T(8,128)(2,1)S(1)}, bf16[64,3072]{1,0:T(8,128)(2,1)S(1)}, u32[]{:S(2)}, u32[]{:S(2)}) collective-permute-start(bf16[64,3072]{1,0:T(8,128)(2,1)S(1)} %add_convert_fusion.1), channel_id=1, source_target_pairs={{0,2},{1,3},{2,4},{3,5},{4,6},{5,7},{6,0},{7,1},{8,10},{9,11},{10,... | collective-permute-start | bytes 1179656 | tf_op jit(solution)/shard_map/ppermute | solution.py:31
  101.2 15.8 %collective-permute-start.28 = (bf16[64,3072]{1,0:T(8,128)(2,1)S(1)}, bf16[64,3072]{1,0:T(8,128)(2,1)S(1)}, u32[]{:S(2)}, u32[]{:S(2)}) collective-permute-start(bf16[64,3072]{1,0:T(8,128)(2,1)S(1)} %add_convert_fusion), channel_id=1, source_target_pairs={{0,6},{1,7},{2,0},{3,1},{4,2},{5,3},{6,4},{7,5},{8,14},{9,15},{10,... | collective-permute-start | bytes 1179656 | tf_op jit(solution)/shard_map/ppermute | solution.py:31
Sparse Core Ops, SparseCore 0:
  9.5 70.1 all-gather.2

commit v11 on v9

--- a/solution.py
+++ b/solution.py
@@ -204,7 +204,7 @@
         out[:, m * width : (m + 1) * width] = part[i * 64 : (i + 1) * 64]
 
 
-def project_first_kernel(normed, w, own, sib, held, sems):
+def project_first_kernel(normed, w, own_low, sib_low, own_high, sib_high, held, sems):
     per = w.shape[0] // 4
     copies = [
         pltpu.make_async_copy(w.at[pl.ds(i * per, per)], held.at[pl.ds(i * per, per)], sems.at[i]) for i in range(4)
@@ -215,7 +215,8 @@
     for i in range(4):
         copies[i].wait()
         for m in range(i * per, (i + 1) * per):
-            project_part(far, held, (own, sib), m)
+            outs = (own_low, sib_low) if i < 2 else (own_high, sib_high)
+            project_part(far, held.at[pl.ds(i // 2 * 2 * per, 2 * per)], outs, m - i // 2 * 2 * per)
 
 
 def project_kernel(blocks, normed, w, *outs):
@@ -327,22 +328,22 @@
         2 * 512 * WIDE * SIZE,
     )
     vmem = pl.BlockSpec(memory_space=pltpu.VMEM)
-    half = jax.ShapeDtypeStruct((64, depth), bf16)
-    far_own, far_sib, w = pl.pallas_call(
+    half = jax.ShapeDtypeStruct((64, mid), bf16)
+    own_low, sib_low, own_high, sib_high, w = pl.pallas_call(
         project_first_kernel,
-        out_shape=[half, half, pltpu.VMEM(w_all.shape, bf16)],
+        out_shape=[half] * 4 + [pltpu.VMEM(w_all.shape, bf16)],
         in_specs=[vmem, pl.BlockSpec(memory_space=pltpu.HBM)],
-        out_specs=[vmem] * 3,
+        out_specs=[vmem] * 5,
         scratch_shapes=[pltpu.SemaphoreType.DMA((4,))],
         compiler_params=params(),
         cost_estimate=cost(256 * w_all.size, 2 * w_all.size),
         name="project",
     )(normed, pltpu.with_memory_space_constraint(w_all, pltpu.HBM))
 
-    far_sib = to_sibling(far_sib)
+    sib_low, sib_high = to_sibling(sib_low), to_sibling(sib_high)
     near_parts = project(normed, w, (0, 4, 1, 5))
-    far_sib = after(far_sib, near_parts)
-    far = plus(far_own[:, :mid], far_sib[:, :mid]), plus(far_own[:, mid:], far_sib[:, mid:])
+    sib_low, sib_high = after((sib_low, sib_high), near_parts)
+    far = plus(own_low, sib_low), plus(own_high, sib_high)
     from_l, from_r = to_y(far[0], 1), to_y(far[1], -1)
     up_own, up_sib, down_own, down_sib = after(near_parts, *far)
     up_sib, down_sib = to_sibling(up_sib), to_sibling(down_sib)

time: 125 us -> 125 us (level)
    ppermute x11 -> x12, starting transfers between devices: 8.38 us -> 8.57 us  [to_sibling(): return lax.ppermute(a, 'tp', [(i, i ^ 1) for i in range(2 * N_Y)])]
  transfers between devices with their start and end apart: 30 -> 31, of which waited for: 12 -> 12; matrix products, arithmetic and copies ran while one was open for 5% -> 5% of each run, Pallas kernels for 18% -> 18%
where the time goes in v11:
time: 125 us
  starting transfers between devices  39.9 us (32%)
  waiting for transfers between devices  36.4 us (29%)
  Pallas kernels  27 us (22%)
  between operations  13.7 us (11%)
  local copies, waits for them, and re-layouts  4.77 us (4%)
  other arithmetic  2.95 us (2%)
    ppermute x12, waiting for transfers between devices, to_y(): lax.ppermute(a, 'tp', [(i, (i // 2 + k) % N_Y * 2 + i % 2) for i in range...  23.3 us
    ppermute x12, starting transfers between devices, to_y(): lax.ppermute(a, 'tp', [(i, (i // 2 + k) % N_Y * 2 + i % 2) for i in range...  16.5 us
    pallas_call x4, Pallas kernels, qkv(): pl.pallas_call(functools.partial(qkv_first_kernel if first else qkv_kerne...  15.1 us
    ppermute x3, starting transfers between devices, to_z(): lax.ppermute(a, 'ctx', [(j, j + N_X * k) for j in range(N_X * N_Z) if j /...  9.34 us
    ppermute x3, waiting for transfers between devices, to_x(): lax.ppermute(a, 'ctx', [(j, j // N_X * N_X + (j + k) % N_X) for j in rang...  8.62 us
    ppermute x12, starting transfers between devices, to_sibling(): return lax.ppermute(a, 'tp', [(i, i ^ 1) for i in range(2 * N_Y)])  8.57 us
    ppermute x3, starting transfers between devices, to_x(): lax.ppermute(a, 'ctx', [(j, j // N_X * N_X + (j + k) % N_X) for j in rang...  5.53 us
    pallas_call x6, Pallas kernels, whole_call(): pl.pallas_call(kernel, out_shape=outs, in_specs=[pl.BlockSpec(memory_spac...  4.96 us
  transfers between devices with their start and end apart: 31, of which 12 were waited for; matrix products, arithmetic and copies ran while one was open for 5% of the time, Pallas kernels for 18%

profile of v11, /device:TPU:1, one launch (start us, length us, event | category | flops | bytes accessed | tf_op | source)
XLA Modules:
  0.0 124.7 jit_solution(11302116273539818548)
XLA Ops:
  6.5 0.7 all-gather.3.cloned.1.call-update
  7.3 1.5 %collective-permute-start.3 = (bf16[64,6144]{1,0:T(8,128)(2,1)}, bf16[64,6144]{1,0:T(8,128)(2,1)S(1)}, u32[]{:S(2)}, u32[]{:S(2)}) collective-permute-start(bf16[64,6144]{1,0:T(8,128)(2,1)} %refs_0_.1), channel_id=1, source_target_pairs={{0,1},{1,0},{2,3},{3,2},{4,5},{5,4},{6,7},{7,6},{8,9},{9,8},{10,11... | collective-permute-start | bytes 2359304 | tf_op jit(solution)/shard_map/ppermute | solution.py:35
  8.8 1.0 slice.63
  9.8 1.4 %collective-permute-start.1 = (bf16[64,3072]{1,0:T(8,128)(2,1)S(1)}, bf16[64,3072]{1,0:T(8,128)(2,1)S(1)}, u32[]{:S(2)}, u32[]{:S(2)}) collective-permute-start(bf16[64,3072]{1,0:T(8,128)(2,1)S(1)} %slice.63), channel_id=1, source_target_pairs={{0,2},{1,3},{2,4},{3,5},{4,6},{5,7},{6,0},{7,1},{8,10},{9,11},{10,... | collective-permute-start | bytes 1179656 | tf_op jit(solution)/shard_map/ppermute | solution.py:31
  11.2 1.0 slice.64
  12.3 1.5 %collective-permute-start.2 = (bf16[64,3072]{1,0:T(8,128)(2,1)S(1)}, bf16[64,3072]{1,0:T(8,128)(2,1)S(1)}, u32[]{:S(2)}, u32[]{:S(2)}) collective-permute-start(bf16[64,3072]{1,0:T(8,128)(2,1)S(1)} %slice.64), channel_id=1, source_target_pairs={{0,6},{1,7},{2,0},{3,1},{4,2},{5,3},{6,4},{7,5},{8,14},{9,15},{10,... | collective-permute-start | bytes 1179656 | tf_op jit(solution)/shard_map/ppermute | solution.py:31
  13.8 0.7 reshape.29
  14.5 1.2 reduce-window.6
  17.6 1.5 %collective-permute-start = (bf16[64,3072]{1,0:T(8,128)(2,1)S(1)}, bf16[64,3072]{1,0:T(8,128)(2,1)S(1)}, u32[]{:S(2)}, u32[]{:S(2)}) collective-permute-start(bf16[64,3072]{1,0:T(8,128)(2,1)S(1)} %slice.63), channel_id=1, source_target_pairs={{0,6},{1,7},{2,0},{3,1},{4,2},{5,3},{6,4},{7,5},{8,14},{9,15},{10,... | collective-permute-start | bytes 1179656 | tf_op jit(solution)/shard_map/ppermute | solution.py:31
  19.0 1.1 copy-done
  20.2 7.3 %qkv.4 = (bf16[128,1536]{1,0:T(8,128)(2,1)S(1)}, bf16[3,6144,512]{2,1,0:T(8,128)(2,1)S(1)}) custom-call(bf16[64,6144]{1,0:T(8,128)(2,1)S(1)} %copy-done, bf16[64,6144]{1,0:T(8,128)(2,1)S(1)} %collective-permute-done.3.refs_1_, bf16[3,6144,512]{2,1,0:T(8,128)(2,1)} %refs_2_.1), custom_call_target="tpu_custom_call" | custom-call | flops 24159192 | bytes 188743 | tf_op jit(solution)/shard_map/qkv/pallas_call | solution.py:97
  27.5 1.1 collective-permute-start.5
  28.8 2.3 %collective-permute-done.refs_0_ = bf16[64,3072]{1,0:T(8,128)(2,1)S(1)} collective-permute-done((bf16[64,3072]{1,0:T(8,128)(2,1)S(1)}, bf16[64,3072]{1,0:T(8,128)(2,1)S(1)}, u32[]{:S(2)}, u32[]{:S(2)}) %collective-permute-start) | collective-permute-done | bytes 393248 | tf_op jit(solution)/shard_map/ppermute | solution.py:31
  31.2 2.8 %collective-permute-start.10 = (bf16[64,3072]{1,0:T(8,128)(2,1)S(1)}, bf16[64,3072]{1,0:T(8,128)(2,1)S(1)}, u32[]{:S(2)}, u32[]{:S(2)}) collective-permute-start(bf16[64,3072]{1,0:T(8,128)(2,1)S(1)} %collective-permute-done.2.refs_1_), channel_id=1, source_target_pairs={{0,6},{1,7},{2,0},{3,1},{4,2},{5,3},{6,4},{7,5},{8,14},{9,15},{10,... | collective-permute-start | bytes 1179656 | tf_op jit(solution)/shard_map/ppermute | solution.py:31
  34.0 1.2 collective-permute-start.7
  35.3 2.6 %qkv.5.a = bf16[128,1536]{1,0:T(8,128)(2,1)S(1)} custom-call(bf16[64,3072]{1,0:T(8,128)(2,1)S(1)} %collective-permute-done.refs_0_, bf16[64,3072]{1,0:T(8,128)(2,1)S(1)} %collective-permute-done.2.refs_1_, bf16[64,3072]{1,0:T(8,128)(2,1)S(1)} %collective-permute-done.1.refs_2_, bf16[64,3072]{1,0:T(8,128)(2,1)S(1)} %collective-permute-done.4.refs_3_, ...), custom_call_target="tpu_custom_call" | custom-call | flops 24159192 | bytes 188743 | tf_op jit(solution)/shard_map/qkv/pallas_call | solution.py:97
  37.9 2.5 %collective-permute-done.9.refs_0_ = bf16[64,3072]{1,0:T(8,128)(2,1)S(1)} collective-permute-done((bf16[64,3072]{1,0:T(8,128)(2,1)S(1)}, bf16[64,3072]{1,0:T(8,128)(2,1)S(1)}, u32[]{:S(2)}, u32[]{:S(2)}) %collective-permute-start.9) | collective-permute-done | bytes 393248 | tf_op jit(solution)/shard_map/ppermute | solution.py:31
  40.4 1.0 collective-permute-done.10.refs_1_
  41.5 1.9 %collective-permute-start.11 = (bf16[64,3072]{1,0:T(8,128)(2,1)S(1)}, bf16[64,3072]{1,0:T(8,128)(2,1)S(1)}, u32[]{:S(2)}, u32[]{:S(2)}) collective-permute-start(bf16[64,3072]{1,0:T(8,128)(2,1)S(1)} %collective-permute-done.9.refs_0_), channel_id=1, source_target_pairs={{0,1},{1,0},{2,3},{3,2},{4,5},{5,4},{6,7},{7,6},{8,9},{9,8},{10,11... | collective-permute-start | bytes 1179656 | tf_op jit(solution)/shard_map/ppermute | solution.py:35
  43.3 2.6 %qkv.6.c = bf16[128,1536]{1,0:T(8,128)(2,1)S(1)} custom-call(bf16[64,3072]{1,0:T(8,128)(2,1)S(1)} %collective-permute-done.7.refs_0_, bf16[64,3072]{1,0:T(8,128)(2,1)S(1)} %collective-permute-done.6.refs_1_, bf16[64,3072]{1,0:T(8,128)(2,1)S(1)} %collective-permute-done.5.refs_2_, bf16[64,3072]{1,0:T(8,128)(2,1)S(1)} %collective-permute-done.8.refs_3_, ...), custom_call_target="tpu_custom_call" | custom-call | flops 24159192 | bytes 188743 | tf_op jit(solution)/shard_map/qkv/pallas_call | solution.py:97
  46.0 2.6 %qkv.7.d = bf16[128,1536]{1,0:T(8,128)(2,1)S(1)} custom-call(bf16[64,3072]{1,0:T(8,128)(2,1)S(1)} %collective-permute-done.9.refs_0_, bf16[64,3072]{1,0:T(8,128)(2,1)S(1)} %collective-permute-done.10.refs_1_, bf16[64,3072]{1,0:T(8,128)(2,1)S(1)} %collective-permute-done.11.refs_2_, bf16[64,3072]{1,0:T(8,128)(2,1)S(1)} %collective-permute-done.12.refs_3_, ...), custom_call_target="tpu_custom_call" | custom-call | flops 24159192 | bytes 188743 | tf_op jit(solution)/shard_map/qkv/pallas_call | solution.py:97
  48.6 1.0 state.1.s0
  49.6 2.9 %collective-permute-start.13 = (bf16[528,128]{1,0:T(8,128)(2,1)S(1)}, bf16[528,128]{1,0:T(8,128)(2,1)S(1)}, u32[]{:S(2)}, u32[]{:S(2)}) collective-permute-start(bf16[528,128]{1,0:T(8,128)(2,1)S(1)} %state.1.s0), channel_id=1, source_target_pairs={{0,16},{8,24},{16,0},{24,8},{32,48},{40,56},{48,32},{56,40},{64,80... | collective-permute-start | bytes 405512 | tf_op jit(solution)/shard_map/ppermute | solution.py:39
  52.8 2.4 %collective-permute-start.15 = (bf16[528,128]{1,0:T(8,128)(2,1)S(1)}, bf16[528,128]{1,0:T(8,128)(2,1)S(1)}, u32[]{:S(2)}, u32[]{:S(2)}) collective-permute-start(bf16[528,128]{1,0:T(8,128)(2,1)S(1)} %state.1.s0), channel_id=1, source_target_pairs={{0,24},{8,0},{16,8},{24,16},{32,56},{40,32},{48,40},{56,48},{64,88... | collective-permute-start | bytes 405512 | tf_op jit(solution)/shard_map/ppermute | solution.py:39
  55.3 1.4 %inner.1 = f32[512,512]{1,0:T(8,128)S(1)} custom-call(bf16[128,1536]{1,0:T(8,128)(2,1)S(1)} %qkv.5.a, bf16[128,1536]{1,0:T(8,128)(2,1)S(1)} %get-tuple-element.56.b, bf16[128,1536]{1,0:T(8,128)(2,1)S(1)} %qkv.6.c, bf16[128,1536]{1,0:T(8,128)(2,1)S(1)} %qkv.7.d, f32[512,4]{1,0:T(8,128)S(1)} %bitcast.20, f32[4,512]{1,0:T(4,128)S(1)} %concatenate.8.gt, ...), custom_call_target="tpu_custom_call" | custom-call | flops 5368709 | bytes 15933 | tf_op jit(solution)/shard_map/inner/pallas_call | solution.py:188
  56.8 2.6 %collective-permute-done.13.s2 = bf16[528,128]{1,0:T(8,128)(2,1)S(1)} collective-permute-done((bf16[528,128]{1,0:T(8,128)(2,1)S(1)}, bf16[528,128]{1,0:T(8,128)(2,1)S(1)}, u32[]{:S(2)}, u32[]{:S(2)}) %collective-permute-start.13) | collective-permute-done | bytes 135200 | tf_op jit(solution)/shard_map/ppermute | solution.py:39
  59.4 4.9 %collective-permute-done.14.s1 = bf16[528,128]{1,0:T(8,128)(2,1)S(1)} collective-permute-done((bf16[528,128]{1,0:T(8,128)(2,1)S(1)}, bf16[528,128]{1,0:T(8,128)(2,1)S(1)}, u32[]{:S(2)}, u32[]{:S(2)}) %collective-permute-start.14) | collective-permute-done | bytes 135200 | tf_op jit(solution)/shard_map/ppermute | solution.py:39
  64.2 1.2 collective-permute-done.15.s3
  65.6 5.4 %collective-permute-start.16 = (bf16[528,128]{1,0:T(8,128)(2,1)S(1)}, bf16[528,128]{1,0:T(8,128)(2,1)S(1)}, u32[]{:S(2)}, u32[]{:S(2)}) collective-permute-start(bf16[528,128]{1,0:T(8,128)(2,1)S(1)} %get-tuple-element.78), channel_id=1, source_target_pairs={{0,64},{8,72},{16,80},{24,88},{32,96},{40,104},{48,112},{56,120},{... | collective-permute-start | bytes 405512 | tf_op jit(solution)/shard_map/ppermute | solution.py:43
  71.0 2.6 %collective-permute-start.17 = (bf16[528,128]{1,0:T(8,128)(2,1)S(1)}, bf16[528,128]{1,0:T(8,128)(2,1)S(1)}, u32[]{:S(2)}, u32[]{:S(2)}) collective-permute-start(bf16[528,128]{1,0:T(8,128)(2,1)S(1)} %get-tuple-element.78), channel_id=1, source_target_pairs={{0,32},{8,40},{16,48},{24,56},{32,64},{40,72},{48,80},{56,88},{64,... | collective-permute-start | bytes 405512 | tf_op jit(solution)/shard_map/ppermute | solution.py:43
  73.6 1.3 %collective-permute-start.18 = (bf16[528,128]{1,0:T(8,128)(2,1)S(1)}, bf16[528,128]{1,0:T(8,128)(2,1)S(1)}, u32[]{:S(2)}, u32[]{:S(2)}) collective-permute-start(bf16[528,128]{1,0:T(8,128)(2,1)S(1)} %get-tuple-element.78), channel_id=1, source_target_pairs={{0,96},{8,104},{16,112},{24,120},{1,97},{9,105},{17,113},{25,121},... | collective-permute-start | bytes 405512 | tf_op jit(solution)/shard_map/ppermute | solution.py:43
  74.9 1.1 collective-permute-done.17.t1
  76.1 1.0 collective-permute-done.18.t3
  77.1 1.0 normed.1
  78.1 1.5 %all-gather.3.cloned.1.call-done = bf16[8192,384]{1,0:T(8,128)(2,1)} async-done(((bf16[512,384]{1,0:T(8,128)(2,1)}), bf16[8192,384]{1,0:T(8,128)(2,1)}) %all-gather.3.cloned.1.call-update) | async-done | bytes 6291472 | tf_op jit(solution)/shard_map/all_gather | solution.py:272
  79.7 3.3 %project.3 = (bf16[64,3072]{1,0:T(8,128)(2,1)S(1)}, bf16[64,3072]{1,0:T(8,128)(2,1)S(1)}, bf16[64,3072]{1,0:T(8,128)(2,1)S(1)}, bf16[64,3072]{1,0:T(8,128)(2,1)S(1)}, bf16[16,512,384]{2,1,0:T(8,128)(2,1)S(1)}) custom-call(bf16[512,512]{1,0:T(8,128)(2,1)S(1)} %normed.1, bf16[16,512,384]{2,1,0:T(8,128)(2,1)} %bitcast.25), custom_call_target="tpu_custom_call" | custom-call | flops 8053063 | bytes 62914 | tf_op jit(solution)/shard_map/project/pallas_call | solution.py:332
  83.0 0.8 collective-permute-start.19
  84.1 2.3 %project.4 = (bf16[64,6144]{1,0:T(8,128)(2,1)S(1)}, bf16[64,6144]{1,0:T(8,128)(2,1)S(1)}, bf16[64,6144]{1,0:T(8,128)(2,1)S(1)}, bf16[64,6144]{1,0:T(8,128)(2,1)S(1)}) custom-call(bf16[512,512]{1,0:T(8,128)(2,1)S(1)} %normed.1, bf16[16,512,384]{2,1,0:T(8,128)(2,1)S(1)} %get-tuple-element.79.w), custom_call_target="tpu_custom_call" | custom-call | flops 16106127 | bytes 62914 | tf_op jit(solution)/shard_map/project/pallas_call | solution.py:232
  87.2 1.2 collective-permute-start.26
  88.4 2.2 %collective-permute-start.27 = (bf16[64,3072]{1,0:T(8,128)(2,1)S(1)}, bf16[64,3072]{1,0:T(8,128)(2,1)S(1)}, u32[]{:S(2)}, u32[]{:S(2)}) collective-permute-start(bf16[64,3072]{1,0:T(8,128)(2,1)S(1)} %add_convert_fusion.4), channel_id=1, source_target_pairs={{0,6},{1,7},{2,0},{3,1},{4,2},{5,3},{6,4},{7,5},{8,14},{9,15},{10,... | collective-permute-start | bytes 1179656 | tf_op jit(solution)/shard_map/ppermute | solution.py:31
  91.0 2.8 %collective-permute-start.25 = (bf16[64,3072]{1,0:T(8,128)(2,1)S(1)}, bf16[64,3072]{1,0:T(8,128)(2,1)S(1)}, u32[]{:S(2)}, u32[]{:S(2)}) collective-permute-start(bf16[64,3072]{1,0:T(8,128)(2,1)S(1)} %add_convert_fusion.2), channel_id=1, source_target_pairs={{0,6},{1,7},{2,0},{3,1},{4,2},{5,3},{6,4},{7,5},{8,14},{9,15},{10,... | collective-permute-start | bytes 1179656 | tf_op jit(solution)/shard_map/ppermute | solution.py:31
  93.7 1.2 %project.5 = (bf16[64,6144]{1,0:T(8,128)(2,1)S(1)}, bf16[64,6144]{1,0:T(8,128)(2,1)S(1)}) custom-call(bf16[512,512]{1,0:T(8,128)(2,1)S(1)} %normed.1, bf16[16,512,384]{2,1,0:T(8,128)(2,1)S(1)} %get-tuple-element.79.w), custom_call_target="tpu_custom_call" | custom-call | flops 8053063 | bytes 62914 | tf_op jit(solution)/shard_map/project/pallas_call | solution.py:232
  95.0 1.1 collective-permute-start.23
  96.0 4.0 %collective-permute-done.26 = bf16[64,3072]{1,0:T(8,128)(2,1)S(1)} collective-permute-done((bf16[64,3072]{1,0:T(8,128)(2,1)S(1)}, bf16[64,3072]{1,0:T(8,128)(2,1)S(1)}, u32[]{:S(2)}, u32[]{:S(2)}) %collective-permute-start.26) | collective-permute-done | bytes 393248 | tf_op jit(solution)/shard_map/ppermute | solution.py:31
  100.9 2.2 %collective-permute-start.29 = (bf16[64,3072]{1,0:T(8,128)(2,1)S(1)}, bf16[64,3072]{1,0:T(8,128)(2,1)S(1)}, u32[]{:S(2)}, u32[]{:S(2)}) collective-permute-start(bf16[64,3072]{1,0:T(8,128)(2,1)S(1)} %add_convert_fusion), channel_id=1, source_target_pairs={{0,6},{1,7},{2,0},{3,1},{4,2},{5,3},{6,4},{7,5},{8,14},{9,15},{10,... | collective-permute-start | bytes 1179656 | tf_op jit(solution)/shard_map/ppermute | solution.py:31
  103.1 5.3 %collective-permute-done.24.up_plain = bf16[64,3072]{1,0:T(8,128)(2,1)S(1)} collective-permute-done((bf16[64,3072]{1,0:T(8,128)(2,1)S(1)}, bf16[64,3072]{1,0:T(8,128)(2,1)S(1)}, u32[]{:S(2)}, u32[]{:S(2)}) %collective-permute-start.24) | collective-permute-done | bytes 393248 | tf_op jit(solution)/shard_map/ppermute | solution.py:31
  108.7 8.2 %collective-permute-done.28.up_sum = bf16[64,3072]{1,0:T(8,128)(2,1)S(1)} collective-permute-done((bf16[64,3072]{1,0:T(8,128)(2,1)S(1)}, bf16[64,3072]{1,0:T(8,128)(2,1)S(1)}, u32[]{:S(2)}, u32[]{:S(2)}) %collective-permute-start.28) | collective-permute-done | bytes 393248 | tf_op jit(solution)/shard_map/ppermute | solution.py:31
  116.9 1.0 final.1
  (57 shorter events, 5.4 us)
Async XLA Ops:
  6.5 73.2 %all-gather.3.cloned.1.call-start = ((), (), s32[]{:S(2)}) async-start(), calls=%async_computation | async-start | bytes 6684672 | tf_op jit(solution)/shard_map/all_gather | solution.py:272
  7.3 11.8 %collective-permute-start.3 = (bf16[64,6144]{1,0:T(8,128)(2,1)}, bf16[64,6144]{1,0:T(8,128)(2,1)S(1)}, u32[]{:S(2)}, u32[]{:S(2)}) collective-permute-start(bf16[64,6144]{1,0:T(8,128)(2,1)} %refs_0_.1), channel_id=1, source_target_pairs={{0,1},{1,0},{2,3},{3,2},{4,5},{5,4},{6,7},{7,6},{8,9},{9,8},{10,11... | collective-permute-start | bytes 2359304 | tf_op jit(solution)/shard_map/ppermute | solution.py:35
  9.8 17.7 %collective-permute-start.1 = (bf16[64,3072]{1,0:T(8,128)(2,1)S(1)}, bf16[64,3072]{1,0:T(8,128)(2,1)S(1)}, u32[]{:S(2)}, u32[]{:S(2)}) collective-permute-start(bf16[64,3072]{1,0:T(8,128)(2,1)S(1)} %slice.63), channel_id=1, source_target_pairs={{0,2},{1,3},{2,4},{3,5},{4,6},{5,7},{6,0},{7,1},{8,10},{9,11},{10,... | collective-permute-start | bytes 1179656 | tf_op jit(solution)/shard_map/ppermute | solution.py:31
  12.3 15.3 %collective-permute-start.2 = (bf16[64,3072]{1,0:T(8,128)(2,1)S(1)}, bf16[64,3072]{1,0:T(8,128)(2,1)S(1)}, u32[]{:S(2)}, u32[]{:S(2)}) collective-permute-start(bf16[64,3072]{1,0:T(8,128)(2,1)S(1)} %slice.64), channel_id=1, source_target_pairs={{0,6},{1,7},{2,0},{3,1},{4,2},{5,3},{6,4},{7,5},{8,14},{9,15},{10,... | collective-permute-start | bytes 1179656 | tf_op jit(solution)/shard_map/ppermute | solution.py:31
  17.6 13.6 %collective-permute-start = (bf16[64,3072]{1,0:T(8,128)(2,1)S(1)}, bf16[64,3072]{1,0:T(8,128)(2,1)S(1)}, u32[]{:S(2)}, u32[]{:S(2)}) collective-permute-start(bf16[64,3072]{1,0:T(8,128)(2,1)S(1)} %slice.63), channel_id=1, source_target_pairs={{0,6},{1,7},{2,0},{3,1},{4,2},{5,3},{6,4},{7,5},{8,14},{9,15},{10,... | collective-permute-start | bytes 1179656 | tf_op jit(solution)/shard_map/ppermute | solution.py:31
  19.0 15.0 %collective-permute-start.4 = (bf16[64,3072]{1,0:T(8,128)(2,1)S(1)}, bf16[64,3072]{1,0:T(8,128)(2,1)S(1)}, u32[]{:S(2)}, u32[]{:S(2)}) collective-permute-start(bf16[64,3072]{1,0:T(8,128)(2,1)S(1)} %slice.64), channel_id=1, source_target_pairs={{0,2},{1,3},{2,4},{3,5},{4,6},{5,7},{6,0},{7,1},{8,10},{9,11},{10,... | collective-permute-start | bytes 1179656 | tf_op jit(solution)/shard_map/ppermute | solution.py:31
  19.0 1.1 copy-start
  27.5 7.7 %collective-permute-start.5 = (bf16[64,3072]{1,0:T(8,128)(2,1)S(1)}, bf16[64,3072]{1,0:T(8,128)(2,1)S(1)}, u32[]{:S(2)}, u32[]{:S(2)}) collective-permute-start(bf16[64,3072]{1,0:T(8,128)(2,1)S(1)} %collective-permute-done.1.refs_2_), channel_id=1, source_target_pairs={{0,1},{1,0},{2,3},{3,2},{4,5},{5,4},{6,7},{7,6},{8,9},{9,8},{10,11... | collective-permute-start | bytes 1179656 | tf_op jit(solution)/shard_map/ppermute | solution.py:35
  28.6 6.7 %collective-permute-start.6 = (bf16[64,3072]{1,0:T(8,128)(2,1)S(1)}, bf16[64,3072]{1,0:T(8,128)(2,1)S(1)}, u32[]{:S(2)}, u32[]{:S(2)}) collective-permute-start(bf16[64,3072]{1,0:T(8,128)(2,1)S(1)} %collective-permute-done.2.refs_1_), channel_id=1, source_target_pairs={{0,1},{1,0},{2,3},{3,2},{4,5},{5,4},{6,7},{7,6},{8,9},{9,8},{10,11... | collective-permute-start | bytes 1179656 | tf_op jit(solution)/shard_map/ppermute | solution.py:35
  28.7 11.8 %collective-permute-start.9 = (bf16[64,3072]{1,0:T(8,128)(2,1)S(1)}, bf16[64,3072]{1,0:T(8,128)(2,1)S(1)}, u32[]{:S(2)}, u32[]{:S(2)}) collective-permute-start(bf16[64,3072]{1,0:T(8,128)(2,1)S(1)} %collective-permute-done.1.refs_2_), channel_id=1, source_target_pairs={{0,2},{1,3},{2,4},{3,5},{4,6},{5,7},{6,0},{7,1},{8,10},{9,11},{10,... | collective-permute-start | bytes 1179656 | tf_op jit(solution)/shard_map/ppermute | solution.py:31
  31.2 10.3 %collective-permute-start.10 = (bf16[64,3072]{1,0:T(8,128)(2,1)S(1)}, bf16[64,3072]{1,0:T(8,128)(2,1)S(1)}, u32[]{:S(2)}, u32[]{:S(2)}) collective-permute-start(bf16[64,3072]{1,0:T(8,128)(2,1)S(1)} %collective-permute-done.2.refs_1_), channel_id=1, source_target_pairs={{0,6},{1,7},{2,0},{3,1},{4,2},{5,3},{6,4},{7,5},{8,14},{9,15},{10,... | collective-permute-start | bytes 1179656 | tf_op jit(solution)/shard_map/ppermute | solution.py:31
  34.0 9.3 %collective-permute-start.7 = (bf16[64,3072]{1,0:T(8,128)(2,1)S(1)}, bf16[64,3072]{1,0:T(8,128)(2,1)S(1)}, u32[]{:S(2)}, u32[]{:S(2)}) collective-permute-start(bf16[64,3072]{1,0:T(8,128)(2,1)S(1)} %collective-permute-done.refs_0_), channel_id=1, source_target_pairs={{0,1},{1,0},{2,3},{3,2},{4,5},{5,4},{6,7},{7,6},{8,9},{9,8},{10,11... | collective-permute-start | bytes 1179656 | tf_op jit(solution)/shard_map/ppermute | solution.py:35
  35.2 8.1 %collective-permute-start.8 = (bf16[64,3072]{1,0:T(8,128)(2,1)S(1)}, bf16[64,3072]{1,0:T(8,128)(2,1)S(1)}, u32[]{:S(2)}, u32[]{:S(2)}) collective-permute-start(bf16[64,3072]{1,0:T(8,128)(2,1)S(1)} %collective-permute-done.4.refs_3_), channel_id=1, source_target_pairs={{0,1},{1,0},{2,3},{3,2},{4,5},{5,4},{6,7},{7,6},{8,9},{9,8},{10,11... | collective-permute-start | bytes 1179656 | tf_op jit(solution)/shard_map/ppermute | solution.py:35
  41.5 4.5 %collective-permute-start.11 = (bf16[64,3072]{1,0:T(8,128)(2,1)S(1)}, bf16[64,3072]{1,0:T(8,128)(2,1)S(1)}, u32[]{:S(2)}, u32[]{:S(2)}) collective-permute-start(bf16[64,3072]{1,0:T(8,128)(2,1)S(1)} %collective-permute-done.9.refs_0_), channel_id=1, source_target_pairs={{0,1},{1,0},{2,3},{3,2},{4,5},{5,4},{6,7},{7,6},{8,9},{9,8},{10,11... | collective-permute-start | bytes 1179656 | tf_op jit(solution)/shard_map/ppermute | solution.py:35
  43.3 2.7 %collective-permute-start.12 = (bf16[64,3072]{1,0:T(8,128)(2,1)S(1)}, bf16[64,3072]{1,0:T(8,128)(2,1)S(1)}, u32[]{:S(2)}, u32[]{:S(2)}) collective-permute-start(bf16[64,3072]{1,0:T(8,128)(2,1)S(1)} %collective-permute-done.10.refs_1_), channel_id=1, source_target_pairs={{0,1},{1,0},{2,3},{3,2},{4,5},{5,4},{6,7},{7,6},{8,9},{9,8},{10,11... | collective-permute-start | bytes 1179656 | tf_op jit(solution)/shard_map/ppermute | solution.py:35
  46.0 31.1 %copy-start.1 = (f32[512]{0:T(512)S(1)}, f32[512]{0:T(512)}, u32[]{:S(2)}) copy-start(f32[512]{0:T(512)} %param.10) | copy-start | bytes 6148
  49.6 9.7 %collective-permute-start.13 = (bf16[528,128]{1,0:T(8,128)(2,1)S(1)}, bf16[528,128]{1,0:T(8,128)(2,1)S(1)}, u32[]{:S(2)}, u32[]{:S(2)}) collective-permute-start(bf16[528,128]{1,0:T(8,128)(2,1)S(1)} %state.1.s0), channel_id=1, source_target_pairs={{0,16},{8,24},{16,0},{24,8},{32,48},{40,56},{48,32},{56,40},{64,80... | collective-permute-start | bytes 405512 | tf_op jit(solution)/shard_map/ppermute | solution.py:39
  52.5 11.7 %collective-permute-start.14 = (bf16[528,128]{1,0:T(8,128)(2,1)S(1)}, bf16[528,128]{1,0:T(8,128)(2,1)S(1)}, u32[]{:S(2)}, u32[]{:S(2)}) collective-permute-start(bf16[528,128]{1,0:T(8,128)(2,1)S(1)} %state.1.s0), channel_id=1, source_target_pairs={{0,8},{8,16},{16,24},{24,0},{32,40},{40,48},{48,56},{56,32},{64,72... | collective-permute-start | bytes 405512 | tf_op jit(solution)/shard_map/ppermute | solution.py:39
  52.8 12.6 %collective-permute-start.15 = (bf16[528,128]{1,0:T(8,128)(2,1)S(1)}, bf16[528,128]{1,0:T(8,128)(2,1)S(1)}, u32[]{:S(2)}, u32[]{:S(2)}) collective-permute-start(bf16[528,128]{1,0:T(8,128)(2,1)S(1)} %state.1.s0), channel_id=1, source_target_pairs={{0,24},{8,0},{16,8},{24,16},{32,56},{40,32},{48,40},{56,48},{64,88... | collective-permute-start | bytes 405512 | tf_op jit(solution)/shard_map/ppermute | solution.py:39
  65.6 9.4 %collective-permute-start.16 = (bf16[528,128]{1,0:T(8,128)(2,1)S(1)}, bf16[528,128]{1,0:T(8,128)(2,1)S(1)}, u32[]{:S(2)}, u32[]{:S(2)}) collective-permute-start(bf16[528,128]{1,0:T(8,128)(2,1)S(1)} %get-tuple-element.78), channel_id=1, source_target_pairs={{0,64},{8,72},{16,80},{24,88},{32,96},{40,104},{48,112},{56,120},{... | collective-permute-start | bytes 405512 | tf_op jit(solution)/shard_map/ppermute | solution.py:43
  71.0 5.1 %collective-permute-start.17 = (bf16[528,128]{1,0:T(8,128)(2,1)S(1)}, bf16[528,128]{1,0:T(8,128)(2,1)S(1)}, u32[]{:S(2)}, u32[]{:S(2)}) collective-permute-start(bf16[528,128]{1,0:T(8,128)(2,1)S(1)} %get-tuple-element.78), channel_id=1, source_target_pairs={{0,32},{8,40},{16,48},{24,56},{32,64},{40,72},{48,80},{56,88},{64,... | collective-permute-start | bytes 405512 | tf_op jit(solution)/shard_map/ppermute | solution.py:43
  73.6 3.5 %collective-permute-start.18 = (bf16[528,128]{1,0:T(8,128)(2,1)S(1)}, bf16[528,128]{1,0:T(8,128)(2,1)S(1)}, u32[]{:S(2)}, u32[]{:S(2)}) collective-permute-start(bf16[528,128]{1,0:T(8,128)(2,1)S(1)} %get-tuple-element.78), channel_id=1, source_target_pairs={{0,96},{8,104},{16,112},{24,120},{1,97},{9,105},{17,113},{25,121},... | collective-permute-start | bytes 405512 | tf_op jit(solution)/shard_map/ppermute | solution.py:43
  83.0 3.4 %collective-permute-start.19 = (bf16[64,3072]{1,0:T(8,128)(2,1)S(1)}, bf16[64,3072]{1,0:T(8,128)(2,1)S(1)}, u32[]{:S(2)}, u32[]{:S(2)}) collective-permute-start(bf16[64,3072]{1,0:T(8,128)(2,1)S(1)} %get-tuple-element.85), channel_id=1, source_target_pairs={{0,1},{1,0},{2,3},{3,2},{4,5},{5,4},{6,7},{7,6},{8,9},{9,8},{10,11... | collective-permute-start | bytes 1179656 | tf_op jit(solution)/shard_map/ppermute | solution.py:35
  83.8 2.7 %collective-permute-start.20 = (bf16[64,3072]{1,0:T(8,128)(2,1)S(1)}, bf16[64,3072]{1,0:T(8,128)(2,1)S(1)}, u32[]{:S(2)}, u32[]{:S(2)}) collective-permute-start(bf16[64,3072]{1,0:T(8,128)(2,1)S(1)} %get-tuple-element.86), channel_id=1, source_target_pairs={{0,1},{1,0},{2,3},{3,2},{4,5},{5,4},{6,7},{7,6},{8,9},{9,8},{10,11... | collective-permute-start | bytes 1179656 | tf_op jit(solution)/shard_map/ppermute | solution.py:35
  86.6 4.0 %collective-permute-start.21 = (bf16[64,6144]{1,0:T(8,128)(2,1)S(1)}, bf16[64,6144]{1,0:T(8,128)(2,1)S(1)}, u32[]{:S(2)}, u32[]{:S(2)}) collective-permute-start(bf16[64,6144]{1,0:T(8,128)(2,1)S(1)} %get-tuple-element.91), channel_id=1, source_target_pairs={{0,1},{1,0},{2,3},{3,2},{4,5},{5,4},{6,7},{7,6},{8,9},{9,8},{10,11... | collective-permute-start | bytes 2359304 | tf_op jit(solution)/shard_map/ppermute | solution.py:35
  86.9 3.9 %collective-permute-start.22 = (bf16[64,6144]{1,0:T(8,128)(2,1)S(1)}, bf16[64,6144]{1,0:T(8,128)(2,1)S(1)}, u32[]{:S(2)}, u32[]{:S(2)}) collective-permute-start(bf16[64,6144]{1,0:T(8,128)(2,1)S(1)} %get-tuple-element.93), channel_id=1, source_target_pairs={{0,1},{1,0},{2,3},{3,2},{4,5},{5,4},{6,7},{7,6},{8,9},{9,8},{10,11... | collective-permute-start | bytes 2359304 | tf_op jit(solution)/shard_map/ppermute | solution.py:35
  87.2 12.8 %collective-permute-start.26 = (bf16[64,3072]{1,0:T(8,128)(2,1)S(1)}, bf16[64,3072]{1,0:T(8,128)(2,1)S(1)}, u32[]{:S(2)}, u32[]{:S(2)}) collective-permute-start(bf16[64,3072]{1,0:T(8,128)(2,1)S(1)} %add_convert_fusion.5), channel_id=1, source_target_pairs={{0,2},{1,3},{2,4},{3,5},{4,6},{5,7},{6,0},{7,1},{8,10},{9,11},{10,... | collective-permute-start | bytes 1179656 | tf_op jit(solution)/shard_map/ppermute | solution.py:31
  88.4 11.6 %collective-permute-start.27 = (bf16[64,3072]{1,0:T(8,128)(2,1)S(1)}, bf16[64,3072]{1,0:T(8,128)(2,1)S(1)}, u32[]{:S(2)}, u32[]{:S(2)}) collective-permute-start(bf16[64,3072]{1,0:T(8,128)(2,1)S(1)} %add_convert_fusion.4), channel_id=1, source_target_pairs={{0,6},{1,7},{2,0},{3,1},{4,2},{5,3},{6,4},{7,5},{8,14},{9,15},{10,... | collective-permute-start | bytes 1179656 | tf_op jit(solution)/shard_map/ppermute | solution.py:31
  90.8 17.7 %collective-permute-start.24 = (bf16[64,3072]{1,0:T(8,128)(2,1)S(1)}, bf16[64,3072]{1,0:T(8,128)(2,1)S(1)}, u32[]{:S(2)}, u32[]{:S(2)}) collective-permute-start(bf16[64,3072]{1,0:T(8,128)(2,1)S(1)} %add_convert_fusion.3), channel_id=1, source_target_pairs={{0,2},{1,3},{2,4},{3,5},{4,6},{5,7},{6,0},{7,1},{8,10},{9,11},{10,... | collective-permute-start | bytes 1179656 | tf_op jit(solution)/shard_map/ppermute | solution.py:31
  91.0 17.5 %collective-permute-start.25 = (bf16[64,3072]{1,0:T(8,128)(2,1)S(1)}, bf16[64,3072]{1,0:T(8,128)(2,1)S(1)}, u32[]{:S(2)}, u32[]{:S(2)}) collective-permute-start(bf16[64,3072]{1,0:T(8,128)(2,1)S(1)} %add_convert_fusion.2), channel_id=1, source_target_pairs={{0,6},{1,7},{2,0},{3,1},{4,2},{5,3},{6,4},{7,5},{8,14},{9,15},{10,... | collective-permute-start | bytes 1179656 | tf_op jit(solution)/shard_map/ppermute | solution.py:31
  95.0 13.5 %collective-permute-start.23 = (bf16[64,6144]{1,0:T(8,128)(2,1)S(1)}, bf16[64,6144]{1,0:T(8,128)(2,1)S(1)}, u32[]{:S(2)}, u32[]{:S(2)}) collective-permute-start(bf16[64,6144]{1,0:T(8,128)(2,1)S(1)} %get-tuple-element.96), channel_id=1, source_target_pairs={{0,1},{1,0},{2,3},{3,2},{4,5},{5,4},{6,7},{7,6},{8,9},{9,8},{10,11... | collective-permute-start | bytes 2359304 | tf_op jit(solution)/shard_map/ppermute | solution.py:35
  100.2 16.7 %collective-permute-start.28 = (bf16[64,3072]{1,0:T(8,128)(2,1)S(1)}, bf16[64,3072]{1,0:T(8,128)(2,1)S(1)}, u32[]{:S(2)}, u32[]{:S(2)}) collective-permute-start(bf16[64,3072]{1,0:T(8,128)(2,1)S(1)} %add_convert_fusion.1), channel_id=1, source_target_pairs={{0,2},{1,3},{2,4},{3,5},{4,6},{5,7},{6,0},{7,1},{8,10},{9,11},{10,... | collective-permute-start | bytes 1179656 | tf_op jit(solution)/shard_map/ppermute | solution.py:31
  100.9 16.0 %collective-permute-start.29 = (bf16[64,3072]{1,0:T(8,128)(2,1)S(1)}, bf16[64,3072]{1,0:T(8,128)(2,1)S(1)}, u32[]{:S(2)}, u32[]{:S(2)}) collective-permute-start(bf16[64,3072]{1,0:T(8,128)(2,1)S(1)} %add_convert_fusion), channel_id=1, source_target_pairs={{0,6},{1,7},{2,0},{3,1},{4,2},{5,3},{6,4},{7,5},{8,14},{9,15},{10,... | collective-permute-start | bytes 1179656 | tf_op jit(solution)/shard_map/ppermute | solution.py:31
Sparse Core Ops, SparseCore 0:
  9.5 70.1 all-gather.2
